TPU v7x, 128 devices: a whole 4x4x4 slice. The times are simulated.
128 devices in a mesh: grp: 8 (over x, core), tp: 16 (over z, y).
Axes of the slice: x: 4, y: 4, z: 4, core: 2. Of those that a mesh axis runs over, the one named last changes fastest.
Arguments:
- activations: bfloat16 [4096, 8192], P('grp', 'tp'), may hold values from -6 to 6
- output_gradient: bfloat16 [4096, 8192], P('grp', 'tp'), may hold values from -6 to 6
- frozen_weight: bfloat16 [8192, 8192], P(None, 'tp'), may hold values from -0.0625 to 0.0625
- adapter_down_factors: bfloat16 [128, 32, 8192], P('grp', None, 'tp'), may hold values from -6 to 6
- adapter_up_factors: bfloat16 [128, 32, 8192], P('grp', None, 'tp'), may hold values from -6 to 6
- first_moment_down: float32 [128, 32, 8192], P('grp', None, 'tp'), may hold values from -6 to 6
- second_moment_down: float32 [128, 32, 8192], P('grp', None, 'tp'), may hold values from 0.5 to 2
- first_moment_up: float32 [128, 32, 8192], P('grp', None, 'tp'), may hold values from -6 to 6
- second_moment_up: float32 [128, 32, 8192], P('grp', None, 'tp'), may hold values from 0.5 to 2
- sample_row_prompt: int32 [8, 512], P('grp'), may hold values from 0 to 15, never falling along the last dimension, each value on 1 to 128 neighbouring positions
- majority_vote_reward: int32 [8, 512], P('grp'), may hold values 0 or 1
- prompt_adapter_slot: int32 [128], replicated, may hold values from 0 to 127, as said below
Outputs:
- layer_out: bfloat16 [4096, 8192], P('grp', 'tp')
- input_grad: bfloat16 [4096, 8192], P('grp', 'tp')
- updated_down_factors: bfloat16 [128, 32, 8192], P('grp', None, 'tp')
- updated_up_factors: bfloat16 [128, 32, 8192], P('grp', None, 'tp')
- updated_first_down: float32 [128, 32, 8192], P('grp', None, 'tp')
- updated_second_down: float32 [128, 32, 8192], P('grp', None, 'tp')
- updated_first_up: float32 [128, 32, 8192], P('grp', None, 'tp')
- updated_second_up: float32 [128, 32, 8192], P('grp', None, 'tp')
Inputs may be any that keep to these rules, and one draw needn't show every extreme that they name: `prompt_adapter_slot`: A permutation. Slots g * 16 to (g + 1) * 16 - 1 lie in group g's shard, and each group's shard holds the slots of exactly 2 prompts of every group.
All inputs are finite; a program needn't handle non-finite values. No bound on the sum of `majority_vote_reward` on one device may be relied on, other than what follows from the above.
Results may differ from a plain program's by a relative error of at most 0.0056.
Values may be sent and summed in bfloat16 or wider, within the bound.
No kernel may reach another device: no remote copies, remote signals or barrier semaphores. Data moves between devices by JAX's collectives and lax.ppermute only.
A program may use at most 192 MiB of HBM per device.

v0:
```python
import jax
import jax.numpy as jnp
from jax import lax
from jax.sharding import PartitionSpec as P

beta_first = 0.9
beta_second = 0.999
step_rate = 0.2
adam_eps = 1e-08
adapter_scale = 2.0


def moment_step_update(param, moment, second, grad):
    moment_new = beta_first * moment + (1.0 - beta_first) * grad
    second_new = beta_second * second + (1.0 - beta_second) * grad * grad
    param_new = param.astype(jnp.float32) - step_rate * moment_new / (
        jnp.sqrt(second_new) + adam_eps
    )
    return (param_new.astype(jnp.bfloat16), moment_new, second_new)


def local(
    activations,
    output_gradient,
    frozen_weight,
    adapter_down_factors,
    adapter_up_factors,
    first_moment_down,
    second_moment_down,
    first_moment_up,
    second_moment_up,
    sample_row_prompt,
    majority_vote_reward,
    prompt_adapter_slot,
):
    width = frozen_weight.shape[0]
    local_width = frozen_weight.shape[1]
    row_count = activations.shape[0]
    adapter_slot_count = adapter_down_factors.shape[0]
    adapter_rank_size = adapter_down_factors.shape[1]
    prompt_count = prompt_adapter_slot.shape[0]
    member = lax.axis_index("grp")
    scale_down = width ** (-0.5)
    scaled_up_factors = adapter_scale / adapter_rank_size**0.5
    contract_cols = (((1,), (1,)), ((), ()))
    contract_rows = (((0,), (0,)), ((), ()))
    labels = sample_row_prompt[0]
    onehot = (labels[:, None] == jnp.arange(adapter_slot_count, dtype=jnp.int32)[None, :]).astype(
        jnp.float32
    )
    reward = majority_vote_reward[0].astype(jnp.float32)
    counts = jnp.sum(onehot, axis=0)
    mean_reward = jnp.sum(onehot * reward[:, None], axis=0) / counts
    advantage = reward - jnp.sum(onehot * mean_reward[None, :], axis=1)
    weighted = (advantage[:, None] * output_gradient.astype(jnp.float32)).astype(jnp.bfloat16)
    my_slots = lax.dynamic_slice_in_dim(
        prompt_adapter_slot, member * adapter_slot_count, adapter_slot_count
    )
    every_down, every_up = (
        lax.all_gather(adapter_down_factors, "grp", axis=0, tiled=True),
        lax.all_gather(adapter_up_factors, "grp", axis=0, tiled=True),
    )
    down_local = jnp.take(every_down, my_slots, axis=0)
    up_local = jnp.take(every_up, my_slots, axis=0)
    flattened_down = down_local.reshape(adapter_slot_count * adapter_rank_size, local_width)
    flattened_up = up_local.reshape(adapter_slot_count * adapter_rank_size, local_width)
    low_all = lax.dot_general(
        activations, flattened_down, contract_cols, preferred_element_type=jnp.float32
    )
    low_part = jnp.sum(
        low_all.reshape(row_count, adapter_slot_count, adapter_rank_size) * onehot[:, :, None],
        axis=1,
    )
    back_all = lax.dot_general(
        weighted, flattened_up, contract_cols, preferred_element_type=jnp.float32
    )
    back_part = jnp.sum(
        back_all.reshape(row_count, adapter_slot_count, adapter_rank_size) * onehot[:, :, None],
        axis=1,
    )
    low_sum, back_sum = lax.psum((low_part, back_part), "tp")
    base_out = jnp.dot(
        lax.all_gather(activations, "tp", axis=1, tiled=True),
        frozen_weight,
        preferred_element_type=jnp.float32,
    )
    low = (scale_down * low_sum).astype(jnp.bfloat16)
    back_low = (scaled_up_factors * back_sum).astype(jnp.bfloat16)
    onehot_half = onehot.astype(jnp.bfloat16)
    low_wide = (onehot_half[:, :, None] * low[:, None, :]).reshape(
        row_count, adapter_slot_count * adapter_rank_size
    )
    back_wide = (onehot_half[:, :, None] * back_low[:, None, :]).reshape(
        row_count, adapter_slot_count * adapter_rank_size
    )
    layer_out = (
        base_out
        + scaled_up_factors * jnp.dot(low_wide, flattened_up, preferred_element_type=jnp.float32)
    ).astype(jnp.bfloat16)
    full_back = lax.dot_general(
        weighted, frozen_weight, contract_cols, preferred_element_type=jnp.float32
    )
    input_sum = lax.psum_scatter(full_back, "tp", scatter_dimension=1, tiled=True)
    input_grad = (
        input_sum
        + scale_down * jnp.dot(back_wide, flattened_down, preferred_element_type=jnp.float32)
    ).astype(jnp.bfloat16)
    grad_down = scale_down * lax.dot_general(
        back_wide, activations, contract_rows, preferred_element_type=jnp.float32
    )
    grad_up = scaled_up_factors * lax.dot_general(
        low_wide, weighted, contract_rows, preferred_element_type=jnp.float32
    )
    grad_down = grad_down.astype(jnp.bfloat16).reshape(
        adapter_slot_count, adapter_rank_size, local_width
    )
    grad_up = grad_up.astype(jnp.bfloat16).reshape(
        adapter_slot_count, adapter_rank_size, local_width
    )
    holder_down = (
        jnp.zeros((prompt_count, adapter_rank_size, local_width), jnp.bfloat16)
        .at[my_slots]
        .set(grad_down)
    )
    holder_up = (
        jnp.zeros((prompt_count, adapter_rank_size, local_width), jnp.bfloat16)
        .at[my_slots]
        .set(grad_up)
    )
    down_factor_slot, up_factor_slot = (
        lax.psum_scatter(holder_down, "grp", scatter_dimension=0, tiled=True).astype(jnp.float32),
        lax.psum_scatter(holder_up, "grp", scatter_dimension=0, tiled=True).astype(jnp.float32),
    )
    updated_down_factors, updated_first_down, updated_second_down = moment_step_update(
        adapter_down_factors, first_moment_down, second_moment_down, down_factor_slot
    )
    updated_up_factors, updated_first_up, updated_second_up = moment_step_update(
        adapter_up_factors, first_moment_up, second_moment_up, up_factor_slot
    )
    return (
        layer_out,
        input_grad,
        updated_down_factors,
        updated_up_factors,
        updated_first_down,
        updated_second_down,
        updated_first_up,
        updated_second_up,
    )


def solution(mesh):
    in_specs = (
        P("grp", "tp"),
        P("grp", "tp"),
        P(None, "tp"),
        P("grp", None, "tp"),
        P("grp", None, "tp"),
        P("grp", None, "tp"),
        P("grp", None, "tp"),
        P("grp", None, "tp"),
        P("grp", None, "tp"),
        P("grp", None),
        P("grp", None),
        P(),
    )
    out_specs = (
        P("grp", "tp"),
        P("grp", "tp"),
        P("grp", None, "tp"),
        P("grp", None, "tp"),
        P("grp", None, "tp"),
        P("grp", None, "tp"),
        P("grp", None, "tp"),
        P("grp", None, "tp"),
    )
    return jax.shard_map(local, mesh=mesh, in_specs=in_specs, out_specs=out_specs, check_vma=False)
```

profile of v0, /device:TPU:1, one launch (start us, length us, event | category | flops | bytes accessed | tf_op | source)
XLA Modules:
  0.0 447.7 jit_solution(7492767387817051464)
XLA Ops:
  7.2 0.0 copy-start
  7.2 0.0 all-gather.6.cloned.1.call-start
  7.2 0.7 all-gather.6.cloned.1.call-update
  7.9 0.0 all-gather.8.cloned.1.call-start
  8.0 0.7 all-gather.8.cloned.1.call-update
  8.7 0.0 all-reduce.3.cloned.1.call-start
  8.7 0.7 convert_element_type.76
  9.4 0.8 fusion.14
  10.2 0.8 select_reduce_fusion
  11.0 0.7 compare_and_fusion
  11.7 0.7 fusion.15
  12.4 33.0 %all-gather.6.cloned.1.call-done = bf16[128,32,512]{2,1,0:T(8,128)(2,1)} async-done(((bf16[16,32,512]{2,1,0:T(8,128)(2,1)}), bf16[128,32,512]{2,1,0:T(8,128)(2,1)}) %all-gather.6.cloned.1.call-update) | async-done | bytes 4194320 | tf_op jit(solution)/shard_map/all_gather | solution.py:60
  45.5 2.8 gather_fusion
  48.2 0.1 broadcast_select_fusion.1
  48.4 1.5 fusion.23
  49.9 0.8 multiply_reduce_fusion
  50.6 28.6 %all-gather.8.cloned.1.call-done = bf16[128,32,512]{2,1,0:T(8,128)(2,1)} async-done(((bf16[16,32,512]{2,1,0:T(8,128)(2,1)}), bf16[128,32,512]{2,1,0:T(8,128)(2,1)}) %all-gather.8.cloned.1.call-update) | async-done | bytes 4194320 | tf_op jit(solution)/shard_map/all_gather | solution.py:61
  79.3 2.8 gather_fusion.1
  82.0 2.3 fusion.7
  84.4 0.0 all-reduce.3.cloned.1.call-update
  84.4 0.0 all-gather.4.cloned.1.call-start
  84.4 0.5 all-gather.4.cloned.1.call-update
  85.0 0.0 reduce-scatter.6.cloned.1.call-start
  85.0 80.4 %all-reduce.3.cloned.1.call-done = (f32[512,32]{0,1:T(8,128)}, f32[512,32]{0,1:T(8,128)}) async-done(((f32[512,32]{0,1:T(8,128)}, f32[512,32]{0,1:T(8,128)}), (f32[512,32]{0,1:T(8,128)}, f32[512,32]{0,1:T(8,128)})) %all-reduce.3.cloned.1.call-update) | async-done | bytes 131088 | tf_op jit(solution)/shard_map/psum | solution.py:81
  165.4 0.8 multiply_convert_fusion.2
  166.2 0.8 multiply_convert_fusion.1
  167.0 0.1 broadcast_multiply_fusion.1
  167.1 0.4 fusion.4
  167.6 2.5 broadcast.85.clone
  170.1 2.6 scatter_fusion
  172.6 0.0 reduce-scatter.6.cloned.1.call-update
  172.7 0.0 reduce-scatter.8.cloned.1.call-start
  172.7 0.5 fusion.5
  173.2 2.5 broadcast.85.clone.1
  175.7 2.6 scatter_fusion.1
  178.3 0.0 reduce-scatter.8.cloned.1.call-update
  178.3 0.0 reduce-scatter.4.cloned.1.call-start
  178.4 11.8 %fusion.18 = f32[512,8192]{1,0:T(8,128)} fusion(bf16[8192,512]{1,0:T(8,128)(2,1)} %param.16, bf16[512,512]{1,0:T(8,128)(2,1)S(1)} %copy-done.4, f32[512]{0:T(512)S(1)} %sub.13), kind=kOutput, calls=%fused_computation.48 | convolution fusion | flops 4295753728 | bytes 25692160 | tf_op jit(solution)/shard_map/dot_general | solution.py:100
  190.2 0.0 reduce-scatter.4.cloned.1.call-update
  190.2 1.5 fusion.1
  191.7 54.1 %all-gather.4.cloned.1.call-done = bf16[512,8192]{1,0:T(8,128)(2,1)} async-done(((bf16[512,512]{1,0:T(8,128)(2,1)}), bf16[512,8192]{1,0:T(8,128)(2,1)}) %all-gather.4.cloned.1.call-update) | async-done | bytes 8388624 | tf_op jit(solution)/shard_map/all_gather | solution.py:83
  245.8 11.3 %fusion.6 = bf16[512,512]{1,0:T(8,128)(2,1)} fusion(f32[512,512]{1,0:T(8,128)} %fusion.1, bf16[512,8192]{1,0:T(8,128)(2,1)} %all-gather.4.cloned.1.call-done, bf16[8192,512]{1,0:T(8,128)(2,1)} %param.16), kind=kOutput, calls=%fused_computation.20 | convolution fusion | flops 4295491584 | bytes 18350080 | tf_op jit(solution)/shard_map/dot_general | solution.py:82
  257.1 26.1 %reduce-scatter.6.cloned.1.call-done = bf16[16,32,512]{2,1,0:T(8,128)(2,1)} async-done(((bf16[128,32,512]{2,1,0:T(8,128)(2,1)}), bf16[16,32,512]{2,1,0:T(8,128)(2,1)}) %reduce-scatter.6.cloned.1.call-update) | async-done | bytes 524304 | tf_op jit(solution)/shard_map/reduce_scatter | solution.py:131
  283.2 3.3 subtract_convert_fusion.1
  286.5 35.9 %reduce-scatter.8.cloned.1.call-done = bf16[16,32,512]{2,1,0:T(8,128)(2,1)} async-done(((bf16[128,32,512]{2,1,0:T(8,128)(2,1)}), bf16[16,32,512]{2,1,0:T(8,128)(2,1)}) %reduce-scatter.8.cloned.1.call-update) | async-done | bytes 524304 | tf_op jit(solution)/shard_map/reduce_scatter | solution.py:132
  322.4 3.6 subtract_convert_fusion
  326.1 112.3 %reduce-scatter.4.cloned.1.call-done = f32[512,512]{1,0:T(8,128)} async-done(((f32[512,8192]{1,0:T(8,128)}), f32[512,512]{1,0:T(8,128)}) %reduce-scatter.4.cloned.1.call-update) | async-done | bytes 1048592 | tf_op jit(solution)/shard_map/reduce_scatter | solution.py:103
  438.3 2.5 fusion.3
  (12 shorter events, 0.0 us)
Async XLA Ops:
  7.2 160.0 %copy-start = (bf16[512,512]{1,0:T(8,128)(2,1)S(1)}, bf16[512,512]{1,0:T(8,128)(2,1)}, u32[]{:S(2)}) copy-start(bf16[512,512]{1,0:T(8,128)(2,1)} %param.14) | copy-start | bytes 1572868
  7.2 38.3 %all-gather.6.cloned.1.call-start = ((), (), s32[]{:S(2)}) async-start(), calls=%async_computation.4 | async-start | bytes 4718592 | tf_op jit(solution)/shard_map/all_gather | solution.py:60
  7.9 71.3 %all-gather.8.cloned.1.call-start = ((), (), s32[]{:S(2)}) async-start(), calls=%async_computation.5 | async-start | bytes 4718592 | tf_op jit(solution)/shard_map/all_gather | solution.py:61
  8.7 156.7 %all-reduce.3.cloned.1.call-start = ((), (), s32[]{:S(2)}) async-start(), calls=%async_computation.9 | async-start | bytes 262144 | tf_op jit(solution)/shard_map/psum | solution.py:81
  82.0 90.7 %copy-start.4 = (bf16[512,512]{1,0:T(8,128)(2,1)S(1)}, bf16[512,512]{1,0:T(8,128)(2,1)}, u32[]{:S(2)}) copy-start(bf16[512,512]{1,0:T(8,128)(2,1)} %param.15) | copy-start | bytes 1572868
  84.4 161.4 %all-gather.4.cloned.1.call-start = ((), (), s32[]{:S(2)}) async-start(), calls=%async_computation.3 | async-start | bytes 8912896 | tf_op jit(solution)/shard_map/all_gather | solution.py:83
  85.0 198.2 %reduce-scatter.6.cloned.1.call-start = ((), (), s32[]{:S(2)}) async-start(), calls=%async_computation.7 | async-start | bytes 4718592 | tf_op jit(solution)/shard_map/reduce_scatter | solution.py:131
  172.7 149.8 %reduce-scatter.8.cloned.1.call-start = ((), (), s32[]{:S(2)}) async-start(), calls=%async_computation.8 | async-start | bytes 4718592 | tf_op jit(solution)/shard_map/reduce_scatter | solution.py:132
  178.3 260.0 %reduce-scatter.4.cloned.1.call-start = ((), (), s32[]{:S(2)}) async-start(), calls=%async_computation.6 | async-start | bytes 17825792 | tf_op jit(solution)/shard_map/reduce_scatter | solution.py:103
  191.7 91.5 %copy-start.1 = (bf16[16,32,512]{2,1,0:T(8,128)(2,1)S(1)}, bf16[16,32,512]{2,1,0:T(8,128)(2,1)}, u32[]{:S(2)}) copy-start(bf16[16,32,512]{2,1,0:T(8,128)(2,1)} %param.17) | copy-start | bytes 1572868
  191.7 91.5 %copy-start.3 = (f32[16,32,512]{2,1,0:T(8,128)S(1)}, f32[16,32,512]{2,1,0:T(8,128)}, u32[]{:S(2)}) copy-start(f32[16,32,512]{2,1,0:T(8,128)} %param.19) | copy-start | bytes 3145732
  191.7 130.7 %copy-start.2 = (bf16[16,32,512]{2,1,0:T(8,128)(2,1)S(1)}, bf16[16,32,512]{2,1,0:T(8,128)(2,1)}, u32[]{:S(2)}) copy-start(bf16[16,32,512]{2,1,0:T(8,128)(2,1)} %param.18) | copy-start | bytes 1572868
Sparse Core Ops, SparseCore 0:
  9.7 35.6 all-gather.5
  47.2 32.0 all-gather.7
  84.5 80.8 all-reduce.2
  167.5 78.2 all-gather.3
  248.2 34.9 reduce-scatter.5
  285.6 36.8 reduce-scatter.7
  326.2 112.0 reduce-scatter.3
where the time goes:
time: 448 us
  waiting for transfers between devices  372 us (83%)
  matrix products  31.8 us (7%)
  local copies, waits for them, and re-layouts  15.7 us (4%)
  between operations  14.2 us (3%)
  other arithmetic  13.3 us (3%)
    reduce_scatter x1, waiting for transfers between devices, local(): lax.psum_scatter(full_back, 'tp', scatter_dimension=1, tiled=True)  112 us
    psum x1, waiting for transfers between devices, local(): low_sum, back_sum = lax.psum((low_part, back_part), 'tp')  80.4 us
    all_gather x1, waiting for transfers between devices, local(): lax.all_gather(activations, 'tp', axis=1, tiled=True)  54.1 us
    reduce_scatter x1, waiting for transfers between devices, local(): lax.psum_scatter(holder_up, 'grp', scatter_dimension=0, tiled=True)  35.9 us
    all_gather x1, waiting for transfers between devices, local(): lax.all_gather(adapter_down_factors, 'grp', axis=0, tiled=True)  33 us
    all_gather x1, waiting for transfers between devices, local(): lax.all_gather(adapter_up_factors, 'grp', axis=0, tiled=True)  28.6 us
    reduce_scatter x1, waiting for transfers between devices, local(): lax.psum_scatter(holder_down, 'grp', scatter_dimension=0, tiled=True)  26.1 us
    dot_general x1, matrix products, local(): lax.dot_general(weighted, frozen_weight, contract_cols, preferred_element...  11.8 us
  transfers between devices with their start and end apart: 7, of which 7 were waited for; matrix products, arithmetic and copies ran while one was open for 12% of the time, Pallas kernels for 0%

commit v1 on v0

v1 whole, which is shorter than its diff:
```python
import functools

import jax
import jax.numpy as jnp
from jax import lax
from jax.experimental import pallas as pl
from jax.experimental.pallas import tpu as pltpu
from jax.sharding import Mesh, PartitionSpec as P

beta_first = 0.9
beta_second = 0.999
step_rate = 0.2
adam_eps = 1e-08
adapter_scale = 2.0

WIDTH = 8192
RANK = 32
COLS = 512
HALF = 256
ROWS = 512
PROMPTS = 16
ANY = pl.BlockSpec(memory_space=pl.ANY)
VMEM = pl.BlockSpec(memory_space=pltpu.VMEM)
F32 = jnp.float32
BF16 = jnp.bfloat16


def params(mib=32):
    return pltpu.CompilerParams(vmem_limit_bytes=mib * 1024 * 1024)


def pick_kernel(slots, member, down, up, out, sem):
    g = member[0]
    for d in range(8):
        def step(p, j):
            s = slots[d * PROMPTS + p]
            mine = lax.div(s, PROMPTS) == g

            @pl.when(mine)
            def _():
                i = lax.rem(s, PROMPTS)
                pltpu.make_async_copy(down.at[i], out.at[d, j, 0], sem.at[0]).start()
                pltpu.make_async_copy(up.at[i], out.at[d, j, 1], sem.at[0]).start()

            return j + mine.astype(jnp.int32)

        lax.fori_loop(0, PROMPTS, step, jnp.int32(0))
    pltpu.make_async_copy(out, out, sem.at[0]).wait()


def pick(slots, member, down, up):
    return pl.pallas_call(
        pick_kernel,
        out_shape=jax.ShapeDtypeStruct((8, 2, 2, RANK, COLS), BF16),
        grid_spec=pltpu.PrefetchScalarGridSpec(
            num_scalar_prefetch=2,
            grid=(),
            in_specs=[ANY, ANY],
            out_specs=ANY,
            scratch_shapes=[pltpu.SemaphoreType.DMA((1,))],
        ),
        compiler_params=params(),
        cost_estimate=pl.CostEstimate(flops=0, bytes_accessed=4 << 20, transcendentals=0),
    )(slots, member, down, up)


def adam_kernel(pos, grads, dn, up, m1d, m2d, m1u, m2u, odn, oup, o1d, o2d, o1u, o2u):
    i0 = pl.program_id(0) * 4
    for k in range(4):
        q = pos[i0 + k]
        for which, (f, m1, m2, of, o1, o2) in enumerate(
            ((dn, m1d, m2d, odn, o1d, o2d), (up, m1u, m2u, oup, o1u, o2u))
        ):
            grad = grads[q, which].astype(F32)
            first = beta_first * m1[k] + (1.0 - beta_first) * grad
            second = beta_second * m2[k] + (1.0 - beta_second) * grad * grad
            of[k] = (
                f[k].astype(F32) - step_rate * first / (jnp.sqrt(second) + adam_eps)
            ).astype(BF16)
            o1[k] = first
            o2[k] = second


def adam(pos, grads, dn, up, m1d, m2d, m1u, m2u):
    block = pl.BlockSpec((4, RANK, COLS), lambda i, pos: (i, 0, 0))
    half = jax.ShapeDtypeStruct((PROMPTS, RANK, COLS), BF16)
    full = jax.ShapeDtypeStruct((PROMPTS, RANK, COLS), F32)
    return pl.pallas_call(
        adam_kernel,
        out_shape=(half, half, full, full, full, full),
        grid_spec=pltpu.PrefetchScalarGridSpec(
            num_scalar_prefetch=1,
            grid=(4,),
            in_specs=[pl.BlockSpec((PROMPTS, 2, RANK, COLS), lambda i, pos: (0, 0, 0, 0))]
            + [block] * 6,
            out_specs=[block] * 6,
        ),
        compiler_params=params(),
        cost_estimate=pl.CostEstimate(flops=8 << 20, bytes_accessed=12 << 20, transcendentals=0),
    )(pos, grads, dn, up, m1d, m2d, m1u, m2u)


def forward_kernel(where, a0, a1, a2, a3, *rest):
    pieces, out = rest[:-1], rest[-1]
    c = where[0]
    here = pl.ds(pl.multiple_of(c * HALF, HALF), HALF)
    there = pl.ds(pl.multiple_of((1 - c) * HALF, HALF), HALF)
    total = None
    for e, a in enumerate((a0, a1, a2, a3)):
        term = jnp.dot(a[:, here], pieces[e][0], preferred_element_type=F32)
        term += jnp.dot(a[:, there], pieces[4 + e][0], preferred_element_type=F32)
        total = term if total is None else total + term
    out[...] = total.astype(out.dtype)


def forward(where, blocks, own, other, d):
    piece = pl.BlockSpec((1, HALF, HALF), lambda n, w: (d - 1, 0, n))
    return pl.pallas_call(
        forward_kernel,
        out_shape=jax.ShapeDtypeStruct((ROWS, COLS), BF16),
        grid_spec=pltpu.PrefetchScalarGridSpec(
            num_scalar_prefetch=1,
            grid=(2,),
            in_specs=[pl.BlockSpec((ROWS, COLS), lambda n, w: (0, 0))] * 4 + [piece] * 8,
            out_specs=pl.BlockSpec((ROWS, HALF), lambda n, w: (0, n)),
        ),
        compiler_params=params(),
        cost_estimate=pl.CostEstimate(
            flops=2 * 512 * 512 * 2048, bytes_accessed=5 << 20, transcendentals=0
        ),
    )(where, *blocks, *own, *other)


def local_kernel(where, a0, a1, a2, a3, w0, w1, w2, w3, out):
    total = None
    for a, w in ((a0, w0), (a1, w1), (a2, w2), (a3, w3)):
        term = jnp.dot(a[...], w[...], preferred_element_type=F32)
        total = term if total is None else total + term
    out[...] = total


def forward_local(where, blocks, weight):
    def piece(e):
        return pl.BlockSpec((COLS, HALF), lambda n, w: (w[1 + e], n))

    return pl.pallas_call(
        local_kernel,
        out_shape=jax.ShapeDtypeStruct((ROWS, COLS), F32),
        grid_spec=pltpu.PrefetchScalarGridSpec(
            num_scalar_prefetch=1,
            grid=(2,),
            in_specs=[pl.BlockSpec((ROWS, COLS), lambda n, w: (0, 0))] * 4
            + [piece(e) for e in range(4)],
            out_specs=pl.BlockSpec((ROWS, HALF), lambda n, w: (0, n)),
        ),
        compiler_params=params(),
        cost_estimate=pl.CostEstimate(
            flops=2 * 512 * 512 * 2048, bytes_accessed=5 << 20, transcendentals=0
        ),
    )(where, *blocks, weight, weight, weight, weight)


def backward_kernel(where, g0, g1, g2, g3, own, other, local, out):
    c = where[0]
    here = pl.ds(pl.multiple_of(c * HALF, HALF), HALF)
    there = pl.ds(pl.multiple_of((1 - c) * HALF, HALF), HALF)
    dims = (((1,), (1,)), ((), ()))
    for span, piece in ((here, own), (there, other)):
        total = lax.dot_general(g0[...], local[span, :], dims, preferred_element_type=F32)
        for d, g in ((1, g1), (2, g2), (3, g3)):
            total += lax.dot_general(g[...], piece[d - 1], dims, preferred_element_type=F32)
        out[:, span] = total.astype(out.dtype)


def backward(where, blocks, own, other, weight, e):
    rows = pl.BlockSpec((HALF, COLS), lambda m, w: (m, 0))
    piece = pl.BlockSpec((3, HALF, COLS), lambda m, w: (0, 0, 0))
    return pl.pallas_call(
        backward_kernel,
        out_shape=jax.ShapeDtypeStruct((ROWS, COLS), BF16),
        grid_spec=pltpu.PrefetchScalarGridSpec(
            num_scalar_prefetch=1,
            grid=(2,),
            in_specs=[rows] * 4
            + [piece, piece, pl.BlockSpec((COLS, COLS), lambda m, w: (w[1 + e], 0))],
            out_specs=pl.BlockSpec((HALF, COLS), lambda m, w: (m, 0)),
        ),
        compiler_params=params(),
        cost_estimate=pl.CostEstimate(
            flops=2 * 512 * 512 * 2048, bytes_accessed=5 << 20, transcendentals=0
        ),
    )(where, *blocks, own, other, weight)


def shift(value, axis, by, size=4):
    return lax.ppermute(value, axis, [(i, (i + by) % size) for i in range(size)])


def flip(value, axis, bit, size=4):
    return lax.ppermute(value, axis, [(i, i ^ bit) for i in range(size)])


def local(
    activations,
    output_gradient,
    frozen_weight,
    adapter_down_factors,
    adapter_up_factors,
    first_moment_down,
    second_moment_down,
    first_moment_up,
    second_moment_up,
    sample_row_prompt,
    majority_vote_reward,
    prompt_adapter_slot,
):
    x, c = lax.axis_index("x"), lax.axis_index("core")
    z, y = lax.axis_index("z"), lax.axis_index("y")
    member = x * 2 + c
    scale_down = WIDTH ** (-0.5)
    scale_up = adapter_scale / RANK**0.5

    received = []
    for d in (1, 2, 3):
        start = lax.rem(z + d, 4) * 2048 + lax.rem(x + y, 4) * COLS + c * HALF
        piece = lax.dynamic_slice_in_dim(frozen_weight, start, HALF, axis=0)
        received.append(shift(piece, "z", d))
    acts = [
        lax.ppermute(
            activations,
            ("x", "y"),
            [(i * 4 + j, i * 4 + (j - i + e) % 4) for i in range(4) for j in range(4)],
        )
        for e in range(4)
    ]
    slots = prompt_adapter_slot
    sent = pick(slots, member[None].astype(jnp.int32), adapter_down_factors, adapter_up_factors)
    adapters = lax.all_to_all(sent, ("x", "core"), 0, 0)
    down = adapters[:, :, 0].reshape(PROMPTS * RANK, COLS)
    up = adapters[:, :, 1].reshape(PROMPTS * RANK, COLS)

    held = slots.reshape(8, PROMPTS)
    mine = (held // PROMPTS == member).astype(jnp.int32)
    turn = jnp.cumsum(mine, axis=1) - 1
    places = jnp.arange(8, dtype=jnp.int32)[:, None] * 2 + turn
    pos = jnp.sum(
        jnp.where(
            held[:, :, None] == member * PROMPTS + jnp.arange(PROMPTS, dtype=jnp.int32),
            places[:, :, None],
            0,
        ),
        axis=(0, 1),
    ).astype(jnp.int32)
    source = lax.dynamic_slice_in_dim(slots, member * PROMPTS, PROMPTS) // PROMPTS
    ids = jnp.arange(PROMPTS, dtype=jnp.int32)
    before = (source[:, None] == source[None, :]) & (ids[:, None] > ids[None, :])
    order = 2 * source + jnp.sum(before.astype(jnp.int32), axis=1)

    labels = sample_row_prompt[0]
    reward = majority_vote_reward[0].astype(F32)
    label = jnp.sum(jnp.where(labels[None, :] == ids[:, None], order[:, None], 0), axis=0)
    onehot = (label[None, :] == ids[:, None]).astype(F32)
    counts = jnp.sum(onehot, axis=1)
    mean_reward = jnp.sum(onehot * reward[None, :], axis=1) / counts
    advantage = reward - jnp.sum(onehot * mean_reward[:, None], axis=0)
    weighted = (advantage[:, None] * output_gradient.astype(F32)).astype(BF16)

    own = [jnp.stack(received)]
    own += [shift(own[0], "x", e) for e in (1, 2, 3)]
    other = [lax.ppermute(piece, "core", [(0, 1), (1, 0)]) for piece in own]
    grads_in = [weighted] + [shift(weighted, "z", d) for d in (1, 2, 3)]

    contract_cols = (((1,), (1,)), ((), ()))
    low_all = lax.dot_general(down, activations, contract_cols, preferred_element_type=F32)
    back_all = lax.dot_general(up, weighted, contract_cols, preferred_element_type=F32)
    low_part = jnp.sum(low_all.reshape(PROMPTS, RANK, ROWS) * onehot[:, None, :], axis=0)
    back_part = jnp.sum(back_all.reshape(PROMPTS, RANK, ROWS) * onehot[:, None, :], axis=0)
    sums = jnp.concatenate([low_part, back_part])
    for axis in ("y", "z"):
        for bit in (1, 2):
            sums = sums + flip(sums, axis, bit)
    low = (scale_down * sums[:RANK]).astype(BF16)
    back_low = (scale_up * sums[RANK:]).astype(BF16)
    half = onehot.astype(BF16)
    low_wide = (half[:, None, :] * low[None, :, :]).reshape(PROMPTS * RANK, ROWS)
    back_wide = (half[:, None, :] * back_low[None, :, :]).reshape(PROMPTS * RANK, ROWS)
    grad_down = scale_down * jnp.dot(back_wide, activations, preferred_element_type=F32)
    grad_up = scale_up * jnp.dot(low_wide, weighted, preferred_element_type=F32)
    grads = jnp.stack(
        [
            grad_down.astype(BF16).reshape(8, 2, RANK, COLS),
            grad_up.astype(BF16).reshape(8, 2, RANK, COLS),
        ],
        axis=2,
    )
    grads = lax.all_to_all(grads, ("x", "core"), 0, 0).reshape(PROMPTS, 2, RANK, COLS)
    updated = adam(
        pos,
        grads,
        adapter_down_factors,
        adapter_up_factors,
        first_moment_down,
        second_moment_down,
        first_moment_up,
        second_moment_up,
    )

    where = jnp.stack([c] + [z * 4 + lax.rem(x + y + 4 - e, 4) for e in range(4)]).astype(jnp.int32)
    input_parts = []
    for e in range(4):
        part = backward(where, grads_in, own[e], other[e], frozen_weight, e)
        input_parts.append(
            lax.ppermute(
                part,
                ("x", "y"),
                [(i * 4 + j, i * 4 + (i + j - e) % 4) for i in range(4) for j in range(4)],
            )
        )
    layer_parts = [
        shift(forward(where, acts, own, other, d), "z", -d) for d in (1, 3, 2)
    ]
    base = forward_local(where, acts, frozen_weight)
    contract_rows = (((0,), (0,)), ((), ()))
    layer = base + scale_up * lax.dot_general(
        low_wide, up, contract_rows, preferred_element_type=F32
    )
    for part in layer_parts:
        layer = layer + part.astype(F32)
    inward = scale_down * lax.dot_general(
        back_wide, down, contract_rows, preferred_element_type=F32
    )
    for part in input_parts:
        inward = inward + part.astype(F32)
    odn, oup, o1d, o2d, o1u, o2u = updated
    return layer.astype(BF16), inward.astype(BF16), odn, oup, o1d, o2d, o1u, o2u


def solution(mesh):
    fine = Mesh(mesh.devices.reshape(4, 2, 4, 4), ("x", "core", "z", "y"))
    grp, tp = ("x", "core"), ("z", "y")
    rows, slab = P(grp, tp), P(grp, None, tp)
    in_specs = (rows, rows, P(None, tp)) + (slab,) * 6 + (P(grp, None), P(grp, None), P())
    out_specs = (rows, rows) + (slab,) * 6
    return jax.shard_map(local, mesh=fine, in_specs=in_specs, out_specs=out_specs, check_vma=False)
```

time: 448 us -> 205 us (0.46)
  the two profiles are of different devices: /device:TPU:1 before, /device:TPU:6 now
where the time goes in v1:
time: 205 us; the launch traced here: 203 us
  starting transfers between devices  70.5 us (34%)
  waiting for transfers between devices  48.8 us (24%)
  Pallas kernels  38.5 us (19%)
  local copies, waits for them, and re-layouts  21.4 us (10%)
  other arithmetic  14.9 us (7%)
  matrix products  7.14 us (3%)
    ppermute x12, waiting for transfers between devices, shift(): lax.ppermute(value, axis, [(i, (i + by) % size) for i in range(size)])  26.5 us
    ppermute x12, starting transfers between devices, shift(): lax.ppermute(value, axis, [(i, (i + by) % size) for i in range(size)])  24.1 us
    unnamed x76, local copies, waits for them, and re-layouts  20.1 us
    pallas_call x4, Pallas kernels, backward(): pl.pallas_call(backward_kernel, out_shape=jax.ShapeDtypeStruct((ROWS, COL...  16.8 us
    ppermute x4, starting transfers between devices, local(): lax.ppermute(activations, ('x', 'y'), [(i * 4 + j, i * 4 + (j - i + e) %...  16.7 us
    ppermute x4, starting transfers between devices, local(): lax.ppermute(part, ('x', 'y'), [(i * 4 + j, i * 4 + (i + j - e) % 4) for...  12.9 us
    pallas_call x3, Pallas kernels, forward(): pl.pallas_call(forward_kernel, out_shape=jax.ShapeDtypeStruct((ROWS, COLS...  11 us
    all_to_all x1, waiting for transfers between devices, local(): adapters = lax.all_to_all(sent, ('x', 'core'), 0, 0)  8.72 us
  transfers between devices with their start and end apart: 30, of which 6 were waited for; matrix products, arithmetic and copies ran while one was open for 10% of the time, Pallas kernels for 19%

profile of v1, /device:TPU:6, one launch (start us, length us, event | category | flops | bytes accessed | tf_op | source)
XLA Modules:
  0.0 202.6 jit_solution(14370310808355915332)
XLA Ops:
  0.6 3.5 %collective-permute-start = (bf16[512,512]{1,0:T(8,128)(2,1)}, bf16[512,512]{1,0:T(8,128)(2,1)S(1)}, u32[]{:S(2)}, u32[]{:S(2)}) collective-permute-start(bf16[512,512]{1,0:T(8,128)(2,1)} %param.12), channel_id=1, source_target_pairs={{0,0},{1,1},{2,2},{3,3},{32,35},{33,32},{34,33},{35,34},{64,66},{6... | collective-permute-start | bytes 1572872 | tf_op jit(solution)/shard_map/ppermute | solution.py:229
  6.9 2.7 %shard_map.180 = bf16[8,2,2,32,512]{4,3,2,1,0:T(8,128)(2,1)} custom-call(s32[128]{0:T(128)S(1)} %copy-done.19, s32[1]{0:T(128)} %bitcast.6.member, bf16[16,32,512]{2,1,0:T(8,128)(2,1)S(1)} %copy-done.11, bf16[16,32,512]{2,1,0:T(8,128)(2,1)S(1)} %copy-done.13), custom_call_target="tpu_custom_call" | custom-call | bytes 4194304 | tf_op jit(solution)/shard_map/pallas_call | solution.py:52
  9.6 6.5 %all-to-all-start = ((bf16[8,2,2,32,512]{4,3,2,1,0:T(8,128)(2,1)}), bf16[8,2,2,32,512]{4,3,2,1,0:T(8,128)(2,1)S(1)}, u32[]{:S(2)}, u32[]{:S(2)}) async-start(bf16[8,2,2,32,512]{4,3,2,1,0:T(8,128)(2,1)} %shard_map.180), calls=%async_computation | async-start | bytes 2097152 | tf_op jit(solution)/shard_map/all_to_all | solution.py:238
  20.1 1.2 multiply_convert_fusion.g0
  21.3 8.7 %all-to-all-done = bf16[8,2,2,32,512]{4,3,2,1,0:T(8,128)(2,1)S(1)} async-done(((bf16[8,2,2,32,512]{4,3,2,1,0:T(8,128)(2,1)}), bf16[8,2,2,32,512]{4,3,2,1,0:T(8,128)(2,1)S(1)}, u32[]{:S(2)}, u32[]{:S(2)}) %all-to-all-start) | async-done | bytes 1048608 | tf_op jit(solution)/shard_map/all_to_all | solution.py:238
  30.1 1.9 fusion.2
  33.2 1.2 constant_dynamic-slice_fusion.2
  34.4 4.1 %collective-permute-start.10 = (bf16[256,512]{1,0:T(8,128)(2,1)S(1)}, bf16[256,512]{1,0:T(8,128)(2,1)S(1)}, u32[]{:S(2)}, u32[]{:S(2)}) collective-permute-start(bf16[256,512]{1,0:T(8,128)(2,1)S(1)} %get-tuple-element.23), channel_id=1, source_target_pairs={{0,12},{4,0},{8,4},{12,8},{1,13},{5,1},{9,5},{13,9},{2,14},{6,2},{... | collective-permute-start | bytes 786440 | tf_op jit(solution)/shard_map/ppermute | solution.py:196
  38.5 1.3 collective-permute-start.8
  39.8 1.9 collective-permute-start.5
  41.7 7.5 %collective-permute-done.10 = bf16[256,512]{1,0:T(8,128)(2,1)S(1)} collective-permute-done((bf16[256,512]{1,0:T(8,128)(2,1)S(1)}, bf16[256,512]{1,0:T(8,128)(2,1)S(1)}, u32[]{:S(2)}, u32[]{:S(2)}) %collective-permute-start.10) | collective-permute-done | bytes 262176 | tf_op jit(solution)/shard_map/ppermute | solution.py:196
  49.2 3.7 %collective-permute-start.1 = (bf16[512,512]{1,0:T(8,128)(2,1)}, bf16[512,512]{1,0:T(8,128)(2,1)S(1)}, u32[]{:S(2)}, u32[]{:S(2)}) collective-permute-start(bf16[512,512]{1,0:T(8,128)(2,1)} %param.12), channel_id=1, source_target_pairs={{0,1},{1,2},{2,3},{3,0},{32,32},{33,33},{34,34},{35,35},{64,67},{6... | collective-permute-start | bytes 1572872 | tf_op jit(solution)/shard_map/ppermute | solution.py:229
  53.0 4.1 %collective-permute-start.2 = (bf16[512,512]{1,0:T(8,128)(2,1)}, bf16[512,512]{1,0:T(8,128)(2,1)S(1)}, u32[]{:S(2)}, u32[]{:S(2)}) collective-permute-start(bf16[512,512]{1,0:T(8,128)(2,1)} %param.12), channel_id=1, source_target_pairs={{0,2},{1,3},{2,0},{3,1},{32,33},{33,34},{34,35},{35,32},{64,64},{6... | collective-permute-start | bytes 1572872 | tf_op jit(solution)/shard_map/ppermute | solution.py:229
  57.1 5.4 %collective-permute-start.3 = (bf16[512,512]{1,0:T(8,128)(2,1)}, bf16[512,512]{1,0:T(8,128)(2,1)}, u32[]{:S(2)}, u32[]{:S(2)}) collective-permute-start(bf16[512,512]{1,0:T(8,128)(2,1)} %param.12), channel_id=1, source_target_pairs={{0,3},{1,0},{2,1},{3,2},{32,34},{33,35},{34,32},{35,33},{64,65},{6... | collective-permute-start | bytes 1572872 | tf_op jit(solution)/shard_map/ppermute | solution.py:229
  63.2 5.1 %collective-permute-start.22 = (bf16[512,512]{1,0:T(8,128)(2,1)S(1)}, bf16[512,512]{1,0:T(8,128)(2,1)}, u32[]{:S(2)}, u32[]{:S(2)}) collective-permute-start(bf16[512,512]{1,0:T(8,128)(2,1)S(1)} %multiply_convert_fusion.g0), channel_id=1, source_target_pairs={{0,8},{4,12},{8,0},{12,4},{1,9},{5,13},{9,1},{13,5},{2,10},{6,14},... | collective-permute-start | bytes 1572872 | tf_op jit(solution)/shard_map/ppermute | solution.py:196
  68.4 1.1 pad_maximum_fusion.1.rest_0_.own
  71.3 7.5 %collective-permute-start.11 = (bf16[3,256,512]{2,1,0:T(8,128)(2,1)S(1)}, bf16[3,256,512]{2,1,0:T(8,128)(2,1)S(1)}, u32[]{:S(2)}, u32[]{:S(2)}) collective-permute-start(bf16[3,256,512]{2,1,0:T(8,128)(2,1)S(1)} %pad_maximum_fusion.1.rest_0_.own), channel_id=1, source_target_pairs={{0,32},{32,64},{64,96},{96,0},{1,33},{33,65},{65,97},{97,1},{2,34}... | collective-permute-start | bytes 2359304 | tf_op jit(solution)/shard_map/ppermute | solution.py:196
  80.6 9.5 %collective-permute-done.22.g2 = bf16[512,512]{1,0:T(8,128)(2,1)} collective-permute-done((bf16[512,512]{1,0:T(8,128)(2,1)S(1)}, bf16[512,512]{1,0:T(8,128)(2,1)}, u32[]{:S(2)}, u32[]{:S(2)}) %collective-permute-start.22) | collective-permute-done | bytes 524320 | tf_op jit(solution)/shard_map/ppermute | solution.py:196
  90.4 6.2 %collective-permute-done.6 = f32[64,512]{1,0:T(8,128)} collective-permute-done((f32[64,512]{1,0:T(8,128)S(1)}, f32[64,512]{1,0:T(8,128)}, u32[]{:S(2)}, u32[]{:S(2)}) %collective-permute-start.6) | collective-permute-done | bytes 131104 | tf_op jit(solution)/shard_map/ppermute | solution.py:200
  97.7 9.5 %collective-permute-done.23.g3 = bf16[512,512]{1,0:T(8,128)(2,1)S(1)} collective-permute-done((bf16[512,512]{1,0:T(8,128)(2,1)S(1)}, bf16[512,512]{1,0:T(8,128)(2,1)S(1)}, u32[]{:S(2)}, u32[]{:S(2)}) %collective-permute-start.23) | collective-permute-done | bytes 524320 | tf_op jit(solution)/shard_map/ppermute | solution.py:196
  107.2 3.6 %copy-done = bf16[8192,512]{1,0:T(8,128)(2,1)S(1)} copy-done((bf16[8192,512]{1,0:T(8,128)(2,1)S(1)}, bf16[8192,512]{1,0:T(8,128)(2,1)}, u32[]{:S(2)}) %copy-start) | copy-done | bytes 8388632
  112.8 3.2 %shard_map.179 = f32[512,512]{1,0:T(8,128)S(1)} custom-call(s32[5]{0:T(128)S(1)} %stack.38.where, bf16[512,512]{1,0:T(8,128)(2,1)S(1)} %collective-permute-done.a0, bf16[512,512]{1,0:T(8,128)(2,1)S(1)} %copy-done.2, bf16[512,512]{1,0:T(8,128)(2,1)S(1)} %copy-done.5, bf16[512,512]{1,0:T(8,128)(2,1)} %collective-permute-done.3.a3, ...), custom_call_target="tpu_custom_call" | custom-call | flops 1073741824 | bytes 5242880 | tf_op jit(solution)/shard_map/pallas_call | solution.py:146
  117.1 4.1 %shard_map.184 = bf16[512,512]{1,0:T(8,128)(2,1)} custom-call(s32[5]{0:T(128)S(1)} %stack.38.where, bf16[512,512]{1,0:T(8,128)(2,1)S(1)} %multiply_convert_fusion.g0, bf16[512,512]{1,0:T(8,128)(2,1)} %collective-permute-done.21.g1, bf16[512,512]{1,0:T(8,128)(2,1)} %collective-permute-done.22.g2, bf16[512,512]{1,0:T(8,128)(2,1)S(1)} %collective-permute-done.23.g3, ...), custom_call_target="tpu_custom_call" | custom-call | flops 1073741824 | bytes 5242880 | tf_op jit(solution)/shard_map/pallas_call | solution.py:178
  121.2 2.2 %collective-permute-start.24 = (bf16[512,512]{1,0:T(8,128)(2,1)}, bf16[512,512]{1,0:T(8,128)(2,1)}, u32[]{:S(2)}, u32[]{:S(2)}) collective-permute-start(bf16[512,512]{1,0:T(8,128)(2,1)} %shard_map.184), channel_id=1, source_target_pairs={{0,0},{1,1},{2,2},{3,3},{32,33},{33,34},{34,35},{35,32},{64,66},{6... | collective-permute-start | bytes 1572872 | tf_op jit(solution)/shard_map/ppermute | solution.py:313
  125.0 1.5 fusion
  127.5 6.9 %all-to-all-start.1 = ((bf16[8,2,2,32,512]{4,3,2,1,0:T(8,128)(2,1)}), bf16[8,2,2,32,512]{4,3,2,1,0:T(8,128)(2,1)}, u32[]{:S(2)}, u32[]{:S(2)}) async-start(bf16[8,2,2,32,512]{4,3,2,1,0:T(8,128)(2,1)} %pad_maximum_fusion), calls=%async_computation.1 | async-start | bytes 2097152 | tf_op jit(solution)/shard_map/all_to_all | solution.py:296
  136.5 3.4 %shard_map.183 = bf16[512,512]{1,0:T(8,128)(2,1)S(1)} custom-call(s32[5]{0:T(128)S(1)} %stack.38.where, bf16[512,512]{1,0:T(8,128)(2,1)S(1)} %collective-permute-done.a0, bf16[512,512]{1,0:T(8,128)(2,1)S(1)} %copy-done.3, bf16[512,512]{1,0:T(8,128)(2,1)S(1)} %copy-done.6, bf16[512,512]{1,0:T(8,128)(2,1)} %collective-permute-done.3.a3, ...), custom_call_target="tpu_custom_call" | custom-call | flops 1073741824 | bytes 5242880 | tf_op jit(solution)/shard_map/pallas_call | solution.py:118
  140.0 1.2 collective-permute-start.20
  141.2 3.4 %shard_map.182 = bf16[512,512]{1,0:T(8,128)(2,1)S(1)} custom-call(s32[5]{0:T(128)S(1)} %stack.38.where, bf16[512,512]{1,0:T(8,128)(2,1)S(1)} %collective-permute-done.a0, bf16[512,512]{1,0:T(8,128)(2,1)S(1)} %copy-done.3, bf16[512,512]{1,0:T(8,128)(2,1)S(1)} %copy-done.6, bf16[512,512]{1,0:T(8,128)(2,1)} %collective-permute-done.3.a3, ...), custom_call_target="tpu_custom_call" | custom-call | flops 1073741824 | bytes 5242880 | tf_op jit(solution)/shard_map/pallas_call | solution.py:118
  144.6 1.9 collective-permute-start.19
  146.5 1.4 convolution_multiply_fusion.3
  147.9 4.1 %shard_map.181 = bf16[512,512]{1,0:T(8,128)(2,1)} custom-call(s32[5]{0:T(128)S(1)} %stack.38.where, bf16[512,512]{1,0:T(8,128)(2,1)S(1)} %collective-permute-done.a0, bf16[512,512]{1,0:T(8,128)(2,1)S(1)} %copy-done.3, bf16[512,512]{1,0:T(8,128)(2,1)S(1)} %copy-done.6, bf16[512,512]{1,0:T(8,128)(2,1)} %collective-permute-done.3.a3, ...), custom_call_target="tpu_custom_call" | custom-call | flops 1073741824 | bytes 5242880 | tf_op jit(solution)/shard_map/pallas_call | solution.py:118
  152.1 2.1 %collective-permute-start.18 = (bf16[512,512]{1,0:T(8,128)(2,1)}, bf16[512,512]{1,0:T(8,128)(2,1)}, u32[]{:S(2)}, u32[]{:S(2)}) collective-permute-start(bf16[512,512]{1,0:T(8,128)(2,1)} %shard_map.181), channel_id=1, source_target_pairs={{0,12},{4,0},{8,4},{12,8},{1,13},{5,1},{9,5},{13,9},{2,14},{6,2},{... | collective-permute-start | bytes 1572872 | tf_op jit(solution)/shard_map/ppermute | solution.py:196
  154.2 4.3 %shard_map.187 = bf16[512,512]{1,0:T(8,128)(2,1)} custom-call(s32[5]{0:T(128)S(1)} %stack.38.where, bf16[512,512]{1,0:T(8,128)(2,1)S(1)} %multiply_convert_fusion.g0, bf16[512,512]{1,0:T(8,128)(2,1)} %collective-permute-done.21.g1, bf16[512,512]{1,0:T(8,128)(2,1)} %collective-permute-done.22.g2, bf16[512,512]{1,0:T(8,128)(2,1)S(1)} %copy-done.8, ...), custom_call_target="tpu_custom_call" | custom-call | flops 1073741824 | bytes 5242880 | tf_op jit(solution)/shard_map/pallas_call | solution.py:178
  158.5 5.4 %collective-permute-start.27 = (bf16[512,512]{1,0:T(8,128)(2,1)}, bf16[512,512]{1,0:T(8,128)(2,1)}, u32[]{:S(2)}, u32[]{:S(2)}) collective-permute-start(bf16[512,512]{1,0:T(8,128)(2,1)} %shard_map.187), channel_id=1, source_target_pairs={{0,1},{1,2},{2,3},{3,0},{32,34},{33,35},{34,32},{35,33},{64,67},{6... | collective-permute-start | bytes 1572872 | tf_op jit(solution)/shard_map/ppermute | solution.py:313
  163.9 4.1 %shard_map.186 = bf16[512,512]{1,0:T(8,128)(2,1)} custom-call(s32[5]{0:T(128)S(1)} %stack.38.where, bf16[512,512]{1,0:T(8,128)(2,1)S(1)} %multiply_convert_fusion.g0, bf16[512,512]{1,0:T(8,128)(2,1)} %collective-permute-done.21.g1, bf16[512,512]{1,0:T(8,128)(2,1)} %collective-permute-done.22.g2, bf16[512,512]{1,0:T(8,128)(2,1)S(1)} %copy-done.8, ...), custom_call_target="tpu_custom_call" | custom-call | flops 1073741824 | bytes 5242880 | tf_op jit(solution)/shard_map/pallas_call | solution.py:178
  168.0 4.3 %shard_map.185 = bf16[512,512]{1,0:T(8,128)(2,1)} custom-call(s32[5]{0:T(128)S(1)} %stack.38.where, bf16[512,512]{1,0:T(8,128)(2,1)S(1)} %multiply_convert_fusion.g0, bf16[512,512]{1,0:T(8,128)(2,1)} %collective-permute-done.21.g1, bf16[512,512]{1,0:T(8,128)(2,1)} %collective-permute-done.22.g2, bf16[512,512]{1,0:T(8,128)(2,1)S(1)} %copy-done.8, ...), custom_call_target="tpu_custom_call" | custom-call | flops 1073741824 | bytes 5242880 | tf_op jit(solution)/shard_map/pallas_call | solution.py:178
  172.3 3.1 %collective-permute-start.26 = (bf16[512,512]{1,0:T(8,128)(2,1)}, bf16[512,512]{1,0:T(8,128)(2,1)S(1)}, u32[]{:S(2)}, u32[]{:S(2)}) collective-permute-start(bf16[512,512]{1,0:T(8,128)(2,1)} %shard_map.186), channel_id=1, source_target_pairs={{0,2},{1,3},{2,0},{3,1},{32,35},{33,32},{34,33},{35,34},{64,64},{6... | collective-permute-start | bytes 1572872 | tf_op jit(solution)/shard_map/ppermute | solution.py:313
  175.4 2.3 %collective-permute-start.25 = (bf16[512,512]{1,0:T(8,128)(2,1)}, bf16[512,512]{1,0:T(8,128)(2,1)S(1)}, u32[]{:S(2)}, u32[]{:S(2)}) collective-permute-start(bf16[512,512]{1,0:T(8,128)(2,1)} %shard_map.185), channel_id=1, source_target_pairs={{0,3},{1,0},{2,1},{3,2},{32,32},{33,33},{34,34},{35,35},{64,65},{6... | collective-permute-start | bytes 1572872 | tf_op jit(solution)/shard_map/ppermute | solution.py:313
  177.8 1.4 convolution_multiply_fusion.2
  180.2 1.2 copy-done.15
  181.5 1.2 copy-done.16
  182.7 1.2 copy-done.17
  183.9 1.2 copy-done.18
  185.1 4.9 %shard_map.188 = (bf16[16,32,512]{2,1,0:T(8,128)(2,1)}, bf16[16,32,512]{2,1,0:T(8,128)(2,1)}, f32[16,32,512]{2,1,0:T(8,128)}, f32[16,32,512]{2,1,0:T(8,128)}, f3...) custom-call(s32[16]{0:T(128)S(1)} %select_reduce_fusion.pos, bf16[16,2,32,512]{3,2,1,0:T(8,128)(2,1)} %bitcast.23.grads, ...), custom_call_target="tpu_custom_call" | custom-call | flops 8388608 | bytes 12582912 | tf_op jit(solution)/shard_map/pallas_call | solution.py:88
  190.0 2.9 %add_convert_fusion.1 = bf16[512,512]{1,0:T(8,128)(2,1)} fusion(bf16[512,512]{1,0:T(8,128)(2,1)} %copy-done.30, bf16[512,512]{1,0:T(8,128)(2,1)} %copy-done.31, bf16[512,512]{1,0:T(8,128)(2,1)} %collective-permute-done.18, f32[512,512]{1,0:T(8,128)S(1)} %copy-done.10, f32[512,512]{1,0:T(8,128)} %convolution_multiply_fusion.3), kind=kLoop, calls=%fused_computation.12 | loop fusion | flops 2097152 | bytes 4194304 | tf_op jit(solution)/shard_map/convert_element_type | solution.py:335
  192.9 7.3 %collective-permute-done.26 = bf16[512,512]{1,0:T(8,128)(2,1)S(1)} collective-permute-done((bf16[512,512]{1,0:T(8,128)(2,1)}, bf16[512,512]{1,0:T(8,128)(2,1)S(1)}, u32[]{:S(2)}, u32[]{:S(2)}) %collective-permute-start.26) | collective-permute-done | bytes 524320 | tf_op jit(solution)/shard_map/ppermute | solution.py:313
  200.2 2.3 %add_convert_fusion = bf16[512,512]{1,0:T(8,128)(2,1)} fusion(bf16[512,512]{1,0:T(8,128)(2,1)} %collective-permute-done.27, bf16[512,512]{1,0:T(8,128)(2,1)S(1)} %collective-permute-done.26, bf16[512,512]{1,0:T(8,128)(2,1)S(1)} %collective-permute-done.25, f32[512,512]{1,0:T(8,128)S(1)} %copy-done.21, bf16[512,512]{1,0:T(8,128)(2,1)} %collective-permute-done.24), kind=kLoop, calls=%fused_computation.11 | loop fusion | flops 2359296 | bytes 3670016 | tf_op jit(solution)/shard_map/convert_element_type | solution.py:335
  (137 shorter events, 22.6 us)
Async XLA Ops:
  0.6 67.7 %copy-start.20 = (s32[128]{0:T(128)S(1)}, s32[128]{0:T(128)}, u32[]{:S(2)}) copy-start(s32[128]{0:T(128)} %slots.1) | copy-start | bytes 1540
  0.6 61.9 %collective-permute-start = (bf16[512,512]{1,0:T(8,128)(2,1)}, bf16[512,512]{1,0:T(8,128)(2,1)S(1)}, u32[]{:S(2)}, u32[]{:S(2)}) collective-permute-start(bf16[512,512]{1,0:T(8,128)(2,1)} %param.12), channel_id=1, source_target_pairs={{0,0},{1,1},{2,2},{3,3},{32,35},{33,32},{34,33},{35,34},{64,66},{6... | collective-permute-start | bytes 1572872 | tf_op jit(solution)/shard_map/ppermute | solution.py:229
  9.6 20.4 %all-to-all-start = ((bf16[8,2,2,32,512]{4,3,2,1,0:T(8,128)(2,1)}), bf16[8,2,2,32,512]{4,3,2,1,0:T(8,128)(2,1)S(1)}, u32[]{:S(2)}, u32[]{:S(2)}) async-start(bf16[8,2,2,32,512]{4,3,2,1,0:T(8,128)(2,1)} %shard_map.180), calls=%async_computation | async-start | bytes 2097152 | tf_op jit(solution)/shard_map/all_to_all | solution.py:238
  30.1 32.4 %copy-start.26 = (bf16[8,2,1,32,512]{4,3,2,1,0:T(8,128)(2,1)}, bf16[8,2,1,32,512]{4,3,2,1,0:T(8,128)(2,1)S(1)}, u32[]{:S(2)}) copy-start(bf16[8,2,1,32,512]{4,3,2,1,0:T(8,128)(2,1)S(1)} %get-tuple-element.25) | copy-start | bytes 1572868
  30.1 32.4 %copy-start.28 = (bf16[8,2,1,32,512]{4,3,2,1,0:T(8,128)(2,1)}, bf16[8,2,1,32,512]{4,3,2,1,0:T(8,128)(2,1)S(1)}, u32[]{:S(2)}) copy-start(bf16[8,2,1,32,512]{4,3,2,1,0:T(8,128)(2,1)S(1)} %get-tuple-element.26) | copy-start | bytes 1572868
  32.5 7.3 %collective-permute-start.4 = (f32[64,512]{1,0:T(8,128)S(1)}, f32[64,512]{1,0:T(8,128)S(1)}, u32[]{:S(2)}, u32[]{:S(2)}) collective-permute-start(f32[64,512]{1,0:T(8,128)S(1)} %pad_maximum_fusion.2), channel_id=1, source_target_pairs={{0,1},{1,0},{2,3},{3,2},{4,5},{5,4},{6,7},{7,6},{8,9},{9,8},{10,11... | collective-permute-start | bytes 393224 | tf_op jit(solution)/shard_map/ppermute | solution.py:200
  34.4 14.8 %collective-permute-start.10 = (bf16[256,512]{1,0:T(8,128)(2,1)S(1)}, bf16[256,512]{1,0:T(8,128)(2,1)S(1)}, u32[]{:S(2)}, u32[]{:S(2)}) collective-permute-start(bf16[256,512]{1,0:T(8,128)(2,1)S(1)} %get-tuple-element.23), channel_id=1, source_target_pairs={{0,12},{4,0},{8,4},{12,8},{1,13},{5,1},{9,5},{13,9},{2,14},{6,2},{... | collective-permute-start | bytes 786440 | tf_op jit(solution)/shard_map/ppermute | solution.py:196
  38.5 14.4 %collective-permute-start.9 = (bf16[256,512]{1,0:T(8,128)(2,1)S(1)}, bf16[256,512]{1,0:T(8,128)(2,1)S(1)}, u32[]{:S(2)}, u32[]{:S(2)}) collective-permute-start(bf16[256,512]{1,0:T(8,128)(2,1)S(1)} %get-tuple-element.24), channel_id=1, source_target_pairs={{0,8},{4,12},{8,0},{12,4},{1,9},{5,13},{9,1},{13,5},{2,10},{6,14},... | collective-permute-start | bytes 786440 | tf_op jit(solution)/shard_map/ppermute | solution.py:196
  38.5 18.6 %collective-permute-start.8 = (bf16[256,512]{1,0:T(8,128)(2,1)S(1)}, bf16[256,512]{1,0:T(8,128)(2,1)S(1)}, u32[]{:S(2)}, u32[]{:S(2)}) collective-permute-start(bf16[256,512]{1,0:T(8,128)(2,1)S(1)} %get-tuple-element.22), channel_id=1, source_target_pairs={{0,4},{4,8},{8,12},{12,0},{1,5},{5,9},{9,13},{13,1},{2,6},{6,10},{... | collective-permute-start | bytes 786440 | tf_op jit(solution)/shard_map/ppermute | solution.py:196
  39.8 22.7 %collective-permute-start.5 = (f32[64,512]{1,0:T(8,128)S(1)}, f32[64,512]{1,0:T(8,128)S(1)}, u32[]{:S(2)}, u32[]{:S(2)}) collective-permute-start(f32[64,512]{1,0:T(8,128)S(1)} %fusion.16), channel_id=1, source_target_pairs={{0,2},{1,3},{2,0},{3,1},{4,6},{5,7},{6,4},{7,5},{8,10},{9,11},{10,... | collective-permute-start | bytes 393224 | tf_op jit(solution)/shard_map/ppermute | solution.py:200
  49.2 21.2 %collective-permute-start.1 = (bf16[512,512]{1,0:T(8,128)(2,1)}, bf16[512,512]{1,0:T(8,128)(2,1)S(1)}, u32[]{:S(2)}, u32[]{:S(2)}) collective-permute-start(bf16[512,512]{1,0:T(8,128)(2,1)} %param.12), channel_id=1, source_target_pairs={{0,1},{1,2},{2,3},{3,0},{32,32},{33,33},{34,34},{35,35},{64,67},{6... | collective-permute-start | bytes 1572872 | tf_op jit(solution)/shard_map/ppermute | solution.py:229
  53.0 15.4 %copy-start.32 = (bf16[256,512]{1,0:T(8,128)(2,1)}, bf16[256,512]{1,0:T(8,128)(2,1)S(1)}, u32[]{:S(2)}) copy-start(bf16[256,512]{1,0:T(8,128)(2,1)S(1)} %collective-permute-done.9) | copy-start | bytes 786436
  53.0 25.8 %collective-permute-start.2 = (bf16[512,512]{1,0:T(8,128)(2,1)}, bf16[512,512]{1,0:T(8,128)(2,1)S(1)}, u32[]{:S(2)}, u32[]{:S(2)}) collective-permute-start(bf16[512,512]{1,0:T(8,128)(2,1)} %param.12), channel_id=1, source_target_pairs={{0,2},{1,3},{2,0},{3,1},{32,33},{33,34},{34,35},{35,32},{64,64},{6... | collective-permute-start | bytes 1572872 | tf_op jit(solution)/shard_map/ppermute | solution.py:229
  57.1 11.3 %copy-start.33 = (bf16[256,512]{1,0:T(8,128)(2,1)}, bf16[256,512]{1,0:T(8,128)(2,1)S(1)}, u32[]{:S(2)}) copy-start(bf16[256,512]{1,0:T(8,128)(2,1)S(1)} %collective-permute-done.8) | copy-start | bytes 786436
  57.1 23.3 %collective-permute-start.3 = (bf16[512,512]{1,0:T(8,128)(2,1)}, bf16[512,512]{1,0:T(8,128)(2,1)}, u32[]{:S(2)}, u32[]{:S(2)}) collective-permute-start(bf16[512,512]{1,0:T(8,128)(2,1)} %param.12), channel_id=1, source_target_pairs={{0,3},{1,0},{2,1},{3,2},{32,34},{33,35},{34,32},{35,33},{64,65},{6... | collective-permute-start | bytes 1572872 | tf_op jit(solution)/shard_map/ppermute | solution.py:229
  62.5 18.0 %collective-permute-start.21 = (bf16[512,512]{1,0:T(8,128)(2,1)S(1)}, bf16[512,512]{1,0:T(8,128)(2,1)}, u32[]{:S(2)}, u32[]{:S(2)}) collective-permute-start(bf16[512,512]{1,0:T(8,128)(2,1)S(1)} %multiply_convert_fusion.g0), channel_id=1, source_target_pairs={{0,4},{4,8},{8,12},{12,0},{1,5},{5,9},{9,13},{13,1},{2,6},{6,10},{... | collective-permute-start | bytes 1572872 | tf_op jit(solution)/shard_map/ppermute | solution.py:196
  63.2 26.9 %collective-permute-start.22 = (bf16[512,512]{1,0:T(8,128)(2,1)S(1)}, bf16[512,512]{1,0:T(8,128)(2,1)}, u32[]{:S(2)}, u32[]{:S(2)}) collective-permute-start(bf16[512,512]{1,0:T(8,128)(2,1)S(1)} %multiply_convert_fusion.g0), channel_id=1, source_target_pairs={{0,8},{4,12},{8,0},{12,4},{1,9},{5,13},{9,1},{13,5},{2,10},{6,14},... | collective-permute-start | bytes 1572872 | tf_op jit(solution)/shard_map/ppermute | solution.py:196
  71.3 52.1 %collective-permute-start.11 = (bf16[3,256,512]{2,1,0:T(8,128)(2,1)S(1)}, bf16[3,256,512]{2,1,0:T(8,128)(2,1)S(1)}, u32[]{:S(2)}, u32[]{:S(2)}) collective-permute-start(bf16[3,256,512]{2,1,0:T(8,128)(2,1)S(1)} %pad_maximum_fusion.1.rest_0_.own), channel_id=1, source_target_pairs={{0,32},{32,64},{64,96},{96,0},{1,33},{33,65},{65,97},{97,1},{2,34}... | collective-permute-start | bytes 2359304 | tf_op jit(solution)/shard_map/ppermute | solution.py:196
  79.5 43.9 %collective-permute-start.12 = (bf16[3,256,512]{2,1,0:T(8,128)(2,1)S(1)}, bf16[3,256,512]{2,1,0:T(8,128)(2,1)S(1)}, u32[]{:S(2)}, u32[]{:S(2)}) collective-permute-start(bf16[3,256,512]{2,1,0:T(8,128)(2,1)S(1)} %pad_maximum_fusion.1.rest_0_.own), channel_id=1, source_target_pairs={{0,64},{32,96},{64,0},{96,32},{1,65},{33,97},{65,1},{97,33},{2,66}... | collective-permute-start | bytes 2359304 | tf_op jit(solution)/shard_map/ppermute | solution.py:196
  80.5 43.5 %collective-permute-start.13 = (bf16[3,256,512]{2,1,0:T(8,128)(2,1)S(1)}, bf16[3,256,512]{2,1,0:T(8,128)(2,1)}, u32[]{:S(2)}, u32[]{:S(2)}) collective-permute-start(bf16[3,256,512]{2,1,0:T(8,128)(2,1)S(1)} %pad_maximum_fusion.1.rest_0_.own), channel_id=1, source_target_pairs={{0,96},{32,0},{64,32},{96,64},{1,97},{33,1},{65,33},{97,65},{2,98}... | collective-permute-start | bytes 2359304 | tf_op jit(solution)/shard_map/ppermute | solution.py:196
  80.5 36.6 %collective-permute-start.14 = (bf16[3,256,512]{2,1,0:T(8,128)(2,1)S(1)}, bf16[3,256,512]{2,1,0:T(8,128)(2,1)}, u32[]{:S(2)}, u32[]{:S(2)}) collective-permute-start(bf16[3,256,512]{2,1,0:T(8,128)(2,1)S(1)} %pad_maximum_fusion.1.rest_0_.own), channel_id=1, source_target_pairs={{0,16},{16,0},{1,17},{17,1},{2,18},{18,2},{3,19},{19,3},{4,20},{20... | collective-permute-start | bytes 2359304 | tf_op jit(solution)/shard_map/ppermute | solution.py:270
  90.1 6.5 %collective-permute-start.6 = (f32[64,512]{1,0:T(8,128)S(1)}, f32[64,512]{1,0:T(8,128)}, u32[]{:S(2)}, u32[]{:S(2)}) collective-permute-start(f32[64,512]{1,0:T(8,128)S(1)} %add.160), channel_id=1, source_target_pairs={{0,4},{4,0},{8,12},{12,8},{1,5},{5,1},{9,13},{13,9},{2,6},{6,2},{1... | collective-permute-start | bytes 393224 | tf_op jit(solution)/shard_map/ppermute | solution.py:200
  96.6 10.6 %collective-permute-start.23 = (bf16[512,512]{1,0:T(8,128)(2,1)S(1)}, bf16[512,512]{1,0:T(8,128)(2,1)S(1)}, u32[]{:S(2)}, u32[]{:S(2)}) collective-permute-start(bf16[512,512]{1,0:T(8,128)(2,1)S(1)} %multiply_convert_fusion.g0), channel_id=1, source_target_pairs={{0,12},{4,0},{8,4},{12,8},{1,13},{5,1},{9,5},{13,9},{2,14},{6,2},{... | collective-permute-start | bytes 1572872 | tf_op jit(solution)/shard_map/ppermute | solution.py:196
  107.2 9.9 %copy-start.7 = (bf16[512,512]{1,0:T(8,128)(2,1)}, bf16[512,512]{1,0:T(8,128)(2,1)S(1)}, u32[]{:S(2)}) copy-start(bf16[512,512]{1,0:T(8,128)(2,1)S(1)} %collective-permute-done.23.g3) | copy-start | bytes 1572868
  107.2 16.9 %collective-permute-start.7 = (f32[64,512]{1,0:T(8,128)S(1)}, f32[64,512]{1,0:T(8,128)S(1)}, u32[]{:S(2)}, u32[]{:S(2)}) collective-permute-start(f32[64,512]{1,0:T(8,128)S(1)} %add.161), channel_id=1, source_target_pairs={{0,8},{4,12},{8,0},{12,4},{1,9},{5,13},{9,1},{13,5},{2,10},{6,14},... | collective-permute-start | bytes 393224 | tf_op jit(solution)/shard_map/ppermute | solution.py:200
  107.2 3.6 %copy-start = (bf16[8192,512]{1,0:T(8,128)(2,1)S(1)}, bf16[8192,512]{1,0:T(8,128)(2,1)}, u32[]{:S(2)}) copy-start(bf16[8192,512]{1,0:T(8,128)(2,1)} %local.7) | copy-start | bytes 25165828
  117.1 7.0 %copy-start.35 = (bf16[16,512]{1,0:T(8,128)(2,1)S(1)}, bf16[16,512]{1,0:T(8,128)(2,1)}, u32[]{:S(2)}) copy-start(bf16[16,512]{1,0:T(8,128)(2,1)} %get-tuple-element.31) | copy-start | bytes 49156
  121.2 71.8 %collective-permute-start.24 = (bf16[512,512]{1,0:T(8,128)(2,1)}, bf16[512,512]{1,0:T(8,128)(2,1)}, u32[]{:S(2)}, u32[]{:S(2)}) collective-permute-start(bf16[512,512]{1,0:T(8,128)(2,1)} %shard_map.184), channel_id=1, source_target_pairs={{0,0},{1,1},{2,2},{3,3},{32,33},{33,34},{34,35},{35,32},{64,66},{6... | collective-permute-start | bytes 1572872 | tf_op jit(solution)/shard_map/ppermute | solution.py:313
  123.3 11.0 %collective-permute-start.15 = (bf16[3,256,512]{2,1,0:T(8,128)(2,1)S(1)}, bf16[3,256,512]{2,1,0:T(8,128)(2,1)}, u32[]{:S(2)}, u32[]{:S(2)}) collective-permute-start(bf16[3,256,512]{2,1,0:T(8,128)(2,1)S(1)} %collective-permute-done.11.rest_1_.own), channel_id=1, source_target_pairs={{0,16},{16,0},{1,17},{17,1},{2,18},{18,2},{3,19},{19,3},{4,20},{20... | collective-permute-start | bytes 2359304 | tf_op jit(solution)/shard_map/ppermute | solution.py:270
  123.4 10.9 %collective-permute-start.16 = (bf16[3,256,512]{2,1,0:T(8,128)(2,1)S(1)}, bf16[3,256,512]{2,1,0:T(8,128)(2,1)}, u32[]{:S(2)}, u32[]{:S(2)}) collective-permute-start(bf16[3,256,512]{2,1,0:T(8,128)(2,1)S(1)} %collective-permute-done.12.rest_2_.own), channel_id=1, source_target_pairs={{0,16},{16,0},{1,17},{17,1},{2,18},{18,2},{3,19},{19,3},{4,20},{20... | collective-permute-start | bytes 2359304 | tf_op jit(solution)/shard_map/ppermute | solution.py:270
  123.9 10.5 %collective-permute-start.17 = (bf16[3,256,512]{2,1,0:T(8,128)(2,1)}, bf16[3,256,512]{2,1,0:T(8,128)(2,1)}, u32[]{:S(2)}, u32[]{:S(2)}) collective-permute-start(bf16[3,256,512]{2,1,0:T(8,128)(2,1)} %collective-permute-done.13.rest_3_.own), channel_id=1, source_target_pairs={{0,16},{16,0},{1,17},{17,1},{2,18},{18,2},{3,19},{19,3},{4,20},{20... | collective-permute-start | bytes 2359304 | tf_op jit(solution)/shard_map/ppermute | solution.py:270
  127.5 51.7 %all-to-all-start.1 = ((bf16[8,2,2,32,512]{4,3,2,1,0:T(8,128)(2,1)}), bf16[8,2,2,32,512]{4,3,2,1,0:T(8,128)(2,1)}, u32[]{:S(2)}, u32[]{:S(2)}) async-start(bf16[8,2,2,32,512]{4,3,2,1,0:T(8,128)(2,1)} %pad_maximum_fusion), calls=%async_computation.1 | async-start | bytes 2097152 | tf_op jit(solution)/shard_map/all_to_all | solution.py:296
  136.5 10.0 %copy-start.25 = (bf16[16,32,512]{2,1,0:T(8,128)(2,1)S(1)}, bf16[16,32,512]{2,1,0:T(8,128)(2,1)}, u32[]{:S(2)}) copy-start(bf16[16,32,512]{2,1,0:T(8,128)(2,1)} %copy-done.24) | copy-start | bytes 1572868
  136.5 10.0 %copy-start.29 = (bf16[8,2,1,32,512]{4,3,2,1,0:T(8,128)(2,1)S(1)}, bf16[8,2,1,32,512]{4,3,2,1,0:T(8,128)(2,1)}, u32[]{:S(2)}) copy-start(bf16[8,2,1,32,512]{4,3,2,1,0:T(8,128)(2,1)} %copy-done.28) | copy-start | bytes 1572868
  139.9 14.2 %slice-start = ((s8[8388608]{0:T(1024)(128)(4,1)}), s8[4194304]{0:T(1024)(128)(4,1)S(1)}, s32[]{:S(2)}) async-start(s8[8388608]{0:T(1024)(128)(4,1)} %bitcast.40), calls=%async_computation.2 | async-start | bytes 8388608
  139.9 14.2 %copy-start.8 = (bf16[512,512]{1,0:T(8,128)(2,1)S(1)}, bf16[512,512]{1,0:T(8,128)(2,1)}, u32[]{:S(2)}) copy-start(bf16[512,512]{1,0:T(8,128)(2,1)} %copy-done.7) | copy-start | bytes 1572868
  140.0 32.3 %collective-permute-start.20 = (bf16[512,512]{1,0:T(8,128)(2,1)S(1)}, bf16[512,512]{1,0:T(8,128)(2,1)S(1)}, u32[]{:S(2)}, u32[]{:S(2)}) collective-permute-start(bf16[512,512]{1,0:T(8,128)(2,1)S(1)} %shard_map.183), channel_id=1, source_target_pairs={{0,8},{4,12},{8,0},{12,4},{1,9},{5,13},{9,1},{13,5},{2,10},{6,14},... | collective-permute-start | bytes 1572872 | tf_op jit(solution)/shard_map/ppermute | solution.py:196
  144.6 30.7 %collective-permute-start.19 = (bf16[512,512]{1,0:T(8,128)(2,1)S(1)}, bf16[512,512]{1,0:T(8,128)(2,1)S(1)}, u32[]{:S(2)}, u32[]{:S(2)}) collective-permute-start(bf16[512,512]{1,0:T(8,128)(2,1)S(1)} %shard_map.182), channel_id=1, source_target_pairs={{0,4},{4,8},{8,12},{12,0},{1,5},{5,9},{9,13},{13,1},{2,6},{6,10},{... | collective-permute-start | bytes 1572872 | tf_op jit(solution)/shard_map/ppermute | solution.py:196
  146.5 7.7 %slice-start.1 = ((s8[8388608]{0:T(1024)(128)(4,1)}), s8[4194304]{0:T(1024)(128)(4,1)S(1)}, s32[]{:S(2)}) async-start(s8[8388608]{0:T(1024)(128)(4,1)} %bitcast.40), calls=%async_computation.3 | async-start | bytes 8388608
  152.1 37.9 %collective-permute-start.18 = (bf16[512,512]{1,0:T(8,128)(2,1)}, bf16[512,512]{1,0:T(8,128)(2,1)}, u32[]{:S(2)}, u32[]{:S(2)}) collective-permute-start(bf16[512,512]{1,0:T(8,128)(2,1)} %shard_map.181), channel_id=1, source_target_pairs={{0,12},{4,0},{8,4},{12,8},{1,13},{5,1},{9,5},{13,9},{2,14},{6,2},{... | collective-permute-start | bytes 1572872 | tf_op jit(solution)/shard_map/ppermute | solution.py:196
  158.5 34.4 %collective-permute-start.27 = (bf16[512,512]{1,0:T(8,128)(2,1)}, bf16[512,512]{1,0:T(8,128)(2,1)}, u32[]{:S(2)}, u32[]{:S(2)}) collective-permute-start(bf16[512,512]{1,0:T(8,128)(2,1)} %shard_map.187), channel_id=1, source_target_pairs={{0,1},{1,2},{2,3},{3,0},{32,34},{33,35},{34,32},{35,33},{64,67},{6... | collective-permute-start | bytes 1572872 | tf_op jit(solution)/shard_map/ppermute | solution.py:313
  167.9 9.8 %copy-start.23 = (bf16[16,32,512]{2,1,0:T(8,128)(2,1)S(1)}, bf16[16,32,512]{2,1,0:T(8,128)(2,1)}, u32[]{:S(2)}) copy-start(bf16[16,32,512]{2,1,0:T(8,128)(2,1)} %copy-done.22) | copy-start | bytes 1572868
  168.0 9.8 %copy-start.27 = (bf16[8,2,1,32,512]{4,3,2,1,0:T(8,128)(2,1)S(1)}, bf16[8,2,1,32,512]{4,3,2,1,0:T(8,128)(2,1)}, u32[]{:S(2)}) copy-start(bf16[8,2,1,32,512]{4,3,2,1,0:T(8,128)(2,1)} %copy-done.26) | copy-start | bytes 1572868
  168.0 11.2 %copy-start.12 = (bf16[16,32,512]{2,1,0:T(8,128)(2,1)S(1)}, bf16[16,32,512]{2,1,0:T(8,128)(2,1)}, u32[]{:S(2)}) copy-start(bf16[16,32,512]{2,1,0:T(8,128)(2,1)} %dn.1) | copy-start | bytes 1572868
  168.0 22.1 %copy-start.10 = (f32[512,512]{1,0:T(8,128)S(1)}, f32[512,512]{1,0:T(8,128)}, u32[]{:S(2)}) copy-start(f32[512,512]{1,0:T(8,128)} %copy-done.9) | copy-start | bytes 3145732
  172.3 28.0 %collective-permute-start.26 = (bf16[512,512]{1,0:T(8,128)(2,1)}, bf16[512,512]{1,0:T(8,128)(2,1)S(1)}, u32[]{:S(2)}, u32[]{:S(2)}) collective-permute-start(bf16[512,512]{1,0:T(8,128)(2,1)} %shard_map.186), channel_id=1, source_target_pairs={{0,2},{1,3},{2,0},{3,1},{32,35},{33,32},{34,33},{35,34},{64,64},{6... | collective-permute-start | bytes 1572872 | tf_op jit(solution)/shard_map/ppermute | solution.py:313
  175.4 24.9 %collective-permute-start.25 = (bf16[512,512]{1,0:T(8,128)(2,1)}, bf16[512,512]{1,0:T(8,128)(2,1)S(1)}, u32[]{:S(2)}, u32[]{:S(2)}) collective-permute-start(bf16[512,512]{1,0:T(8,128)(2,1)} %shard_map.185), channel_id=1, source_target_pairs={{0,3},{1,0},{2,1},{3,2},{32,32},{33,33},{34,34},{35,35},{64,65},{6... | collective-permute-start | bytes 1572872 | tf_op jit(solution)/shard_map/ppermute | solution.py:313
  185.1 15.1 %copy-start.21 = (f32[512,512]{1,0:T(8,128)S(1)}, f32[512,512]{1,0:T(8,128)}, u32[]{:S(2)}) copy-start(f32[512,512]{1,0:T(8,128)} %convolution_multiply_fusion.2) | copy-start | bytes 3145732
  (20 other events, 24.6 us)

commit v2 on v1

v2 whole, which is shorter than its diff:
```python
import functools

import jax
import jax.numpy as jnp
from jax import lax
from jax.experimental import pallas as pl
from jax.experimental.pallas import tpu as pltpu
from jax.sharding import Mesh, PartitionSpec as P

beta_first = 0.9
beta_second = 0.999
step_rate = 0.2
adam_eps = 1e-08
adapter_scale = 2.0

WIDTH = 8192
RANK = 32
COLS = 512
HALF = 256
ROWS = 512
PROMPTS = 16
ANY = pl.BlockSpec(memory_space=pl.ANY)
VMEM = pl.BlockSpec(memory_space=pltpu.VMEM)
F32 = jnp.float32
BF16 = jnp.bfloat16


def params(mib=60):
    return pltpu.CompilerParams(vmem_limit_bytes=mib * 1024 * 1024)


def pick_kernel(slots, member, down, up, out):
    g = member[0]

    def group(d, carry):
        def step(p, j):
            s = slots[d * PROMPTS + p]
            mine = lax.div(s, PROMPTS) == g

            @pl.when(mine)
            def _():
                i = lax.rem(s, PROMPTS)
                out[d * 2 + j, 0] = down[i]
                out[d * 2 + j, 1] = up[i]

            return j + mine.astype(jnp.int32)

        lax.fori_loop(0, PROMPTS, step, jnp.int32(0))
        return carry

    lax.fori_loop(0, 8, group, 0)


def pick(slots, member, down, up):
    return pl.pallas_call(
        pick_kernel,
        out_shape=jax.ShapeDtypeStruct((PROMPTS, 2, RANK, COLS), BF16),
        grid_spec=pltpu.PrefetchScalarGridSpec(
            num_scalar_prefetch=2, grid=(), in_specs=[VMEM, VMEM], out_specs=VMEM
        ),
        compiler_params=params(),
        cost_estimate=pl.CostEstimate(flops=0, bytes_accessed=4 << 20, transcendentals=0),
    )(slots, member, down, up)


def adam_kernel(pos, grads, dn, up, m1d, m2d, m1u, m2u, odn, oup, o1d, o2d, o1u, o2u):
    i0 = pl.program_id(0) * 4
    for k in range(4):
        q = pos[i0 + k]
        for which, (f, m1, m2, of, o1, o2) in enumerate(
            ((dn, m1d, m2d, odn, o1d, o2d), (up, m1u, m2u, oup, o1u, o2u))
        ):
            grad = grads[q, which].astype(F32)
            first = beta_first * m1[k] + (1.0 - beta_first) * grad
            second = beta_second * m2[k] + (1.0 - beta_second) * grad * grad
            of[k] = (
                f[k].astype(F32) - step_rate * first / (jnp.sqrt(second) + adam_eps)
            ).astype(BF16)
            o1[k] = first
            o2[k] = second


def adam(pos, grads, dn, up, m1d, m2d, m1u, m2u):
    block = pl.BlockSpec((4, RANK, COLS), lambda i, pos: (i, 0, 0))
    half = jax.ShapeDtypeStruct((PROMPTS, RANK, COLS), BF16)
    full = jax.ShapeDtypeStruct((PROMPTS, RANK, COLS), F32)
    return pl.pallas_call(
        adam_kernel,
        out_shape=(half, half, full, full, full, full),
        grid_spec=pltpu.PrefetchScalarGridSpec(
            num_scalar_prefetch=1,
            grid=(4,),
            in_specs=[pl.BlockSpec((PROMPTS, 2, RANK, COLS), lambda i, pos: (0, 0, 0, 0))]
            + [block] * 6,
            out_specs=[block] * 6,
        ),
        compiler_params=params(),
        cost_estimate=pl.CostEstimate(flops=8 << 20, bytes_accessed=12 << 20, transcendentals=0),
    )(pos, grads, dn, up, m1d, m2d, m1u, m2u)


def partial_kernel(where, advantage, acts, *refs):
    grads, own, other, weight = refs[0:4], refs[4:8], refs[8:12], refs[12]
    forward, backward = refs[13:17], refs[17:21]
    a_held, g_held, w_held, a_sem, g_sem, w_sem = refs[21:]
    x, c, z, y = (where[i] for i in range(4))

    def span(i):
        return pl.ds(i * COLS, COLS)

    a_loads, g_loads, w_loads = [], [], []
    for i in range(4):
        a_loads.append(
            pltpu.make_async_copy(acts.at[lax.rem(y + i, 4)], a_held.at[:, span(i)], a_sem)
        )
        g_loads.append(pltpu.make_async_copy(grads[i], g_held.at[:, span(i)], g_sem))
    for d in range(4):
        for i in range(4):
            if d == 0:
                first = pl.multiple_of((z * 4 + lax.rem(y + i, 4)) * COLS, COLS)
                copies = [(weight.at[pl.ds(first, COLS)], i * COLS, COLS)]
            else:
                turn = lax.rem(x - i + 4, 4) * COLS
                copies = [
                    (own[i].at[d - 1], turn + c * HALF, HALF),
                    (other[i].at[d - 1], turn + (1 - c) * HALF, HALF),
                ]
            for source, first, length in copies:
                rows = pl.ds(pl.multiple_of(first, HALF), length)
                w_loads.append(
                    pltpu.make_async_copy(source, w_held.at[rows, span(d)], w_sem.at[d])
                )
    local, remote = w_loads[:4], w_loads[4:]
    groups = {0: local, 1: remote[:8], 2: remote[8:16], 3: remote[16:]}
    order = (1, 3, 2, 0)
    for copy in a_loads:
        copy.start()
    for d in order:
        for copy in groups[d]:
            copy.start()
    for copy in g_loads:
        copy.start()
    for copy in a_loads:
        copy.wait()
    for d in order:
        for copy in groups[d]:
            copy.wait()
        forward[d][...] = jnp.dot(
            a_held[...], w_held[:, span(d)], preferred_element_type=F32
        ).astype(BF16)
    for copy in g_loads:
        copy.wait()
    gain = advantage[...]
    for d in range(4):
        g_held[:, span(d)] = (gain * g_held[:, span(d)].astype(F32)).astype(BF16)
    dims = (((1,), (1,)), ((), ()))
    for i in order:
        backward[i][...] = lax.dot_general(
            g_held[...], w_held[span(i)], dims, preferred_element_type=F32
        ).astype(BF16)


def partials(where, advantage, acts, grads, own, other, weight):
    block = jax.ShapeDtypeStruct((ROWS, COLS), BF16)
    outs = pl.pallas_call(
        partial_kernel,
        out_shape=[block] * 8,
        grid_spec=pltpu.PrefetchScalarGridSpec(
            num_scalar_prefetch=1,
            grid=(),
            in_specs=[VMEM] + [ANY] * 14,
            out_specs=[VMEM] * 8,
            scratch_shapes=[
                pltpu.VMEM((ROWS, 4 * COLS), BF16),
                pltpu.VMEM((ROWS, 4 * COLS), BF16),
                pltpu.VMEM((4 * COLS, 4 * COLS), BF16),
                pltpu.SemaphoreType.DMA(()),
                pltpu.SemaphoreType.DMA(()),
                pltpu.SemaphoreType.DMA((4,)),
            ],
        ),
        compiler_params=params(),
        cost_estimate=pl.CostEstimate(
            flops=4 * 512 * 2048 * 2048, bytes_accessed=16 << 20, transcendentals=0
        ),
    )(where, advantage, acts, *grads, *own, *other, weight)
    return outs[:4], outs[4:]


def shift(value, axis, by, size=4):
    return lax.ppermute(value, axis, [(i, (i + by) % size) for i in range(size)])


def flip(value, axis, bit, size=4):
    return lax.ppermute(value, axis, [(i, i ^ bit) for i in range(size)])


def local(
    activations,
    output_gradient,
    frozen_weight,
    adapter_down_factors,
    adapter_up_factors,
    first_moment_down,
    second_moment_down,
    first_moment_up,
    second_moment_up,
    sample_row_prompt,
    majority_vote_reward,
    prompt_adapter_slot,
):
    x, c = lax.axis_index("x"), lax.axis_index("core")
    z, y = lax.axis_index("z"), lax.axis_index("y")
    member = x * 2 + c
    scale_down = WIDTH ** (-0.5)
    scale_up = adapter_scale / RANK**0.5

    acts = lax.all_gather(activations, "y", axis=0)
    parts = []
    source = frozen_weight
    for turn in (0, 2):
        received = []
        for d in (1, 2, 3):
            start = lax.rem(z + d, 4) * 2048 + lax.rem(x + y + turn, 4) * COLS + c * HALF
            piece = lax.dynamic_slice_in_dim(source, start, HALF, axis=0)
            received.append(shift(piece, "z", d))
        parts.append(jnp.stack(received))
        parts[0], source = lax.optimization_barrier((parts[0], frozen_weight))
    grad, pieces = lax.optimization_barrier((output_gradient, parts[1]))
    parts[1] = pieces
    grads_in = [output_gradient] + [shift(grad, "z", d) for d in (1, 2, 3)]
    slots = prompt_adapter_slot
    sent = pick(slots, member[None].astype(jnp.int32), adapter_down_factors, adapter_up_factors)
    adapters = lax.all_to_all(sent.reshape(8, 2, 2, RANK, COLS), ("x", "core"), 0, 0)
    adapters, parts[0] = lax.optimization_barrier((adapters, parts[0]))
    down = adapters[:, :, 0].reshape(PROMPTS * RANK, COLS)
    up = adapters[:, :, 1].reshape(PROMPTS * RANK, COLS)

    held = slots.reshape(8, PROMPTS)
    mine = (held // PROMPTS == member).astype(jnp.int32)
    turn = jnp.cumsum(mine, axis=1) - 1
    places = jnp.arange(8, dtype=jnp.int32)[:, None] * 2 + turn
    pos = jnp.sum(
        jnp.where(
            held[:, :, None] == member * PROMPTS + jnp.arange(PROMPTS, dtype=jnp.int32),
            places[:, :, None],
            0,
        ),
        axis=(0, 1),
    ).astype(jnp.int32)
    source = lax.dynamic_slice_in_dim(slots, member * PROMPTS, PROMPTS) // PROMPTS
    ids = jnp.arange(PROMPTS, dtype=jnp.int32)
    before = (source[:, None] == source[None, :]) & (ids[:, None] > ids[None, :])
    order = 2 * source + jnp.sum(before.astype(jnp.int32), axis=1)

    labels = sample_row_prompt[0]
    reward = majority_vote_reward[0].astype(F32)
    label = jnp.sum(jnp.where(labels[None, :] == ids[:, None], order[:, None], 0), axis=0)
    onehot = (label[None, :] == ids[:, None]).astype(F32)
    counts = jnp.sum(onehot, axis=1)
    mean_reward = jnp.sum(onehot * reward[None, :], axis=1) / counts
    advantage = reward - jnp.sum(onehot * mean_reward[:, None], axis=0)
    weighted = (advantage[:, None] * output_gradient.astype(F32)).astype(BF16)

    own = [parts[0], shift(parts[0], "x", 1), parts[1], shift(parts[0], "x", 3)]
    other = [lax.ppermute(piece, "core", [(0, 1), (1, 0)]) for piece in own]

    contract_cols = (((1,), (1,)), ((), ()))
    low_all = lax.dot_general(down, activations, contract_cols, preferred_element_type=F32)
    back_all = lax.dot_general(up, weighted, contract_cols, preferred_element_type=F32)
    low_part = jnp.sum(low_all.reshape(PROMPTS, RANK, ROWS) * onehot[:, None, :], axis=0)
    back_part = jnp.sum(back_all.reshape(PROMPTS, RANK, ROWS) * onehot[:, None, :], axis=0)
    sums = jnp.concatenate([low_part, back_part])
    for axis in ("y", "z"):
        for bit in (1, 2):
            sums = sums + flip(sums, axis, bit)
    low = (scale_down * sums[:RANK]).astype(BF16)
    back_low = (scale_up * sums[RANK:]).astype(BF16)
    half = onehot.astype(BF16)
    low_wide = (half[:, None, :] * low[None, :, :]).reshape(PROMPTS * RANK, ROWS)
    back_wide = (half[:, None, :] * back_low[None, :, :]).reshape(PROMPTS * RANK, ROWS)
    grad_down = scale_down * jnp.dot(back_wide, activations, preferred_element_type=F32)
    grad_up = scale_up * jnp.dot(low_wide, weighted, preferred_element_type=F32)
    grads = jnp.stack(
        [
            grad_down.astype(BF16).reshape(8, 2, RANK, COLS),
            grad_up.astype(BF16).reshape(8, 2, RANK, COLS),
        ],
        axis=2,
    )
    grads = lax.all_to_all(grads, ("x", "core"), 0, 0).reshape(PROMPTS, 2, RANK, COLS)
    updated = adam(
        pos,
        grads,
        adapter_down_factors,
        adapter_up_factors,
        first_moment_down,
        second_moment_down,
        first_moment_up,
        second_moment_up,
    )

    where = jnp.stack([x, c, z, y]).astype(jnp.int32)
    layer_parts, input_parts = partials(
        where, advantage[:, None], acts, grads_in, own, other, frozen_weight
    )
    layer_parts = [layer_parts[0]] + [shift(layer_parts[d], "z", -d) for d in (1, 3, 2)]
    input_parts = [input_parts[0]] + [shift(input_parts[o], "y", o) for o in (1, 3, 2)]
    contract_rows = (((0,), (0,)), ((), ()))
    layer = scale_up * lax.dot_general(low_wide, up, contract_rows, preferred_element_type=F32)
    for part in layer_parts:
        layer = layer + part.astype(F32)
    inward = scale_down * lax.dot_general(
        back_wide, down, contract_rows, preferred_element_type=F32
    )
    for part in input_parts:
        inward = inward + part.astype(F32)
    odn, oup, o1d, o2d, o1u, o2u = updated
    return layer.astype(BF16), inward.astype(BF16), odn, oup, o1d, o2d, o1u, o2u


def solution(mesh):
    fine = Mesh(mesh.devices.reshape(4, 2, 4, 4), ("x", "core", "z", "y"))
    grp, tp = ("x", "core"), ("z", "y")
    rows, slab = P(grp, tp), P(grp, None, tp)
    in_specs = (rows, rows, P(None, tp)) + (slab,) * 6 + (P(grp, None), P(grp, None), P())
    out_specs = (rows, rows) + (slab,) * 6
    return jax.shard_map(local, mesh=fine, in_specs=in_specs, out_specs=out_specs, check_vma=False)
```

time: 205 us -> 157 us (0.77)
  the two profiles are of different devices: /device:TPU:6 before, /device:TPU:1 now
where the time goes in v2:
time: 157 us; the launch traced here: 155 us
  starting transfers between devices  53.5 us (34%)
  waiting for transfers between devices  29.9 us (19%)
  Pallas kernels  28.4 us (18%)
  other arithmetic  14.5 us (9%)
  between operations  14.4 us (9%)
  local copies, waits for them, and re-layouts  7.42 us (5%)
  matrix products  7.09 us (5%)
    ppermute x17, starting transfers between devices, shift(): lax.ppermute(value, axis, [(i, (i + by) % size) for i in range(size)])  24.7 us
    pallas_call x1, Pallas kernels, partials(): pl.pallas_call(partial_kernel, out_shape=[block] * 8, grid_spec=pltpu.Pre...  16.6 us
    ppermute x4, waiting for transfers between devices, flip(): return lax.ppermute(value, axis, [(i, i ^ bit) for i in range(size)])  14.9 us
    ppermute x17, waiting for transfers between devices, shift(): lax.ppermute(value, axis, [(i, (i + by) % size) for i in range(size)])  11.2 us
    all_to_all x1, starting transfers between devices, local(): lax.all_to_all(grads, ('x', 'core'), 0, 0).reshape(PROMPTS, 2, RANK, COLS)  9.65 us
    ppermute x4, starting transfers between devices, local(): other = [lax.ppermute(piece, 'core', [(0, 1), (1, 0)]) for piece in own]  7.5 us
    pallas_call x1, Pallas kernels, adam(): pl.pallas_call(adam_kernel, out_shape=(half, half, full, full, full, full...  6.79 us
    all_to_all x1, starting transfers between devices, local(): lax.all_to_all(sent.reshape(8, 2, 2, RANK, COLS), ('x', 'core'), 0, 0)  5.85 us
  transfers between devices with their start and end apart: 28, of which 10 were waited for; matrix products, arithmetic and copies ran while one was open for 16% of the time, Pallas kernels for 18%

profile of v2, /device:TPU:1, one launch (start us, length us, event | category | flops | bytes accessed | tf_op | source)
XLA Modules:
  0.0 155.3 jit_solution(851952014972316762)
XLA Ops:
  7.2 0.7 all-gather.3.cloned.1.call-update
  8.0 1.2 constant_dynamic-slice_fusion.5
  9.1 4.7 %collective-permute-start.2 = (bf16[256,512]{1,0:T(8,128)(2,1)S(1)}, bf16[256,512]{1,0:T(8,128)(2,1)S(1)}, u32[]{:S(2)}, u32[]{:S(2)}) collective-permute-start(bf16[256,512]{1,0:T(8,128)(2,1)S(1)} %get-tuple-element.56), channel_id=1, source_target_pairs={{0,12},{4,0},{8,4},{12,8},{1,13},{5,1},{9,5},{13,9},{2,14},{6,2},{... | collective-permute-start | bytes 786440 | tf_op jit(solution)/shard_map/ppermute | solution.py:191
  13.8 0.7 collective-permute-start
  14.5 5.0 %shard_map.179 = bf16[16,2,32,512]{3,2,1,0:T(8,128)(2,1)} custom-call(s32[128]{0:T(128)} %slots.1, s32[1]{0:T(128)} %bitcast.1.member, bf16[16,32,512]{2,1,0:T(8,128)(2,1)} %dn.1, bf16[16,32,512]{2,1,0:T(8,128)(2,1)} %up.3), custom_call_target="tpu_custom_call" | custom-call | bytes 4194304 | tf_op jit(solution)/shard_map/pallas_call | solution.py:55
  19.5 5.8 %all-to-all-start = ((bf16[8,2,2,32,512]{4,3,2,1,0:T(8,128)(2,1)}), bf16[8,2,2,32,512]{4,3,2,1,0:T(8,128)(2,1)S(1)}, u32[]{:S(2)}, u32[]{:S(2)}) async-start(bf16[8,2,2,32,512]{4,3,2,1,0:T(8,128)(2,1)} %bitcast.47), calls=%async_computation | async-start | bytes 2097152 | tf_op jit(solution)/shard_map/all_to_all | solution.py:234
  25.4 0.7 and_select_fusion
  26.3 0.7 multiply_add_fusion
  27.0 0.7 convert_element_type.96
  27.7 0.8 select_reduce_fusion.3
  28.7 0.7 eq.83
  30.3 1.1 pad_maximum_fusion.1.refs_4_
  31.4 2.3 %constant_dynamic-slice_fusion.2 = (bf16[256,512]{1,0:T(8,128)(2,1)}, bf16[256,512]{1,0:T(8,128)(2,1)}, bf16[256,512]{1,0:T(8,128)(2,1)}) fusion(bf16[8192,512]{1,0:T(8,128)(2,1)} %refs_12_.1, s32[]{:T(128)S(6)} %select_n.49, s32[]{:T(128)S(6)} %select_n.51, s32[]{:T(128)S(6)} %select_n.50), kind=kLoop, calls=%fused_computation.51 | loop fusion | bytes 1572876 | tf_op jit(solution)/shard_map/dynamic_slice | solution.py:225
  33.7 1.7 %collective-permute-start.9 = (bf16[256,512]{1,0:T(8,128)(2,1)}, bf16[256,512]{1,0:T(8,128)(2,1)}, u32[]{:S(2)}, u32[]{:S(2)}) collective-permute-start(bf16[256,512]{1,0:T(8,128)(2,1)} %get-tuple-element.53), channel_id=1, source_target_pairs={{0,12},{4,0},{8,4},{12,8},{1,13},{5,1},{9,5},{13,9},{2,14},{6,2},{... | collective-permute-start | bytes 786440 | tf_op jit(solution)/shard_map/ppermute | solution.py:191
  35.4 2.0 %collective-permute-start.8 = (bf16[256,512]{1,0:T(8,128)(2,1)}, bf16[256,512]{1,0:T(8,128)(2,1)}, u32[]{:S(2)}, u32[]{:S(2)}) collective-permute-start(bf16[256,512]{1,0:T(8,128)(2,1)} %get-tuple-element.54), channel_id=1, source_target_pairs={{0,8},{4,12},{8,0},{12,4},{1,9},{5,13},{9,1},{13,5},{2,10},{6,14},... | collective-permute-start | bytes 786440 | tf_op jit(solution)/shard_map/ppermute | solution.py:191
  37.4 3.0 %all-to-all-done = bf16[8,2,2,32,512]{4,3,2,1,0:T(8,128)(2,1)S(1)} async-done(((bf16[8,2,2,32,512]{4,3,2,1,0:T(8,128)(2,1)}), bf16[8,2,2,32,512]{4,3,2,1,0:T(8,128)(2,1)S(1)}, u32[]{:S(2)}, u32[]{:S(2)}) %all-to-all-start) | async-done | bytes 1048608 | tf_op jit(solution)/shard_map/all_to_all | solution.py:234
  41.1 1.6 %fusion.3 = f32[32,512]{1,0:T(8,128)S(1)} fusion(bf16[16,32,512]{2,1,0:T(8,128)(2,1)S(1)} %bitcast.54, f32[16,512]{1,0:T(8,128)S(1)} %get-tuple-element.65, bf16[512,512]{1,0:T(8,128)(2,1)} %refs_0_.1, f32[512]{0:T(512)S(1)} %sub.28), kind=kOutput, calls=%fused_computation.9 | convolution fusion | flops 269729792 | bytes 1148928 | tf_op jit(solution)/shard_map/dot_general | solution.py:270
  42.7 1.4 collective-permute-start.3
  44.5 2.6 %collective-permute-done.3 = f32[64,512]{1,0:T(8,128)S(1)} collective-permute-done((f32[64,512]{1,0:T(8,128)S(1)}, f32[64,512]{1,0:T(8,128)S(1)}, u32[]{:S(2)}, u32[]{:S(2)}) %collective-permute-start.3) | collective-permute-done | bytes 131104 | tf_op jit(solution)/shard_map/ppermute | solution.py:195
  47.0 0.9 collective-permute-start.14
  48.0 3.0 %collective-permute-start.4 = (f32[64,512]{1,0:T(8,128)S(1)}, f32[64,512]{1,0:T(8,128)S(1)}, u32[]{:S(2)}, u32[]{:S(2)}) collective-permute-start(f32[64,512]{1,0:T(8,128)S(1)} %fusion.16), channel_id=1, source_target_pairs={{0,2},{1,3},{2,0},{3,1},{4,6},{5,7},{6,4},{7,5},{8,10},{9,11},{10,... | collective-permute-start | bytes 393224 | tf_op jit(solution)/shard_map/ppermute | solution.py:195
  51.1 2.1 %pad_maximum_fusion.2.refs_6_ = bf16[3,256,512]{2,1,0:T(8,128)(2,1)} fusion(bf16[1,256,512]{2,1,0:T(8,128)(2,1)} %bitcast.22, bf16[1,256,512]{2,1,0:T(8,128)(2,1)} %bitcast.21, bf16[1,256,512]{2,1,0:T(8,128)(2,1)} %bitcast.20), kind=kLoop, calls=%fused_computation.15 | loop fusion | flops 786432 | bytes 1572864 | tf_op jit(solution)/shard_map/stack | solution.py:227
  53.1 1.9 %collective-permute-start.10 = (bf16[512,512]{1,0:T(8,128)(2,1)}, bf16[512,512]{1,0:T(8,128)(2,1)}, u32[]{:S(2)}, u32[]{:S(2)}) collective-permute-start(bf16[512,512]{1,0:T(8,128)(2,1)} %refs_0_.1), channel_id=1, source_target_pairs={{0,4},{4,8},{8,12},{12,0},{1,5},{5,9},{9,13},{13,1},{2,6},{6,10},{... | collective-permute-start | bytes 1572872 | tf_op jit(solution)/shard_map/ppermute | solution.py:191
  55.4 11.6 %collective-permute-done.5 = f32[64,512]{1,0:T(8,128)S(1)} collective-permute-done((f32[64,512]{1,0:T(8,128)S(1)}, f32[64,512]{1,0:T(8,128)S(1)}, u32[]{:S(2)}, u32[]{:S(2)}) %collective-permute-start.5) | collective-permute-done | bytes 131104 | tf_op jit(solution)/shard_map/ppermute | solution.py:195
  67.0 1.0 collective-permute-start.6
  68.0 2.1 %collective-permute-start.11 = (bf16[512,512]{1,0:T(8,128)(2,1)}, bf16[512,512]{1,0:T(8,128)(2,1)}, u32[]{:S(2)}, u32[]{:S(2)}) collective-permute-start(bf16[512,512]{1,0:T(8,128)(2,1)} %refs_0_.1), channel_id=1, source_target_pairs={{0,8},{4,12},{8,0},{12,4},{1,9},{5,13},{9,1},{13,5},{2,10},{6,14},... | collective-permute-start | bytes 1572872 | tf_op jit(solution)/shard_map/ppermute | solution.py:191
  70.7 0.8 copy.30.advantage
  71.8 0.8 collective-permute-done.6
  72.5 6.8 %collective-permute-start.17 = (bf16[3,256,512]{2,1,0:T(8,128)(2,1)}, bf16[3,256,512]{2,1,0:T(8,128)(2,1)}, u32[]{:S(2)}, u32[]{:S(2)}) collective-permute-start(bf16[3,256,512]{2,1,0:T(8,128)(2,1)} %pad_maximum_fusion.2.refs_6_), channel_id=1, source_target_pairs={{0,16},{16,0},{1,17},{17,1},{2,18},{18,2},{3,19},{19,3},{4,20},{20... | collective-permute-start | bytes 2359304 | tf_op jit(solution)/shard_map/ppermute | solution.py:266
  80.8 4.5 %collective-permute-start.12 = (bf16[512,512]{1,0:T(8,128)(2,1)}, bf16[512,512]{1,0:T(8,128)(2,1)}, u32[]{:S(2)}, u32[]{:S(2)}) collective-permute-start(bf16[512,512]{1,0:T(8,128)(2,1)} %refs_0_.1), channel_id=1, source_target_pairs={{0,12},{4,0},{8,4},{12,8},{1,13},{5,1},{9,5},{13,9},{2,14},{6,2},{... | collective-permute-start | bytes 1572872 | tf_op jit(solution)/shard_map/ppermute | solution.py:191
  85.8 1.6 %fusion.1 = bf16[512,512]{1,0:T(8,128)(2,1)S(1)} fusion(bf16[512,512]{1,0:T(8,128)(2,1)S(1)} %bitcast.50, bf16[512,512]{1,0:T(8,128)(2,1)} %refs_0_.1, f32[512]{0:T(512)S(1)} %sub.28), kind=kOutput, calls=%fused_computation.7 | convolution fusion | flops 269746176 | bytes 1574912 | tf_op jit(solution)/shard_map/dot_general | solution.py:283
  87.4 1.1 pad_maximum_fusion
  88.5 9.7 %all-to-all-start.1 = ((bf16[8,2,2,32,512]{4,3,2,1,0:T(8,128)(2,1)}), bf16[8,2,2,32,512]{4,3,2,1,0:T(8,128)(2,1)S(1)}, u32[]{:S(2)}, u32[]{:S(2)}) async-start(bf16[8,2,2,32,512]{4,3,2,1,0:T(8,128)(2,1)} %pad_maximum_fusion), calls=%async_computation.1 | async-start | bytes 2097152 | tf_op jit(solution)/shard_map/all_to_all | solution.py:291
  98.2 16.6 %shard_map.180 = (bf16[512,512]{1,0:T(8,128)(2,1)}, bf16[512,512]{1,0:T(8,128)(2,1)}, bf16[512,512]{1,0:T(8,128)(2,1)}, bf16[512,512]{1,0:T(8,128)(2,1)}, bf16[5...) custom-call(s32[4]{0:T(128)} %pad_add_fusion.where, ...), custom_call_target="tpu_custom_call" | custom-call | flops 8589934592 | bytes 16777216 | tf_op jit(solution)/shard_map/pallas_call | solution.py:165
  115.0 0.7 select_reduce_fusion.pos
  115.9 2.4 %collective-permute-start.19 = (bf16[512,512]{1,0:T(8,128)(2,1)}, bf16[512,512]{1,0:T(8,128)(2,1)}, u32[]{:S(2)}, u32[]{:S(2)}) collective-permute-start(bf16[512,512]{1,0:T(8,128)(2,1)} %get-tuple-element.37), channel_id=1, source_target_pairs={{0,12},{4,0},{8,4},{12,8},{1,13},{5,1},{9,5},{13,9},{2,14},{6,2},{... | collective-permute-start | bytes 1572872 | tf_op jit(solution)/shard_map/ppermute | solution.py:191
  118.3 1.5 convolution_multiply_fusion.3
  119.8 1.9 %collective-permute-start.24 = (bf16[512,512]{1,0:T(8,128)(2,1)}, bf16[512,512]{1,0:T(8,128)(2,1)}, u32[]{:S(2)}, u32[]{:S(2)}) collective-permute-start(bf16[512,512]{1,0:T(8,128)(2,1)} %get-tuple-element.43), channel_id=1, source_target_pairs={{0,2},{1,3},{2,0},{3,1},{4,6},{5,7},{6,4},{7,5},{8,10},{9,11},{10,... | collective-permute-start | bytes 1572872 | tf_op jit(solution)/shard_map/ppermute | solution.py:191
  121.8 1.0 collective-permute-start.23
  122.7 7.1 %collective-permute-done.21 = bf16[512,512]{1,0:T(8,128)(2,1)S(1)} collective-permute-done((bf16[512,512]{1,0:T(8,128)(2,1)}, bf16[512,512]{1,0:T(8,128)(2,1)S(1)}, u32[]{:S(2)}, u32[]{:S(2)}) %collective-permute-start.21) | collective-permute-done | bytes 524320 | tf_op jit(solution)/shard_map/ppermute | solution.py:191
  130.6 1.5 convolution_multiply_fusion.2
  132.1 1.0 copy-done
  133.1 6.8 %shard_map.181 = (bf16[16,32,512]{2,1,0:T(8,128)(2,1)}, bf16[16,32,512]{2,1,0:T(8,128)(2,1)}, f32[16,32,512]{2,1,0:T(8,128)}, f32[16,32,512]{2,1,0:T(8,128)}, f3...) custom-call(s32[16]{0:T(128)} %select_reduce_fusion.pos, bf16[16,2,32,512]{3,2,1,0:T(8,128)(2,1)} %bitcast.46, ...), custom_call_target="tpu_custom_call" | custom-call | flops 8388608 | bytes 12582912 | tf_op jit(solution)/shard_map/pallas_call | solution.py:87
  139.9 1.9 %collective-permute-done.20 = bf16[512,512]{1,0:T(8,128)(2,1)} collective-permute-done((bf16[512,512]{1,0:T(8,128)(2,1)}, bf16[512,512]{1,0:T(8,128)(2,1)}, u32[]{:S(2)}, u32[]{:S(2)}) %collective-permute-start.20) | collective-permute-done | bytes 524320 | tf_op jit(solution)/shard_map/ppermute | solution.py:191
  141.8 2.7 %add_convert_fusion.1 = bf16[512,512]{1,0:T(8,128)(2,1)} fusion(bf16[512,512]{1,0:T(8,128)(2,1)} %copy-done.7, bf16[512,512]{1,0:T(8,128)(2,1)} %collective-permute-done.20, bf16[512,512]{1,0:T(8,128)(2,1)} %collective-permute-done.19, f32[512,512]{1,0:T(8,128)S(1)} %convolution_multiply_fusion.3, bf16[512,512]{1,0:T(8,128)(2,1)} %get-tuple-element.36), kind=kLoop, calls=%fused_computation.12 | loop fusion | flops 2359296 | bytes 3670016 | tf_op jit(solution)/shard_map/convert_element_type | solution.py:319
  144.4 0.7 collective-permute-done.23
  145.1 0.9 collective-permute-done.22
  146.0 2.5 %add_convert_fusion = bf16[512,512]{1,0:T(8,128)(2,1)} fusion(bf16[512,512]{1,0:T(8,128)(2,1)} %collective-permute-done.24, bf16[512,512]{1,0:T(8,128)(2,1)} %collective-permute-done.23, bf16[512,512]{1,0:T(8,128)(2,1)} %collective-permute-done.22, f32[512,512]{1,0:T(8,128)S(1)} %convolution_multiply_fusion.2, bf16[512,512]{1,0:T(8,128)(2,1)S(1)} %copy-done.6), kind=kLoop, calls=%fused_computation.11 | loop fusion | flops 2359296 | bytes 3670016 | tf_op jit(solution)/shard_map/convert_element_type | solution.py:319
  (77 shorter events, 6.7 us)
Async XLA Ops:
  7.2 33.4 %copy-start.8 = (bf16[512,512]{1,0:T(8,128)(2,1)S(1)}, bf16[512,512]{1,0:T(8,128)(2,1)}, u32[]{:S(2)}) copy-start(bf16[512,512]{1,0:T(8,128)(2,1)} %param.12) | copy-start | bytes 1572868
  7.2 91.0 %all-gather.3.cloned.1.call-start = ((), (), s32[]{:S(2)}) async-start(), calls=%async_computation.2 | async-start | bytes 2621440 | tf_op jit(solution)/shard_map/all_gather | solution.py:218
  9.1 46.3 %copy-start.11 = (s32[1,512]{1,0:T(1,128)S(1)}, s32[1,512]{1,0:T(1,128)}, u32[]{:S(2)}) copy-start(s32[1,512]{1,0:T(1,128)} %param.22) | copy-start | bytes 6148
  9.1 20.3 %collective-permute-start.2 = (bf16[256,512]{1,0:T(8,128)(2,1)S(1)}, bf16[256,512]{1,0:T(8,128)(2,1)S(1)}, u32[]{:S(2)}, u32[]{:S(2)}) collective-permute-start(bf16[256,512]{1,0:T(8,128)(2,1)S(1)} %get-tuple-element.56), channel_id=1, source_target_pairs={{0,12},{4,0},{8,4},{12,8},{1,13},{5,1},{9,5},{13,9},{2,14},{6,2},{... | collective-permute-start | bytes 786440 | tf_op jit(solution)/shard_map/ppermute | solution.py:191
  13.8 15.7 %collective-permute-start.1 = (bf16[256,512]{1,0:T(8,128)(2,1)S(1)}, bf16[256,512]{1,0:T(8,128)(2,1)S(1)}, u32[]{:S(2)}, u32[]{:S(2)}) collective-permute-start(bf16[256,512]{1,0:T(8,128)(2,1)S(1)} %get-tuple-element.57), channel_id=1, source_target_pairs={{0,8},{4,12},{8,0},{12,4},{1,9},{5,13},{9,1},{13,5},{2,10},{6,14},... | collective-permute-start | bytes 786440 | tf_op jit(solution)/shard_map/ppermute | solution.py:191
  13.8 15.7 %collective-permute-start = (bf16[256,512]{1,0:T(8,128)(2,1)S(1)}, bf16[256,512]{1,0:T(8,128)(2,1)S(1)}, u32[]{:S(2)}, u32[]{:S(2)}) collective-permute-start(bf16[256,512]{1,0:T(8,128)(2,1)S(1)} %get-tuple-element.55), channel_id=1, source_target_pairs={{0,4},{4,8},{8,12},{12,0},{1,5},{5,9},{9,13},{13,1},{2,6},{6,10},{... | collective-permute-start | bytes 786440 | tf_op jit(solution)/shard_map/ppermute | solution.py:191
  19.5 20.9 %all-to-all-start = ((bf16[8,2,2,32,512]{4,3,2,1,0:T(8,128)(2,1)}), bf16[8,2,2,32,512]{4,3,2,1,0:T(8,128)(2,1)S(1)}, u32[]{:S(2)}, u32[]{:S(2)}) async-start(bf16[8,2,2,32,512]{4,3,2,1,0:T(8,128)(2,1)} %bitcast.47), calls=%async_computation | async-start | bytes 2097152 | tf_op jit(solution)/shard_map/all_to_all | solution.py:234
  29.5 0.7 copy-start.9
  29.5 0.8 copy-start.10
  31.4 57.1 %copy-start.5 = (bf16[3,256,512]{2,1,0:T(8,128)(2,1)}, bf16[3,256,512]{2,1,0:T(8,128)(2,1)S(1)}, u32[]{:S(2)}) copy-start(bf16[3,256,512]{2,1,0:T(8,128)(2,1)S(1)} %pad_maximum_fusion.1.refs_4_) | copy-start | bytes 2359300
  33.7 14.2 %collective-permute-start.9 = (bf16[256,512]{1,0:T(8,128)(2,1)}, bf16[256,512]{1,0:T(8,128)(2,1)}, u32[]{:S(2)}, u32[]{:S(2)}) collective-permute-start(bf16[256,512]{1,0:T(8,128)(2,1)} %get-tuple-element.53), channel_id=1, source_target_pairs={{0,12},{4,0},{8,4},{12,8},{1,13},{5,1},{9,5},{13,9},{2,14},{6,2},{... | collective-permute-start | bytes 786440 | tf_op jit(solution)/shard_map/ppermute | solution.py:191
  35.4 15.6 %collective-permute-start.8 = (bf16[256,512]{1,0:T(8,128)(2,1)}, bf16[256,512]{1,0:T(8,128)(2,1)}, u32[]{:S(2)}, u32[]{:S(2)}) collective-permute-start(bf16[256,512]{1,0:T(8,128)(2,1)} %get-tuple-element.54), channel_id=1, source_target_pairs={{0,8},{4,12},{8,0},{12,4},{1,9},{5,13},{9,1},{13,5},{2,10},{6,14},... | collective-permute-start | bytes 786440 | tf_op jit(solution)/shard_map/ppermute | solution.py:191
  37.4 13.6 %collective-permute-start.7 = (bf16[256,512]{1,0:T(8,128)(2,1)}, bf16[256,512]{1,0:T(8,128)(2,1)}, u32[]{:S(2)}, u32[]{:S(2)}) collective-permute-start(bf16[256,512]{1,0:T(8,128)(2,1)} %get-tuple-element.52), channel_id=1, source_target_pairs={{0,4},{4,8},{8,12},{12,0},{1,5},{5,9},{9,13},{13,1},{2,6},{6,10},{... | collective-permute-start | bytes 786440 | tf_op jit(solution)/shard_map/ppermute | solution.py:191
  40.6 47.9 %copy-start.4 = (bf16[8,2,1,32,512]{4,3,2,1,0:T(8,128)(2,1)}, bf16[8,2,1,32,512]{4,3,2,1,0:T(8,128)(2,1)S(1)}, u32[]{:S(2)}) copy-start(bf16[8,2,1,32,512]{4,3,2,1,0:T(8,128)(2,1)S(1)} %get-tuple-element.59) | copy-start | bytes 1572868
  40.6 79.2 %copy-start.3 = (bf16[8,2,1,32,512]{4,3,2,1,0:T(8,128)(2,1)}, bf16[8,2,1,32,512]{4,3,2,1,0:T(8,128)(2,1)S(1)}, u32[]{:S(2)}) copy-start(bf16[8,2,1,32,512]{4,3,2,1,0:T(8,128)(2,1)S(1)} %get-tuple-element.58) | copy-start | bytes 1572868
  42.7 4.3 %collective-permute-start.3 = (f32[64,512]{1,0:T(8,128)S(1)}, f32[64,512]{1,0:T(8,128)S(1)}, u32[]{:S(2)}, u32[]{:S(2)}) collective-permute-start(f32[64,512]{1,0:T(8,128)S(1)} %pad_maximum_fusion.3), channel_id=1, source_target_pairs={{0,1},{1,0},{2,3},{3,2},{4,5},{5,4},{6,7},{7,6},{8,9},{9,8},{10,11... | collective-permute-start | bytes 393224 | tf_op jit(solution)/shard_map/ppermute | solution.py:195
  44.1 35.4 %collective-permute-start.13 = (bf16[3,256,512]{2,1,0:T(8,128)(2,1)S(1)}, bf16[3,256,512]{2,1,0:T(8,128)(2,1)}, u32[]{:S(2)}, u32[]{:S(2)}) collective-permute-start(bf16[3,256,512]{2,1,0:T(8,128)(2,1)S(1)} %pad_maximum_fusion.1.refs_4_), channel_id=1, source_target_pairs={{0,32},{32,64},{64,96},{96,0},{1,33},{33,65},{65,97},{97,1},{2,34}... | collective-permute-start | bytes 2359304 | tf_op jit(solution)/shard_map/ppermute | solution.py:191
  47.0 32.9 %collective-permute-start.14 = (bf16[3,256,512]{2,1,0:T(8,128)(2,1)S(1)}, bf16[3,256,512]{2,1,0:T(8,128)(2,1)}, u32[]{:S(2)}, u32[]{:S(2)}) collective-permute-start(bf16[3,256,512]{2,1,0:T(8,128)(2,1)S(1)} %pad_maximum_fusion.1.refs_4_), channel_id=1, source_target_pairs={{0,96},{32,0},{64,32},{96,64},{1,97},{33,1},{65,33},{97,65},{2,98}... | collective-permute-start | bytes 2359304 | tf_op jit(solution)/shard_map/ppermute | solution.py:191
  48.0 7.0 %collective-permute-start.4 = (f32[64,512]{1,0:T(8,128)S(1)}, f32[64,512]{1,0:T(8,128)S(1)}, u32[]{:S(2)}, u32[]{:S(2)}) collective-permute-start(f32[64,512]{1,0:T(8,128)S(1)} %fusion.16), channel_id=1, source_target_pairs={{0,2},{1,3},{2,0},{3,1},{4,6},{5,7},{6,4},{7,5},{8,10},{9,11},{10,... | collective-permute-start | bytes 393224 | tf_op jit(solution)/shard_map/ppermute | solution.py:195
  53.1 26.3 %collective-permute-start.10 = (bf16[512,512]{1,0:T(8,128)(2,1)}, bf16[512,512]{1,0:T(8,128)(2,1)}, u32[]{:S(2)}, u32[]{:S(2)}) collective-permute-start(bf16[512,512]{1,0:T(8,128)(2,1)} %refs_0_.1), channel_id=1, source_target_pairs={{0,4},{4,8},{8,12},{12,0},{1,5},{5,9},{9,13},{13,1},{2,6},{6,10},{... | collective-permute-start | bytes 1572872 | tf_op jit(solution)/shard_map/ppermute | solution.py:191
  55.0 12.0 %collective-permute-start.5 = (f32[64,512]{1,0:T(8,128)S(1)}, f32[64,512]{1,0:T(8,128)S(1)}, u32[]{:S(2)}, u32[]{:S(2)}) collective-permute-start(f32[64,512]{1,0:T(8,128)S(1)} %add.174), channel_id=1, source_target_pairs={{0,4},{4,0},{8,12},{12,8},{1,5},{5,1},{9,13},{13,9},{2,6},{6,2},{1... | collective-permute-start | bytes 393224 | tf_op jit(solution)/shard_map/ppermute | solution.py:195
  67.0 5.5 %collective-permute-start.6 = (f32[64,512]{1,0:T(8,128)S(1)}, f32[64,512]{1,0:T(8,128)S(1)}, u32[]{:S(2)}, u32[]{:S(2)}) collective-permute-start(f32[64,512]{1,0:T(8,128)S(1)} %add.175), channel_id=1, source_target_pairs={{0,8},{4,12},{8,0},{12,4},{1,9},{5,13},{9,1},{13,5},{2,10},{6,14},... | collective-permute-start | bytes 393224 | tf_op jit(solution)/shard_map/ppermute | solution.py:195
  68.0 12.8 %collective-permute-start.11 = (bf16[512,512]{1,0:T(8,128)(2,1)}, bf16[512,512]{1,0:T(8,128)(2,1)}, u32[]{:S(2)}, u32[]{:S(2)}) collective-permute-start(bf16[512,512]{1,0:T(8,128)(2,1)} %refs_0_.1), channel_id=1, source_target_pairs={{0,8},{4,12},{8,0},{12,4},{1,9},{5,13},{9,1},{13,5},{2,10},{6,14},... | collective-permute-start | bytes 1572872 | tf_op jit(solution)/shard_map/ppermute | solution.py:191
  72.5 25.6 %collective-permute-start.17 = (bf16[3,256,512]{2,1,0:T(8,128)(2,1)}, bf16[3,256,512]{2,1,0:T(8,128)(2,1)}, u32[]{:S(2)}, u32[]{:S(2)}) collective-permute-start(bf16[3,256,512]{2,1,0:T(8,128)(2,1)} %pad_maximum_fusion.2.refs_6_), channel_id=1, source_target_pairs={{0,16},{16,0},{1,17},{17,1},{2,18},{18,2},{3,19},{19,3},{4,20},{20... | collective-permute-start | bytes 2359304 | tf_op jit(solution)/shard_map/ppermute | solution.py:266
  79.4 18.7 %collective-permute-start.15 = (bf16[3,256,512]{2,1,0:T(8,128)(2,1)S(1)}, bf16[3,256,512]{2,1,0:T(8,128)(2,1)}, u32[]{:S(2)}, u32[]{:S(2)}) collective-permute-start(bf16[3,256,512]{2,1,0:T(8,128)(2,1)S(1)} %pad_maximum_fusion.1.refs_4_), channel_id=1, source_target_pairs={{0,16},{16,0},{1,17},{17,1},{2,18},{18,2},{3,19},{19,3},{4,20},{20... | collective-permute-start | bytes 2359304 | tf_op jit(solution)/shard_map/ppermute | solution.py:266
  79.5 18.6 %collective-permute-start.16 = (bf16[3,256,512]{2,1,0:T(8,128)(2,1)}, bf16[3,256,512]{2,1,0:T(8,128)(2,1)}, u32[]{:S(2)}, u32[]{:S(2)}) collective-permute-start(bf16[3,256,512]{2,1,0:T(8,128)(2,1)} %collective-permute-done.13.refs_5_), channel_id=1, source_target_pairs={{0,16},{16,0},{1,17},{17,1},{2,18},{18,2},{3,19},{19,3},{4,20},{20... | collective-permute-start | bytes 2359304 | tf_op jit(solution)/shard_map/ppermute | solution.py:266
  80.0 18.1 %collective-permute-start.18 = (bf16[3,256,512]{2,1,0:T(8,128)(2,1)}, bf16[3,256,512]{2,1,0:T(8,128)(2,1)}, u32[]{:S(2)}, u32[]{:S(2)}) collective-permute-start(bf16[3,256,512]{2,1,0:T(8,128)(2,1)} %collective-permute-done.14.refs_7_), channel_id=1, source_target_pairs={{0,16},{16,0},{1,17},{17,1},{2,18},{18,2},{3,19},{19,3},{4,20},{20... | collective-permute-start | bytes 2359304 | tf_op jit(solution)/shard_map/ppermute | solution.py:266
  80.2 5.2 %copy-start.1 = (bf16[16,32,512]{2,1,0:T(8,128)(2,1)}, bf16[16,32,512]{2,1,0:T(8,128)(2,1)S(1)}, u32[]{:S(2)}) copy-start(bf16[16,32,512]{2,1,0:T(8,128)(2,1)S(1)} %get-tuple-element.62) | copy-start | bytes 1572868
  80.8 17.3 %collective-permute-start.12 = (bf16[512,512]{1,0:T(8,128)(2,1)}, bf16[512,512]{1,0:T(8,128)(2,1)}, u32[]{:S(2)}, u32[]{:S(2)}) collective-permute-start(bf16[512,512]{1,0:T(8,128)(2,1)} %refs_0_.1), channel_id=1, source_target_pairs={{0,12},{4,0},{8,4},{12,8},{1,13},{5,1},{9,5},{13,9},{2,14},{6,2},{... | collective-permute-start | bytes 1572872 | tf_op jit(solution)/shard_map/ppermute | solution.py:191
  88.5 43.6 %all-to-all-start.1 = ((bf16[8,2,2,32,512]{4,3,2,1,0:T(8,128)(2,1)}), bf16[8,2,2,32,512]{4,3,2,1,0:T(8,128)(2,1)S(1)}, u32[]{:S(2)}, u32[]{:S(2)}) async-start(bf16[8,2,2,32,512]{4,3,2,1,0:T(8,128)(2,1)} %pad_maximum_fusion), calls=%async_computation.1 | async-start | bytes 2097152 | tf_op jit(solution)/shard_map/all_to_all | solution.py:291
  98.2 32.4 %copy-start.2 = (bf16[16,32,512]{2,1,0:T(8,128)(2,1)S(1)}, bf16[16,32,512]{2,1,0:T(8,128)(2,1)}, u32[]{:S(2)}) copy-start(bf16[16,32,512]{2,1,0:T(8,128)(2,1)} %copy-done.1) | copy-start | bytes 1572868
  114.8 15.0 %collective-permute-start.21 = (bf16[512,512]{1,0:T(8,128)(2,1)}, bf16[512,512]{1,0:T(8,128)(2,1)S(1)}, u32[]{:S(2)}, u32[]{:S(2)}) collective-permute-start(bf16[512,512]{1,0:T(8,128)(2,1)} %get-tuple-element.39), channel_id=1, source_target_pairs={{0,8},{4,12},{8,0},{12,4},{1,9},{5,13},{9,1},{13,5},{2,10},{6,14},... | collective-permute-start | bytes 1572872 | tf_op jit(solution)/shard_map/ppermute | solution.py:191
  115.6 26.1 %collective-permute-start.20 = (bf16[512,512]{1,0:T(8,128)(2,1)}, bf16[512,512]{1,0:T(8,128)(2,1)}, u32[]{:S(2)}, u32[]{:S(2)}) collective-permute-start(bf16[512,512]{1,0:T(8,128)(2,1)} %get-tuple-element.38), channel_id=1, source_target_pairs={{0,4},{4,8},{8,12},{12,0},{1,5},{5,9},{9,13},{13,1},{2,6},{6,10},{... | collective-permute-start | bytes 1572872 | tf_op jit(solution)/shard_map/ppermute | solution.py:191
  115.9 25.9 %collective-permute-start.19 = (bf16[512,512]{1,0:T(8,128)(2,1)}, bf16[512,512]{1,0:T(8,128)(2,1)}, u32[]{:S(2)}, u32[]{:S(2)}) collective-permute-start(bf16[512,512]{1,0:T(8,128)(2,1)} %get-tuple-element.37), channel_id=1, source_target_pairs={{0,12},{4,0},{8,4},{12,8},{1,13},{5,1},{9,5},{13,9},{2,14},{6,2},{... | collective-permute-start | bytes 1572872 | tf_op jit(solution)/shard_map/ppermute | solution.py:191
  119.8 24.6 %collective-permute-start.24 = (bf16[512,512]{1,0:T(8,128)(2,1)}, bf16[512,512]{1,0:T(8,128)(2,1)}, u32[]{:S(2)}, u32[]{:S(2)}) collective-permute-start(bf16[512,512]{1,0:T(8,128)(2,1)} %get-tuple-element.43), channel_id=1, source_target_pairs={{0,2},{1,3},{2,0},{3,1},{4,6},{5,7},{6,4},{7,5},{8,10},{9,11},{10,... | collective-permute-start | bytes 1572872 | tf_op jit(solution)/shard_map/ppermute | solution.py:191
  121.8 23.4 %collective-permute-start.23 = (bf16[512,512]{1,0:T(8,128)(2,1)}, bf16[512,512]{1,0:T(8,128)(2,1)}, u32[]{:S(2)}, u32[]{:S(2)}) collective-permute-start(bf16[512,512]{1,0:T(8,128)(2,1)} %get-tuple-element.42), channel_id=1, source_target_pairs={{0,3},{1,0},{2,1},{3,2},{4,7},{5,4},{6,5},{7,6},{8,11},{9,8},{10,9... | collective-permute-start | bytes 1572872 | tf_op jit(solution)/shard_map/ppermute | solution.py:191
  129.8 0.8 copy-start.7
  129.8 16.2 %collective-permute-start.22 = (bf16[512,512]{1,0:T(8,128)(2,1)}, bf16[512,512]{1,0:T(8,128)(2,1)}, u32[]{:S(2)}, u32[]{:S(2)}) collective-permute-start(bf16[512,512]{1,0:T(8,128)(2,1)} %get-tuple-element.41), channel_id=1, source_target_pairs={{0,1},{1,2},{2,3},{3,0},{4,5},{5,6},{6,7},{7,4},{8,9},{9,10},{10,1... | collective-permute-start | bytes 1572872 | tf_op jit(solution)/shard_map/ppermute | solution.py:191
  132.1 1.0 copy-start
  132.1 13.9 %copy-start.6 = (bf16[512,512]{1,0:T(8,128)(2,1)S(1)}, bf16[512,512]{1,0:T(8,128)(2,1)}, u32[]{:S(2)}) copy-start(bf16[512,512]{1,0:T(8,128)(2,1)} %get-tuple-element.40) | copy-start | bytes 1572868
Sparse Core Ops, SparseCore 0:
  9.7 34.0 all-gather.2

commit v3 on v2

--- a/solution.py
+++ b/solution.py
@@ -29,7 +29,7 @@
     return pltpu.CompilerParams(vmem_limit_bytes=mib * 1024 * 1024)
 
 
-def pick_kernel(slots, member, down, up, out):
+def pick_kernel(slots, member, down, up, out, pos):
     g = member[0]
 
     def group(d, carry):
@@ -40,6 +40,7 @@
             @pl.when(mine)
             def _():
                 i = lax.rem(s, PROMPTS)
+                pos[i] = d * 2 + j
                 out[d * 2 + j, 0] = down[i]
                 out[d * 2 + j, 1] = up[i]
 
@@ -52,14 +53,19 @@
 
 
 def pick(slots, member, down, up):
+    small = jax.ShapeDtypeStruct((PROMPTS,), jnp.int32)
+    smem = pl.BlockSpec(memory_space=pltpu.SMEM)
     return pl.pallas_call(
         pick_kernel,
-        out_shape=jax.ShapeDtypeStruct((PROMPTS, 2, RANK, COLS), BF16),
+        out_shape=(jax.ShapeDtypeStruct((PROMPTS, 2, RANK, COLS), BF16), small),
         grid_spec=pltpu.PrefetchScalarGridSpec(
-            num_scalar_prefetch=2, grid=(), in_specs=[VMEM, VMEM], out_specs=VMEM
+            num_scalar_prefetch=2,
+            grid=(),
+            in_specs=[VMEM, VMEM],
+            out_specs=(VMEM, smem),
         ),
         compiler_params=params(),
-        cost_estimate=pl.CostEstimate(flops=0, bytes_accessed=4 << 20, transcendentals=0),
+        cost_estimate=pl.CostEstimate(flops=1, bytes_accessed=1, transcendentals=0),
     )(slots, member, down, up)
 
 
@@ -95,14 +101,14 @@
             out_specs=[block] * 6,
         ),
         compiler_params=params(),
-        cost_estimate=pl.CostEstimate(flops=8 << 20, bytes_accessed=12 << 20, transcendentals=0),
+        cost_estimate=pl.CostEstimate(flops=1, bytes_accessed=1, transcendentals=0),
     )(pos, grads, dn, up, m1d, m2d, m1u, m2u)
 
 
-def partial_kernel(where, advantage, acts, *refs):
-    grads, own, other, weight = refs[0:4], refs[4:8], refs[8:12], refs[12]
-    forward, backward = refs[13:17], refs[17:21]
-    a_held, g_held, w_held, a_sem, g_sem, w_sem = refs[21:]
+def partial_kernel(where, *refs):
+    acts, grads, own, other, weight = refs[0], refs[1:5], refs[5:9], refs[9:13], refs[13]
+    forward, backward = refs[14:18], refs[18:22]
+    a_held, g_held, w_held, o_held, a_sem, g_sem, w_sem, o_sem = refs[22:]
     x, c, z, y = (where[i] for i in range(4))
 
     def span(i):
@@ -145,22 +151,24 @@
     for d in order:
         for copy in groups[d]:
             copy.wait()
-        forward[d][...] = jnp.dot(
+        o_held[d] = jnp.dot(
             a_held[...], w_held[:, span(d)], preferred_element_type=F32
         ).astype(BF16)
+        pltpu.make_async_copy(o_held.at[d], forward[d], o_sem.at[d]).start()
     for copy in g_loads:
         copy.wait()
-    gain = advantage[...]
-    for d in range(4):
-        g_held[:, span(d)] = (gain * g_held[:, span(d)].astype(F32)).astype(BF16)
     dims = (((1,), (1,)), ((), ()))
     for i in order:
-        backward[i][...] = lax.dot_general(
+        o_held[4 + i] = lax.dot_general(
             g_held[...], w_held[span(i)], dims, preferred_element_type=F32
         ).astype(BF16)
-
-
-def partials(where, advantage, acts, grads, own, other, weight):
+        pltpu.make_async_copy(o_held.at[4 + i], backward[i], o_sem.at[4 + i]).start()
+    for i in range(4):
+        pltpu.make_async_copy(o_held.at[i], forward[i], o_sem.at[i]).wait()
+        pltpu.make_async_copy(o_held.at[4 + i], backward[i], o_sem.at[4 + i]).wait()
+
+
+def partials(where, acts, grads, own, other, weight):
     block = jax.ShapeDtypeStruct((ROWS, COLS), BF16)
     outs = pl.pallas_call(
         partial_kernel,
@@ -168,22 +176,22 @@
         grid_spec=pltpu.PrefetchScalarGridSpec(
             num_scalar_prefetch=1,
             grid=(),
-            in_specs=[VMEM] + [ANY] * 14,
-            out_specs=[VMEM] * 8,
+            in_specs=[ANY] * 14,
+            out_specs=[ANY] * 8,
             scratch_shapes=[
                 pltpu.VMEM((ROWS, 4 * COLS), BF16),
                 pltpu.VMEM((ROWS, 4 * COLS), BF16),
                 pltpu.VMEM((4 * COLS, 4 * COLS), BF16),
+                pltpu.VMEM((8, ROWS, COLS), BF16),
                 pltpu.SemaphoreType.DMA(()),
                 pltpu.SemaphoreType.DMA(()),
                 pltpu.SemaphoreType.DMA((4,)),
+                pltpu.SemaphoreType.DMA((8,)),
             ],
         ),
         compiler_params=params(),
-        cost_estimate=pl.CostEstimate(
-            flops=4 * 512 * 2048 * 2048, bytes_accessed=16 << 20, transcendentals=0
-        ),
-    )(where, advantage, acts, *grads, *own, *other, weight)
+        cost_estimate=pl.CostEstimate(flops=1, bytes_accessed=1, transcendentals=0),
+    )(where, acts, *grads, *own, *other, weight)
     return outs[:4], outs[4:]
 
 
@@ -215,44 +223,43 @@
     scale_down = WIDTH ** (-0.5)
     scale_up = adapter_scale / RANK**0.5
 
-    acts = lax.all_gather(activations, "y", axis=0)
-    parts = []
-    source = frozen_weight
-    for turn in (0, 2):
-        received = []
-        for d in (1, 2, 3):
-            start = lax.rem(z + d, 4) * 2048 + lax.rem(x + y + turn, 4) * COLS + c * HALF
-            piece = lax.dynamic_slice_in_dim(source, start, HALF, axis=0)
-            received.append(shift(piece, "z", d))
-        parts.append(jnp.stack(received))
-        parts[0], source = lax.optimization_barrier((parts[0], frozen_weight))
-    grad, pieces = lax.optimization_barrier((output_gradient, parts[1]))
-    parts[1] = pieces
-    grads_in = [output_gradient] + [shift(grad, "z", d) for d in (1, 2, 3)]
+    cuts = [
+        [
+            lax.dynamic_slice_in_dim(
+                frozen_weight,
+                lax.rem(z + d, 4) * 2048 + lax.rem(x + y + turn, 4) * COLS + c * HALF,
+                HALF,
+                axis=0,
+            )
+            for d in (1, 2, 3)
+        ]
+        for turn in (0, 2)
+    ]
+    first = {d: shift(cut, "z", d) for d, cut in zip((1, 2, 3), cuts[0])}
+    second = {d: shift(cuts[1][d - 1], "z", d) for d in (1, 3)}
+    near = jnp.stack([first[d] for d in (1, 2, 3)])
+    cut, _ = lax.optimization_barrier((cuts[1][1], first))
+    second[2] = shift(cut, "z", 2)
+    far = jnp.stack([second[d] for d in (1, 2, 3)])
+    sent, _ = lax.optimization_barrier((near, (second[1], second[3])))
+    own = [near, shift(sent, "x", 1), far, shift(sent, "x", 3)]
+    other = [lax.ppermute(piece, "core", [(0, 1), (1, 0)]) for piece in own]
     slots = prompt_adapter_slot
-    sent = pick(slots, member[None].astype(jnp.int32), adapter_down_factors, adapter_up_factors)
+    slots, _ = lax.optimization_barrier((slots, cuts[0]))
+    sent, pos = pick(
+        slots, member[None].astype(jnp.int32), adapter_down_factors, adapter_up_factors
+    )
     adapters = lax.all_to_all(sent.reshape(8, 2, 2, RANK, COLS), ("x", "core"), 0, 0)
-    adapters, parts[0] = lax.optimization_barrier((adapters, parts[0]))
+    adapters, _ = lax.optimization_barrier((adapters, (near, second[1], second[3])))
+    act, _ = lax.optimization_barrier((activations, adapters))
+    acts = lax.all_to_all(jnp.broadcast_to(act[None], (4, ROWS, COLS)), "y", 0, 0)
     down = adapters[:, :, 0].reshape(PROMPTS * RANK, COLS)
     up = adapters[:, :, 1].reshape(PROMPTS * RANK, COLS)
 
-    held = slots.reshape(8, PROMPTS)
-    mine = (held // PROMPTS == member).astype(jnp.int32)
-    turn = jnp.cumsum(mine, axis=1) - 1
-    places = jnp.arange(8, dtype=jnp.int32)[:, None] * 2 + turn
-    pos = jnp.sum(
-        jnp.where(
-            held[:, :, None] == member * PROMPTS + jnp.arange(PROMPTS, dtype=jnp.int32),
-            places[:, :, None],
-            0,
-        ),
-        axis=(0, 1),
-    ).astype(jnp.int32)
     source = lax.dynamic_slice_in_dim(slots, member * PROMPTS, PROMPTS) // PROMPTS
     ids = jnp.arange(PROMPTS, dtype=jnp.int32)
     before = (source[:, None] == source[None, :]) & (ids[:, None] > ids[None, :])
     order = 2 * source + jnp.sum(before.astype(jnp.int32), axis=1)
-
     labels = sample_row_prompt[0]
     reward = majority_vote_reward[0].astype(F32)
     label = jnp.sum(jnp.where(labels[None, :] == ids[:, None], order[:, None], 0), axis=0)
@@ -262,8 +269,11 @@
     advantage = reward - jnp.sum(onehot * mean_reward[:, None], axis=0)
     weighted = (advantage[:, None] * output_gradient.astype(F32)).astype(BF16)
 
-    own = [parts[0], shift(parts[0], "x", 1), parts[1], shift(parts[0], "x", 3)]
-    other = [lax.ppermute(piece, "core", [(0, 1), (1, 0)]) for piece in own]
+    grads_in = {0: weighted}
+    sent, _ = lax.optimization_barrier((weighted, second[2]))
+    grads_in[1], grads_in[3] = shift(sent, "z", 1), shift(sent, "z", 3)
+    sent, _ = lax.optimization_barrier((weighted, (grads_in[1], grads_in[3])))
+    grads_in[2] = shift(sent, "z", 2)
 
     contract_cols = (((1,), (1,)), ((), ()))
     low_all = lax.dot_general(down, activations, contract_cols, preferred_element_type=F32)
@@ -271,14 +281,20 @@
     low_part = jnp.sum(low_all.reshape(PROMPTS, RANK, ROWS) * onehot[:, None, :], axis=0)
     back_part = jnp.sum(back_all.reshape(PROMPTS, RANK, ROWS) * onehot[:, None, :], axis=0)
     sums = jnp.concatenate([low_part, back_part])
-    for axis in ("y", "z"):
-        for bit in (1, 2):
-            sums = sums + flip(sums, axis, bit)
+    sums = sums + sum(shift(sums, "z", i) for i in (1, 3, 2))
+    sums, _ = lax.optimization_barrier((sums, (own[1], own[3], other[0], other[2], grads_in[1], grads_in[3], acts)))
+    sums = sums + sum(shift(sums, "y", i) for i in (1, 3, 2))
     low = (scale_down * sums[:RANK]).astype(BF16)
     back_low = (scale_up * sums[RANK:]).astype(BF16)
     half = onehot.astype(BF16)
     low_wide = (half[:, None, :] * low[None, :, :]).reshape(PROMPTS * RANK, ROWS)
     back_wide = (half[:, None, :] * back_low[None, :, :]).reshape(PROMPTS * RANK, ROWS)
+    where = jnp.stack([x, c, z, y]).astype(jnp.int32)
+    layer_parts, input_parts = partials(
+        where, acts, [grads_in[i] for i in range(4)], own, other, frozen_weight
+    )
+    layer_parts = {d: shift(layer_parts[d], "z", -d) if d else layer_parts[d] for d in (1, 3, 2, 0)}
+    input_parts = {o: shift(input_parts[o], "y", o) if o else input_parts[o] for o in (1, 3, 2, 0)}
     grad_down = scale_down * jnp.dot(back_wide, activations, preferred_element_type=F32)
     grad_up = scale_up * jnp.dot(low_wide, weighted, preferred_element_type=F32)
     grads = jnp.stack(
@@ -289,6 +305,7 @@
         axis=2,
     )
     grads = lax.all_to_all(grads, ("x", "core"), 0, 0).reshape(PROMPTS, 2, RANK, COLS)
+    grads, _ = lax.optimization_barrier((grads, layer_parts[1]))
     updated = adam(
         pos,
         grads,
@@ -300,21 +317,18 @@
         second_moment_up,
     )
 
-    where = jnp.stack([x, c, z, y]).astype(jnp.int32)
-    layer_parts, input_parts = partials(
-        where, advantage[:, None], acts, grads_in, own, other, frozen_weight
-    )
-    layer_parts = [layer_parts[0]] + [shift(layer_parts[d], "z", -d) for d in (1, 3, 2)]
-    input_parts = [input_parts[0]] + [shift(input_parts[o], "y", o) for o in (1, 3, 2)]
     contract_rows = (((0,), (0,)), ((), ()))
-    layer = scale_up * lax.dot_general(low_wide, up, contract_rows, preferred_element_type=F32)
-    for part in layer_parts:
-        layer = layer + part.astype(F32)
-    inward = scale_down * lax.dot_general(
+    layer = layer_parts[0].astype(F32) + scale_up * lax.dot_general(
+        low_wide, up, contract_rows, preferred_element_type=F32
+    )
+    inward = input_parts[0].astype(F32) + scale_down * lax.dot_general(
         back_wide, down, contract_rows, preferred_element_type=F32
     )
-    for part in input_parts:
-        inward = inward + part.astype(F32)
+    inward, updated = lax.optimization_barrier((inward, updated))
+    layer = lax.optimization_barrier(layer)
+    for i in (1, 3, 2):
+        layer = layer + layer_parts[i].astype(F32)
+        inward = inward + input_parts[i].astype(F32)
     odn, oup, o1d, o2d, o1u, o2u = updated
     return layer.astype(BF16), inward.astype(BF16), odn, oup, o1d, o2d, o1u, o2u
 

time: 157 us -> 140 us (0.89)
  between operations: 14.4 us -> 1.01 us
  local copies, waits for them, and re-layouts: 7.42 us -> 4.15 us
  other arithmetic: 14.5 us -> 17.5 us
  starting transfers between devices: 53.5 us -> 51.5 us
    ppermute x4 -> x0, waiting for transfers between devices: 14.9 us -> none  [flip(): return lax.ppermute(value, axis, [(i, i ^ bit) for i in range(size)])]
    ppermute x17 -> x23, waiting for transfers between devices: 11.2 us -> 26 us  [shift(): lax.ppermute(value, axis, [(i, (i + by) % size) for i in range(size)])]
    ppermute x4 -> x0, starting transfers between devices: 5.75 us -> none  [flip(): return lax.ppermute(value, axis, [(i, i ^ bit) for i in range(size)])]
    all_to_all x0 -> x1, starting transfers between devices: none -> 4.18 us  [local(): lax.all_to_all(jnp.broadcast_to(act[None], (4, ROWS, COLS)), 'y', 0, 0)]
    all_to_all x1, waiting for transfers between devices: 3.03 us -> 0.01 us  [local(): lax.all_to_all(sent.reshape(8, 2, 2, RANK, COLS), ('x', 'core'), 0, 0)]
    all_to_all x0 -> x1, waiting for transfers between devices: none -> 2.98 us  [local(): lax.all_to_all(jnp.broadcast_to(act[None], (4, ROWS, COLS)), 'y', 0, 0)]
    add x6 -> x3, other arithmetic: 0.15 us -> 2.49 us  [the longest x1 1.51 us: local(): input_parts[0].astype(F32)]
    all_to_all x1, waiting for transfers between devices: 0.01 us -> 2.07 us  [local(): lax.all_to_all(grads, ('x', 'core'), 0, 0).reshape(PROMPTS, 2, RANK, COLS)]
  transfers between devices with their start and end apart: 28 -> 30, of which waited for: 10 -> 9; matrix products, arithmetic and copies ran while one was open for 16% -> 17% of each run, Pallas kernels for 18% -> 20%
where the time goes in v3:
time: 140 us; the launch traced here: 139 us
  starting transfers between devices  51.5 us (37%)
  waiting for transfers between devices  31 us (22%)
  Pallas kernels  27.4 us (20%)
  other arithmetic  17.5 us (12%)
  matrix products  6.26 us (4%)
  local copies, waits for them, and re-layouts  4.15 us (3%)
    ppermute x23, waiting for transfers between devices, shift(): lax.ppermute(value, axis, [(i, (i + by) % size) for i in range(size)])  26 us
    ppermute x23, starting transfers between devices, shift(): lax.ppermute(value, axis, [(i, (i + by) % size) for i in range(size)])  25.4 us
    pallas_call x1, Pallas kernels, partials(): pl.pallas_call(partial_kernel, out_shape=[block] * 8, grid_spec=pltpu.Pre...  15.6 us
    ppermute x4, starting transfers between devices, local(): other = [lax.ppermute(piece, 'core', [(0, 1), (1, 0)]) for piece in own]  8.21 us
    all_to_all x1, starting transfers between devices, local(): lax.all_to_all(grads, ('x', 'core'), 0, 0).reshape(PROMPTS, 2, RANK, COLS)  7.95 us
    pallas_call x1, Pallas kernels, adam(): pl.pallas_call(adam_kernel, out_shape=(half, half, full, full, full, full...  6.79 us
    all_to_all x1, starting transfers between devices, local(): lax.all_to_all(sent.reshape(8, 2, 2, RANK, COLS), ('x', 'core'), 0, 0)  5.77 us
    pallas_call x1, Pallas kernels, pick(): pl.pallas_call(pick_kernel, out_shape=(jax.ShapeDtypeStruct((PROMPTS, 2,...  5.05 us
  transfers between devices with their start and end apart: 30, of which 9 were waited for; matrix products, arithmetic and copies ran while one was open for 17% of the time, Pallas kernels for 20%

profile of v3, /device:TPU:1, one launch (start us, length us, event | category | flops | bytes accessed | tf_op | source)
XLA Modules:
  0.0 138.9 jit_solution(10458587123490712836)
XLA Ops:
  0.7 1.5 %constant_dynamic-slice_fusion = (bf16[256,512]{1,0:T(8,128)(2,1)S(1)}, bf16[256,512]{1,0:T(8,128)(2,1)S(1)}, bf16[256,512]{1,0:T(8,128)(2,1)S(1)}, bf16[256,512...) fusion(bf16[8192,512]{1,0:T(8,128)(2,1)} %refs_13_.1, s32[]{:T(128)S(6)} %select_n.38, ...), kind=kLoop, calls=%fused_computation.41 | loop fusion | bytes 3145752 | tf_op jit(solution)/shard_map/dynamic_slice | solution.py:228
  2.2 4.7 %collective-permute-start.2 = (bf16[256,512]{1,0:T(8,128)(2,1)S(1)}, bf16[256,512]{1,0:T(8,128)(2,1)}, u32[]{:S(2)}, u32[]{:S(2)}) collective-permute-start(bf16[256,512]{1,0:T(8,128)(2,1)S(1)} %get-tuple-element.77), channel_id=1, source_target_pairs={{0,12},{4,0},{8,4},{12,8},{1,13},{5,1},{9,5},{13,9},{2,14},{6,2},{... | collective-permute-start | bytes 786440 | tf_op jit(solution)/shard_map/ppermute | solution.py:199
  7.6 5.1 %shard_map.179 = (bf16[16,2,32,512]{3,2,1,0:T(8,128)(2,1)}, s32[16]{0:T(128)}) custom-call(s32[128]{0:T(128)} %slots, s32[1]{0:T(128)} %bitcast.4.member, bf16[16,32,512]{2,1,0:T(8,128)(2,1)} %dn.1, bf16[16,32,512]{2,1,0:T(8,128)(2,1)} %up.3), custom_call_target="tpu_custom_call" | custom-call | flops 1 | bytes 1 | tf_op jit(solution)/shard_map/pallas_call | solution.py:58
  12.6 5.8 %all-to-all-start = ((bf16[8,2,2,32,512]{4,3,2,1,0:T(8,128)(2,1)}), bf16[8,2,2,32,512]{4,3,2,1,0:T(8,128)(2,1)S(1)}, u32[]{:S(2)}, u32[]{:S(2)}) async-start(bf16[8,2,2,32,512]{4,3,2,1,0:T(8,128)(2,1)} %bitcast.52), calls=%async_computation | async-start | bytes 2097152 | tf_op jit(solution)/shard_map/all_to_all | solution.py:252
  18.4 1.9 %collective-permute-start.3 = (bf16[256,512]{1,0:T(8,128)(2,1)S(1)}, bf16[256,512]{1,0:T(8,128)(2,1)S(1)}, u32[]{:S(2)}, u32[]{:S(2)}) collective-permute-start(bf16[256,512]{1,0:T(8,128)(2,1)S(1)} %get-tuple-element.76), channel_id=1, source_target_pairs={{0,4},{4,8},{8,12},{12,0},{1,5},{5,9},{9,13},{13,1},{2,6},{6,10},{... | collective-permute-start | bytes 786440 | tf_op jit(solution)/shard_map/ppermute | solution.py:199
  21.8 0.7 and_select_fusion
  22.7 0.7 multiply_add_fusion
  23.4 0.8 select_reduce_fusion.2
  24.4 2.0 %multiply_convert_fusion.refs_1_ = bf16[512,512]{1,0:T(8,128)(2,1)} fusion(bf16[512,512]{1,0:T(8,128)(2,1)} %param.13, f32[512]{0:T(512)S(1)} %sub.12), kind=kLoop, calls=%fused_computation.15 | loop fusion | flops 786432 | bytes 1050624 | tf_op jit(solution)/shard_map/convert_element_type | solution.py:270
  26.4 1.2 collective-permute-start.5
  27.6 2.1 %pad_maximum_fusion.1.refs_5_ = bf16[3,256,512]{2,1,0:T(8,128)(2,1)} fusion(bf16[1,256,512]{2,1,0:T(8,128)(2,1)} %bitcast.8, bf16[1,256,512]{2,1,0:T(8,128)(2,1)} %bitcast.7, bf16[1,256,512]{2,1,0:T(8,128)(2,1)} %bitcast.6), kind=kLoop, calls=%fused_computation.16 | loop fusion | flops 786432 | bytes 1572864 | tf_op jit(solution)/shard_map/stack | solution.py:240
  29.7 1.4 collective-permute-start.9
  31.0 1.3 collective-permute-start.10
  32.3 1.2 collective-permute-start.11
  33.5 1.8 %collective-permute-done.5 = bf16[256,512]{1,0:T(8,128)(2,1)S(1)} collective-permute-done((bf16[256,512]{1,0:T(8,128)(2,1)S(1)}, bf16[256,512]{1,0:T(8,128)(2,1)S(1)}, u32[]{:S(2)}, u32[]{:S(2)}) %collective-permute-start.5) | collective-permute-done | bytes 262176 | tf_op jit(solution)/shard_map/ppermute | solution.py:199
  35.3 0.8 collective-permute-start.6
  36.2 1.8 %collective-permute-start.7 = (bf16[512,512]{1,0:T(8,128)(2,1)}, bf16[512,512]{1,0:T(8,128)(2,1)}, u32[]{:S(2)}, u32[]{:S(2)}) collective-permute-start(bf16[512,512]{1,0:T(8,128)(2,1)} %multiply_convert_fusion.refs_1_), channel_id=1, source_target_pairs={{0,12},{4,0},{8,4},{12,8},{1,13},{5,1},{9,5},{13,9},{2,14},{6,2},{... | collective-permute-start | bytes 1572872 | tf_op jit(solution)/shard_map/ppermute | solution.py:199
  38.0 1.5 %broadcast_in_dim.13 = bf16[4,512,512]{2,1,0:T(8,128)(2,1)} broadcast(bf16[512,512]{1,0:T(8,128)(2,1)S(1)} %copy-done.8), dimensions={1,2} | broadcast | bytes 2621440 | tf_op jit(solution)/shard_map/broadcast_in_dim | solution.py:255
  39.5 4.2 %all-to-all-start.1 = ((bf16[4,512,512]{2,1,0:T(8,128)(2,1)}), bf16[4,512,512]{2,1,0:T(8,128)(2,1)S(1)}, u32[]{:S(2)}, u32[]{:S(2)}) async-start(bf16[4,512,512]{2,1,0:T(8,128)(2,1)} %broadcast_in_dim.13), calls=%async_computation.1 | async-start | bytes 4194304 | tf_op jit(solution)/shard_map/all_to_all | solution.py:255
  43.7 1.1 pad_maximum_fusion.2.refs_7_
  45.0 1.9 %fusion.3 = f32[32,512]{1,0:T(8,128)S(1)} fusion(bf16[16,32,512]{2,1,0:T(8,128)(2,1)S(1)} %bitcast.48, bf16[512,512]{1,0:T(8,128)(2,1)} %multiply_convert_fusion.refs_1_, f32[16,512]{1,0:T(8,128)S(1)} %get-tuple-element.87), kind=kOutput, calls=%fused_computation.9 | convolution fusion | flops 268943360 | bytes 1146880 | tf_op jit(solution)/shard_map/dot_general | solution.py:280
  46.9 1.5 %fusion.2 = f32[32,512]{1,0:T(8,128)S(1)} fusion(bf16[16,32,512]{2,1,0:T(8,128)(2,1)S(1)} %bitcast.50, bf16[512,512]{1,0:T(8,128)(2,1)} %param.12, f32[16,512]{1,0:T(8,128)S(1)} %get-tuple-element.87), kind=kOutput, calls=%fused_computation.8 | convolution fusion | flops 268943360 | bytes 1146880 | tf_op jit(solution)/shard_map/dot_general | solution.py:279
  49.2 2.7 %collective-permute-start.13 = (bf16[3,256,512]{2,1,0:T(8,128)(2,1)S(1)}, bf16[3,256,512]{2,1,0:T(8,128)(2,1)S(1)}, u32[]{:S(2)}, u32[]{:S(2)}) collective-permute-start(bf16[3,256,512]{2,1,0:T(8,128)(2,1)S(1)} %pad_maximum_fusion.2.refs_7_), channel_id=1, source_target_pairs={{0,16},{16,0},{1,17},{17,1},{2,18},{18,2},{3,19},{19,3},{4,20},{20... | collective-permute-start | bytes 2359304 | tf_op jit(solution)/shard_map/ppermute | solution.py:246
  51.9 0.9 collective-permute-start.15
  52.8 0.8 collective-permute-start.12
  54.2 3.6 %collective-permute-start.14 = (bf16[3,256,512]{2,1,0:T(8,128)(2,1)}, bf16[3,256,512]{2,1,0:T(8,128)(2,1)}, u32[]{:S(2)}, u32[]{:S(2)}) collective-permute-start(bf16[3,256,512]{2,1,0:T(8,128)(2,1)} %collective-permute-done.10.refs_8_), channel_id=1, source_target_pairs={{0,16},{16,0},{1,17},{17,1},{2,18},{18,2},{3,19},{19,3},{4,20},{20... | collective-permute-start | bytes 2359304 | tf_op jit(solution)/shard_map/ppermute | solution.py:246
  57.7 2.3 %collective-permute-done.15 = f32[64,512]{1,0:T(8,128)S(1)} collective-permute-done((f32[64,512]{1,0:T(8,128)S(1)}, f32[64,512]{1,0:T(8,128)S(1)}, u32[]{:S(2)}, u32[]{:S(2)}) %collective-permute-start.15) | collective-permute-done | bytes 131104 | tf_op jit(solution)/shard_map/ppermute | solution.py:199
  60.4 4.3 %collective-permute-done.16 = f32[64,512]{1,0:T(8,128)S(1)} collective-permute-done((f32[64,512]{1,0:T(8,128)S(1)}, f32[64,512]{1,0:T(8,128)S(1)}, u32[]{:S(2)}, u32[]{:S(2)}) %collective-permute-start.16) | collective-permute-done | bytes 131104 | tf_op jit(solution)/shard_map/ppermute | solution.py:199
  64.8 3.0 %all-to-all-done.1.refs_0_ = bf16[4,512,512]{2,1,0:T(8,128)(2,1)S(1)} async-done(((bf16[4,512,512]{2,1,0:T(8,128)(2,1)}), bf16[4,512,512]{2,1,0:T(8,128)(2,1)S(1)}, u32[]{:S(2)}, u32[]{:S(2)}) %all-to-all-start.1) | async-done | bytes 2097184 | tf_op jit(solution)/shard_map/all_to_all | solution.py:255
  68.1 1.1 collective-permute-start.18
  69.3 9.4 %collective-permute-done.8.refs_3_ = bf16[512,512]{1,0:T(8,128)(2,1)} collective-permute-done((bf16[512,512]{1,0:T(8,128)(2,1)}, bf16[512,512]{1,0:T(8,128)(2,1)}, u32[]{:S(2)}, u32[]{:S(2)}) %collective-permute-start.8) | collective-permute-done | bytes 524320 | tf_op jit(solution)/shard_map/ppermute | solution.py:199
  78.7 2.7 %collective-permute-start.19 = (f32[64,512]{1,0:T(8,128)S(1)}, f32[64,512]{1,0:T(8,128)}, u32[]{:S(2)}, u32[]{:S(2)}) collective-permute-start(f32[64,512]{1,0:T(8,128)S(1)} %add_add_fusion.1), channel_id=1, source_target_pairs={{0,3},{1,0},{2,1},{3,2},{4,7},{5,4},{6,5},{7,6},{8,11},{9,8},{10,9... | collective-permute-start | bytes 393224 | tf_op jit(solution)/shard_map/ppermute | solution.py:199
  82.1 15.6 %shard_map.180 = (bf16[512,512]{1,0:T(8,128)(2,1)}, bf16[512,512]{1,0:T(8,128)(2,1)}, bf16[512,512]{1,0:T(8,128)(2,1)}, bf16[512,512]{1,0:T(8,128)(2,1)}, bf16[5...) custom-call(s32[4]{0:T(128)} %pad_add_fusion.where, ...), custom_call_target="tpu_custom_call" | custom-call | flops 1 | bytes 1 | tf_op jit(solution)/shard_map/pallas_call | solution.py:173
  97.8 1.3 collective-permute-start.22
  99.1 1.5 %collective-permute-start.21 = (bf16[512,512]{1,0:T(8,128)(2,1)}, bf16[512,512]{1,0:T(8,128)(2,1)}, u32[]{:S(2)}, u32[]{:S(2)}) collective-permute-start(bf16[512,512]{1,0:T(8,128)(2,1)} %get-tuple-element.50), channel_id=1, source_target_pairs={{0,12},{4,0},{8,4},{12,8},{1,13},{5,1},{9,5},{13,9},{2,14},{6,2},{... | collective-permute-start | bytes 1572872 | tf_op jit(solution)/shard_map/ppermute | solution.py:199
  100.9 0.7 collective-permute-start.25
  101.7 0.9 add_add_fusion
  102.7 1.5 %fusion.1 = bf16[512,512]{1,0:T(8,128)(2,1)S(1)} fusion(bf16[512,512]{1,0:T(8,128)(2,1)S(1)} %bitcast.44, bf16[512,512]{1,0:T(8,128)(2,1)} %multiply_convert_fusion.refs_1_), kind=kOutput, calls=%fused_computation.7 | convolution fusion | flops 268959744 | bytes 1572864 | tf_op jit(solution)/shard_map/dot_general | solution.py:299
  104.7 1.1 pad_maximum_fusion
  105.7 7.9 %all-to-all-start.2 = ((bf16[8,2,2,32,512]{4,3,2,1,0:T(8,128)(2,1)}), bf16[8,2,2,32,512]{4,3,2,1,0:T(8,128)(2,1)S(1)}, u32[]{:S(2)}, u32[]{:S(2)}) async-start(bf16[8,2,2,32,512]{4,3,2,1,0:T(8,128)(2,1)} %pad_maximum_fusion), calls=%async_computation.2 | async-start | bytes 2097152 | tf_op jit(solution)/shard_map/all_to_all | solution.py:307
  114.6 1.1 collective-permute-start.24
  115.7 1.5 %convert_add_fusion = (f32[512,512]{1,0:T(8,128)S(1)}, f32[512,512]{1,0:T(8,128)S(1)}) fusion(f32[512,512]{1,0:T(8,128)S(1)} %convolution_multiply_fusion.2, bf16[512,512]{1,0:T(8,128)(2,1)} %get-tuple-element.53, f32[512,512]{1,0:T(8,128)S(1)} %convolution_multiply_fusion.3, bf16[512,512]{1,0:T(8,128)(2,1)} %get-tuple-element.48), kind=kLoop, calls=%fused_computation.12 | loop fusion | flops 1048576 | bytes 5242880 | tf_op jit(solution)/shard_map/add | solution.py:324
  117.2 7.1 %collective-permute-done.22 = bf16[512,512]{1,0:T(8,128)(2,1)} collective-permute-done((bf16[512,512]{1,0:T(8,128)(2,1)}, bf16[512,512]{1,0:T(8,128)(2,1)}, u32[]{:S(2)}, u32[]{:S(2)}) %collective-permute-start.22) | collective-permute-done | bytes 524320 | tf_op jit(solution)/shard_map/ppermute | solution.py:199
  124.3 2.4 %add_convert_fusion.1 = bf16[512,512]{1,0:T(8,128)(2,1)} fusion(bf16[512,512]{1,0:T(8,128)(2,1)} %collective-permute-done.23, bf16[512,512]{1,0:T(8,128)(2,1)} %collective-permute-done.22, f32[512,512]{1,0:T(8,128)S(1)} %get-tuple-element.89, bf16[512,512]{1,0:T(8,128)(2,1)} %collective-permute-done.21), kind=kLoop, calls=%fused_computation.13 | loop fusion | flops 1835008 | bytes 3145728 | tf_op jit(solution)/shard_map/convert_element_type | solution.py:333
  126.7 2.1 %all-to-all-done.2 = bf16[8,2,2,32,512]{4,3,2,1,0:T(8,128)(2,1)S(1)} async-done(((bf16[8,2,2,32,512]{4,3,2,1,0:T(8,128)(2,1)}), bf16[8,2,2,32,512]{4,3,2,1,0:T(8,128)(2,1)S(1)}, u32[]{:S(2)}, u32[]{:S(2)}) %all-to-all-start.2) | async-done | bytes 1048608 | tf_op jit(solution)/shard_map/all_to_all | solution.py:307
  128.8 1.0 copy-done.1
  129.7 6.8 %shard_map.181 = (bf16[16,32,512]{2,1,0:T(8,128)(2,1)}, bf16[16,32,512]{2,1,0:T(8,128)(2,1)}, f32[16,32,512]{2,1,0:T(8,128)}, f32[16,32,512]{2,1,0:T(8,128)}, f3...) custom-call(s32[16]{0:T(128)} %get-tuple-element.54.pos, bf16[16,2,32,512]{3,2,1,0:T(8,128)(2,1)} %bitcast.43, ...), custom_call_target="tpu_custom_call" | custom-call | flops 1 | bytes 1 | tf_op jit(solution)/shard_map/pallas_call | solution.py:93
  136.6 2.3 %add_convert_fusion = bf16[512,512]{1,0:T(8,128)(2,1)} fusion(bf16[512,512]{1,0:T(8,128)(2,1)} %collective-permute-done.26, bf16[512,512]{1,0:T(8,128)(2,1)} %collective-permute-done.25, f32[512,512]{1,0:T(8,128)S(1)} %get-tuple-element.62, bf16[512,512]{1,0:T(8,128)(2,1)S(1)} %collective-permute-done.24), kind=kLoop, calls=%fused_computation.11 | loop fusion | flops 1835008 | bytes 3145728 | tf_op jit(solution)/shard_map/convert_element_type | solution.py:333
  (69 shorter events, 7.4 us)
Async XLA Ops:
  0.6 37.4 %copy-start.8 = (bf16[512,512]{1,0:T(8,128)(2,1)S(1)}, bf16[512,512]{1,0:T(8,128)(2,1)}, u32[]{:S(2)}) copy-start(bf16[512,512]{1,0:T(8,128)(2,1)} %param.12) | copy-start | bytes 1572868
  2.2 24.2 %collective-permute-start.2 = (bf16[256,512]{1,0:T(8,128)(2,1)S(1)}, bf16[256,512]{1,0:T(8,128)(2,1)}, u32[]{:S(2)}, u32[]{:S(2)}) collective-permute-start(bf16[256,512]{1,0:T(8,128)(2,1)S(1)} %get-tuple-element.77), channel_id=1, source_target_pairs={{0,12},{4,0},{8,4},{12,8},{1,13},{5,1},{9,5},{13,9},{2,14},{6,2},{... | collective-permute-start | bytes 786440 | tf_op jit(solution)/shard_map/ppermute | solution.py:199
  6.9 19.6 %collective-permute-start.1 = (bf16[256,512]{1,0:T(8,128)(2,1)S(1)}, bf16[256,512]{1,0:T(8,128)(2,1)}, u32[]{:S(2)}, u32[]{:S(2)}) collective-permute-start(bf16[256,512]{1,0:T(8,128)(2,1)S(1)} %get-tuple-element.78), channel_id=1, source_target_pairs={{0,8},{4,12},{8,0},{12,4},{1,9},{5,13},{9,1},{13,5},{2,10},{6,14},... | collective-permute-start | bytes 786440 | tf_op jit(solution)/shard_map/ppermute | solution.py:199
  6.9 19.6 %collective-permute-start = (bf16[256,512]{1,0:T(8,128)(2,1)S(1)}, bf16[256,512]{1,0:T(8,128)(2,1)}, u32[]{:S(2)}, u32[]{:S(2)}) collective-permute-start(bf16[256,512]{1,0:T(8,128)(2,1)S(1)} %get-tuple-element.79), channel_id=1, source_target_pairs={{0,4},{4,8},{8,12},{12,0},{1,5},{5,9},{9,13},{13,1},{2,6},{6,10},{... | collective-permute-start | bytes 786440 | tf_op jit(solution)/shard_map/ppermute | solution.py:199
  12.6 25.4 %all-to-all-start = ((bf16[8,2,2,32,512]{4,3,2,1,0:T(8,128)(2,1)}), bf16[8,2,2,32,512]{4,3,2,1,0:T(8,128)(2,1)S(1)}, u32[]{:S(2)}, u32[]{:S(2)}) async-start(bf16[8,2,2,32,512]{4,3,2,1,0:T(8,128)(2,1)} %bitcast.52), calls=%async_computation | async-start | bytes 2097152 | tf_op jit(solution)/shard_map/all_to_all | solution.py:252
  18.4 11.3 %collective-permute-start.3 = (bf16[256,512]{1,0:T(8,128)(2,1)S(1)}, bf16[256,512]{1,0:T(8,128)(2,1)S(1)}, u32[]{:S(2)}, u32[]{:S(2)}) collective-permute-start(bf16[256,512]{1,0:T(8,128)(2,1)S(1)} %get-tuple-element.76), channel_id=1, source_target_pairs={{0,4},{4,8},{8,12},{12,0},{1,5},{5,9},{9,13},{13,1},{2,6},{6,10},{... | collective-permute-start | bytes 786440 | tf_op jit(solution)/shard_map/ppermute | solution.py:199
  20.3 9.3 %collective-permute-start.4 = (bf16[256,512]{1,0:T(8,128)(2,1)S(1)}, bf16[256,512]{1,0:T(8,128)(2,1)}, u32[]{:S(2)}, u32[]{:S(2)}) collective-permute-start(bf16[256,512]{1,0:T(8,128)(2,1)S(1)} %get-tuple-element.75), channel_id=1, source_target_pairs={{0,12},{4,0},{8,4},{12,8},{1,13},{5,1},{9,5},{13,9},{2,14},{6,2},{... | collective-permute-start | bytes 786440 | tf_op jit(solution)/shard_map/ppermute | solution.py:199
  26.4 8.9 %collective-permute-start.5 = (bf16[256,512]{1,0:T(8,128)(2,1)S(1)}, bf16[256,512]{1,0:T(8,128)(2,1)S(1)}, u32[]{:S(2)}, u32[]{:S(2)}) collective-permute-start(bf16[256,512]{1,0:T(8,128)(2,1)S(1)} %get-tuple-element.44), channel_id=1, source_target_pairs={{0,8},{4,12},{8,0},{12,4},{1,9},{5,13},{9,1},{13,5},{2,10},{6,14},... | collective-permute-start | bytes 786440 | tf_op jit(solution)/shard_map/ppermute | solution.py:199
  29.7 22.2 %collective-permute-start.9 = (bf16[3,256,512]{2,1,0:T(8,128)(2,1)}, bf16[3,256,512]{2,1,0:T(8,128)(2,1)}, u32[]{:S(2)}, u32[]{:S(2)}) collective-permute-start(bf16[3,256,512]{2,1,0:T(8,128)(2,1)} %pad_maximum_fusion.1.refs_5_), channel_id=1, source_target_pairs={{0,32},{32,64},{64,96},{96,0},{1,33},{33,65},{65,97},{97,1},{2,34}... | collective-permute-start | bytes 2359304 | tf_op jit(solution)/shard_map/ppermute | solution.py:199
  31.0 21.7 %collective-permute-start.10 = (bf16[3,256,512]{2,1,0:T(8,128)(2,1)}, bf16[3,256,512]{2,1,0:T(8,128)(2,1)}, u32[]{:S(2)}, u32[]{:S(2)}) collective-permute-start(bf16[3,256,512]{2,1,0:T(8,128)(2,1)} %pad_maximum_fusion.1.refs_5_), channel_id=1, source_target_pairs={{0,96},{32,0},{64,32},{96,64},{1,97},{33,1},{65,33},{97,65},{2,98}... | collective-permute-start | bytes 2359304 | tf_op jit(solution)/shard_map/ppermute | solution.py:199
  32.3 32.4 %collective-permute-start.11 = (bf16[3,256,512]{2,1,0:T(8,128)(2,1)}, bf16[3,256,512]{2,1,0:T(8,128)(2,1)}, u32[]{:S(2)}, u32[]{:S(2)}) collective-permute-start(bf16[3,256,512]{2,1,0:T(8,128)(2,1)} %pad_maximum_fusion.1.refs_5_), channel_id=1, source_target_pairs={{0,16},{16,0},{1,17},{17,1},{2,18},{18,2},{3,19},{19,3},{4,20},{20... | collective-permute-start | bytes 2359304 | tf_op jit(solution)/shard_map/ppermute | solution.py:246
  35.3 4.2 %copy-start.10 = (bf16[256,512]{1,0:T(8,128)(2,1)}, bf16[256,512]{1,0:T(8,128)(2,1)S(1)}, u32[]{:S(2)}) copy-start(bf16[256,512]{1,0:T(8,128)(2,1)S(1)} %collective-permute-done.5) | copy-start | bytes 786436
  35.3 13.5 %collective-permute-start.6 = (bf16[512,512]{1,0:T(8,128)(2,1)}, bf16[512,512]{1,0:T(8,128)(2,1)}, u32[]{:S(2)}, u32[]{:S(2)}) collective-permute-start(bf16[512,512]{1,0:T(8,128)(2,1)} %multiply_convert_fusion.refs_1_), channel_id=1, source_target_pairs={{0,4},{4,8},{8,12},{12,0},{1,5},{5,9},{9,13},{13,1},{2,6},{6,10},{... | collective-permute-start | bytes 1572872 | tf_op jit(solution)/shard_map/ppermute | solution.py:199
  36.2 13.0 %collective-permute-start.7 = (bf16[512,512]{1,0:T(8,128)(2,1)}, bf16[512,512]{1,0:T(8,128)(2,1)}, u32[]{:S(2)}, u32[]{:S(2)}) collective-permute-start(bf16[512,512]{1,0:T(8,128)(2,1)} %multiply_convert_fusion.refs_1_), channel_id=1, source_target_pairs={{0,12},{4,0},{8,4},{12,8},{1,13},{5,1},{9,5},{13,9},{2,14},{6,2},{... | collective-permute-start | bytes 1572872 | tf_op jit(solution)/shard_map/ppermute | solution.py:199
  39.5 28.3 %all-to-all-start.1 = ((bf16[4,512,512]{2,1,0:T(8,128)(2,1)}), bf16[4,512,512]{2,1,0:T(8,128)(2,1)S(1)}, u32[]{:S(2)}, u32[]{:S(2)}) async-start(bf16[4,512,512]{2,1,0:T(8,128)(2,1)} %broadcast_in_dim.13), calls=%async_computation.1 | async-start | bytes 4194304 | tf_op jit(solution)/shard_map/all_to_all | solution.py:255
  44.8 20.0 %copy-start.2 = (bf16[3,256,512]{2,1,0:T(8,128)(2,1)}, bf16[3,256,512]{2,1,0:T(8,128)(2,1)S(1)}, u32[]{:S(2)}) copy-start(bf16[3,256,512]{2,1,0:T(8,128)(2,1)S(1)} %pad_maximum_fusion.2.refs_7_) | copy-start | bytes 2359300
  44.9 19.8 %copy-start.3 = (bf16[8,2,1,32,512]{4,3,2,1,0:T(8,128)(2,1)}, bf16[8,2,1,32,512]{4,3,2,1,0:T(8,128)(2,1)S(1)}, u32[]{:S(2)}) copy-start(bf16[8,2,1,32,512]{4,3,2,1,0:T(8,128)(2,1)S(1)} %get-tuple-element.81) | copy-start | bytes 1572868
  45.0 19.8 %copy-start.5 = (bf16[8,2,1,32,512]{4,3,2,1,0:T(8,128)(2,1)}, bf16[8,2,1,32,512]{4,3,2,1,0:T(8,128)(2,1)S(1)}, u32[]{:S(2)}) copy-start(bf16[8,2,1,32,512]{4,3,2,1,0:T(8,128)(2,1)S(1)} %get-tuple-element.80) | copy-start | bytes 1572868
  48.8 5.3 %collective-permute-start.17 = (f32[64,512]{1,0:T(8,128)S(1)}, f32[64,512]{1,0:T(8,128)S(1)}, u32[]{:S(2)}, u32[]{:S(2)}) collective-permute-start(f32[64,512]{1,0:T(8,128)S(1)} %pad_maximum_fusion.3), channel_id=1, source_target_pairs={{0,8},{4,12},{8,0},{12,4},{1,9},{5,13},{9,1},{13,5},{2,10},{6,14},... | collective-permute-start | bytes 393224 | tf_op jit(solution)/shard_map/ppermute | solution.py:199
  49.2 15.6 %collective-permute-start.13 = (bf16[3,256,512]{2,1,0:T(8,128)(2,1)S(1)}, bf16[3,256,512]{2,1,0:T(8,128)(2,1)S(1)}, u32[]{:S(2)}, u32[]{:S(2)}) collective-permute-start(bf16[3,256,512]{2,1,0:T(8,128)(2,1)S(1)} %pad_maximum_fusion.2.refs_7_), channel_id=1, source_target_pairs={{0,16},{16,0},{1,17},{17,1},{2,18},{18,2},{3,19},{19,3},{4,20},{20... | collective-permute-start | bytes 2359304 | tf_op jit(solution)/shard_map/ppermute | solution.py:246
  51.9 8.2 %collective-permute-start.15 = (f32[64,512]{1,0:T(8,128)S(1)}, f32[64,512]{1,0:T(8,128)S(1)}, u32[]{:S(2)}, u32[]{:S(2)}) collective-permute-start(f32[64,512]{1,0:T(8,128)S(1)} %pad_maximum_fusion.3), channel_id=1, source_target_pairs={{0,4},{4,8},{8,12},{12,0},{1,5},{5,9},{9,13},{13,1},{2,6},{6,10},{... | collective-permute-start | bytes 393224 | tf_op jit(solution)/shard_map/ppermute | solution.py:199
  52.8 29.3 %collective-permute-start.12 = (bf16[3,256,512]{2,1,0:T(8,128)(2,1)}, bf16[3,256,512]{2,1,0:T(8,128)(2,1)}, u32[]{:S(2)}, u32[]{:S(2)}) collective-permute-start(bf16[3,256,512]{2,1,0:T(8,128)(2,1)} %collective-permute-done.9.refs_6_), channel_id=1, source_target_pairs={{0,16},{16,0},{1,17},{17,1},{2,18},{18,2},{3,19},{19,3},{4,20},{20... | collective-permute-start | bytes 2359304 | tf_op jit(solution)/shard_map/ppermute | solution.py:246
  54.2 27.9 %collective-permute-start.14 = (bf16[3,256,512]{2,1,0:T(8,128)(2,1)}, bf16[3,256,512]{2,1,0:T(8,128)(2,1)}, u32[]{:S(2)}, u32[]{:S(2)}) collective-permute-start(bf16[3,256,512]{2,1,0:T(8,128)(2,1)} %collective-permute-done.10.refs_8_), channel_id=1, source_target_pairs={{0,16},{16,0},{1,17},{17,1},{2,18},{18,2},{3,19},{19,3},{4,20},{20... | collective-permute-start | bytes 2359304 | tf_op jit(solution)/shard_map/ppermute | solution.py:246
  60.0 4.7 %collective-permute-start.16 = (f32[64,512]{1,0:T(8,128)S(1)}, f32[64,512]{1,0:T(8,128)S(1)}, u32[]{:S(2)}, u32[]{:S(2)}) collective-permute-start(f32[64,512]{1,0:T(8,128)S(1)} %pad_maximum_fusion.3), channel_id=1, source_target_pairs={{0,12},{4,0},{8,4},{12,8},{1,13},{5,1},{9,5},{13,9},{2,14},{6,2},{... | collective-permute-start | bytes 393224 | tf_op jit(solution)/shard_map/ppermute | solution.py:199
  64.7 14.0 %collective-permute-start.8 = (bf16[512,512]{1,0:T(8,128)(2,1)}, bf16[512,512]{1,0:T(8,128)(2,1)}, u32[]{:S(2)}, u32[]{:S(2)}) collective-permute-start(bf16[512,512]{1,0:T(8,128)(2,1)} %multiply_convert_fusion.refs_1_), channel_id=1, source_target_pairs={{0,8},{4,12},{8,0},{12,4},{1,9},{5,13},{9,1},{13,5},{2,10},{6,14},... | collective-permute-start | bytes 1572872 | tf_op jit(solution)/shard_map/ppermute | solution.py:199
  64.8 17.3 %copy-start.7 = (bf16[3,256,512]{2,1,0:T(8,128)(2,1)}, bf16[3,256,512]{2,1,0:T(8,128)(2,1)S(1)}, u32[]{:S(2)}) copy-start(bf16[3,256,512]{2,1,0:T(8,128)(2,1)S(1)} %collective-permute-done.13.refs_11_) | copy-start | bytes 2359300
  67.8 14.3 %copy-start = (bf16[4,512,512]{2,1,0:T(8,128)(2,1)}, bf16[4,512,512]{2,1,0:T(8,128)(2,1)S(1)}, u32[]{:S(2)}) copy-start(bf16[4,512,512]{2,1,0:T(8,128)(2,1)S(1)} %all-to-all-done.1.refs_0_) | copy-start | bytes 6291460
  67.8 31.2 %collective-permute-start.20 = (f32[64,512]{1,0:T(8,128)S(1)}, f32[64,512]{1,0:T(8,128)S(1)}, u32[]{:S(2)}, u32[]{:S(2)}) collective-permute-start(f32[64,512]{1,0:T(8,128)S(1)} %add_add_fusion.1), channel_id=1, source_target_pairs={{0,2},{1,3},{2,0},{3,1},{4,6},{5,7},{6,4},{7,5},{8,10},{9,11},{10,... | collective-permute-start | bytes 393224 | tf_op jit(solution)/shard_map/ppermute | solution.py:199
  68.1 32.4 %collective-permute-start.18 = (f32[64,512]{1,0:T(8,128)S(1)}, f32[64,512]{1,0:T(8,128)S(1)}, u32[]{:S(2)}, u32[]{:S(2)}) collective-permute-start(f32[64,512]{1,0:T(8,128)S(1)} %add_add_fusion.1), channel_id=1, source_target_pairs={{0,1},{1,2},{2,3},{3,0},{4,5},{5,6},{6,7},{7,4},{8,9},{9,10},{10,1... | collective-permute-start | bytes 393224 | tf_op jit(solution)/shard_map/ppermute | solution.py:199
  78.7 22.2 %collective-permute-start.19 = (f32[64,512]{1,0:T(8,128)S(1)}, f32[64,512]{1,0:T(8,128)}, u32[]{:S(2)}, u32[]{:S(2)}) collective-permute-start(f32[64,512]{1,0:T(8,128)S(1)} %add_add_fusion.1), channel_id=1, source_target_pairs={{0,3},{1,0},{2,1},{3,2},{4,7},{5,4},{6,5},{7,6},{8,11},{9,8},{10,9... | collective-permute-start | bytes 393224 | tf_op jit(solution)/shard_map/ppermute | solution.py:199
  82.1 22.1 %copy-start.9 = (bf16[512,512]{1,0:T(8,128)(2,1)S(1)}, bf16[512,512]{1,0:T(8,128)(2,1)}, u32[]{:S(2)}) copy-start(bf16[512,512]{1,0:T(8,128)(2,1)} %param.12) | copy-start | bytes 1572868
  97.7 16.0 %copy-start.6 = (bf16[8,2,1,32,512]{4,3,2,1,0:T(8,128)(2,1)S(1)}, bf16[8,2,1,32,512]{4,3,2,1,0:T(8,128)(2,1)}, u32[]{:S(2)}) copy-start(bf16[8,2,1,32,512]{4,3,2,1,0:T(8,128)(2,1)} %copy-done.5) | copy-start | bytes 1572868
  97.7 16.5 %copy-start.4 = (bf16[8,2,1,32,512]{4,3,2,1,0:T(8,128)(2,1)S(1)}, bf16[8,2,1,32,512]{4,3,2,1,0:T(8,128)(2,1)}, u32[]{:S(2)}) copy-start(bf16[8,2,1,32,512]{4,3,2,1,0:T(8,128)(2,1)} %copy-done.3) | copy-start | bytes 1572868
  97.7 16.9 %collective-permute-start.23 = (bf16[512,512]{1,0:T(8,128)(2,1)}, bf16[512,512]{1,0:T(8,128)(2,1)}, u32[]{:S(2)}, u32[]{:S(2)}) collective-permute-start(bf16[512,512]{1,0:T(8,128)(2,1)} %get-tuple-element.52), channel_id=1, source_target_pairs={{0,8},{4,12},{8,0},{12,4},{1,9},{5,13},{9,1},{13,5},{2,10},{6,14},... | collective-permute-start | bytes 1572872 | tf_op jit(solution)/shard_map/ppermute | solution.py:199
  97.8 26.5 %collective-permute-start.22 = (bf16[512,512]{1,0:T(8,128)(2,1)}, bf16[512,512]{1,0:T(8,128)(2,1)}, u32[]{:S(2)}, u32[]{:S(2)}) collective-permute-start(bf16[512,512]{1,0:T(8,128)(2,1)} %get-tuple-element.51), channel_id=1, source_target_pairs={{0,4},{4,8},{8,12},{12,0},{1,5},{5,9},{9,13},{13,1},{2,6},{6,10},{... | collective-permute-start | bytes 1572872 | tf_op jit(solution)/shard_map/ppermute | solution.py:199
  99.1 25.2 %collective-permute-start.21 = (bf16[512,512]{1,0:T(8,128)(2,1)}, bf16[512,512]{1,0:T(8,128)(2,1)}, u32[]{:S(2)}, u32[]{:S(2)}) collective-permute-start(bf16[512,512]{1,0:T(8,128)(2,1)} %get-tuple-element.50), channel_id=1, source_target_pairs={{0,12},{4,0},{8,4},{12,8},{1,13},{5,1},{9,5},{13,9},{2,14},{6,2},{... | collective-permute-start | bytes 1572872 | tf_op jit(solution)/shard_map/ppermute | solution.py:199
  100.5 36.0 %collective-permute-start.26 = (bf16[512,512]{1,0:T(8,128)(2,1)}, bf16[512,512]{1,0:T(8,128)(2,1)}, u32[]{:S(2)}, u32[]{:S(2)}) collective-permute-start(bf16[512,512]{1,0:T(8,128)(2,1)} %get-tuple-element.65), channel_id=1, source_target_pairs={{0,2},{1,3},{2,0},{3,1},{4,6},{5,7},{6,4},{7,5},{8,10},{9,11},{10,... | collective-permute-start | bytes 1572872 | tf_op jit(solution)/shard_map/ppermute | solution.py:199
  100.9 35.6 %collective-permute-start.25 = (bf16[512,512]{1,0:T(8,128)(2,1)}, bf16[512,512]{1,0:T(8,128)(2,1)}, u32[]{:S(2)}, u32[]{:S(2)}) collective-permute-start(bf16[512,512]{1,0:T(8,128)(2,1)} %get-tuple-element.64), channel_id=1, source_target_pairs={{0,3},{1,0},{2,1},{3,2},{4,7},{5,4},{6,5},{7,6},{8,11},{9,8},{10,9... | collective-permute-start | bytes 1572872 | tf_op jit(solution)/shard_map/ppermute | solution.py:199
  105.7 23.0 %all-to-all-start.2 = ((bf16[8,2,2,32,512]{4,3,2,1,0:T(8,128)(2,1)}), bf16[8,2,2,32,512]{4,3,2,1,0:T(8,128)(2,1)S(1)}, u32[]{:S(2)}, u32[]{:S(2)}) async-start(bf16[8,2,2,32,512]{4,3,2,1,0:T(8,128)(2,1)} %pad_maximum_fusion), calls=%async_computation.2 | async-start | bytes 2097152 | tf_op jit(solution)/shard_map/all_to_all | solution.py:307
  114.6 21.9 %collective-permute-start.24 = (bf16[512,512]{1,0:T(8,128)(2,1)}, bf16[512,512]{1,0:T(8,128)(2,1)S(1)}, u32[]{:S(2)}, u32[]{:S(2)}) collective-permute-start(bf16[512,512]{1,0:T(8,128)(2,1)} %get-tuple-element.63), channel_id=1, source_target_pairs={{0,1},{1,2},{2,3},{3,0},{4,5},{5,6},{6,7},{7,4},{8,9},{9,10},{10,1... | collective-permute-start | bytes 1572872 | tf_op jit(solution)/shard_map/ppermute | solution.py:199
  128.8 1.0 copy-start.1

commit v4 on v3

--- a/solution.py
+++ b/solution.py
@@ -46,7 +46,7 @@
 
             return j + mine.astype(jnp.int32)
 
-        lax.fori_loop(0, PROMPTS, step, jnp.int32(0))
+        lax.fori_loop(0, PROMPTS, step, jnp.int32(0), unroll=True)
         return carry
 
     lax.fori_loop(0, 8, group, 0)
@@ -195,6 +195,33 @@
     return outs[:4], outs[4:]
 
 
+def grads_kernel(scale_down, scale_up, t0, t1, t2, t3, hot, acts, weighted, out, low_wide, back_wide):
+    sums = (t0[...] + t1[...]) + (t2[...] + t3[...])
+    low = (scale_down * sums[:RANK]).astype(BF16)
+    back = (scale_up * sums[RANK:]).astype(BF16)
+    for p in range(PROMPTS):
+        rows = pl.ds(p * RANK, RANK)
+        low_wide[rows] = hot[p : p + 1, :] * low
+        back_wide[rows] = hot[p : p + 1, :] * back
+    for which, (scale, wide, other) in enumerate(
+        ((scale_down, back_wide, acts), (scale_up, low_wide, weighted))
+    ):
+        grad = scale * jnp.dot(wide[...], other[...], preferred_element_type=F32)
+        out[:, which] = grad.astype(BF16).reshape(PROMPTS, RANK, COLS)
+
+
+def adapter_grads(terms, hot, acts, weighted, scale_down, scale_up):
+    wide = jax.ShapeDtypeStruct((PROMPTS * RANK, ROWS), BF16)
+    return pl.pallas_call(
+        functools.partial(grads_kernel, scale_down, scale_up),
+        out_shape=(jax.ShapeDtypeStruct((PROMPTS, 2, RANK, COLS), BF16), wide, wide),
+        in_specs=[VMEM] * 7,
+        out_specs=(VMEM,) * 3,
+        compiler_params=params(),
+        cost_estimate=pl.CostEstimate(flops=1, bytes_accessed=1, transcendentals=0),
+    )(*terms, hot, acts, weighted)
+
+
 def shift(value, axis, by, size=4):
     return lax.ppermute(value, axis, [(i, (i + by) % size) for i in range(size)])
 
@@ -269,11 +296,8 @@
     advantage = reward - jnp.sum(onehot * mean_reward[:, None], axis=0)
     weighted = (advantage[:, None] * output_gradient.astype(F32)).astype(BF16)
 
-    grads_in = {0: weighted}
     sent, _ = lax.optimization_barrier((weighted, second[2]))
-    grads_in[1], grads_in[3] = shift(sent, "z", 1), shift(sent, "z", 3)
-    sent, _ = lax.optimization_barrier((weighted, (grads_in[1], grads_in[3])))
-    grads_in[2] = shift(sent, "z", 2)
+    grads_in = {0: weighted} | {d: shift(sent, "z", d) for d in (1, 3, 2)}
 
     contract_cols = (((1,), (1,)), ((), ()))
     low_all = lax.dot_general(down, activations, contract_cols, preferred_element_type=F32)
@@ -281,29 +305,21 @@
     low_part = jnp.sum(low_all.reshape(PROMPTS, RANK, ROWS) * onehot[:, None, :], axis=0)
     back_part = jnp.sum(back_all.reshape(PROMPTS, RANK, ROWS) * onehot[:, None, :], axis=0)
     sums = jnp.concatenate([low_part, back_part])
-    sums = sums + sum(shift(sums, "z", i) for i in (1, 3, 2))
-    sums, _ = lax.optimization_barrier((sums, (own[1], own[3], other[0], other[2], grads_in[1], grads_in[3], acts)))
-    sums = sums + sum(shift(sums, "y", i) for i in (1, 3, 2))
-    low = (scale_down * sums[:RANK]).astype(BF16)
-    back_low = (scale_up * sums[RANK:]).astype(BF16)
-    half = onehot.astype(BF16)
-    low_wide = (half[:, None, :] * low[None, :, :]).reshape(PROMPTS * RANK, ROWS)
-    back_wide = (half[:, None, :] * back_low[None, :, :]).reshape(PROMPTS * RANK, ROWS)
+    sums, _ = lax.optimization_barrier((sums, other[0]))
+    last, _ = lax.optimization_barrier((sums, grads_in))
+    sums = (sums + shift(sums, "z", 1)) + (shift(sums, "z", 3) + shift(last, "z", 2))
+    sums, _ = lax.optimization_barrier((sums, (own[1], own[3], other[2], acts)))
+    terms = [sums] + [shift(sums, "y", i) for i in (1, 3, 2)]
     where = jnp.stack([x, c, z, y]).astype(jnp.int32)
     layer_parts, input_parts = partials(
         where, acts, [grads_in[i] for i in range(4)], own, other, frozen_weight
     )
     layer_parts = {d: shift(layer_parts[d], "z", -d) if d else layer_parts[d] for d in (1, 3, 2, 0)}
     input_parts = {o: shift(input_parts[o], "y", o) if o else input_parts[o] for o in (1, 3, 2, 0)}
-    grad_down = scale_down * jnp.dot(back_wide, activations, preferred_element_type=F32)
-    grad_up = scale_up * jnp.dot(low_wide, weighted, preferred_element_type=F32)
-    grads = jnp.stack(
-        [
-            grad_down.astype(BF16).reshape(8, 2, RANK, COLS),
-            grad_up.astype(BF16).reshape(8, 2, RANK, COLS),
-        ],
-        axis=2,
-    )
+    grads, low_wide, back_wide = adapter_grads(
+        terms, onehot.astype(BF16), activations, weighted, scale_down, scale_up
+    )
+    grads = grads.reshape(8, 2, 2, RANK, COLS)
     grads = lax.all_to_all(grads, ("x", "core"), 0, 0).reshape(PROMPTS, 2, RANK, COLS)
     grads, _ = lax.optimization_barrier((grads, layer_parts[1]))
     updated = adam(

time: 140 us -> 141 us (level)
  local copies, waits for them, and re-layouts: 4.15 us -> 8.63 us
  other arithmetic: 17.5 us -> 14.4 us
  Pallas kernels: 27.4 us -> 29.8 us
  waiting for transfers between devices: 31 us -> 29 us
    ppermute x23, starting transfers between devices: 25.4 us -> 28.8 us  [shift(): lax.ppermute(value, axis, [(i, (i + by) % size) for i in range(size)])]
    pallas_call x0 -> x1, Pallas kernels: none -> 3.28 us  [adapter_grads(): pl.pallas_call(functools.partial(grads_kernel, scale_down, scale_up), out...]
    ppermute x4, starting transfers between devices: 8.21 us -> 4.99 us  [local(): other = [lax.ppermute(piece, 'core', [(0, 1), (1, 0)]) for piece in own]]
    all_to_all x1, waiting for transfers between devices: 2.98 us -> 0.01 us  [local(): lax.all_to_all(jnp.broadcast_to(act[None], (4, ROWS, COLS)), 'y', 0, 0)]
    unnamed x22 -> x38, local copies, waits for them, and re-layouts: 1.02 us -> 3.18 us
    dot_general x2 -> x0, matrix products: 1.91 us -> none  [the longest x1 1.48 us: local(): grad_up = scale_up * jnp.dot(low_wide, weighted, preferred_element_type=F32)]
    slice x1, local copies, waits for them, and re-layouts: 0.1 us -> 1.56 us  [local(): down = adapters[:, :, 0].reshape(PROMPTS * RANK, COLS)]
    dot_general x1, matrix products: 1.9 us -> 0.47 us  [local(): lax.dot_general(up, weighted, contract_cols, preferred_element_type=F32)]
  transfers between devices with their start and end apart: 30 -> 30, of which waited for: 9 -> 10; matrix products, arithmetic and copies ran while one was open for 17% -> 15% of each run, Pallas kernels for 20% -> 21%
where the time goes in v4:
time: 141 us; the launch traced here: 140 us
  starting transfers between devices  51.9 us (37%)
  Pallas kernels  29.8 us (21%)
  waiting for transfers between devices  29 us (21%)
  other arithmetic  14.4 us (10%)
  local copies, waits for them, and re-layouts  8.63 us (6%)
  matrix products  5.31 us (4%)
    ppermute x23, starting transfers between devices, shift(): lax.ppermute(value, axis, [(i, (i + by) % size) for i in range(size)])  28.8 us
    ppermute x23, waiting for transfers between devices, shift(): lax.ppermute(value, axis, [(i, (i + by) % size) for i in range(size)])  26.3 us
    pallas_call x1, Pallas kernels, partials(): pl.pallas_call(partial_kernel, out_shape=[block] * 8, grid_spec=pltpu.Pre...  15.4 us
    all_to_all x1, starting transfers between devices, local(): lax.all_to_all(grads, ('x', 'core'), 0, 0).reshape(PROMPTS, 2, RANK, COLS)  8.11 us
    pallas_call x1, Pallas kernels, adam(): pl.pallas_call(adam_kernel, out_shape=(half, half, full, full, full, full...  6.79 us
    all_to_all x1, starting transfers between devices, local(): lax.all_to_all(sent.reshape(8, 2, 2, RANK, COLS), ('x', 'core'), 0, 0)  5.83 us
    ppermute x4, starting transfers between devices, local(): other = [lax.ppermute(piece, 'core', [(0, 1), (1, 0)]) for piece in own]  4.99 us
    pallas_call x1, Pallas kernels, pick(): pl.pallas_call(pick_kernel, out_shape=(jax.ShapeDtypeStruct((PROMPTS, 2,...  4.31 us
  transfers between devices with their start and end apart: 30, of which 10 were waited for; matrix products, arithmetic and copies ran while one was open for 15% of the time, Pallas kernels for 21%

profile of v4, /device:TPU:1, one launch (start us, length us, event | category | flops | bytes accessed | tf_op | source)
XLA Modules:
  0.0 140.1 jit_solution(11089174630869155887)
XLA Ops:
  0.7 2.2 %constant_dynamic-slice_fusion = (bf16[256,512]{1,0:T(8,128)(2,1)S(1)}, bf16[256,512]{1,0:T(8,128)(2,1)S(1)}, bf16[256,512]{1,0:T(8,128)(2,1)}, bf16[256,512]{1,...) fusion(bf16[8192,512]{1,0:T(8,128)(2,1)} %refs_13_.1, s32[]{:T(128)S(6)} %select_n.38, ...), kind=kLoop, calls=%fused_computation.29 | loop fusion | bytes 3145752 | tf_op jit(solution)/shard_map/dynamic_slice | solution.py:255
  2.9 4.6 %collective-permute-start.2 = (bf16[256,512]{1,0:T(8,128)(2,1)S(1)}, bf16[256,512]{1,0:T(8,128)(2,1)S(1)}, u32[]{:S(2)}, u32[]{:S(2)}) collective-permute-start(bf16[256,512]{1,0:T(8,128)(2,1)S(1)} %get-tuple-element.85), channel_id=1, source_target_pairs={{0,12},{4,0},{8,4},{12,8},{1,13},{5,1},{9,5},{13,9},{2,14},{6,2},{... | collective-permute-start | bytes 786440 | tf_op jit(solution)/shard_map/ppermute | solution.py:226
  8.2 4.3 %shard_map.179 = (bf16[16,2,32,512]{3,2,1,0:T(8,128)(2,1)}, s32[16]{0:T(128)}) custom-call(s32[128]{0:T(128)} %slots, s32[1]{0:T(128)} %bitcast.4.member, bf16[16,32,512]{2,1,0:T(8,128)(2,1)} %dn.1, bf16[16,32,512]{2,1,0:T(8,128)(2,1)} %up.3), custom_call_target="tpu_custom_call" | custom-call | flops 1 | bytes 1 | tf_op jit(solution)/shard_map/pallas_call | solution.py:58
  12.5 5.8 %all-to-all-start = ((bf16[8,2,2,32,512]{4,3,2,1,0:T(8,128)(2,1)}), bf16[8,2,2,32,512]{4,3,2,1,0:T(8,128)(2,1)S(1)}, u32[]{:S(2)}, u32[]{:S(2)}) async-start(bf16[8,2,2,32,512]{4,3,2,1,0:T(8,128)(2,1)} %bitcast.37), calls=%async_computation | async-start | bytes 2097152 | tf_op jit(solution)/shard_map/all_to_all | solution.py:279
  18.4 1.9 %collective-permute-start.3 = (bf16[256,512]{1,0:T(8,128)(2,1)}, bf16[256,512]{1,0:T(8,128)(2,1)}, u32[]{:S(2)}, u32[]{:S(2)}) collective-permute-start(bf16[256,512]{1,0:T(8,128)(2,1)} %get-tuple-element.84), channel_id=1, source_target_pairs={{0,4},{4,8},{8,12},{12,0},{1,5},{5,9},{9,13},{13,1},{2,6},{6,10},{... | collective-permute-start | bytes 786440 | tf_op jit(solution)/shard_map/ppermute | solution.py:226
  22.7 0.8 select_reduce_fusion.2
  25.2 1.1 collective-permute-start.5
  26.3 1.2 multiply_convert_fusion.refs_1_.weighted
  27.5 1.4 pad_maximum_fusion.refs_5_
  28.9 1.4 %collective-permute-start.9 = (bf16[3,256,512]{2,1,0:T(8,128)(2,1)S(1)}, bf16[3,256,512]{2,1,0:T(8,128)(2,1)}, u32[]{:S(2)}, u32[]{:S(2)}) collective-permute-start(bf16[3,256,512]{2,1,0:T(8,128)(2,1)S(1)} %pad_maximum_fusion.refs_5_), channel_id=1, source_target_pairs={{0,32},{32,64},{64,96},{96,0},{1,33},{33,65},{65,97},{97,1},{2,34}... | collective-permute-start | bytes 2359304 | tf_op jit(solution)/shard_map/ppermute | solution.py:226
  30.4 1.3 collective-permute-start.10
  31.7 1.5 %collective-permute-start.11 = (bf16[3,256,512]{2,1,0:T(8,128)(2,1)S(1)}, bf16[3,256,512]{2,1,0:T(8,128)(2,1)}, u32[]{:S(2)}, u32[]{:S(2)}) collective-permute-start(bf16[3,256,512]{2,1,0:T(8,128)(2,1)S(1)} %pad_maximum_fusion.refs_5_), channel_id=1, source_target_pairs={{0,16},{16,0},{1,17},{17,1},{2,18},{18,2},{3,19},{19,3},{4,20},{20... | collective-permute-start | bytes 2359304 | tf_op jit(solution)/shard_map/ppermute | solution.py:273
  33.1 0.9 collective-permute-done.5
  35.4 1.6 %broadcast_in_dim.13 = bf16[4,512,512]{2,1,0:T(8,128)(2,1)} broadcast(bf16[512,512]{1,0:T(8,128)(2,1)S(1)} %copy-done.6), dimensions={1,2} | broadcast | bytes 2621440 | tf_op jit(solution)/shard_map/broadcast_in_dim | solution.py:282
  37.1 4.2 %all-to-all-start.1 = ((bf16[4,512,512]{2,1,0:T(8,128)(2,1)}), bf16[4,512,512]{2,1,0:T(8,128)(2,1)S(1)}, u32[]{:S(2)}, u32[]{:S(2)}) async-start(bf16[4,512,512]{2,1,0:T(8,128)(2,1)} %broadcast_in_dim.13), calls=%async_computation.1 | async-start | bytes 4194304 | tf_op jit(solution)/shard_map/all_to_all | solution.py:282
  41.9 2.4 %collective-permute-start.7 = (bf16[512,512]{1,0:T(8,128)(2,1)S(1)}, bf16[512,512]{1,0:T(8,128)(2,1)S(1)}, u32[]{:S(2)}, u32[]{:S(2)}) collective-permute-start(bf16[512,512]{1,0:T(8,128)(2,1)S(1)} %multiply_convert_fusion.refs_1_.weighted), channel_id=1, source_target_pairs={{0,8},{4,12},{8,0},{12,4},{1,9},{5,13},{9,1},{13,5},{2,10},{6,14},... | collective-permute-start | bytes 1572872 | tf_op jit(solution)/shard_map/ppermute | solution.py:226
  44.3 1.2 pad_maximum_fusion.1.refs_7_
  45.5 1.6 %fusion.8 = (bf16[8,2,1,32,512]{4,3,2,1,0:T(8,128)(2,1)S(1)}, bf16[8,2,1,32,512]{4,3,2,1,0:T(8,128)(2,1)S(1)}) fusion(bf16[8,2,2,32,512]{4,3,2,1,0:T(8,128)(2,1)} %copy-done.3), kind=kLoop, calls=%fused_computation.40 | loop fusion | bytes 2097152 | tf_op jit(solution)/shard_map/slice | solution.py:283
  47.1 0.9 collective-permute-done.6.refs_2_
  48.0 1.1 collective-permute-start.8
  49.6 1.0 collective-permute-done.9.refs_6_
  50.6 3.0 %collective-permute-start.13 = (bf16[3,256,512]{2,1,0:T(8,128)(2,1)S(1)}, bf16[3,256,512]{2,1,0:T(8,128)(2,1)}, u32[]{:S(2)}, u32[]{:S(2)}) collective-permute-start(bf16[3,256,512]{2,1,0:T(8,128)(2,1)S(1)} %pad_maximum_fusion.1.refs_7_), channel_id=1, source_target_pairs={{0,16},{16,0},{1,17},{17,1},{2,18},{18,2},{3,19},{19,3},{4,20},{20... | collective-permute-start | bytes 2359304 | tf_op jit(solution)/shard_map/ppermute | solution.py:273
  54.1 1.5 %fusion = f32[32,512]{1,0:T(8,128)S(1)} fusion(bf16[16,32,512]{2,1,0:T(8,128)(2,1)S(1)} %bitcast.35, bf16[512,512]{1,0:T(8,128)(2,1)} %acts.1, f32[16,512]{1,0:T(8,128)S(1)} %get-tuple-element.91), kind=kOutput, calls=%fused_computation.4 | convolution fusion | flops 268943360 | bytes 1146880 | tf_op jit(solution)/shard_map/dot_general | solution.py:303
  55.6 4.3 %collective-permute-done.7.refs_3_ = bf16[512,512]{1,0:T(8,128)(2,1)S(1)} collective-permute-done((bf16[512,512]{1,0:T(8,128)(2,1)S(1)}, bf16[512,512]{1,0:T(8,128)(2,1)S(1)}, u32[]{:S(2)}, u32[]{:S(2)}) %collective-permute-start.7) | collective-permute-done | bytes 524320 | tf_op jit(solution)/shard_map/ppermute | solution.py:226
  59.9 7.0 %collective-permute-done.8.refs_4_ = bf16[512,512]{1,0:T(8,128)(2,1)S(1)} collective-permute-done((bf16[512,512]{1,0:T(8,128)(2,1)S(1)}, bf16[512,512]{1,0:T(8,128)(2,1)S(1)}, u32[]{:S(2)}, u32[]{:S(2)}) %collective-permute-start.8) | collective-permute-done | bytes 524320 | tf_op jit(solution)/shard_map/ppermute | solution.py:226
  66.9 1.4 %collective-permute-start.17 = (f32[64,512]{1,0:T(8,128)S(1)}, f32[64,512]{1,0:T(8,128)S(1)}, u32[]{:S(2)}, u32[]{:S(2)}) collective-permute-start(f32[64,512]{1,0:T(8,128)S(1)} %pad_maximum_fusion.2), channel_id=1, source_target_pairs={{0,8},{4,12},{8,0},{12,4},{1,9},{5,13},{9,1},{13,5},{2,10},{6,14},... | collective-permute-start | bytes 393224 | tf_op jit(solution)/shard_map/ppermute | solution.py:226
  68.3 1.4 collective-permute-done.16
  69.7 1.8 %collective-permute-start.15 = (f32[64,512]{1,0:T(8,128)S(1)}, f32[64,512]{1,0:T(8,128)S(1)}, u32[]{:S(2)}, u32[]{:S(2)}) collective-permute-start(f32[64,512]{1,0:T(8,128)S(1)} %pad_maximum_fusion.2), channel_id=1, source_target_pairs={{0,4},{4,8},{8,12},{12,0},{1,5},{5,9},{9,13},{13,1},{2,6},{6,10},{... | collective-permute-start | bytes 393224 | tf_op jit(solution)/shard_map/ppermute | solution.py:226
  72.2 5.8 %collective-permute-done.15 = f32[64,512]{1,0:T(8,128)S(1)} collective-permute-done((f32[64,512]{1,0:T(8,128)S(1)}, f32[64,512]{1,0:T(8,128)S(1)}, u32[]{:S(2)}, u32[]{:S(2)}) %collective-permute-start.15) | collective-permute-done | bytes 131104 | tf_op jit(solution)/shard_map/ppermute | solution.py:226
  78.2 1.4 collective-permute-start.18
  79.6 1.4 collective-permute-start.19
  80.9 1.5 %collective-permute-start.20 = (f32[64,512]{1,0:T(8,128)S(1)}, f32[64,512]{1,0:T(8,128)S(1)}, u32[]{:S(2)}, u32[]{:S(2)}) collective-permute-start(f32[64,512]{1,0:T(8,128)S(1)} %add_add_fusion.t0), channel_id=1, source_target_pairs={{0,2},{1,3},{2,0},{3,1},{4,6},{5,7},{6,4},{7,5},{8,10},{9,11},{10,... | collective-permute-start | bytes 393224 | tf_op jit(solution)/shard_map/ppermute | solution.py:226
  83.0 15.4 %shard_map.180 = (bf16[512,512]{1,0:T(8,128)(2,1)}, bf16[512,512]{1,0:T(8,128)(2,1)}, bf16[512,512]{1,0:T(8,128)(2,1)}, bf16[512,512]{1,0:T(8,128)(2,1)}, bf16[5...) custom-call(s32[4]{0:T(128)} %pad_add_fusion.where, ...), custom_call_target="tpu_custom_call" | custom-call | flops 1 | bytes 1 | tf_op jit(solution)/shard_map/pallas_call | solution.py:173
  98.5 1.3 collective-permute-start.22
  99.8 1.4 %collective-permute-start.21 = (bf16[512,512]{1,0:T(8,128)(2,1)}, bf16[512,512]{1,0:T(8,128)(2,1)}, u32[]{:S(2)}, u32[]{:S(2)}) collective-permute-start(bf16[512,512]{1,0:T(8,128)(2,1)} %get-tuple-element.56), channel_id=1, source_target_pairs={{0,12},{4,0},{8,4},{12,8},{1,13},{5,1},{9,5},{13,9},{2,14},{6,2},{... | collective-permute-start | bytes 1572872 | tf_op jit(solution)/shard_map/ppermute | solution.py:226
  101.3 1.5 %collective-permute-start.26 = (bf16[512,512]{1,0:T(8,128)(2,1)}, bf16[512,512]{1,0:T(8,128)(2,1)S(1)}, u32[]{:S(2)}, u32[]{:S(2)}) collective-permute-start(bf16[512,512]{1,0:T(8,128)(2,1)} %get-tuple-element.73), channel_id=1, source_target_pairs={{0,2},{1,3},{2,0},{3,1},{4,6},{5,7},{6,4},{7,5},{8,10},{9,11},{10,... | collective-permute-start | bytes 1572872 | tf_op jit(solution)/shard_map/ppermute | solution.py:226
  102.8 0.9 collective-permute-start.25
  103.7 3.3 %shard_map.181 = (bf16[16,2,32,512]{3,2,1,0:T(8,128)(2,1)}, bf16[512,512]{1,0:T(8,128)(2,1)}, bf16[512,512]{1,0:T(8,128)(2,1)}) custom-call(f32[64,512]{1,0:T(8,128)} %copy-done.11, f32[64,512]{1,0:T(8,128)} %copy-done.16, f32[64,512]{1,0:T(8,128)} %copy-done.17, f32[64,512]{1,0:T(8,128)} %copy-done.18, bf16[16,512]{1,0:T(8,128)(2,1)} %get-tuple-element.90.hot, ...), custom_call_target="tpu_custom_call" | custom-call | flops 1 | bytes 1 | tf_op jit(solution)/shard_map/pallas_call | solution.py:215
  107.0 8.1 %all-to-all-start.2 = ((bf16[8,2,2,32,512]{4,3,2,1,0:T(8,128)(2,1)}), bf16[8,2,2,32,512]{4,3,2,1,0:T(8,128)(2,1)S(1)}, u32[]{:S(2)}, u32[]{:S(2)}) async-start(bf16[8,2,2,32,512]{4,3,2,1,0:T(8,128)(2,1)} %bitcast.38), calls=%async_computation.2 | async-start | bytes 2097152 | tf_op jit(solution)/shard_map/all_to_all | solution.py:323
  115.1 1.7 %convolution_multiply_fusion = f32[512,512]{1,0:T(8,128)S(1)} fusion(bf16[512,512]{1,0:T(8,128)(2,1)} %get-tuple-element.60, bf16[512,512]{1,0:T(8,128)(2,1)} %bitcast.36), kind=kOutput, calls=%fused_computation | convolution fusion | flops 268697600 | bytes 2097152 | tf_op jit(solution)/shard_map/dot_general | solution.py:340
  116.7 1.7 %convolution_multiply_fusion.1 = f32[512,512]{1,0:T(8,128)S(1)} fusion(bf16[512,512]{1,0:T(8,128)(2,1)} %get-tuple-element.55, bf16[512,512]{1,0:T(8,128)(2,1)} %bitcast.34), kind=kOutput, calls=%fused_computation.1 | convolution fusion | flops 268697600 | bytes 2097152 | tf_op jit(solution)/shard_map/dot_general | solution.py:337
  119.2 1.5 %convert_add_fusion = (f32[512,512]{1,0:T(8,128)S(1)}, f32[512,512]{1,0:T(8,128)S(1)}) fusion(f32[512,512]{1,0:T(8,128)S(1)} %convolution_multiply_fusion, bf16[512,512]{1,0:T(8,128)(2,1)} %get-tuple-element.59, f32[512,512]{1,0:T(8,128)S(1)} %convolution_multiply_fusion.1, bf16[512,512]{1,0:T(8,128)(2,1)} %get-tuple-element.51), kind=kLoop, calls=%fused_computation.7 | loop fusion | flops 1048576 | bytes 5242880 | tf_op jit(solution)/shard_map/add | solution.py:340
  120.7 4.3 %collective-permute-done.22 = bf16[512,512]{1,0:T(8,128)(2,1)} collective-permute-done((bf16[512,512]{1,0:T(8,128)(2,1)}, bf16[512,512]{1,0:T(8,128)(2,1)}, u32[]{:S(2)}, u32[]{:S(2)}) %collective-permute-start.22) | collective-permute-done | bytes 524320 | tf_op jit(solution)/shard_map/ppermute | solution.py:226
  125.0 2.4 %add_convert_fusion.1 = bf16[512,512]{1,0:T(8,128)(2,1)} fusion(bf16[512,512]{1,0:T(8,128)(2,1)} %copy-done.12, bf16[512,512]{1,0:T(8,128)(2,1)} %collective-permute-done.22, f32[512,512]{1,0:T(8,128)S(1)} %get-tuple-element.93, bf16[512,512]{1,0:T(8,128)(2,1)} %collective-permute-done.21), kind=kLoop, calls=%fused_computation.8 | loop fusion | flops 1835008 | bytes 3145728 | tf_op jit(solution)/shard_map/convert_element_type | solution.py:349
  127.4 2.7 %all-to-all-done.2 = bf16[8,2,2,32,512]{4,3,2,1,0:T(8,128)(2,1)S(1)} async-done(((bf16[8,2,2,32,512]{4,3,2,1,0:T(8,128)(2,1)}), bf16[8,2,2,32,512]{4,3,2,1,0:T(8,128)(2,1)S(1)}, u32[]{:S(2)}, u32[]{:S(2)}) %all-to-all-start.2) | async-done | bytes 1048608 | tf_op jit(solution)/shard_map/all_to_all | solution.py:323
  130.2 1.0 copy-done.2
  131.2 6.8 %shard_map.182 = (bf16[16,32,512]{2,1,0:T(8,128)(2,1)}, bf16[16,32,512]{2,1,0:T(8,128)(2,1)}, f32[16,32,512]{2,1,0:T(8,128)}, f32[16,32,512]{2,1,0:T(8,128)}, f3...) custom-call(s32[16]{0:T(128)} %get-tuple-element.61.pos, bf16[16,2,32,512]{3,2,1,0:T(8,128)(2,1)} %bitcast.32, ...), custom_call_target="tpu_custom_call" | custom-call | flops 1 | bytes 1 | tf_op jit(solution)/shard_map/pallas_call | solution.py:93
  138.0 2.1 %add_convert_fusion = bf16[512,512]{1,0:T(8,128)(2,1)} fusion(bf16[512,512]{1,0:T(8,128)(2,1)S(1)} %collective-permute-done.26, bf16[512,512]{1,0:T(8,128)(2,1)S(1)} %collective-permute-done.25, f32[512,512]{1,0:T(8,128)S(1)} %get-tuple-element.70, bf16[512,512]{1,0:T(8,128)(2,1)} %collective-permute-done.24), kind=kLoop, calls=%fused_computation.6 | loop fusion | flops 1835008 | bytes 3145728 | tf_op jit(solution)/shard_map/convert_element_type | solution.py:349
  (80 shorter events, 10.1 us)
Async XLA Ops:
  0.6 34.8 %copy-start.6 = (bf16[512,512]{1,0:T(8,128)(2,1)S(1)}, bf16[512,512]{1,0:T(8,128)(2,1)}, u32[]{:S(2)}) copy-start(bf16[512,512]{1,0:T(8,128)(2,1)} %acts.1) | copy-start | bytes 1572868
  2.9 21.5 %collective-permute-start.2 = (bf16[256,512]{1,0:T(8,128)(2,1)S(1)}, bf16[256,512]{1,0:T(8,128)(2,1)S(1)}, u32[]{:S(2)}, u32[]{:S(2)}) collective-permute-start(bf16[256,512]{1,0:T(8,128)(2,1)S(1)} %get-tuple-element.85), channel_id=1, source_target_pairs={{0,12},{4,0},{8,4},{12,8},{1,13},{5,1},{9,5},{13,9},{2,14},{6,2},{... | collective-permute-start | bytes 786440 | tf_op jit(solution)/shard_map/ppermute | solution.py:226
  7.5 16.9 %collective-permute-start.1 = (bf16[256,512]{1,0:T(8,128)(2,1)S(1)}, bf16[256,512]{1,0:T(8,128)(2,1)S(1)}, u32[]{:S(2)}, u32[]{:S(2)}) collective-permute-start(bf16[256,512]{1,0:T(8,128)(2,1)S(1)} %get-tuple-element.86), channel_id=1, source_target_pairs={{0,8},{4,12},{8,0},{12,4},{1,9},{5,13},{9,1},{13,5},{2,10},{6,14},... | collective-permute-start | bytes 786440 | tf_op jit(solution)/shard_map/ppermute | solution.py:226
  7.5 16.9 %collective-permute-start = (bf16[256,512]{1,0:T(8,128)(2,1)S(1)}, bf16[256,512]{1,0:T(8,128)(2,1)}, u32[]{:S(2)}, u32[]{:S(2)}) collective-permute-start(bf16[256,512]{1,0:T(8,128)(2,1)S(1)} %get-tuple-element.87), channel_id=1, source_target_pairs={{0,4},{4,8},{8,12},{12,0},{1,5},{5,9},{9,13},{13,1},{2,6},{6,10},{... | collective-permute-start | bytes 786440 | tf_op jit(solution)/shard_map/ppermute | solution.py:226
  12.5 22.9 %all-to-all-start = ((bf16[8,2,2,32,512]{4,3,2,1,0:T(8,128)(2,1)}), bf16[8,2,2,32,512]{4,3,2,1,0:T(8,128)(2,1)S(1)}, u32[]{:S(2)}, u32[]{:S(2)}) async-start(bf16[8,2,2,32,512]{4,3,2,1,0:T(8,128)(2,1)} %bitcast.37), calls=%async_computation | async-start | bytes 2097152 | tf_op jit(solution)/shard_map/all_to_all | solution.py:279
  18.4 10.5 %collective-permute-start.3 = (bf16[256,512]{1,0:T(8,128)(2,1)}, bf16[256,512]{1,0:T(8,128)(2,1)}, u32[]{:S(2)}, u32[]{:S(2)}) collective-permute-start(bf16[256,512]{1,0:T(8,128)(2,1)} %get-tuple-element.84), channel_id=1, source_target_pairs={{0,4},{4,8},{8,12},{12,0},{1,5},{5,9},{9,13},{13,1},{2,6},{6,10},{... | collective-permute-start | bytes 786440 | tf_op jit(solution)/shard_map/ppermute | solution.py:226
  20.3 8.6 %collective-permute-start.4 = (bf16[256,512]{1,0:T(8,128)(2,1)S(1)}, bf16[256,512]{1,0:T(8,128)(2,1)}, u32[]{:S(2)}, u32[]{:S(2)}) collective-permute-start(bf16[256,512]{1,0:T(8,128)(2,1)S(1)} %get-tuple-element.83), channel_id=1, source_target_pairs={{0,12},{4,0},{8,4},{12,8},{1,13},{5,1},{9,5},{13,9},{2,14},{6,2},{... | collective-permute-start | bytes 786440 | tf_op jit(solution)/shard_map/ppermute | solution.py:226
  24.4 0.7 copy-start.13
  24.4 0.8 copy-start.14
  25.2 8.8 %collective-permute-start.5 = (bf16[256,512]{1,0:T(8,128)(2,1)S(1)}, bf16[256,512]{1,0:T(8,128)(2,1)S(1)}, u32[]{:S(2)}, u32[]{:S(2)}) collective-permute-start(bf16[256,512]{1,0:T(8,128)(2,1)S(1)} %get-tuple-element.48), channel_id=1, source_target_pairs={{0,8},{4,12},{8,0},{12,4},{1,9},{5,13},{9,1},{13,5},{2,10},{6,14},... | collective-permute-start | bytes 786440 | tf_op jit(solution)/shard_map/ppermute | solution.py:226
  27.5 54.9 %copy-start.1 = (bf16[512,512]{1,0:T(8,128)(2,1)}, bf16[512,512]{1,0:T(8,128)(2,1)S(1)}, u32[]{:S(2)}) copy-start(bf16[512,512]{1,0:T(8,128)(2,1)S(1)} %multiply_convert_fusion.refs_1_.weighted) | copy-start | bytes 1572868
  28.9 54.1 %copy-start.4 = (bf16[3,256,512]{2,1,0:T(8,128)(2,1)}, bf16[3,256,512]{2,1,0:T(8,128)(2,1)S(1)}, u32[]{:S(2)}) copy-start(bf16[3,256,512]{2,1,0:T(8,128)(2,1)S(1)} %pad_maximum_fusion.refs_5_) | copy-start | bytes 2359300
  28.9 21.7 %collective-permute-start.9 = (bf16[3,256,512]{2,1,0:T(8,128)(2,1)S(1)}, bf16[3,256,512]{2,1,0:T(8,128)(2,1)}, u32[]{:S(2)}, u32[]{:S(2)}) collective-permute-start(bf16[3,256,512]{2,1,0:T(8,128)(2,1)S(1)} %pad_maximum_fusion.refs_5_), channel_id=1, source_target_pairs={{0,32},{32,64},{64,96},{96,0},{1,33},{33,65},{65,97},{97,1},{2,34}... | collective-permute-start | bytes 2359304 | tf_op jit(solution)/shard_map/ppermute | solution.py:226
  30.4 23.2 %collective-permute-start.10 = (bf16[3,256,512]{2,1,0:T(8,128)(2,1)S(1)}, bf16[3,256,512]{2,1,0:T(8,128)(2,1)}, u32[]{:S(2)}, u32[]{:S(2)}) collective-permute-start(bf16[3,256,512]{2,1,0:T(8,128)(2,1)S(1)} %pad_maximum_fusion.refs_5_), channel_id=1, source_target_pairs={{0,96},{32,0},{64,32},{96,64},{1,97},{33,1},{65,33},{97,65},{2,98}... | collective-permute-start | bytes 2359304 | tf_op jit(solution)/shard_map/ppermute | solution.py:226
  31.7 22.0 %collective-permute-start.11 = (bf16[3,256,512]{2,1,0:T(8,128)(2,1)S(1)}, bf16[3,256,512]{2,1,0:T(8,128)(2,1)}, u32[]{:S(2)}, u32[]{:S(2)}) collective-permute-start(bf16[3,256,512]{2,1,0:T(8,128)(2,1)S(1)} %pad_maximum_fusion.refs_5_), channel_id=1, source_target_pairs={{0,16},{16,0},{1,17},{17,1},{2,18},{18,2},{3,19},{19,3},{4,20},{20... | collective-permute-start | bytes 2359304 | tf_op jit(solution)/shard_map/ppermute | solution.py:273
  34.7 13.3 %collective-permute-start.6 = (bf16[512,512]{1,0:T(8,128)(2,1)S(1)}, bf16[512,512]{1,0:T(8,128)(2,1)}, u32[]{:S(2)}, u32[]{:S(2)}) collective-permute-start(bf16[512,512]{1,0:T(8,128)(2,1)S(1)} %multiply_convert_fusion.refs_1_.weighted), channel_id=1, source_target_pairs={{0,4},{4,8},{8,12},{12,0},{1,5},{5,9},{9,13},{13,1},{2,6},{6,10},{... | collective-permute-start | bytes 1572872 | tf_op jit(solution)/shard_map/ppermute | solution.py:226
  35.4 1.7 %copy-start.3 = (bf16[8,2,2,32,512]{4,3,2,1,0:T(8,128)(2,1)}, bf16[8,2,2,32,512]{4,3,2,1,0:T(8,128)(2,1)S(1)}, u32[]{:S(2)}) copy-start(bf16[8,2,2,32,512]{4,3,2,1,0:T(8,128)(2,1)S(1)} %all-to-all-done) | copy-start | bytes 3145732
  37.1 41.1 %all-to-all-start.1 = ((bf16[4,512,512]{2,1,0:T(8,128)(2,1)}), bf16[4,512,512]{2,1,0:T(8,128)(2,1)S(1)}, u32[]{:S(2)}, u32[]{:S(2)}) async-start(bf16[4,512,512]{2,1,0:T(8,128)(2,1)} %broadcast_in_dim.13), calls=%async_computation.1 | async-start | bytes 4194304 | tf_op jit(solution)/shard_map/all_to_all | solution.py:282
  41.9 18.0 %collective-permute-start.7 = (bf16[512,512]{1,0:T(8,128)(2,1)S(1)}, bf16[512,512]{1,0:T(8,128)(2,1)S(1)}, u32[]{:S(2)}, u32[]{:S(2)}) collective-permute-start(bf16[512,512]{1,0:T(8,128)(2,1)S(1)} %multiply_convert_fusion.refs_1_.weighted), channel_id=1, source_target_pairs={{0,8},{4,12},{8,0},{12,4},{1,9},{5,13},{9,1},{13,5},{2,10},{6,14},... | collective-permute-start | bytes 1572872 | tf_op jit(solution)/shard_map/ppermute | solution.py:226
  45.5 32.6 %copy-start.5 = (bf16[3,256,512]{2,1,0:T(8,128)(2,1)}, bf16[3,256,512]{2,1,0:T(8,128)(2,1)S(1)}, u32[]{:S(2)}) copy-start(bf16[3,256,512]{2,1,0:T(8,128)(2,1)S(1)} %pad_maximum_fusion.1.refs_7_) | copy-start | bytes 2359300
  47.1 31.0 %copy-start.7 = (bf16[8,2,1,32,512]{4,3,2,1,0:T(8,128)(2,1)}, bf16[8,2,1,32,512]{4,3,2,1,0:T(8,128)(2,1)S(1)}, u32[]{:S(2)}) copy-start(bf16[8,2,1,32,512]{4,3,2,1,0:T(8,128)(2,1)S(1)} %get-tuple-element.89) | copy-start | bytes 1572868
  47.1 31.0 %copy-start.8 = (bf16[8,2,1,32,512]{4,3,2,1,0:T(8,128)(2,1)}, bf16[8,2,1,32,512]{4,3,2,1,0:T(8,128)(2,1)S(1)}, u32[]{:S(2)}) copy-start(bf16[8,2,1,32,512]{4,3,2,1,0:T(8,128)(2,1)S(1)} %get-tuple-element.88) | copy-start | bytes 1572868
  48.0 18.9 %collective-permute-start.8 = (bf16[512,512]{1,0:T(8,128)(2,1)S(1)}, bf16[512,512]{1,0:T(8,128)(2,1)S(1)}, u32[]{:S(2)}, u32[]{:S(2)}) collective-permute-start(bf16[512,512]{1,0:T(8,128)(2,1)S(1)} %multiply_convert_fusion.refs_1_.weighted), channel_id=1, source_target_pairs={{0,12},{4,0},{8,4},{12,8},{1,13},{5,1},{9,5},{13,9},{2,14},{6,2},{... | collective-permute-start | bytes 1572872 | tf_op jit(solution)/shard_map/ppermute | solution.py:226
  50.6 27.6 %collective-permute-start.13 = (bf16[3,256,512]{2,1,0:T(8,128)(2,1)S(1)}, bf16[3,256,512]{2,1,0:T(8,128)(2,1)}, u32[]{:S(2)}, u32[]{:S(2)}) collective-permute-start(bf16[3,256,512]{2,1,0:T(8,128)(2,1)S(1)} %pad_maximum_fusion.1.refs_7_), channel_id=1, source_target_pairs={{0,16},{16,0},{1,17},{17,1},{2,18},{18,2},{3,19},{19,3},{4,20},{20... | collective-permute-start | bytes 2359304 | tf_op jit(solution)/shard_map/ppermute | solution.py:273
  53.6 29.4 %collective-permute-start.12 = (bf16[3,256,512]{2,1,0:T(8,128)(2,1)}, bf16[3,256,512]{2,1,0:T(8,128)(2,1)}, u32[]{:S(2)}, u32[]{:S(2)}) collective-permute-start(bf16[3,256,512]{2,1,0:T(8,128)(2,1)} %collective-permute-done.9.refs_6_), channel_id=1, source_target_pairs={{0,16},{16,0},{1,17},{17,1},{2,18},{18,2},{3,19},{19,3},{4,20},{20... | collective-permute-start | bytes 2359304 | tf_op jit(solution)/shard_map/ppermute | solution.py:273
  53.7 29.3 %collective-permute-start.14 = (bf16[3,256,512]{2,1,0:T(8,128)(2,1)}, bf16[3,256,512]{2,1,0:T(8,128)(2,1)}, u32[]{:S(2)}, u32[]{:S(2)}) collective-permute-start(bf16[3,256,512]{2,1,0:T(8,128)(2,1)} %collective-permute-done.10.refs_8_), channel_id=1, source_target_pairs={{0,16},{16,0},{1,17},{17,1},{2,18},{18,2},{3,19},{19,3},{4,20},{20... | collective-permute-start | bytes 2359304 | tf_op jit(solution)/shard_map/ppermute | solution.py:273
  59.9 18.2 %copy-start.9 = (bf16[512,512]{1,0:T(8,128)(2,1)}, bf16[512,512]{1,0:T(8,128)(2,1)S(1)}, u32[]{:S(2)}) copy-start(bf16[512,512]{1,0:T(8,128)(2,1)S(1)} %collective-permute-done.7.refs_3_) | copy-start | bytes 1572868
  59.9 9.8 %collective-permute-start.16 = (f32[64,512]{1,0:T(8,128)S(1)}, f32[64,512]{1,0:T(8,128)S(1)}, u32[]{:S(2)}, u32[]{:S(2)}) collective-permute-start(f32[64,512]{1,0:T(8,128)S(1)} %pad_maximum_fusion.2), channel_id=1, source_target_pairs={{0,12},{4,0},{8,4},{12,8},{1,13},{5,1},{9,5},{13,9},{2,14},{6,2},{... | collective-permute-start | bytes 393224 | tf_op jit(solution)/shard_map/ppermute | solution.py:226
  66.9 11.2 %copy-start.10 = (bf16[512,512]{1,0:T(8,128)(2,1)}, bf16[512,512]{1,0:T(8,128)(2,1)S(1)}, u32[]{:S(2)}) copy-start(bf16[512,512]{1,0:T(8,128)(2,1)S(1)} %collective-permute-done.8.refs_4_) | copy-start | bytes 1572868
  66.9 5.3 %collective-permute-start.17 = (f32[64,512]{1,0:T(8,128)S(1)}, f32[64,512]{1,0:T(8,128)S(1)}, u32[]{:S(2)}, u32[]{:S(2)}) collective-permute-start(f32[64,512]{1,0:T(8,128)S(1)} %pad_maximum_fusion.2), channel_id=1, source_target_pairs={{0,8},{4,12},{8,0},{12,4},{1,9},{5,13},{9,1},{13,5},{2,10},{6,14},... | collective-permute-start | bytes 393224 | tf_op jit(solution)/shard_map/ppermute | solution.py:226
  69.7 8.3 %collective-permute-start.15 = (f32[64,512]{1,0:T(8,128)S(1)}, f32[64,512]{1,0:T(8,128)S(1)}, u32[]{:S(2)}, u32[]{:S(2)}) collective-permute-start(f32[64,512]{1,0:T(8,128)S(1)} %pad_maximum_fusion.2), channel_id=1, source_target_pairs={{0,4},{4,8},{8,12},{12,0},{1,5},{5,9},{9,13},{13,1},{2,6},{6,10},{... | collective-permute-start | bytes 393224 | tf_op jit(solution)/shard_map/ppermute | solution.py:226
  78.2 25.5 %copy-start.11 = (f32[64,512]{1,0:T(8,128)}, f32[64,512]{1,0:T(8,128)S(1)}, u32[]{:S(2)}) copy-start(f32[64,512]{1,0:T(8,128)S(1)} %add_add_fusion.t0) | copy-start | bytes 393220
  78.2 4.8 %copy-start = (bf16[4,512,512]{2,1,0:T(8,128)(2,1)}, bf16[4,512,512]{2,1,0:T(8,128)(2,1)S(1)}, u32[]{:S(2)}) copy-start(bf16[4,512,512]{2,1,0:T(8,128)(2,1)S(1)} %all-to-all-done.1.refs_0_) | copy-start | bytes 6291460
  78.2 21.6 %collective-permute-start.18 = (f32[64,512]{1,0:T(8,128)S(1)}, f32[64,512]{1,0:T(8,128)S(1)}, u32[]{:S(2)}, u32[]{:S(2)}) collective-permute-start(f32[64,512]{1,0:T(8,128)S(1)} %add_add_fusion.t0), channel_id=1, source_target_pairs={{0,1},{1,2},{2,3},{3,0},{4,5},{5,6},{6,7},{7,4},{8,9},{9,10},{10,1... | collective-permute-start | bytes 393224 | tf_op jit(solution)/shard_map/ppermute | solution.py:226
  79.6 21.7 %collective-permute-start.19 = (f32[64,512]{1,0:T(8,128)S(1)}, f32[64,512]{1,0:T(8,128)S(1)}, u32[]{:S(2)}, u32[]{:S(2)}) collective-permute-start(f32[64,512]{1,0:T(8,128)S(1)} %add_add_fusion.t0), channel_id=1, source_target_pairs={{0,3},{1,0},{2,1},{3,2},{4,7},{5,4},{6,5},{7,6},{8,11},{9,8},{10,9... | collective-permute-start | bytes 393224 | tf_op jit(solution)/shard_map/ppermute | solution.py:226
  80.9 21.9 %collective-permute-start.20 = (f32[64,512]{1,0:T(8,128)S(1)}, f32[64,512]{1,0:T(8,128)S(1)}, u32[]{:S(2)}, u32[]{:S(2)}) collective-permute-start(f32[64,512]{1,0:T(8,128)S(1)} %add_add_fusion.t0), channel_id=1, source_target_pairs={{0,2},{1,3},{2,0},{3,1},{4,6},{5,7},{6,4},{7,5},{8,10},{9,11},{10,... | collective-permute-start | bytes 393224 | tf_op jit(solution)/shard_map/ppermute | solution.py:226
  98.5 20.0 %collective-permute-start.23 = (bf16[512,512]{1,0:T(8,128)(2,1)}, bf16[512,512]{1,0:T(8,128)(2,1)S(1)}, u32[]{:S(2)}, u32[]{:S(2)}) collective-permute-start(bf16[512,512]{1,0:T(8,128)(2,1)} %get-tuple-element.58), channel_id=1, source_target_pairs={{0,8},{4,12},{8,0},{12,4},{1,9},{5,13},{9,1},{13,5},{2,10},{6,14},... | collective-permute-start | bytes 1572872 | tf_op jit(solution)/shard_map/ppermute | solution.py:226
  98.5 26.5 %collective-permute-start.22 = (bf16[512,512]{1,0:T(8,128)(2,1)}, bf16[512,512]{1,0:T(8,128)(2,1)}, u32[]{:S(2)}, u32[]{:S(2)}) collective-permute-start(bf16[512,512]{1,0:T(8,128)(2,1)} %get-tuple-element.57), channel_id=1, source_target_pairs={{0,4},{4,8},{8,12},{12,0},{1,5},{5,9},{9,13},{13,1},{2,6},{6,10},{... | collective-permute-start | bytes 1572872 | tf_op jit(solution)/shard_map/ppermute | solution.py:226
  99.8 3.8 %copy-start.16 = (f32[64,512]{1,0:T(8,128)}, f32[64,512]{1,0:T(8,128)S(1)}, u32[]{:S(2)}) copy-start(f32[64,512]{1,0:T(8,128)S(1)} %collective-permute-done.18.t1) | copy-start | bytes 393220
  99.8 25.2 %collective-permute-start.21 = (bf16[512,512]{1,0:T(8,128)(2,1)}, bf16[512,512]{1,0:T(8,128)(2,1)}, u32[]{:S(2)}, u32[]{:S(2)}) collective-permute-start(bf16[512,512]{1,0:T(8,128)(2,1)} %get-tuple-element.56), channel_id=1, source_target_pairs={{0,12},{4,0},{8,4},{12,8},{1,13},{5,1},{9,5},{13,9},{2,14},{6,2},{... | collective-permute-start | bytes 1572872 | tf_op jit(solution)/shard_map/ppermute | solution.py:226
  101.3 2.4 %copy-start.17 = (f32[64,512]{1,0:T(8,128)}, f32[64,512]{1,0:T(8,128)S(1)}, u32[]{:S(2)}) copy-start(f32[64,512]{1,0:T(8,128)S(1)} %collective-permute-done.19.t2) | copy-start | bytes 393220
  101.3 36.7 %collective-permute-start.26 = (bf16[512,512]{1,0:T(8,128)(2,1)}, bf16[512,512]{1,0:T(8,128)(2,1)S(1)}, u32[]{:S(2)}, u32[]{:S(2)}) collective-permute-start(bf16[512,512]{1,0:T(8,128)(2,1)} %get-tuple-element.73), channel_id=1, source_target_pairs={{0,2},{1,3},{2,0},{3,1},{4,6},{5,7},{6,4},{7,5},{8,10},{9,11},{10,... | collective-permute-start | bytes 1572872 | tf_op jit(solution)/shard_map/ppermute | solution.py:226
  102.8 0.9 copy-start.18
  102.8 35.1 %collective-permute-start.25 = (bf16[512,512]{1,0:T(8,128)(2,1)}, bf16[512,512]{1,0:T(8,128)(2,1)S(1)}, u32[]{:S(2)}, u32[]{:S(2)}) collective-permute-start(bf16[512,512]{1,0:T(8,128)(2,1)} %get-tuple-element.72), channel_id=1, source_target_pairs={{0,3},{1,0},{2,1},{3,2},{4,7},{5,4},{6,5},{7,6},{8,11},{9,8},{10,9... | collective-permute-start | bytes 1572872 | tf_op jit(solution)/shard_map/ppermute | solution.py:226
  107.0 23.2 %all-to-all-start.2 = ((bf16[8,2,2,32,512]{4,3,2,1,0:T(8,128)(2,1)}), bf16[8,2,2,32,512]{4,3,2,1,0:T(8,128)(2,1)S(1)}, u32[]{:S(2)}, u32[]{:S(2)}) async-start(bf16[8,2,2,32,512]{4,3,2,1,0:T(8,128)(2,1)} %bitcast.38), calls=%async_computation.2 | async-start | bytes 2097152 | tf_op jit(solution)/shard_map/all_to_all | solution.py:323
  118.4 0.8 copy-start.12
  118.4 19.5 %collective-permute-start.24 = (bf16[512,512]{1,0:T(8,128)(2,1)}, bf16[512,512]{1,0:T(8,128)(2,1)}, u32[]{:S(2)}, u32[]{:S(2)}) collective-permute-start(bf16[512,512]{1,0:T(8,128)(2,1)} %get-tuple-element.71), channel_id=1, source_target_pairs={{0,1},{1,2},{2,3},{3,0},{4,5},{5,6},{6,7},{7,4},{8,9},{9,10},{10,1... | collective-permute-start | bytes 1572872 | tf_op jit(solution)/shard_map/ppermute | solution.py:226
  130.2 1.0 copy-start.2
  (1 other events, 0.7 us)

commit v5 on v4

--- a/solution.py
+++ b/solution.py
@@ -270,7 +270,8 @@
     far = jnp.stack([second[d] for d in (1, 2, 3)])
     sent, _ = lax.optimization_barrier((near, (second[1], second[3])))
     own = [near, shift(sent, "x", 1), far, shift(sent, "x", 3)]
-    other = [lax.ppermute(piece, "core", [(0, 1), (1, 0)]) for piece in own]
+    swap = [(0, 1), (1, 0)]
+    other = {e: lax.ppermute(own[e], "core", swap) for e in (0, 2)}
     slots = prompt_adapter_slot
     slots, _ = lax.optimization_barrier((slots, cuts[0]))
     sent, pos = pick(
@@ -298,6 +299,9 @@
 
     sent, _ = lax.optimization_barrier((weighted, second[2]))
     grads_in = {0: weighted} | {d: shift(sent, "z", d) for d in (1, 3, 2)}
+    late, _ = lax.optimization_barrier(((own[1], own[3]), (grads_in[1], grads_in[3])))
+    other[1], other[3] = (lax.ppermute(piece, "core", swap) for piece in late)
+    other = [other[e] for e in range(4)]
 
     contract_cols = (((1,), (1,)), ((), ()))
     low_all = lax.dot_general(down, activations, contract_cols, preferred_element_type=F32)
@@ -305,10 +309,9 @@
     low_part = jnp.sum(low_all.reshape(PROMPTS, RANK, ROWS) * onehot[:, None, :], axis=0)
     back_part = jnp.sum(back_all.reshape(PROMPTS, RANK, ROWS) * onehot[:, None, :], axis=0)
     sums = jnp.concatenate([low_part, back_part])
-    sums, _ = lax.optimization_barrier((sums, other[0]))
-    last, _ = lax.optimization_barrier((sums, grads_in))
-    sums = (sums + shift(sums, "z", 1)) + (shift(sums, "z", 3) + shift(last, "z", 2))
-    sums, _ = lax.optimization_barrier((sums, (own[1], own[3], other[2], acts)))
+    sums, _ = lax.optimization_barrier((sums, other))
+    sums = sums + sum(shift(sums, "z", i) for i in (1, 3, 2))
+    sums, _ = lax.optimization_barrier((sums, (grads_in, acts)))
     terms = [sums] + [shift(sums, "y", i) for i in (1, 3, 2)]
     where = jnp.stack([x, c, z, y]).astype(jnp.int32)
     layer_parts, input_parts = partials(
@@ -340,8 +343,7 @@
     inward = input_parts[0].astype(F32) + scale_down * lax.dot_general(
         back_wide, down, contract_rows, preferred_element_type=F32
     )
-    inward, updated = lax.optimization_barrier((inward, updated))
-    layer = lax.optimization_barrier(layer)
+    layer, inward = lax.optimization_barrier((layer, inward))
     for i in (1, 3, 2):
         layer = layer + layer_parts[i].astype(F32)
         inward = inward + input_parts[i].astype(F32)

time: 141 us -> 144 us (1.021)
  starting transfers between devices: 51.9 us -> 62.3 us
  waiting for transfers between devices: 29 us -> 24.7 us
  other arithmetic: 14.4 us -> 11.5 us
    all_to_all x1, starting transfers between devices: 8.11 us -> 14 us  [local(): lax.all_to_all(grads, ('x', 'core'), 0, 0).reshape(PROMPTS, 2, RANK, COLS)]
    ppermute x23, starting transfers between devices: 28.8 us -> 31.8 us  [shift(): lax.ppermute(value, axis, [(i, (i + by) % size) for i in range(size)])]
    all_to_all x1, waiting for transfers between devices: 2.73 us -> 0.01 us  [local(): lax.all_to_all(grads, ('x', 'core'), 0, 0).reshape(PROMPTS, 2, RANK, COLS)]
    ppermute x23, waiting for transfers between devices: 26.3 us -> 24.6 us  [shift(): lax.ppermute(value, axis, [(i, (i + by) % size) for i in range(size)])]
    ppermute x4, starting transfers between devices: 4.99 us -> 6.49 us  [the longest x2 5.9 us: local(): other = {e: lax.ppermute(own[e], 'core', swap) for e in (0, 2)}]
  transfers between devices with their start and end apart: 30 -> 30, of which waited for: 10 -> 5; matrix products, arithmetic and copies ran while one was open for 15% -> 14% of each run, Pallas kernels for 21% -> 16%
where the time goes in v5:
time: 144 us; the launch traced here: 143 us
  starting transfers between devices  62.3 us (43%)
  Pallas kernels  29.8 us (21%)
  waiting for transfers between devices  24.7 us (17%)
  other arithmetic  11.5 us (8%)
  local copies, waits for them, and re-layouts  7.62 us (5%)
  matrix products  5.63 us (4%)
    ppermute x23, starting transfers between devices, shift(): lax.ppermute(value, axis, [(i, (i + by) % size) for i in range(size)])  31.8 us
    ppermute x23, waiting for transfers between devices, shift(): lax.ppermute(value, axis, [(i, (i + by) % size) for i in range(size)])  24.6 us
    pallas_call x1, Pallas kernels, partials(): pl.pallas_call(partial_kernel, out_shape=[block] * 8, grid_spec=pltpu.Pre...  15.4 us
    all_to_all x1, starting transfers between devices, local(): lax.all_to_all(grads, ('x', 'core'), 0, 0).reshape(PROMPTS, 2, RANK, COLS)  14 us
    pallas_call x1, Pallas kernels, adam(): pl.pallas_call(adam_kernel, out_shape=(half, half, full, full, full, full...  6.79 us
    ppermute x2, starting transfers between devices, local(): other = {e: lax.ppermute(own[e], 'core', swap) for e in (0, 2)}  5.9 us
    all_to_all x1, starting transfers between devices, local(): lax.all_to_all(sent.reshape(8, 2, 2, RANK, COLS), ('x', 'core'), 0, 0)  5.84 us
    pallas_call x1, Pallas kernels, pick(): pl.pallas_call(pick_kernel, out_shape=(jax.ShapeDtypeStruct((PROMPTS, 2,...  4.31 us
  transfers between devices with their start and end apart: 30, of which 5 were waited for; matrix products, arithmetic and copies ran while one was open for 14% of the time, Pallas kernels for 16%

profile of v5, /device:TPU:1, one launch (start us, length us, event | category | flops | bytes accessed | tf_op | source)
XLA Modules:
  0.0 142.7 jit_solution(16090892177599181230)
XLA Ops:
  0.7 2.2 %constant_dynamic-slice_fusion = (bf16[256,512]{1,0:T(8,128)(2,1)}, bf16[256,512]{1,0:T(8,128)(2,1)S(1)}, bf16[256,512]{1,0:T(8,128)(2,1)S(1)}, bf16[256,512]{1,...) fusion(bf16[8192,512]{1,0:T(8,128)(2,1)} %refs_13_.1, s32[]{:T(128)S(6)} %select_n.38, ...), kind=kLoop, calls=%fused_computation.29 | loop fusion | bytes 3145752 | tf_op jit(solution)/shard_map/dynamic_slice | solution.py:255
  2.9 4.6 %collective-permute-start.2 = (bf16[256,512]{1,0:T(8,128)(2,1)S(1)}, bf16[256,512]{1,0:T(8,128)(2,1)}, u32[]{:S(2)}, u32[]{:S(2)}) collective-permute-start(bf16[256,512]{1,0:T(8,128)(2,1)S(1)} %get-tuple-element.77), channel_id=1, source_target_pairs={{0,12},{4,0},{8,4},{12,8},{1,13},{5,1},{9,5},{13,9},{2,14},{6,2},{... | collective-permute-start | bytes 786440 | tf_op jit(solution)/shard_map/ppermute | solution.py:226
  8.2 4.3 %shard_map.179 = (bf16[16,2,32,512]{3,2,1,0:T(8,128)(2,1)}, s32[16]{0:T(128)}) custom-call(s32[128]{0:T(128)} %slots, s32[1]{0:T(128)} %bitcast.4.member, bf16[16,32,512]{2,1,0:T(8,128)(2,1)} %dn.1, bf16[16,32,512]{2,1,0:T(8,128)(2,1)} %up.3), custom_call_target="tpu_custom_call" | custom-call | flops 1 | bytes 1 | tf_op jit(solution)/shard_map/pallas_call | solution.py:58
  12.5 5.8 %all-to-all-start = ((bf16[8,2,2,32,512]{4,3,2,1,0:T(8,128)(2,1)}), bf16[8,2,2,32,512]{4,3,2,1,0:T(8,128)(2,1)S(1)}, u32[]{:S(2)}, u32[]{:S(2)}) async-start(bf16[8,2,2,32,512]{4,3,2,1,0:T(8,128)(2,1)} %bitcast.37), calls=%async_computation | async-start | bytes 2097152 | tf_op jit(solution)/shard_map/all_to_all | solution.py:280
  18.4 1.9 %collective-permute-start.3 = (bf16[256,512]{1,0:T(8,128)(2,1)S(1)}, bf16[256,512]{1,0:T(8,128)(2,1)}, u32[]{:S(2)}, u32[]{:S(2)}) collective-permute-start(bf16[256,512]{1,0:T(8,128)(2,1)S(1)} %get-tuple-element.76), channel_id=1, source_target_pairs={{0,4},{4,8},{8,12},{12,0},{1,5},{5,9},{9,13},{13,1},{2,6},{6,10},{... | collective-permute-start | bytes 786440 | tf_op jit(solution)/shard_map/ppermute | solution.py:226
  20.3 0.7 collective-permute-start.4
  21.1 0.7 and_select_fusion
  22.0 0.7 multiply_add_fusion
  22.7 0.8 select_reduce_fusion.2
  24.3 1.2 pad_maximum_fusion.refs_5_
  25.5 2.5 %collective-permute-done.3 = bf16[256,512]{1,0:T(8,128)(2,1)} collective-permute-done((bf16[256,512]{1,0:T(8,128)(2,1)S(1)}, bf16[256,512]{1,0:T(8,128)(2,1)}, u32[]{:S(2)}, u32[]{:S(2)}) %collective-permute-start.3) | collective-permute-done | bytes 262176 | tf_op jit(solution)/shard_map/ppermute | solution.py:226
  28.1 0.9 collective-permute-start.9
  29.0 1.7 %collective-permute-start.10 = (bf16[3,256,512]{2,1,0:T(8,128)(2,1)S(1)}, bf16[3,256,512]{2,1,0:T(8,128)(2,1)}, u32[]{:S(2)}, u32[]{:S(2)}) collective-permute-start(bf16[3,256,512]{2,1,0:T(8,128)(2,1)S(1)} %pad_maximum_fusion.refs_5_), channel_id=1, source_target_pairs={{0,96},{32,0},{64,32},{96,64},{1,97},{33,1},{65,33},{97,65},{2,98}... | collective-permute-start | bytes 2359304 | tf_op jit(solution)/shard_map/ppermute | solution.py:226
  30.8 0.9 collective-permute-start.5
  32.0 6.7 %collective-permute-done.5 = bf16[256,512]{1,0:T(8,128)(2,1)S(1)} collective-permute-done((bf16[256,512]{1,0:T(8,128)(2,1)}, bf16[256,512]{1,0:T(8,128)(2,1)S(1)}, u32[]{:S(2)}, u32[]{:S(2)}) %collective-permute-start.5) | collective-permute-done | bytes 262176 | tf_op jit(solution)/shard_map/ppermute | solution.py:226
  39.4 2.0 %collective-permute-start.8 = (bf16[512,512]{1,0:T(8,128)(2,1)S(1)}, bf16[512,512]{1,0:T(8,128)(2,1)}, u32[]{:S(2)}, u32[]{:S(2)}) collective-permute-start(bf16[512,512]{1,0:T(8,128)(2,1)S(1)} %multiply_convert_fusion.refs_1_.weighted), channel_id=1, source_target_pairs={{0,12},{4,0},{8,4},{12,8},{1,13},{5,1},{9,5},{13,9},{2,14},{6,2},{... | collective-permute-start | bytes 1572872 | tf_op jit(solution)/shard_map/ppermute | solution.py:226
  41.3 1.6 %broadcast_in_dim.13 = bf16[4,512,512]{2,1,0:T(8,128)(2,1)} broadcast(bf16[512,512]{1,0:T(8,128)(2,1)S(1)} %copy-done.6), dimensions={1,2} | broadcast | bytes 2621440 | tf_op jit(solution)/shard_map/broadcast_in_dim | solution.py:283
  43.0 4.2 %all-to-all-start.1 = ((bf16[4,512,512]{2,1,0:T(8,128)(2,1)}), bf16[4,512,512]{2,1,0:T(8,128)(2,1)S(1)}, u32[]{:S(2)}, u32[]{:S(2)}) async-start(bf16[4,512,512]{2,1,0:T(8,128)(2,1)} %broadcast_in_dim.13), calls=%async_computation.1 | async-start | bytes 4194304 | tf_op jit(solution)/shard_map/all_to_all | solution.py:283
  47.2 3.4 %collective-permute-start.11 = (bf16[3,256,512]{2,1,0:T(8,128)(2,1)S(1)}, bf16[3,256,512]{2,1,0:T(8,128)(2,1)S(1)}, u32[]{:S(2)}, u32[]{:S(2)}) collective-permute-start(bf16[3,256,512]{2,1,0:T(8,128)(2,1)S(1)} %pad_maximum_fusion.refs_5_), channel_id=1, source_target_pairs={{0,16},{16,0},{1,17},{17,1},{2,18},{18,2},{3,19},{19,3},{4,20},{20... | collective-permute-start | bytes 2359304 | tf_op jit(solution)/shard_map/ppermute | solution.py:274
  50.6 1.2 pad_maximum_fusion.1.refs_7_
  51.8 2.5 %collective-permute-start.13 = (bf16[3,256,512]{2,1,0:T(8,128)(2,1)S(1)}, bf16[3,256,512]{2,1,0:T(8,128)(2,1)S(1)}, u32[]{:S(2)}, u32[]{:S(2)}) collective-permute-start(bf16[3,256,512]{2,1,0:T(8,128)(2,1)S(1)} %pad_maximum_fusion.1.refs_7_), channel_id=1, source_target_pairs={{0,16},{16,0},{1,17},{17,1},{2,18},{18,2},{3,19},{19,3},{4,20},{20... | collective-permute-start | bytes 2359304 | tf_op jit(solution)/shard_map/ppermute | solution.py:274
  55.5 1.3 collective-permute-start.7
  56.9 1.3 fusion.8
  58.6 1.5 %fusion = f32[32,512]{1,0:T(8,128)S(1)} fusion(bf16[16,32,512]{2,1,0:T(8,128)(2,1)S(1)} %bitcast.33, bf16[512,512]{1,0:T(8,128)(2,1)} %acts.1, f32[16,512]{1,0:T(8,128)S(1)} %get-tuple-element.83), kind=kOutput, calls=%fused_computation.4 | convolution fusion | flops 268943360 | bytes 1146880 | tf_op jit(solution)/shard_map/dot_general | solution.py:307
  60.3 1.7 %collective-permute-start.17 = (f32[64,512]{1,0:T(8,128)S(1)}, f32[64,512]{1,0:T(8,128)}, u32[]{:S(2)}, u32[]{:S(2)}) collective-permute-start(f32[64,512]{1,0:T(8,128)S(1)} %pad_maximum_fusion.2), channel_id=1, source_target_pairs={{0,8},{4,12},{8,0},{12,4},{1,9},{5,13},{9,1},{13,5},{2,10},{6,14},... | collective-permute-start | bytes 393224 | tf_op jit(solution)/shard_map/ppermute | solution.py:226
  62.0 2.7 %collective-permute-start.16 = (f32[64,512]{1,0:T(8,128)S(1)}, f32[64,512]{1,0:T(8,128)}, u32[]{:S(2)}, u32[]{:S(2)}) collective-permute-start(f32[64,512]{1,0:T(8,128)S(1)} %pad_maximum_fusion.2), channel_id=1, source_target_pairs={{0,12},{4,0},{8,4},{12,8},{1,13},{5,1},{9,5},{13,9},{2,14},{6,2},{... | collective-permute-start | bytes 393224 | tf_op jit(solution)/shard_map/ppermute | solution.py:226
  65.3 5.3 %collective-permute-done.7.refs_3_ = bf16[512,512]{1,0:T(8,128)(2,1)} collective-permute-done((bf16[512,512]{1,0:T(8,128)(2,1)S(1)}, bf16[512,512]{1,0:T(8,128)(2,1)}, u32[]{:S(2)}, u32[]{:S(2)}) %collective-permute-start.7) | collective-permute-done | bytes 524320 | tf_op jit(solution)/shard_map/ppermute | solution.py:226
  70.7 1.4 copy-done
  72.0 15.4 %shard_map.180 = (bf16[512,512]{1,0:T(8,128)(2,1)}, bf16[512,512]{1,0:T(8,128)(2,1)}, bf16[512,512]{1,0:T(8,128)(2,1)}, bf16[512,512]{1,0:T(8,128)(2,1)}, bf16[5...) custom-call(s32[4]{0:T(128)} %pad_add_fusion.where, ...), custom_call_target="tpu_custom_call" | custom-call | flops 1 | bytes 1 | tf_op jit(solution)/shard_map/pallas_call | solution.py:173
  87.5 1.0 collective-permute-start.23
  88.5 1.1 add_add_fusion.t0
  89.6 1.4 collective-permute-start.18
  91.0 1.5 %collective-permute-start.19 = (f32[64,512]{1,0:T(8,128)S(1)}, f32[64,512]{1,0:T(8,128)S(1)}, u32[]{:S(2)}, u32[]{:S(2)}) collective-permute-start(f32[64,512]{1,0:T(8,128)S(1)} %add_add_fusion.t0), channel_id=1, source_target_pairs={{0,3},{1,0},{2,1},{3,2},{4,7},{5,4},{6,5},{7,6},{8,11},{9,8},{10,9... | collective-permute-start | bytes 393224 | tf_op jit(solution)/shard_map/ppermute | solution.py:226
  92.5 1.6 %collective-permute-start.20 = (f32[64,512]{1,0:T(8,128)S(1)}, f32[64,512]{1,0:T(8,128)S(1)}, u32[]{:S(2)}, u32[]{:S(2)}) collective-permute-start(f32[64,512]{1,0:T(8,128)S(1)} %add_add_fusion.t0), channel_id=1, source_target_pairs={{0,2},{1,3},{2,0},{3,1},{4,6},{5,7},{6,4},{7,5},{8,10},{9,11},{10,... | collective-permute-start | bytes 393224 | tf_op jit(solution)/shard_map/ppermute | solution.py:226
  94.0 1.4 collective-permute-start.22
  95.5 1.3 collective-permute-start.21
  96.7 1.4 collective-permute-start.26
  98.4 1.1 collective-permute-start.25
  99.5 3.3 %shard_map.181 = (bf16[16,2,32,512]{3,2,1,0:T(8,128)(2,1)}, bf16[512,512]{1,0:T(8,128)(2,1)}, bf16[512,512]{1,0:T(8,128)(2,1)}) custom-call(f32[64,512]{1,0:T(8,128)} %copy-done.13, f32[64,512]{1,0:T(8,128)} %copy-done.16, f32[64,512]{1,0:T(8,128)} %copy-done.17, f32[64,512]{1,0:T(8,128)} %copy-done.18, bf16[16,512]{1,0:T(8,128)(2,1)} %get-tuple-element.82.hot, ...), custom_call_target="tpu_custom_call" | custom-call | flops 1 | bytes 1 | tf_op jit(solution)/shard_map/pallas_call | solution.py:215
  102.8 14.0 %all-to-all-start.2 = ((bf16[8,2,2,32,512]{4,3,2,1,0:T(8,128)(2,1)}), bf16[8,2,2,32,512]{4,3,2,1,0:T(8,128)(2,1)S(1)}, u32[]{:S(2)}, u32[]{:S(2)}) async-start(bf16[8,2,2,32,512]{4,3,2,1,0:T(8,128)(2,1)} %bitcast.38), calls=%async_computation.2 | async-start | bytes 2097152 | tf_op jit(solution)/shard_map/all_to_all | solution.py:326
  116.9 1.8 %convert_add_fusion.1 = f32[512,512]{1,0:T(8,128)S(1)} fusion(bf16[512,512]{1,0:T(8,128)(2,1)} %get-tuple-element.49, bf16[512,512]{1,0:T(8,128)(2,1)} %get-tuple-element.52, bf16[512,512]{1,0:T(8,128)(2,1)} %bitcast.36), kind=kOutput, calls=%fused_computation.9 | convolution fusion | flops 269221888 | bytes 2621440 | tf_op jit(solution)/shard_map/dot_general | solution.py:340
  118.7 1.2 collective-permute-start.24
  119.9 1.8 %convert_add_fusion = f32[512,512]{1,0:T(8,128)S(1)} fusion(bf16[512,512]{1,0:T(8,128)(2,1)} %get-tuple-element.53, bf16[512,512]{1,0:T(8,128)(2,1)} %get-tuple-element.54, bf16[512,512]{1,0:T(8,128)(2,1)} %bitcast.34), kind=kOutput, calls=%fused_computation.8 | convolution fusion | flops 269221888 | bytes 2621440 | tf_op jit(solution)/shard_map/dot_general | solution.py:343
  121.8 2.2 %add_convert_fusion.1 = bf16[512,512]{1,0:T(8,128)(2,1)} fusion(bf16[512,512]{1,0:T(8,128)(2,1)S(1)} %collective-permute-done.23, bf16[512,512]{1,0:T(8,128)(2,1)S(1)} %collective-permute-done.22, f32[512,512]{1,0:T(8,128)S(1)} %convert_add_fusion.1, bf16[512,512]{1,0:T(8,128)(2,1)} %collective-permute-done.21), kind=kLoop, calls=%fused_computation.7 | loop fusion | flops 1835008 | bytes 3145728 | tf_op jit(solution)/shard_map/convert_element_type | solution.py:351
  124.0 9.7 %collective-permute-done.24 = bf16[512,512]{1,0:T(8,128)(2,1)S(1)} collective-permute-done((bf16[512,512]{1,0:T(8,128)(2,1)}, bf16[512,512]{1,0:T(8,128)(2,1)S(1)}, u32[]{:S(2)}, u32[]{:S(2)}) %collective-permute-start.24) | collective-permute-done | bytes 524320 | tf_op jit(solution)/shard_map/ppermute | solution.py:226
  133.7 1.1 add_convert_fusion
  134.8 1.0 copy-done.2
  135.8 6.8 %shard_map.182 = (bf16[16,32,512]{2,1,0:T(8,128)(2,1)}, bf16[16,32,512]{2,1,0:T(8,128)(2,1)}, f32[16,32,512]{2,1,0:T(8,128)}, f32[16,32,512]{2,1,0:T(8,128)}, f3...) custom-call(s32[16]{0:T(128)} %get-tuple-element.63.pos, bf16[16,2,32,512]{3,2,1,0:T(8,128)(2,1)} %bitcast.32, ...), custom_call_target="tpu_custom_call" | custom-call | flops 1 | bytes 1 | tf_op jit(solution)/shard_map/pallas_call | solution.py:93
  (79 shorter events, 5.4 us)
Async XLA Ops:
  0.6 31.1 %copy-start.14 = (bf16[512,512]{1,0:T(8,128)(2,1)S(1)}, bf16[512,512]{1,0:T(8,128)(2,1)}, u32[]{:S(2)}) copy-start(bf16[512,512]{1,0:T(8,128)(2,1)} %param.13) | copy-start | bytes 1572868
  0.6 40.7 %copy-start.6 = (bf16[512,512]{1,0:T(8,128)(2,1)S(1)}, bf16[512,512]{1,0:T(8,128)(2,1)}, u32[]{:S(2)}) copy-start(bf16[512,512]{1,0:T(8,128)(2,1)} %acts.1) | copy-start | bytes 1572868
  2.9 21.4 %collective-permute-start.2 = (bf16[256,512]{1,0:T(8,128)(2,1)S(1)}, bf16[256,512]{1,0:T(8,128)(2,1)}, u32[]{:S(2)}, u32[]{:S(2)}) collective-permute-start(bf16[256,512]{1,0:T(8,128)(2,1)S(1)} %get-tuple-element.77), channel_id=1, source_target_pairs={{0,12},{4,0},{8,4},{12,8},{1,13},{5,1},{9,5},{13,9},{2,14},{6,2},{... | collective-permute-start | bytes 786440 | tf_op jit(solution)/shard_map/ppermute | solution.py:226
  7.5 16.8 %collective-permute-start.1 = (bf16[256,512]{1,0:T(8,128)(2,1)S(1)}, bf16[256,512]{1,0:T(8,128)(2,1)}, u32[]{:S(2)}, u32[]{:S(2)}) collective-permute-start(bf16[256,512]{1,0:T(8,128)(2,1)S(1)} %get-tuple-element.78), channel_id=1, source_target_pairs={{0,8},{4,12},{8,0},{12,4},{1,9},{5,13},{9,1},{13,5},{2,10},{6,14},... | collective-permute-start | bytes 786440 | tf_op jit(solution)/shard_map/ppermute | solution.py:226
  7.5 16.8 %collective-permute-start = (bf16[256,512]{1,0:T(8,128)(2,1)S(1)}, bf16[256,512]{1,0:T(8,128)(2,1)}, u32[]{:S(2)}, u32[]{:S(2)}) collective-permute-start(bf16[256,512]{1,0:T(8,128)(2,1)S(1)} %get-tuple-element.79), channel_id=1, source_target_pairs={{0,4},{4,8},{8,12},{12,0},{1,5},{5,9},{9,13},{13,1},{2,6},{6,10},{... | collective-permute-start | bytes 786440 | tf_op jit(solution)/shard_map/ppermute | solution.py:226
  12.5 28.8 %all-to-all-start = ((bf16[8,2,2,32,512]{4,3,2,1,0:T(8,128)(2,1)}), bf16[8,2,2,32,512]{4,3,2,1,0:T(8,128)(2,1)S(1)}, u32[]{:S(2)}, u32[]{:S(2)}) async-start(bf16[8,2,2,32,512]{4,3,2,1,0:T(8,128)(2,1)} %bitcast.37), calls=%async_computation | async-start | bytes 2097152 | tf_op jit(solution)/shard_map/all_to_all | solution.py:280
  18.4 9.7 %collective-permute-start.3 = (bf16[256,512]{1,0:T(8,128)(2,1)S(1)}, bf16[256,512]{1,0:T(8,128)(2,1)}, u32[]{:S(2)}, u32[]{:S(2)}) collective-permute-start(bf16[256,512]{1,0:T(8,128)(2,1)S(1)} %get-tuple-element.76), channel_id=1, source_target_pairs={{0,4},{4,8},{8,12},{12,0},{1,5},{5,9},{9,13},{13,1},{2,6},{6,10},{... | collective-permute-start | bytes 786440 | tf_op jit(solution)/shard_map/ppermute | solution.py:226
  20.3 7.8 %collective-permute-start.4 = (bf16[256,512]{1,0:T(8,128)(2,1)S(1)}, bf16[256,512]{1,0:T(8,128)(2,1)}, u32[]{:S(2)}, u32[]{:S(2)}) collective-permute-start(bf16[256,512]{1,0:T(8,128)(2,1)S(1)} %get-tuple-element.75), channel_id=1, source_target_pairs={{0,12},{4,0},{8,4},{12,8},{1,13},{5,1},{9,5},{13,9},{2,14},{6,2},{... | collective-permute-start | bytes 786440 | tf_op jit(solution)/shard_map/ppermute | solution.py:226
  25.5 45.1 %copy-start.4 = (bf16[3,256,512]{2,1,0:T(8,128)(2,1)}, bf16[3,256,512]{2,1,0:T(8,128)(2,1)S(1)}, u32[]{:S(2)}) copy-start(bf16[3,256,512]{2,1,0:T(8,128)(2,1)S(1)} %pad_maximum_fusion.refs_5_) | copy-start | bytes 2359300
  28.1 26.2 %collective-permute-start.9 = (bf16[3,256,512]{2,1,0:T(8,128)(2,1)S(1)}, bf16[3,256,512]{2,1,0:T(8,128)(2,1)}, u32[]{:S(2)}, u32[]{:S(2)}) collective-permute-start(bf16[3,256,512]{2,1,0:T(8,128)(2,1)S(1)} %pad_maximum_fusion.refs_5_), channel_id=1, source_target_pairs={{0,32},{32,64},{64,96},{96,0},{1,33},{33,65},{65,97},{97,1},{2,34}... | collective-permute-start | bytes 2359304 | tf_op jit(solution)/shard_map/ppermute | solution.py:226
  29.0 25.3 %collective-permute-start.10 = (bf16[3,256,512]{2,1,0:T(8,128)(2,1)S(1)}, bf16[3,256,512]{2,1,0:T(8,128)(2,1)}, u32[]{:S(2)}, u32[]{:S(2)}) collective-permute-start(bf16[3,256,512]{2,1,0:T(8,128)(2,1)S(1)} %pad_maximum_fusion.refs_5_), channel_id=1, source_target_pairs={{0,96},{32,0},{64,32},{96,64},{1,97},{33,1},{65,33},{97,65},{2,98}... | collective-permute-start | bytes 2359304 | tf_op jit(solution)/shard_map/ppermute | solution.py:226
  30.8 7.9 %collective-permute-start.5 = (bf16[256,512]{1,0:T(8,128)(2,1)}, bf16[256,512]{1,0:T(8,128)(2,1)S(1)}, u32[]{:S(2)}, u32[]{:S(2)}) collective-permute-start(bf16[256,512]{1,0:T(8,128)(2,1)} %get-tuple-element.44), channel_id=1, source_target_pairs={{0,8},{4,12},{8,0},{12,4},{1,9},{5,13},{9,1},{13,5},{2,10},{6,14},... | collective-permute-start | bytes 786440 | tf_op jit(solution)/shard_map/ppermute | solution.py:226
  31.9 38.7 %copy-start.1 = (bf16[512,512]{1,0:T(8,128)(2,1)}, bf16[512,512]{1,0:T(8,128)(2,1)S(1)}, u32[]{:S(2)}) copy-start(bf16[512,512]{1,0:T(8,128)(2,1)S(1)} %multiply_convert_fusion.refs_1_.weighted) | copy-start | bytes 1572868
  38.7 13.1 %collective-permute-start.6 = (bf16[512,512]{1,0:T(8,128)(2,1)S(1)}, bf16[512,512]{1,0:T(8,128)(2,1)}, u32[]{:S(2)}, u32[]{:S(2)}) collective-permute-start(bf16[512,512]{1,0:T(8,128)(2,1)S(1)} %multiply_convert_fusion.refs_1_.weighted), channel_id=1, source_target_pairs={{0,4},{4,8},{8,12},{12,0},{1,5},{5,9},{9,13},{13,1},{2,6},{6,10},{... | collective-permute-start | bytes 1572872 | tf_op jit(solution)/shard_map/ppermute | solution.py:226
  39.4 15.0 %collective-permute-start.8 = (bf16[512,512]{1,0:T(8,128)(2,1)S(1)}, bf16[512,512]{1,0:T(8,128)(2,1)}, u32[]{:S(2)}, u32[]{:S(2)}) collective-permute-start(bf16[512,512]{1,0:T(8,128)(2,1)S(1)} %multiply_convert_fusion.refs_1_.weighted), channel_id=1, source_target_pairs={{0,12},{4,0},{8,4},{12,8},{1,13},{5,1},{9,5},{13,9},{2,14},{6,2},{... | collective-permute-start | bytes 1572872 | tf_op jit(solution)/shard_map/ppermute | solution.py:226
  41.3 1.7 %copy-start.3 = (bf16[8,2,2,32,512]{4,3,2,1,0:T(8,128)(2,1)}, bf16[8,2,2,32,512]{4,3,2,1,0:T(8,128)(2,1)S(1)}, u32[]{:S(2)}) copy-start(bf16[8,2,2,32,512]{4,3,2,1,0:T(8,128)(2,1)S(1)} %all-to-all-done) | copy-start | bytes 3145732
  43.0 27.7 %all-to-all-start.1 = ((bf16[4,512,512]{2,1,0:T(8,128)(2,1)}), bf16[4,512,512]{2,1,0:T(8,128)(2,1)S(1)}, u32[]{:S(2)}, u32[]{:S(2)}) async-start(bf16[4,512,512]{2,1,0:T(8,128)(2,1)} %broadcast_in_dim.13), calls=%async_computation.1 | async-start | bytes 4194304 | tf_op jit(solution)/shard_map/all_to_all | solution.py:283
  47.2 13.0 %collective-permute-start.11 = (bf16[3,256,512]{2,1,0:T(8,128)(2,1)S(1)}, bf16[3,256,512]{2,1,0:T(8,128)(2,1)S(1)}, u32[]{:S(2)}, u32[]{:S(2)}) collective-permute-start(bf16[3,256,512]{2,1,0:T(8,128)(2,1)S(1)} %pad_maximum_fusion.refs_5_), channel_id=1, source_target_pairs={{0,16},{16,0},{1,17},{17,1},{2,18},{18,2},{3,19},{19,3},{4,20},{20... | collective-permute-start | bytes 2359304 | tf_op jit(solution)/shard_map/ppermute | solution.py:274
  51.8 13.5 %copy-start.5 = (bf16[3,256,512]{2,1,0:T(8,128)(2,1)}, bf16[3,256,512]{2,1,0:T(8,128)(2,1)S(1)}, u32[]{:S(2)}) copy-start(bf16[3,256,512]{2,1,0:T(8,128)(2,1)S(1)} %pad_maximum_fusion.1.refs_7_) | copy-start | bytes 2359300
  51.8 8.4 %collective-permute-start.13 = (bf16[3,256,512]{2,1,0:T(8,128)(2,1)S(1)}, bf16[3,256,512]{2,1,0:T(8,128)(2,1)S(1)}, u32[]{:S(2)}, u32[]{:S(2)}) collective-permute-start(bf16[3,256,512]{2,1,0:T(8,128)(2,1)S(1)} %pad_maximum_fusion.1.refs_7_), channel_id=1, source_target_pairs={{0,16},{16,0},{1,17},{17,1},{2,18},{18,2},{3,19},{19,3},{4,20},{20... | collective-permute-start | bytes 2359304 | tf_op jit(solution)/shard_map/ppermute | solution.py:274
  54.3 5.9 %collective-permute-start.12 = (bf16[3,256,512]{2,1,0:T(8,128)(2,1)}, bf16[3,256,512]{2,1,0:T(8,128)(2,1)S(1)}, u32[]{:S(2)}, u32[]{:S(2)}) collective-permute-start(bf16[3,256,512]{2,1,0:T(8,128)(2,1)} %collective-permute-done.9.refs_6_), channel_id=1, source_target_pairs={{0,16},{16,0},{1,17},{17,1},{2,18},{18,2},{3,19},{19,3},{4,20},{20... | collective-permute-start | bytes 2359304 | tf_op jit(solution)/shard_map/ppermute | solution.py:303
  54.4 5.8 %collective-permute-start.14 = (bf16[3,256,512]{2,1,0:T(8,128)(2,1)}, bf16[3,256,512]{2,1,0:T(8,128)(2,1)S(1)}, u32[]{:S(2)}, u32[]{:S(2)}) collective-permute-start(bf16[3,256,512]{2,1,0:T(8,128)(2,1)} %collective-permute-done.10.refs_8_), channel_id=1, source_target_pairs={{0,16},{16,0},{1,17},{17,1},{2,18},{18,2},{3,19},{19,3},{4,20},{20... | collective-permute-start | bytes 2359304 | tf_op jit(solution)/shard_map/ppermute | solution.py:303
  55.5 15.1 %collective-permute-start.7 = (bf16[512,512]{1,0:T(8,128)(2,1)S(1)}, bf16[512,512]{1,0:T(8,128)(2,1)}, u32[]{:S(2)}, u32[]{:S(2)}) collective-permute-start(bf16[512,512]{1,0:T(8,128)(2,1)S(1)} %multiply_convert_fusion.refs_1_.weighted), channel_id=1, source_target_pairs={{0,8},{4,12},{8,0},{12,4},{1,9},{5,13},{9,1},{13,5},{2,10},{6,14},... | collective-permute-start | bytes 1572872 | tf_op jit(solution)/shard_map/ppermute | solution.py:226
  58.1 7.2 %copy-start.7 = (bf16[8,2,1,32,512]{4,3,2,1,0:T(8,128)(2,1)}, bf16[8,2,1,32,512]{4,3,2,1,0:T(8,128)(2,1)S(1)}, u32[]{:S(2)}) copy-start(bf16[8,2,1,32,512]{4,3,2,1,0:T(8,128)(2,1)S(1)} %get-tuple-element.80) | copy-start | bytes 1572868
  58.2 7.1 %copy-start.8 = (bf16[8,2,1,32,512]{4,3,2,1,0:T(8,128)(2,1)}, bf16[8,2,1,32,512]{4,3,2,1,0:T(8,128)(2,1)S(1)}, u32[]{:S(2)}) copy-start(bf16[8,2,1,32,512]{4,3,2,1,0:T(8,128)(2,1)S(1)} %get-tuple-element.81) | copy-start | bytes 1572868
  60.2 5.1 %copy-start.9 = (bf16[3,256,512]{2,1,0:T(8,128)(2,1)}, bf16[3,256,512]{2,1,0:T(8,128)(2,1)S(1)}, u32[]{:S(2)}) copy-start(bf16[3,256,512]{2,1,0:T(8,128)(2,1)S(1)} %collective-permute-done.11.refs_9_) | copy-start | bytes 2359300
  60.2 5.1 %copy-start.10 = (bf16[3,256,512]{2,1,0:T(8,128)(2,1)}, bf16[3,256,512]{2,1,0:T(8,128)(2,1)S(1)}, u32[]{:S(2)}) copy-start(bf16[3,256,512]{2,1,0:T(8,128)(2,1)S(1)} %collective-permute-done.13.refs_11_) | copy-start | bytes 2359300
  60.2 5.1 %copy-start.11 = (bf16[3,256,512]{2,1,0:T(8,128)(2,1)}, bf16[3,256,512]{2,1,0:T(8,128)(2,1)S(1)}, u32[]{:S(2)}) copy-start(bf16[3,256,512]{2,1,0:T(8,128)(2,1)S(1)} %collective-permute-done.12.refs_10_) | copy-start | bytes 2359300
  60.3 5.1 %copy-start.12 = (bf16[3,256,512]{2,1,0:T(8,128)(2,1)}, bf16[3,256,512]{2,1,0:T(8,128)(2,1)S(1)}, u32[]{:S(2)}) copy-start(bf16[3,256,512]{2,1,0:T(8,128)(2,1)S(1)} %collective-permute-done.14.refs_12_) | copy-start | bytes 2359300
  60.3 28.2 %collective-permute-start.17 = (f32[64,512]{1,0:T(8,128)S(1)}, f32[64,512]{1,0:T(8,128)}, u32[]{:S(2)}, u32[]{:S(2)}) collective-permute-start(f32[64,512]{1,0:T(8,128)S(1)} %pad_maximum_fusion.2), channel_id=1, source_target_pairs={{0,8},{4,12},{8,0},{12,4},{1,9},{5,13},{9,1},{13,5},{2,10},{6,14},... | collective-permute-start | bytes 393224 | tf_op jit(solution)/shard_map/ppermute | solution.py:226
  62.0 26.5 %collective-permute-start.15 = (f32[64,512]{1,0:T(8,128)S(1)}, f32[64,512]{1,0:T(8,128)}, u32[]{:S(2)}, u32[]{:S(2)}) collective-permute-start(f32[64,512]{1,0:T(8,128)S(1)} %pad_maximum_fusion.2), channel_id=1, source_target_pairs={{0,4},{4,8},{8,12},{12,0},{1,5},{5,9},{9,13},{13,1},{2,6},{6,10},{... | collective-permute-start | bytes 393224 | tf_op jit(solution)/shard_map/ppermute | solution.py:226
  62.0 26.5 %collective-permute-start.16 = (f32[64,512]{1,0:T(8,128)S(1)}, f32[64,512]{1,0:T(8,128)}, u32[]{:S(2)}, u32[]{:S(2)}) collective-permute-start(f32[64,512]{1,0:T(8,128)S(1)} %pad_maximum_fusion.2), channel_id=1, source_target_pairs={{0,12},{4,0},{8,4},{12,8},{1,13},{5,1},{9,5},{13,9},{2,14},{6,2},{... | collective-permute-start | bytes 393224 | tf_op jit(solution)/shard_map/ppermute | solution.py:226
  70.7 1.4 copy-start
  87.5 31.2 %collective-permute-start.23 = (bf16[512,512]{1,0:T(8,128)(2,1)}, bf16[512,512]{1,0:T(8,128)(2,1)S(1)}, u32[]{:S(2)}, u32[]{:S(2)}) collective-permute-start(bf16[512,512]{1,0:T(8,128)(2,1)} %get-tuple-element.58), channel_id=1, source_target_pairs={{0,8},{4,12},{8,0},{12,4},{1,9},{5,13},{9,1},{13,5},{2,10},{6,14},... | collective-permute-start | bytes 1572872 | tf_op jit(solution)/shard_map/ppermute | solution.py:226
  89.6 10.0 %copy-start.13 = (f32[64,512]{1,0:T(8,128)}, f32[64,512]{1,0:T(8,128)S(1)}, u32[]{:S(2)}) copy-start(f32[64,512]{1,0:T(8,128)S(1)} %add_add_fusion.t0) | copy-start | bytes 393220
  89.6 5.9 %collective-permute-start.18 = (f32[64,512]{1,0:T(8,128)S(1)}, f32[64,512]{1,0:T(8,128)S(1)}, u32[]{:S(2)}, u32[]{:S(2)}) collective-permute-start(f32[64,512]{1,0:T(8,128)S(1)} %add_add_fusion.t0), channel_id=1, source_target_pairs={{0,1},{1,2},{2,3},{3,0},{4,5},{5,6},{6,7},{7,4},{8,9},{9,10},{10,1... | collective-permute-start | bytes 393224 | tf_op jit(solution)/shard_map/ppermute | solution.py:226
  91.0 5.8 %collective-permute-start.19 = (f32[64,512]{1,0:T(8,128)S(1)}, f32[64,512]{1,0:T(8,128)S(1)}, u32[]{:S(2)}, u32[]{:S(2)}) collective-permute-start(f32[64,512]{1,0:T(8,128)S(1)} %add_add_fusion.t0), channel_id=1, source_target_pairs={{0,3},{1,0},{2,1},{3,2},{4,7},{5,4},{6,5},{7,6},{8,11},{9,8},{10,9... | collective-permute-start | bytes 393224 | tf_op jit(solution)/shard_map/ppermute | solution.py:226
  92.5 6.0 %collective-permute-start.20 = (f32[64,512]{1,0:T(8,128)S(1)}, f32[64,512]{1,0:T(8,128)S(1)}, u32[]{:S(2)}, u32[]{:S(2)}) collective-permute-start(f32[64,512]{1,0:T(8,128)S(1)} %add_add_fusion.t0), channel_id=1, source_target_pairs={{0,2},{1,3},{2,0},{3,1},{4,6},{5,7},{6,4},{7,5},{8,10},{9,11},{10,... | collective-permute-start | bytes 393224 | tf_op jit(solution)/shard_map/ppermute | solution.py:226
  94.0 27.7 %collective-permute-start.22 = (bf16[512,512]{1,0:T(8,128)(2,1)}, bf16[512,512]{1,0:T(8,128)(2,1)S(1)}, u32[]{:S(2)}, u32[]{:S(2)}) collective-permute-start(bf16[512,512]{1,0:T(8,128)(2,1)} %get-tuple-element.57), channel_id=1, source_target_pairs={{0,4},{4,8},{8,12},{12,0},{1,5},{5,9},{9,13},{13,1},{2,6},{6,10},{... | collective-permute-start | bytes 1572872 | tf_op jit(solution)/shard_map/ppermute | solution.py:226
  95.5 4.1 %copy-start.16 = (f32[64,512]{1,0:T(8,128)}, f32[64,512]{1,0:T(8,128)S(1)}, u32[]{:S(2)}) copy-start(f32[64,512]{1,0:T(8,128)S(1)} %collective-permute-done.18.t1) | copy-start | bytes 393220
  95.5 26.3 %collective-permute-start.21 = (bf16[512,512]{1,0:T(8,128)(2,1)}, bf16[512,512]{1,0:T(8,128)(2,1)}, u32[]{:S(2)}, u32[]{:S(2)}) collective-permute-start(bf16[512,512]{1,0:T(8,128)(2,1)} %get-tuple-element.56), channel_id=1, source_target_pairs={{0,12},{4,0},{8,4},{12,8},{1,13},{5,1},{9,5},{13,9},{2,14},{6,2},{... | collective-permute-start | bytes 1572872 | tf_op jit(solution)/shard_map/ppermute | solution.py:226
  96.7 2.8 %copy-start.17 = (f32[64,512]{1,0:T(8,128)}, f32[64,512]{1,0:T(8,128)S(1)}, u32[]{:S(2)}) copy-start(f32[64,512]{1,0:T(8,128)S(1)} %collective-permute-done.19.t2) | copy-start | bytes 393220
  96.7 27.2 %collective-permute-start.26 = (bf16[512,512]{1,0:T(8,128)(2,1)}, bf16[512,512]{1,0:T(8,128)(2,1)S(1)}, u32[]{:S(2)}, u32[]{:S(2)}) collective-permute-start(bf16[512,512]{1,0:T(8,128)(2,1)} %get-tuple-element.62), channel_id=1, source_target_pairs={{0,2},{1,3},{2,0},{3,1},{4,6},{5,7},{6,4},{7,5},{8,10},{9,11},{10,... | collective-permute-start | bytes 1572872 | tf_op jit(solution)/shard_map/ppermute | solution.py:226
  98.4 1.1 copy-start.18
  98.4 25.5 %collective-permute-start.25 = (bf16[512,512]{1,0:T(8,128)(2,1)}, bf16[512,512]{1,0:T(8,128)(2,1)S(1)}, u32[]{:S(2)}, u32[]{:S(2)}) collective-permute-start(bf16[512,512]{1,0:T(8,128)(2,1)} %get-tuple-element.61), channel_id=1, source_target_pairs={{0,3},{1,0},{2,1},{3,2},{4,7},{5,4},{6,5},{7,6},{8,11},{9,8},{10,9... | collective-permute-start | bytes 1572872 | tf_op jit(solution)/shard_map/ppermute | solution.py:226
  102.8 32.0 %all-to-all-start.2 = ((bf16[8,2,2,32,512]{4,3,2,1,0:T(8,128)(2,1)}), bf16[8,2,2,32,512]{4,3,2,1,0:T(8,128)(2,1)S(1)}, u32[]{:S(2)}, u32[]{:S(2)}) async-start(bf16[8,2,2,32,512]{4,3,2,1,0:T(8,128)(2,1)} %bitcast.38), calls=%async_computation.2 | async-start | bytes 2097152 | tf_op jit(solution)/shard_map/all_to_all | solution.py:326
  118.7 15.0 %collective-permute-start.24 = (bf16[512,512]{1,0:T(8,128)(2,1)}, bf16[512,512]{1,0:T(8,128)(2,1)S(1)}, u32[]{:S(2)}, u32[]{:S(2)}) collective-permute-start(bf16[512,512]{1,0:T(8,128)(2,1)} %get-tuple-element.60), channel_id=1, source_target_pairs={{0,1},{1,2},{2,3},{3,0},{4,5},{5,6},{6,7},{7,4},{8,9},{9,10},{10,1... | collective-permute-start | bytes 1572872 | tf_op jit(solution)/shard_map/ppermute | solution.py:226
  134.8 1.0 copy-start.2
  (1 other events, 0.7 us)

commit v6 on v5

--- a/solution.py
+++ b/solution.py
@@ -70,8 +70,8 @@
 
 
 def adam_kernel(pos, grads, dn, up, m1d, m2d, m1u, m2u, odn, oup, o1d, o2d, o1u, o2u):
-    i0 = pl.program_id(0) * 4
-    for k in range(4):
+    i0 = pl.program_id(0) * 8
+    for k in range(8):
         q = pos[i0 + k]
         for which, (f, m1, m2, of, o1, o2) in enumerate(
             ((dn, m1d, m2d, odn, o1d, o2d), (up, m1u, m2u, oup, o1u, o2u))
@@ -87,7 +87,7 @@
 
 
 def adam(pos, grads, dn, up, m1d, m2d, m1u, m2u):
-    block = pl.BlockSpec((4, RANK, COLS), lambda i, pos: (i, 0, 0))
+    block = pl.BlockSpec((8, RANK, COLS), lambda i, pos: (i, 0, 0))
     half = jax.ShapeDtypeStruct((PROMPTS, RANK, COLS), BF16)
     full = jax.ShapeDtypeStruct((PROMPTS, RANK, COLS), F32)
     return pl.pallas_call(
@@ -95,7 +95,7 @@
         out_shape=(half, half, full, full, full, full),
         grid_spec=pltpu.PrefetchScalarGridSpec(
             num_scalar_prefetch=1,
-            grid=(4,),
+            grid=(2,),
             in_specs=[pl.BlockSpec((PROMPTS, 2, RANK, COLS), lambda i, pos: (0, 0, 0, 0))]
             + [block] * 6,
             out_specs=[block] * 6,
@@ -311,8 +311,9 @@
     sums = jnp.concatenate([low_part, back_part])
     sums, _ = lax.optimization_barrier((sums, other))
     sums = sums + sum(shift(sums, "z", i) for i in (1, 3, 2))
-    sums, _ = lax.optimization_barrier((sums, (grads_in, acts)))
+    sums, _ = lax.optimization_barrier((sums, (grads_in[1], grads_in[3])))
     terms = [sums] + [shift(sums, "y", i) for i in (1, 3, 2)]
+    terms, acts = lax.optimization_barrier((terms, acts))
     where = jnp.stack([x, c, z, y]).astype(jnp.int32)
     layer_parts, input_parts = partials(
         where, acts, [grads_in[i] for i in range(4)], own, other, frozen_weight

time: 144 us -> 145 us (level)
  waiting for transfers between devices: 24.7 us -> 37.5 us
  starting transfers between devices: 62.3 us -> 51.5 us
    ppermute x23, waiting for transfers between devices: 24.6 us -> 37.5 us  [shift(): lax.ppermute(value, axis, [(i, (i + by) % size) for i in range(size)])]
    all_to_all x1, starting transfers between devices: 14 us -> 5.34 us  [local(): lax.all_to_all(grads, ('x', 'core'), 0, 0).reshape(PROMPTS, 2, RANK, COLS)]
    ppermute x23, starting transfers between devices: 31.8 us -> 28.8 us  [shift(): lax.ppermute(value, axis, [(i, (i + by) % size) for i in range(size)])]
    add x0 -> x1, other arithmetic: none -> 1.56 us  [local(): input_parts[0].astype(F32)]
    unnamed x38 -> x34, local copies, waits for them, and re-layouts: 2.47 us -> 3.02 us
  transfers between devices with their start and end apart: 30 -> 30, of which waited for: 5 -> 10; matrix products, arithmetic and copies ran while one was open for 14% -> 14% of each run, Pallas kernels for 16% -> 5%
where the time goes in v6:
time: 145 us
  starting transfers between devices  51.5 us (36%)
  waiting for transfers between devices  37.5 us (26%)
  Pallas kernels  28.9 us (20%)
  other arithmetic  12 us (8%)
  local copies, waits for them, and re-layouts  8.18 us (6%)
  matrix products  5.32 us (4%)
    ppermute x23, waiting for transfers between devices, shift(): lax.ppermute(value, axis, [(i, (i + by) % size) for i in range(size)])  37.5 us
    ppermute x23, starting transfers between devices, shift(): lax.ppermute(value, axis, [(i, (i + by) % size) for i in range(size)])  28.8 us
    pallas_call x1, Pallas kernels, partials(): pl.pallas_call(partial_kernel, out_shape=[block] * 8, grid_spec=pltpu.Pre...  15.4 us
    all_to_all x1, starting transfers between devices, local(): lax.all_to_all(sent.reshape(8, 2, 2, RANK, COLS), ('x', 'core'), 0, 0)  6.09 us
    pallas_call x1, Pallas kernels, adam(): pl.pallas_call(adam_kernel, out_shape=(half, half, full, full, full, full...  5.92 us
    ppermute x2, starting transfers between devices, local(): other = {e: lax.ppermute(own[e], 'core', swap) for e in (0, 2)}  5.9 us
    all_to_all x1, starting transfers between devices, local(): lax.all_to_all(grads, ('x', 'core'), 0, 0).reshape(PROMPTS, 2, RANK, COLS)  5.34 us
    pallas_call x1, Pallas kernels, pick(): pl.pallas_call(pick_kernel, out_shape=(jax.ShapeDtypeStruct((PROMPTS, 2,...  4.35 us
  transfers between devices with their start and end apart: 30, of which 10 were waited for; matrix products, arithmetic and copies ran while one was open for 14% of the time, Pallas kernels for 5%

profile of v6, /device:TPU:1, one launch (start us, length us, event | category | flops | bytes accessed | tf_op | source)
XLA Modules:
  0.0 144.7 jit_solution(16735376338025617277)
XLA Ops:
  0.7 2.2 %constant_dynamic-slice_fusion = (bf16[256,512]{1,0:T(8,128)(2,1)}, bf16[256,512]{1,0:T(8,128)(2,1)S(1)}, bf16[256,512]{1,0:T(8,128)(2,1)S(1)}, bf16[256,512]{1,...) fusion(bf16[8192,512]{1,0:T(8,128)(2,1)} %refs_13_.1, s32[]{:T(128)S(6)} %select_n.38, ...), kind=kLoop, calls=%fused_computation.29 | loop fusion | bytes 3145752 | tf_op jit(solution)/shard_map/dynamic_slice | solution.py:255
  2.9 4.6 %collective-permute-start.4 = (bf16[256,512]{1,0:T(8,128)(2,1)S(1)}, bf16[256,512]{1,0:T(8,128)(2,1)}, u32[]{:S(2)}, u32[]{:S(2)}) collective-permute-start(bf16[256,512]{1,0:T(8,128)(2,1)S(1)} %get-tuple-element.85), channel_id=1, source_target_pairs={{0,12},{4,0},{8,4},{12,8},{1,13},{5,1},{9,5},{13,9},{2,14},{6,2},{... | collective-permute-start | bytes 786440 | tf_op jit(solution)/shard_map/ppermute | solution.py:226
  7.5 2.7 %collective-permute-start.2 = (bf16[256,512]{1,0:T(8,128)(2,1)S(1)}, bf16[256,512]{1,0:T(8,128)(2,1)}, u32[]{:S(2)}, u32[]{:S(2)}) collective-permute-start(bf16[256,512]{1,0:T(8,128)(2,1)S(1)} %get-tuple-element.87), channel_id=1, source_target_pairs={{0,12},{4,0},{8,4},{12,8},{1,13},{5,1},{9,5},{13,9},{2,14},{6,2},{... | collective-permute-start | bytes 786440 | tf_op jit(solution)/shard_map/ppermute | solution.py:226
  10.8 4.3 %shard_map.179 = (bf16[16,2,32,512]{3,2,1,0:T(8,128)(2,1)}, s32[16]{0:T(128)}) custom-call(s32[128]{0:T(128)} %slots, s32[1]{0:T(128)} %bitcast.4.member, bf16[16,32,512]{2,1,0:T(8,128)(2,1)} %dn.1, bf16[16,32,512]{2,1,0:T(8,128)(2,1)} %up.3), custom_call_target="tpu_custom_call" | custom-call | flops 1 | bytes 1 | tf_op jit(solution)/shard_map/pallas_call | solution.py:58
  15.1 6.1 %all-to-all-start = ((bf16[8,2,2,32,512]{4,3,2,1,0:T(8,128)(2,1)}), bf16[8,2,2,32,512]{4,3,2,1,0:T(8,128)(2,1)S(1)}, u32[]{:S(2)}, u32[]{:S(2)}) async-start(bf16[8,2,2,32,512]{4,3,2,1,0:T(8,128)(2,1)} %bitcast.37), calls=%async_computation | async-start | bytes 2097152 | tf_op jit(solution)/shard_map/all_to_all | solution.py:280
  22.2 0.7 multiply_add_fusion
  22.9 0.8 select_reduce_fusion.2
  24.5 2.4 %collective-permute-done = bf16[256,512]{1,0:T(8,128)(2,1)} collective-permute-done((bf16[256,512]{1,0:T(8,128)(2,1)S(1)}, bf16[256,512]{1,0:T(8,128)(2,1)}, u32[]{:S(2)}, u32[]{:S(2)}) %collective-permute-start) | collective-permute-done | bytes 262176 | tf_op jit(solution)/shard_map/ppermute | solution.py:226
  26.9 1.2 pad_maximum_fusion.refs_5_
  28.2 2.5 %collective-permute-start.7 = (bf16[3,256,512]{2,1,0:T(8,128)(2,1)S(1)}, bf16[3,256,512]{2,1,0:T(8,128)(2,1)}, u32[]{:S(2)}, u32[]{:S(2)}) collective-permute-start(bf16[3,256,512]{2,1,0:T(8,128)(2,1)S(1)} %pad_maximum_fusion.refs_5_), channel_id=1, source_target_pairs={{0,96},{32,0},{64,32},{96,64},{1,97},{33,1},{65,33},{97,65},{2,98}... | collective-permute-start | bytes 2359304 | tf_op jit(solution)/shard_map/ppermute | solution.py:226
  31.1 7.0 %collective-permute-done.8 = bf16[256,512]{1,0:T(8,128)(2,1)S(1)} collective-permute-done((bf16[256,512]{1,0:T(8,128)(2,1)}, bf16[256,512]{1,0:T(8,128)(2,1)S(1)}, u32[]{:S(2)}, u32[]{:S(2)}) %collective-permute-start.8) | collective-permute-done | bytes 262176 | tf_op jit(solution)/shard_map/ppermute | solution.py:226
  38.7 0.8 collective-permute-start.9
  39.6 3.6 %collective-permute-start.5 = (bf16[3,256,512]{2,1,0:T(8,128)(2,1)S(1)}, bf16[3,256,512]{2,1,0:T(8,128)(2,1)}, u32[]{:S(2)}, u32[]{:S(2)}) collective-permute-start(bf16[3,256,512]{2,1,0:T(8,128)(2,1)S(1)} %pad_maximum_fusion.refs_5_), channel_id=1, source_target_pairs={{0,16},{16,0},{1,17},{17,1},{2,18},{18,2},{3,19},{19,3},{4,20},{20... | collective-permute-start | bytes 2359304 | tf_op jit(solution)/shard_map/ppermute | solution.py:274
  43.2 1.6 %broadcast_in_dim.19 = bf16[4,512,512]{2,1,0:T(8,128)(2,1)} broadcast(bf16[512,512]{1,0:T(8,128)(2,1)S(1)} %copy-done.6), dimensions={1,2} | broadcast | bytes 2621440 | tf_op jit(solution)/shard_map/broadcast_in_dim | solution.py:283
  44.9 4.2 %all-to-all-start.1 = ((bf16[4,512,512]{2,1,0:T(8,128)(2,1)}), bf16[4,512,512]{2,1,0:T(8,128)(2,1)S(1)}, u32[]{:S(2)}, u32[]{:S(2)}) async-start(bf16[4,512,512]{2,1,0:T(8,128)(2,1)} %broadcast_in_dim.19), calls=%async_computation.1 | async-start | bytes 4194304 | tf_op jit(solution)/shard_map/all_to_all | solution.py:283
  49.0 1.2 pad_maximum_fusion.1.refs_7_
  50.3 2.3 %collective-permute-start.12 = (bf16[3,256,512]{2,1,0:T(8,128)(2,1)S(1)}, bf16[3,256,512]{2,1,0:T(8,128)(2,1)S(1)}, u32[]{:S(2)}, u32[]{:S(2)}) collective-permute-start(bf16[3,256,512]{2,1,0:T(8,128)(2,1)S(1)} %pad_maximum_fusion.1.refs_7_), channel_id=1, source_target_pairs={{0,16},{16,0},{1,17},{17,1},{2,18},{18,2},{3,19},{19,3},{4,20},{20... | collective-permute-start | bytes 2359304 | tf_op jit(solution)/shard_map/ppermute | solution.py:274
  53.2 1.2 collective-permute-start.11
  55.1 1.8 %collective-permute-start.20 = (bf16[512,512]{1,0:T(8,128)(2,1)S(1)}, bf16[512,512]{1,0:T(8,128)(2,1)}, u32[]{:S(2)}, u32[]{:S(2)}) collective-permute-start(bf16[512,512]{1,0:T(8,128)(2,1)S(1)} %multiply_convert_fusion.refs_1_.weighted), channel_id=1, source_target_pairs={{0,8},{4,12},{8,0},{12,4},{1,9},{5,13},{9,1},{13,5},{2,10},{6,14},... | collective-permute-start | bytes 1572872 | tf_op jit(solution)/shard_map/ppermute | solution.py:226
  56.9 1.3 fusion.8
  58.7 1.5 %fusion = f32[32,512]{1,0:T(8,128)S(1)} fusion(bf16[16,32,512]{2,1,0:T(8,128)(2,1)S(1)} %bitcast.33, bf16[512,512]{1,0:T(8,128)(2,1)} %acts.1, f32[16,512]{1,0:T(8,128)S(1)} %get-tuple-element.93), kind=kOutput, calls=%fused_computation.4 | convolution fusion | flops 268943360 | bytes 1146880 | tf_op jit(solution)/shard_map/dot_general | solution.py:307
  60.3 1.3 collective-permute-start.16
  61.5 1.5 %collective-permute-start.15 = (f32[64,512]{1,0:T(8,128)S(1)}, f32[64,512]{1,0:T(8,128)S(1)}, u32[]{:S(2)}, u32[]{:S(2)}) collective-permute-start(f32[64,512]{1,0:T(8,128)S(1)} %pad_maximum_fusion.2), channel_id=1, source_target_pairs={{0,12},{4,0},{8,4},{12,8},{1,13},{5,1},{9,5},{13,9},{2,14},{6,2},{... | collective-permute-start | bytes 393224 | tf_op jit(solution)/shard_map/ppermute | solution.py:226
  63.3 9.2 %collective-permute-done.16 = f32[64,512]{1,0:T(8,128)S(1)} collective-permute-done((f32[64,512]{1,0:T(8,128)S(1)}, f32[64,512]{1,0:T(8,128)S(1)}, u32[]{:S(2)}, u32[]{:S(2)}) %collective-permute-start.16) | collective-permute-done | bytes 131104 | tf_op jit(solution)/shard_map/ppermute | solution.py:226
  72.5 1.8 %collective-permute-done.15 = f32[64,512]{1,0:T(8,128)S(1)} collective-permute-done((f32[64,512]{1,0:T(8,128)S(1)}, f32[64,512]{1,0:T(8,128)S(1)}, u32[]{:S(2)}, u32[]{:S(2)}) %collective-permute-start.15) | collective-permute-done | bytes 131104 | tf_op jit(solution)/shard_map/ppermute | solution.py:226
  74.3 1.7 %collective-permute-done.14 = f32[64,512]{1,0:T(8,128)S(1)} collective-permute-done((f32[64,512]{1,0:T(8,128)S(1)}, f32[64,512]{1,0:T(8,128)S(1)}, u32[]{:S(2)}, u32[]{:S(2)}) %collective-permute-start.14) | collective-permute-done | bytes 131104 | tf_op jit(solution)/shard_map/ppermute | solution.py:226
  76.1 3.0 %collective-permute-start.19 = (f32[64,512]{1,0:T(8,128)S(1)}, f32[64,512]{1,0:T(8,128)S(1)}, u32[]{:S(2)}, u32[]{:S(2)}) collective-permute-start(f32[64,512]{1,0:T(8,128)S(1)} %add_add_fusion.t0), channel_id=1, source_target_pairs={{0,2},{1,3},{2,0},{3,1},{4,6},{5,7},{6,4},{7,5},{8,10},{9,11},{10,... | collective-permute-start | bytes 393224 | tf_op jit(solution)/shard_map/ppermute | solution.py:226
  79.1 0.8 collective-permute-start.18
  81.2 1.0 collective-permute-done.19.t3
  82.3 3.3 %collective-permute-done.18.t2 = f32[64,512]{1,0:T(8,128)S(1)} collective-permute-done((f32[64,512]{1,0:T(8,128)S(1)}, f32[64,512]{1,0:T(8,128)S(1)}, u32[]{:S(2)}, u32[]{:S(2)}) %collective-permute-start.18) | collective-permute-done | bytes 131104 | tf_op jit(solution)/shard_map/ppermute | solution.py:226
  86.3 1.3 copy-done
  87.6 15.4 %shard_map.180 = (bf16[512,512]{1,0:T(8,128)(2,1)}, bf16[512,512]{1,0:T(8,128)(2,1)}, bf16[512,512]{1,0:T(8,128)(2,1)}, bf16[512,512]{1,0:T(8,128)(2,1)}, bf16[5...) custom-call(s32[4]{0:T(128)} %pad_add_fusion.where, ...), custom_call_target="tpu_custom_call" | custom-call | flops 1 | bytes 1 | tf_op jit(solution)/shard_map/pallas_call | solution.py:173
  103.0 1.6 %collective-permute-start.21 = (bf16[512,512]{1,0:T(8,128)(2,1)}, bf16[512,512]{1,0:T(8,128)(2,1)S(1)}, u32[]{:S(2)}, u32[]{:S(2)}) collective-permute-start(bf16[512,512]{1,0:T(8,128)(2,1)} %get-tuple-element.66), channel_id=1, source_target_pairs={{0,12},{4,0},{8,4},{12,8},{1,13},{5,1},{9,5},{13,9},{2,14},{6,2},{... | collective-permute-start | bytes 1572872 | tf_op jit(solution)/shard_map/ppermute | solution.py:226
  104.9 1.8 %collective-permute-start.24 = (bf16[512,512]{1,0:T(8,128)(2,1)}, bf16[512,512]{1,0:T(8,128)(2,1)S(1)}, u32[]{:S(2)}, u32[]{:S(2)}) collective-permute-start(bf16[512,512]{1,0:T(8,128)(2,1)} %get-tuple-element.70), channel_id=1, source_target_pairs={{0,1},{1,2},{2,3},{3,0},{4,5},{5,6},{6,7},{7,4},{8,9},{9,10},{10,1... | collective-permute-start | bytes 1572872 | tf_op jit(solution)/shard_map/ppermute | solution.py:226
  106.7 1.3 collective-permute-start.25
  108.0 1.2 collective-permute-start.26
  109.2 3.3 %shard_map.181 = (bf16[16,2,32,512]{3,2,1,0:T(8,128)(2,1)}, bf16[512,512]{1,0:T(8,128)(2,1)}, bf16[512,512]{1,0:T(8,128)(2,1)}) custom-call(f32[64,512]{1,0:T(8,128)} %copy-done.12, f32[64,512]{1,0:T(8,128)} %collective-permute-done.17.t1, f32[64,512]{1,0:T(8,128)} %copy-done.16, f32[64,512]{1,0:T(8,128)} %copy-done.15, ...), custom_call_target="tpu_custom_call" | custom-call | flops 1 | bytes 1 | tf_op jit(solution)/shard_map/pallas_call | solution.py:215
  112.5 5.3 %all-to-all-start.2 = ((bf16[8,2,2,32,512]{4,3,2,1,0:T(8,128)(2,1)}), bf16[8,2,2,32,512]{4,3,2,1,0:T(8,128)(2,1)S(1)}, u32[]{:S(2)}, u32[]{:S(2)}) async-start(bf16[8,2,2,32,512]{4,3,2,1,0:T(8,128)(2,1)} %bitcast.38), calls=%async_computation.2 | async-start | bytes 2097152 | tf_op jit(solution)/shard_map/all_to_all | solution.py:327
  117.8 1.7 %convolution_multiply_fusion.1 = f32[512,512]{1,0:T(8,128)S(1)} fusion(bf16[512,512]{1,0:T(8,128)(2,1)} %get-tuple-element.62, bf16[512,512]{1,0:T(8,128)(2,1)} %bitcast.36), kind=kOutput, calls=%fused_computation.1 | convolution fusion | flops 268697600 | bytes 2097152 | tf_op jit(solution)/shard_map/dot_general | solution.py:341
  119.5 1.7 %convolution_multiply_fusion = f32[512,512]{1,0:T(8,128)S(1)} fusion(bf16[512,512]{1,0:T(8,128)(2,1)} %get-tuple-element.64, bf16[512,512]{1,0:T(8,128)(2,1)} %bitcast.34), kind=kOutput, calls=%fused_computation | convolution fusion | flops 268697600 | bytes 2097152 | tf_op jit(solution)/shard_map/dot_general | solution.py:344
  121.2 1.4 collective-permute-start.23
  122.6 1.6 %convert_add_fusion = (f32[512,512]{1,0:T(8,128)S(1)}, f32[512,512]{1,0:T(8,128)S(1)}) fusion(f32[512,512]{1,0:T(8,128)S(1)} %convolution_multiply_fusion, bf16[512,512]{1,0:T(8,128)(2,1)} %get-tuple-element.63, f32[512,512]{1,0:T(8,128)S(1)} %convolution_multiply_fusion.1, bf16[512,512]{1,0:T(8,128)(2,1)} %get-tuple-element.57), kind=kLoop, calls=%fused_computation.8 | loop fusion | flops 1048576 | bytes 5242880 | tf_op jit(solution)/shard_map/add | solution.py:344
  124.1 7.8 %collective-permute-done.26 = bf16[512,512]{1,0:T(8,128)(2,1)} collective-permute-done((bf16[512,512]{1,0:T(8,128)(2,1)}, bf16[512,512]{1,0:T(8,128)(2,1)}, u32[]{:S(2)}, u32[]{:S(2)}) %collective-permute-start.26) | collective-permute-done | bytes 524320 | tf_op jit(solution)/shard_map/ppermute | solution.py:226
  132.0 2.1 %add_convert_fusion = bf16[512,512]{1,0:T(8,128)(2,1)} fusion(bf16[512,512]{1,0:T(8,128)(2,1)} %collective-permute-done.26, bf16[512,512]{1,0:T(8,128)(2,1)S(1)} %collective-permute-done.25, f32[512,512]{1,0:T(8,128)S(1)} %get-tuple-element.69, bf16[512,512]{1,0:T(8,128)(2,1)S(1)} %collective-permute-done.24), kind=kLoop, calls=%fused_computation.6 | loop fusion | flops 1835008 | bytes 3145728 | tf_op jit(solution)/shard_map/convert_element_type | solution.py:352
  134.1 2.4 %collective-permute-done.23 = bf16[512,512]{1,0:T(8,128)(2,1)S(1)} collective-permute-done((bf16[512,512]{1,0:T(8,128)(2,1)}, bf16[512,512]{1,0:T(8,128)(2,1)S(1)}, u32[]{:S(2)}, u32[]{:S(2)}) %collective-permute-start.23) | collective-permute-done | bytes 524320 | tf_op jit(solution)/shard_map/ppermute | solution.py:226
  136.6 1.1 add_convert_fusion.1
  137.6 1.0 copy-done.2
  138.6 5.9 %shard_map.182 = (bf16[16,32,512]{2,1,0:T(8,128)(2,1)}, bf16[16,32,512]{2,1,0:T(8,128)(2,1)}, f32[16,32,512]{2,1,0:T(8,128)}, f32[16,32,512]{2,1,0:T(8,128)}, f3...) custom-call(s32[16]{0:T(128)} %get-tuple-element.73.pos, bf16[16,2,32,512]{3,2,1,0:T(8,128)(2,1)} %bitcast.32, ...), custom_call_target="tpu_custom_call" | custom-call | flops 1 | bytes 1 | tf_op jit(solution)/shard_map/pallas_call | solution.py:93
  (76 shorter events, 7.9 us)
Async XLA Ops:
  0.6 30.3 %copy-start.13 = (bf16[512,512]{1,0:T(8,128)(2,1)S(1)}, bf16[512,512]{1,0:T(8,128)(2,1)}, u32[]{:S(2)}) copy-start(bf16[512,512]{1,0:T(8,128)(2,1)} %param.13) | copy-start | bytes 1572868
  0.6 42.5 %copy-start.6 = (bf16[512,512]{1,0:T(8,128)(2,1)S(1)}, bf16[512,512]{1,0:T(8,128)(2,1)}, u32[]{:S(2)}) copy-start(bf16[512,512]{1,0:T(8,128)(2,1)} %acts.1) | copy-start | bytes 1572868
  2.9 25.2 %collective-permute-start.4 = (bf16[256,512]{1,0:T(8,128)(2,1)S(1)}, bf16[256,512]{1,0:T(8,128)(2,1)}, u32[]{:S(2)}, u32[]{:S(2)}) collective-permute-start(bf16[256,512]{1,0:T(8,128)(2,1)S(1)} %get-tuple-element.85), channel_id=1, source_target_pairs={{0,12},{4,0},{8,4},{12,8},{1,13},{5,1},{9,5},{13,9},{2,14},{6,2},{... | collective-permute-start | bytes 786440 | tf_op jit(solution)/shard_map/ppermute | solution.py:226
  7.5 20.6 %collective-permute-start.3 = (bf16[256,512]{1,0:T(8,128)(2,1)S(1)}, bf16[256,512]{1,0:T(8,128)(2,1)}, u32[]{:S(2)}, u32[]{:S(2)}) collective-permute-start(bf16[256,512]{1,0:T(8,128)(2,1)S(1)} %get-tuple-element.86), channel_id=1, source_target_pairs={{0,4},{4,8},{8,12},{12,0},{1,5},{5,9},{9,13},{13,1},{2,6},{6,10},{... | collective-permute-start | bytes 786440 | tf_op jit(solution)/shard_map/ppermute | solution.py:226
  7.5 16.9 %collective-permute-start.2 = (bf16[256,512]{1,0:T(8,128)(2,1)S(1)}, bf16[256,512]{1,0:T(8,128)(2,1)}, u32[]{:S(2)}, u32[]{:S(2)}) collective-permute-start(bf16[256,512]{1,0:T(8,128)(2,1)S(1)} %get-tuple-element.87), channel_id=1, source_target_pairs={{0,12},{4,0},{8,4},{12,8},{1,13},{5,1},{9,5},{13,9},{2,14},{6,2},{... | collective-permute-start | bytes 786440 | tf_op jit(solution)/shard_map/ppermute | solution.py:226
  10.2 14.3 %collective-permute-start.1 = (bf16[256,512]{1,0:T(8,128)(2,1)S(1)}, bf16[256,512]{1,0:T(8,128)(2,1)}, u32[]{:S(2)}, u32[]{:S(2)}) collective-permute-start(bf16[256,512]{1,0:T(8,128)(2,1)S(1)} %get-tuple-element.88), channel_id=1, source_target_pairs={{0,8},{4,12},{8,0},{12,4},{1,9},{5,13},{9,1},{13,5},{2,10},{6,14},... | collective-permute-start | bytes 786440 | tf_op jit(solution)/shard_map/ppermute | solution.py:226
  10.2 16.7 %collective-permute-start = (bf16[256,512]{1,0:T(8,128)(2,1)S(1)}, bf16[256,512]{1,0:T(8,128)(2,1)}, u32[]{:S(2)}, u32[]{:S(2)}) collective-permute-start(bf16[256,512]{1,0:T(8,128)(2,1)S(1)} %get-tuple-element.89), channel_id=1, source_target_pairs={{0,4},{4,8},{8,12},{12,0},{1,5},{5,9},{9,13},{13,1},{2,6},{6,10},{... | collective-permute-start | bytes 786440 | tf_op jit(solution)/shard_map/ppermute | solution.py:226
  15.1 28.0 %all-to-all-start = ((bf16[8,2,2,32,512]{4,3,2,1,0:T(8,128)(2,1)}), bf16[8,2,2,32,512]{4,3,2,1,0:T(8,128)(2,1)S(1)}, u32[]{:S(2)}, u32[]{:S(2)}) async-start(bf16[8,2,2,32,512]{4,3,2,1,0:T(8,128)(2,1)} %bitcast.37), calls=%async_computation | async-start | bytes 2097152 | tf_op jit(solution)/shard_map/all_to_all | solution.py:280
  28.1 58.1 %copy-start.4 = (bf16[3,256,512]{2,1,0:T(8,128)(2,1)}, bf16[3,256,512]{2,1,0:T(8,128)(2,1)S(1)}, u32[]{:S(2)}) copy-start(bf16[3,256,512]{2,1,0:T(8,128)(2,1)S(1)} %pad_maximum_fusion.refs_5_) | copy-start | bytes 2359300
  28.2 24.4 %collective-permute-start.7 = (bf16[3,256,512]{2,1,0:T(8,128)(2,1)S(1)}, bf16[3,256,512]{2,1,0:T(8,128)(2,1)}, u32[]{:S(2)}, u32[]{:S(2)}) collective-permute-start(bf16[3,256,512]{2,1,0:T(8,128)(2,1)S(1)} %pad_maximum_fusion.refs_5_), channel_id=1, source_target_pairs={{0,96},{32,0},{64,32},{96,64},{1,97},{33,1},{65,33},{97,65},{2,98}... | collective-permute-start | bytes 2359304 | tf_op jit(solution)/shard_map/ppermute | solution.py:226
  30.7 22.5 %collective-permute-start.6 = (bf16[3,256,512]{2,1,0:T(8,128)(2,1)S(1)}, bf16[3,256,512]{2,1,0:T(8,128)(2,1)}, u32[]{:S(2)}, u32[]{:S(2)}) collective-permute-start(bf16[3,256,512]{2,1,0:T(8,128)(2,1)S(1)} %pad_maximum_fusion.refs_5_), channel_id=1, source_target_pairs={{0,32},{32,64},{64,96},{96,0},{1,33},{33,65},{65,97},{97,1},{2,34}... | collective-permute-start | bytes 2359304 | tf_op jit(solution)/shard_map/ppermute | solution.py:226
  30.7 7.4 %collective-permute-start.8 = (bf16[256,512]{1,0:T(8,128)(2,1)}, bf16[256,512]{1,0:T(8,128)(2,1)S(1)}, u32[]{:S(2)}, u32[]{:S(2)}) collective-permute-start(bf16[256,512]{1,0:T(8,128)(2,1)} %get-tuple-element.49), channel_id=1, source_target_pairs={{0,8},{4,12},{8,0},{12,4},{1,9},{5,13},{9,1},{13,5},{2,10},{6,14},... | collective-permute-start | bytes 786440 | tf_op jit(solution)/shard_map/ppermute | solution.py:226
  31.1 55.2 %copy-start.1 = (bf16[512,512]{1,0:T(8,128)(2,1)}, bf16[512,512]{1,0:T(8,128)(2,1)S(1)}, u32[]{:S(2)}) copy-start(bf16[512,512]{1,0:T(8,128)(2,1)S(1)} %multiply_convert_fusion.refs_1_.weighted) | copy-start | bytes 1572868
  38.1 1.5 %copy-start.14 = (bf16[256,512]{1,0:T(8,128)(2,1)}, bf16[256,512]{1,0:T(8,128)(2,1)S(1)}, u32[]{:S(2)}) copy-start(bf16[256,512]{1,0:T(8,128)(2,1)S(1)} %collective-permute-done.8) | copy-start | bytes 786436
  38.1 12.2 %collective-permute-start.10 = (bf16[512,512]{1,0:T(8,128)(2,1)S(1)}, bf16[512,512]{1,0:T(8,128)(2,1)}, u32[]{:S(2)}, u32[]{:S(2)}) collective-permute-start(bf16[512,512]{1,0:T(8,128)(2,1)S(1)} %multiply_convert_fusion.refs_1_.weighted), channel_id=1, source_target_pairs={{0,12},{4,0},{8,4},{12,8},{1,13},{5,1},{9,5},{13,9},{2,14},{6,2},{... | collective-permute-start | bytes 1572872 | tf_op jit(solution)/shard_map/ppermute | solution.py:226
  38.7 13.8 %collective-permute-start.9 = (bf16[512,512]{1,0:T(8,128)(2,1)S(1)}, bf16[512,512]{1,0:T(8,128)(2,1)}, u32[]{:S(2)}, u32[]{:S(2)}) collective-permute-start(bf16[512,512]{1,0:T(8,128)(2,1)S(1)} %multiply_convert_fusion.refs_1_.weighted), channel_id=1, source_target_pairs={{0,4},{4,8},{8,12},{12,0},{1,5},{5,9},{9,13},{13,1},{2,6},{6,10},{... | collective-permute-start | bytes 1572872 | tf_op jit(solution)/shard_map/ppermute | solution.py:226
  39.6 20.6 %collective-permute-start.5 = (bf16[3,256,512]{2,1,0:T(8,128)(2,1)S(1)}, bf16[3,256,512]{2,1,0:T(8,128)(2,1)}, u32[]{:S(2)}, u32[]{:S(2)}) collective-permute-start(bf16[3,256,512]{2,1,0:T(8,128)(2,1)S(1)} %pad_maximum_fusion.refs_5_), channel_id=1, source_target_pairs={{0,16},{16,0},{1,17},{17,1},{2,18},{18,2},{3,19},{19,3},{4,20},{20... | collective-permute-start | bytes 2359304 | tf_op jit(solution)/shard_map/ppermute | solution.py:274
  43.2 1.7 %copy-start.3 = (bf16[8,2,2,32,512]{4,3,2,1,0:T(8,128)(2,1)}, bf16[8,2,2,32,512]{4,3,2,1,0:T(8,128)(2,1)S(1)}, u32[]{:S(2)}) copy-start(bf16[8,2,2,32,512]{4,3,2,1,0:T(8,128)(2,1)S(1)} %all-to-all-done) | copy-start | bytes 3145732
  44.9 41.4 %all-to-all-start.1 = ((bf16[4,512,512]{2,1,0:T(8,128)(2,1)}), bf16[4,512,512]{2,1,0:T(8,128)(2,1)S(1)}, u32[]{:S(2)}, u32[]{:S(2)}) async-start(bf16[4,512,512]{2,1,0:T(8,128)(2,1)} %broadcast_in_dim.19), calls=%async_computation.1 | async-start | bytes 4194304 | tf_op jit(solution)/shard_map/all_to_all | solution.py:283
  50.2 35.3 %copy-start.5 = (bf16[3,256,512]{2,1,0:T(8,128)(2,1)}, bf16[3,256,512]{2,1,0:T(8,128)(2,1)S(1)}, u32[]{:S(2)}) copy-start(bf16[3,256,512]{2,1,0:T(8,128)(2,1)S(1)} %pad_maximum_fusion.1.refs_7_) | copy-start | bytes 2359300
  50.3 10.0 %collective-permute-start.12 = (bf16[3,256,512]{2,1,0:T(8,128)(2,1)S(1)}, bf16[3,256,512]{2,1,0:T(8,128)(2,1)S(1)}, u32[]{:S(2)}, u32[]{:S(2)}) collective-permute-start(bf16[3,256,512]{2,1,0:T(8,128)(2,1)S(1)} %pad_maximum_fusion.1.refs_7_), channel_id=1, source_target_pairs={{0,16},{16,0},{1,17},{17,1},{2,18},{18,2},{3,19},{19,3},{4,20},{20... | collective-permute-start | bytes 2359304 | tf_op jit(solution)/shard_map/ppermute | solution.py:274
  53.2 7.0 %collective-permute-start.11 = (bf16[3,256,512]{2,1,0:T(8,128)(2,1)}, bf16[3,256,512]{2,1,0:T(8,128)(2,1)S(1)}, u32[]{:S(2)}, u32[]{:S(2)}) collective-permute-start(bf16[3,256,512]{2,1,0:T(8,128)(2,1)} %collective-permute-done.6.refs_6_), channel_id=1, source_target_pairs={{0,16},{16,0},{1,17},{17,1},{2,18},{18,2},{3,19},{19,3},{4,20},{20... | collective-permute-start | bytes 2359304 | tf_op jit(solution)/shard_map/ppermute | solution.py:303
  54.4 5.9 %collective-permute-start.13 = (bf16[3,256,512]{2,1,0:T(8,128)(2,1)}, bf16[3,256,512]{2,1,0:T(8,128)(2,1)S(1)}, u32[]{:S(2)}, u32[]{:S(2)}) collective-permute-start(bf16[3,256,512]{2,1,0:T(8,128)(2,1)} %collective-permute-done.7.refs_8_), channel_id=1, source_target_pairs={{0,16},{16,0},{1,17},{17,1},{2,18},{18,2},{3,19},{19,3},{4,20},{20... | collective-permute-start | bytes 2359304 | tf_op jit(solution)/shard_map/ppermute | solution.py:303
  55.1 31.1 %collective-permute-start.20 = (bf16[512,512]{1,0:T(8,128)(2,1)S(1)}, bf16[512,512]{1,0:T(8,128)(2,1)}, u32[]{:S(2)}, u32[]{:S(2)}) collective-permute-start(bf16[512,512]{1,0:T(8,128)(2,1)S(1)} %multiply_convert_fusion.refs_1_.weighted), channel_id=1, source_target_pairs={{0,8},{4,12},{8,0},{12,4},{1,9},{5,13},{9,1},{13,5},{2,10},{6,14},... | collective-permute-start | bytes 1572872 | tf_op jit(solution)/shard_map/ppermute | solution.py:226
  58.2 27.4 %copy-start.7 = (bf16[8,2,1,32,512]{4,3,2,1,0:T(8,128)(2,1)}, bf16[8,2,1,32,512]{4,3,2,1,0:T(8,128)(2,1)S(1)}, u32[]{:S(2)}) copy-start(bf16[8,2,1,32,512]{4,3,2,1,0:T(8,128)(2,1)S(1)} %get-tuple-element.90) | copy-start | bytes 1572868
  58.2 27.4 %copy-start.8 = (bf16[8,2,1,32,512]{4,3,2,1,0:T(8,128)(2,1)}, bf16[8,2,1,32,512]{4,3,2,1,0:T(8,128)(2,1)S(1)}, u32[]{:S(2)}) copy-start(bf16[8,2,1,32,512]{4,3,2,1,0:T(8,128)(2,1)S(1)} %get-tuple-element.91) | copy-start | bytes 1572868
  60.2 25.3 %copy-start.9 = (bf16[3,256,512]{2,1,0:T(8,128)(2,1)}, bf16[3,256,512]{2,1,0:T(8,128)(2,1)S(1)}, u32[]{:S(2)}) copy-start(bf16[3,256,512]{2,1,0:T(8,128)(2,1)S(1)} %collective-permute-done.12.refs_11_) | copy-start | bytes 2359300
  60.2 25.3 %copy-start.10 = (bf16[3,256,512]{2,1,0:T(8,128)(2,1)}, bf16[3,256,512]{2,1,0:T(8,128)(2,1)S(1)}, u32[]{:S(2)}) copy-start(bf16[3,256,512]{2,1,0:T(8,128)(2,1)S(1)} %collective-permute-done.11.refs_10_) | copy-start | bytes 2359300
  60.3 25.3 %copy-start.11 = (bf16[3,256,512]{2,1,0:T(8,128)(2,1)}, bf16[3,256,512]{2,1,0:T(8,128)(2,1)S(1)}, u32[]{:S(2)}) copy-start(bf16[3,256,512]{2,1,0:T(8,128)(2,1)S(1)} %collective-permute-done.13.refs_12_) | copy-start | bytes 2359300
  60.3 12.2 %collective-permute-start.16 = (f32[64,512]{1,0:T(8,128)S(1)}, f32[64,512]{1,0:T(8,128)S(1)}, u32[]{:S(2)}, u32[]{:S(2)}) collective-permute-start(f32[64,512]{1,0:T(8,128)S(1)} %pad_maximum_fusion.2), channel_id=1, source_target_pairs={{0,8},{4,12},{8,0},{12,4},{1,9},{5,13},{9,1},{13,5},{2,10},{6,14},... | collective-permute-start | bytes 393224 | tf_op jit(solution)/shard_map/ppermute | solution.py:226
  61.5 12.8 %collective-permute-start.15 = (f32[64,512]{1,0:T(8,128)S(1)}, f32[64,512]{1,0:T(8,128)S(1)}, u32[]{:S(2)}, u32[]{:S(2)}) collective-permute-start(f32[64,512]{1,0:T(8,128)S(1)} %pad_maximum_fusion.2), channel_id=1, source_target_pairs={{0,12},{4,0},{8,4},{12,8},{1,13},{5,1},{9,5},{13,9},{2,14},{6,2},{... | collective-permute-start | bytes 393224 | tf_op jit(solution)/shard_map/ppermute | solution.py:226
  63.0 13.0 %collective-permute-start.14 = (f32[64,512]{1,0:T(8,128)S(1)}, f32[64,512]{1,0:T(8,128)S(1)}, u32[]{:S(2)}, u32[]{:S(2)}) collective-permute-start(f32[64,512]{1,0:T(8,128)S(1)} %pad_maximum_fusion.2), channel_id=1, source_target_pairs={{0,4},{4,8},{8,12},{12,0},{1,5},{5,9},{9,13},{13,1},{2,6},{6,10},{... | collective-permute-start | bytes 393224 | tf_op jit(solution)/shard_map/ppermute | solution.py:226
  76.1 33.1 %copy-start.12 = (f32[64,512]{1,0:T(8,128)}, f32[64,512]{1,0:T(8,128)S(1)}, u32[]{:S(2)}) copy-start(f32[64,512]{1,0:T(8,128)S(1)} %add_add_fusion.t0) | copy-start | bytes 393220
  76.1 6.2 %collective-permute-start.19 = (f32[64,512]{1,0:T(8,128)S(1)}, f32[64,512]{1,0:T(8,128)S(1)}, u32[]{:S(2)}, u32[]{:S(2)}) collective-permute-start(f32[64,512]{1,0:T(8,128)S(1)} %add_add_fusion.t0), channel_id=1, source_target_pairs={{0,2},{1,3},{2,0},{3,1},{4,6},{5,7},{6,4},{7,5},{8,10},{9,11},{10,... | collective-permute-start | bytes 393224 | tf_op jit(solution)/shard_map/ppermute | solution.py:226
  79.1 6.4 %collective-permute-start.18 = (f32[64,512]{1,0:T(8,128)S(1)}, f32[64,512]{1,0:T(8,128)S(1)}, u32[]{:S(2)}, u32[]{:S(2)}) collective-permute-start(f32[64,512]{1,0:T(8,128)S(1)} %add_add_fusion.t0), channel_id=1, source_target_pairs={{0,3},{1,0},{2,1},{3,2},{4,7},{5,4},{6,5},{7,6},{8,11},{9,8},{10,9... | collective-permute-start | bytes 393224 | tf_op jit(solution)/shard_map/ppermute | solution.py:226
  79.9 6.3 %collective-permute-start.17 = (f32[64,512]{1,0:T(8,128)S(1)}, f32[64,512]{1,0:T(8,128)}, u32[]{:S(2)}, u32[]{:S(2)}) collective-permute-start(f32[64,512]{1,0:T(8,128)S(1)} %add_add_fusion.t0), channel_id=1, source_target_pairs={{0,1},{1,2},{2,3},{3,0},{4,5},{5,6},{6,7},{7,4},{8,9},{9,10},{10,1... | collective-permute-start | bytes 393224 | tf_op jit(solution)/shard_map/ppermute | solution.py:226
  82.3 3.3 %copy-start.15 = (f32[64,512]{1,0:T(8,128)}, f32[64,512]{1,0:T(8,128)S(1)}, u32[]{:S(2)}) copy-start(f32[64,512]{1,0:T(8,128)S(1)} %collective-permute-done.19.t3) | copy-start | bytes 393220
  85.6 0.6 copy-start.16
  86.2 1.4 copy-start
  103.0 31.1 %collective-permute-start.21 = (bf16[512,512]{1,0:T(8,128)(2,1)}, bf16[512,512]{1,0:T(8,128)(2,1)S(1)}, u32[]{:S(2)}, u32[]{:S(2)}) collective-permute-start(bf16[512,512]{1,0:T(8,128)(2,1)} %get-tuple-element.66), channel_id=1, source_target_pairs={{0,12},{4,0},{8,4},{12,8},{1,13},{5,1},{9,5},{13,9},{2,14},{6,2},{... | collective-permute-start | bytes 1572872 | tf_op jit(solution)/shard_map/ppermute | solution.py:226
  104.6 29.5 %collective-permute-start.22 = (bf16[512,512]{1,0:T(8,128)(2,1)}, bf16[512,512]{1,0:T(8,128)(2,1)S(1)}, u32[]{:S(2)}, u32[]{:S(2)}) collective-permute-start(bf16[512,512]{1,0:T(8,128)(2,1)} %get-tuple-element.67), channel_id=1, source_target_pairs={{0,4},{4,8},{8,12},{12,0},{1,5},{5,9},{9,13},{13,1},{2,6},{6,10},{... | collective-permute-start | bytes 1572872 | tf_op jit(solution)/shard_map/ppermute | solution.py:226
  104.9 16.3 %collective-permute-start.24 = (bf16[512,512]{1,0:T(8,128)(2,1)}, bf16[512,512]{1,0:T(8,128)(2,1)S(1)}, u32[]{:S(2)}, u32[]{:S(2)}) collective-permute-start(bf16[512,512]{1,0:T(8,128)(2,1)} %get-tuple-element.70), channel_id=1, source_target_pairs={{0,1},{1,2},{2,3},{3,0},{4,5},{5,6},{6,7},{7,4},{8,9},{9,10},{10,1... | collective-permute-start | bytes 1572872 | tf_op jit(solution)/shard_map/ppermute | solution.py:226
  106.7 17.4 %collective-permute-start.25 = (bf16[512,512]{1,0:T(8,128)(2,1)}, bf16[512,512]{1,0:T(8,128)(2,1)S(1)}, u32[]{:S(2)}, u32[]{:S(2)}) collective-permute-start(bf16[512,512]{1,0:T(8,128)(2,1)} %get-tuple-element.71), channel_id=1, source_target_pairs={{0,3},{1,0},{2,1},{3,2},{4,7},{5,4},{6,5},{7,6},{8,11},{9,8},{10,9... | collective-permute-start | bytes 1572872 | tf_op jit(solution)/shard_map/ppermute | solution.py:226
  108.0 23.9 %collective-permute-start.26 = (bf16[512,512]{1,0:T(8,128)(2,1)}, bf16[512,512]{1,0:T(8,128)(2,1)}, u32[]{:S(2)}, u32[]{:S(2)}) collective-permute-start(bf16[512,512]{1,0:T(8,128)(2,1)} %get-tuple-element.72), channel_id=1, source_target_pairs={{0,2},{1,3},{2,0},{3,1},{4,6},{5,7},{6,4},{7,5},{8,10},{9,11},{10,... | collective-permute-start | bytes 1572872 | tf_op jit(solution)/shard_map/ppermute | solution.py:226
  112.5 25.1 %all-to-all-start.2 = ((bf16[8,2,2,32,512]{4,3,2,1,0:T(8,128)(2,1)}), bf16[8,2,2,32,512]{4,3,2,1,0:T(8,128)(2,1)S(1)}, u32[]{:S(2)}, u32[]{:S(2)}) async-start(bf16[8,2,2,32,512]{4,3,2,1,0:T(8,128)(2,1)} %bitcast.38), calls=%async_computation.2 | async-start | bytes 2097152 | tf_op jit(solution)/shard_map/all_to_all | solution.py:327
  121.2 15.3 %collective-permute-start.23 = (bf16[512,512]{1,0:T(8,128)(2,1)}, bf16[512,512]{1,0:T(8,128)(2,1)S(1)}, u32[]{:S(2)}, u32[]{:S(2)}) collective-permute-start(bf16[512,512]{1,0:T(8,128)(2,1)} %get-tuple-element.68), channel_id=1, source_target_pairs={{0,8},{4,12},{8,0},{12,4},{1,9},{5,13},{9,1},{13,5},{2,10},{6,14},... | collective-permute-start | bytes 1572872 | tf_op jit(solution)/shard_map/ppermute | solution.py:226
  137.6 1.0 copy-start.2

commit v7 on v4

--- a/solution.py
+++ b/solution.py
@@ -70,8 +70,8 @@
 
 
 def adam_kernel(pos, grads, dn, up, m1d, m2d, m1u, m2u, odn, oup, o1d, o2d, o1u, o2u):
-    i0 = pl.program_id(0) * 4
-    for k in range(4):
+    i0 = pl.program_id(0) * 8
+    for k in range(8):
         q = pos[i0 + k]
         for which, (f, m1, m2, of, o1, o2) in enumerate(
             ((dn, m1d, m2d, odn, o1d, o2d), (up, m1u, m2u, oup, o1u, o2u))
@@ -87,7 +87,7 @@
 
 
 def adam(pos, grads, dn, up, m1d, m2d, m1u, m2u):
-    block = pl.BlockSpec((4, RANK, COLS), lambda i, pos: (i, 0, 0))
+    block = pl.BlockSpec((8, RANK, COLS), lambda i, pos: (i, 0, 0))
     half = jax.ShapeDtypeStruct((PROMPTS, RANK, COLS), BF16)
     full = jax.ShapeDtypeStruct((PROMPTS, RANK, COLS), F32)
     return pl.pallas_call(
@@ -95,7 +95,7 @@
         out_shape=(half, half, full, full, full, full),
         grid_spec=pltpu.PrefetchScalarGridSpec(
             num_scalar_prefetch=1,
-            grid=(4,),
+            grid=(2,),
             in_specs=[pl.BlockSpec((PROMPTS, 2, RANK, COLS), lambda i, pos: (0, 0, 0, 0))]
             + [block] * 6,
             out_specs=[block] * 6,
@@ -296,8 +296,11 @@
     advantage = reward - jnp.sum(onehot * mean_reward[:, None], axis=0)
     weighted = (advantage[:, None] * output_gradient.astype(F32)).astype(BF16)
 
+    grads_in = {0: weighted}
     sent, _ = lax.optimization_barrier((weighted, second[2]))
-    grads_in = {0: weighted} | {d: shift(sent, "z", d) for d in (1, 3, 2)}
+    grads_in[1], grads_in[3] = shift(sent, "z", 1), shift(sent, "z", 3)
+    sent, _ = lax.optimization_barrier((weighted, (grads_in[1], grads_in[3])))
+    grads_in[2] = shift(sent, "z", 2)
 
     contract_cols = (((1,), (1,)), ((), ()))
     low_all = lax.dot_general(down, activations, contract_cols, preferred_element_type=F32)
@@ -306,9 +309,8 @@
     back_part = jnp.sum(back_all.reshape(PROMPTS, RANK, ROWS) * onehot[:, None, :], axis=0)
     sums = jnp.concatenate([low_part, back_part])
     sums, _ = lax.optimization_barrier((sums, other[0]))
-    last, _ = lax.optimization_barrier((sums, grads_in))
-    sums = (sums + shift(sums, "z", 1)) + (shift(sums, "z", 3) + shift(last, "z", 2))
-    sums, _ = lax.optimization_barrier((sums, (own[1], own[3], other[2], acts)))
+    sums = sums + sum(shift(sums, "z", i) for i in (1, 3, 2))
+    sums, _ = lax.optimization_barrier((sums, (own[1], own[3], other[0], other[2], grads_in[1], grads_in[3], acts)))
     terms = [sums] + [shift(sums, "y", i) for i in (1, 3, 2)]
     where = jnp.stack([x, c, z, y]).astype(jnp.int32)
     layer_parts, input_parts = partials(

time: 141 us -> 143 us (1.014)
  waiting for transfers between devices: 29 us -> 34.1 us
  local copies, waits for them, and re-layouts: 8.63 us -> 7.17 us
    ppermute x23, waiting for transfers between devices: 26.3 us -> 30.3 us  [shift(): lax.ppermute(value, axis, [(i, (i + by) % size) for i in range(size)])]
    ppermute x23, starting transfers between devices: 28.8 us -> 30.8 us  [shift(): lax.ppermute(value, axis, [(i, (i + by) % size) for i in range(size)])]
    ppermute x4, starting transfers between devices: 4.99 us -> 3.1 us  [local(): other = [lax.ppermute(piece, 'core', [(0, 1), (1, 0)]) for piece in own]]
    unnamed x38 -> x32, local copies, waits for them, and re-layouts: 3.18 us -> 1.77 us
  transfers between devices with their start and end apart: 30 -> 30, of which waited for: 10 -> 8; matrix products, arithmetic and copies ran while one was open for 15% -> 15% of each run, Pallas kernels for 21% -> 20%
where the time goes in v7:
time: 143 us; the launch traced here: 142 us
  starting transfers between devices  51 us (36%)
  waiting for transfers between devices  34.1 us (24%)
  Pallas kernels  29 us (20%)
  other arithmetic  14.2 us (10%)
  local copies, waits for them, and re-layouts  7.17 us (5%)
  matrix products  5.3 us (4%)
    ppermute x23, starting transfers between devices, shift(): lax.ppermute(value, axis, [(i, (i + by) % size) for i in range(size)])  30.8 us
    ppermute x23, waiting for transfers between devices, shift(): lax.ppermute(value, axis, [(i, (i + by) % size) for i in range(size)])  30.3 us
    pallas_call x1, Pallas kernels, partials(): pl.pallas_call(partial_kernel, out_shape=[block] * 8, grid_spec=pltpu.Pre...  15.5 us
    all_to_all x1, starting transfers between devices, local(): lax.all_to_all(grads, ('x', 'core'), 0, 0).reshape(PROMPTS, 2, RANK, COLS)  7.04 us
    pallas_call x1, Pallas kernels, adam(): pl.pallas_call(adam_kernel, out_shape=(half, half, full, full, full, full...  5.92 us
    all_to_all x1, starting transfers between devices, local(): lax.all_to_all(sent.reshape(8, 2, 2, RANK, COLS), ('x', 'core'), 0, 0)  5.83 us
    pallas_call x1, Pallas kernels, pick(): pl.pallas_call(pick_kernel, out_shape=(jax.ShapeDtypeStruct((PROMPTS, 2,...  4.35 us
    all_to_all x1, starting transfers between devices, local(): lax.all_to_all(jnp.broadcast_to(act[None], (4, ROWS, COLS)), 'y', 0, 0)  4.18 us
  transfers between devices with their start and end apart: 30, of which 8 were waited for; matrix products, arithmetic and copies ran while one was open for 15% of the time, Pallas kernels for 20%

profile of v7, /device:TPU:1, one launch (start us, length us, event | category | flops | bytes accessed | tf_op | source)
XLA Modules:
  0.0 141.8 jit_solution(8142082564889108203)
XLA Ops:
  0.7 2.2 %constant_dynamic-slice_fusion = (bf16[256,512]{1,0:T(8,128)(2,1)}, bf16[256,512]{1,0:T(8,128)(2,1)S(1)}, bf16[256,512]{1,0:T(8,128)(2,1)S(1)}, bf16[256,512]{1,...) fusion(bf16[8192,512]{1,0:T(8,128)(2,1)} %refs_13_.1, s32[]{:T(128)S(6)} %select_n.38, ...), kind=kLoop, calls=%fused_computation.29 | loop fusion | bytes 3145752 | tf_op jit(solution)/shard_map/dynamic_slice | solution.py:255
  2.9 4.6 %collective-permute-start.2 = (bf16[256,512]{1,0:T(8,128)(2,1)S(1)}, bf16[256,512]{1,0:T(8,128)(2,1)}, u32[]{:S(2)}, u32[]{:S(2)}) collective-permute-start(bf16[256,512]{1,0:T(8,128)(2,1)S(1)} %get-tuple-element.85), channel_id=1, source_target_pairs={{0,12},{4,0},{8,4},{12,8},{1,13},{5,1},{9,5},{13,9},{2,14},{6,2},{... | collective-permute-start | bytes 786440 | tf_op jit(solution)/shard_map/ppermute | solution.py:226
  8.2 4.3 %shard_map.179 = (bf16[16,2,32,512]{3,2,1,0:T(8,128)(2,1)}, s32[16]{0:T(128)}) custom-call(s32[128]{0:T(128)} %slots, s32[1]{0:T(128)} %bitcast.4.member, bf16[16,32,512]{2,1,0:T(8,128)(2,1)} %dn.1, bf16[16,32,512]{2,1,0:T(8,128)(2,1)} %up.3), custom_call_target="tpu_custom_call" | custom-call | flops 1 | bytes 1 | tf_op jit(solution)/shard_map/pallas_call | solution.py:58
  12.6 5.8 %all-to-all-start = ((bf16[8,2,2,32,512]{4,3,2,1,0:T(8,128)(2,1)}), bf16[8,2,2,32,512]{4,3,2,1,0:T(8,128)(2,1)S(1)}, u32[]{:S(2)}, u32[]{:S(2)}) async-start(bf16[8,2,2,32,512]{4,3,2,1,0:T(8,128)(2,1)} %bitcast.37), calls=%async_computation | async-start | bytes 2097152 | tf_op jit(solution)/shard_map/all_to_all | solution.py:279
  18.4 1.9 %collective-permute-start.3 = (bf16[256,512]{1,0:T(8,128)(2,1)S(1)}, bf16[256,512]{1,0:T(8,128)(2,1)}, u32[]{:S(2)}, u32[]{:S(2)}) collective-permute-start(bf16[256,512]{1,0:T(8,128)(2,1)S(1)} %get-tuple-element.84), channel_id=1, source_target_pairs={{0,4},{4,8},{8,12},{12,0},{1,5},{5,9},{9,13},{13,1},{2,6},{6,10},{... | collective-permute-start | bytes 786440 | tf_op jit(solution)/shard_map/ppermute | solution.py:226
  21.7 0.7 and_select_fusion
  22.7 0.7 multiply_add_fusion
  23.4 0.8 select_reduce_fusion.2
  24.4 1.2 multiply_convert_fusion.refs_1_.weighted
  25.7 1.2 collective-permute-start.5
  26.8 1.2 pad_maximum_fusion.refs_5_
  28.1 1.4 collective-permute-start.9
  29.5 1.3 collective-permute-start.10
  30.8 1.9 %collective-permute-start.11 = (bf16[3,256,512]{2,1,0:T(8,128)(2,1)S(1)}, bf16[3,256,512]{2,1,0:T(8,128)(2,1)}, u32[]{:S(2)}, u32[]{:S(2)}) collective-permute-start(bf16[3,256,512]{2,1,0:T(8,128)(2,1)S(1)} %pad_maximum_fusion.refs_5_), channel_id=1, source_target_pairs={{0,16},{16,0},{1,17},{17,1},{2,18},{18,2},{3,19},{19,3},{4,20},{20... | collective-permute-start | bytes 2359304 | tf_op jit(solution)/shard_map/ppermute | solution.py:273
  32.7 0.9 all-to-all-done
  33.6 1.6 %broadcast_in_dim.13 = bf16[4,512,512]{2,1,0:T(8,128)(2,1)} broadcast(bf16[512,512]{1,0:T(8,128)(2,1)S(1)} %copy-done.6), dimensions={1,2} | broadcast | bytes 2621440 | tf_op jit(solution)/shard_map/broadcast_in_dim | solution.py:282
  35.3 4.2 %all-to-all-start.1 = ((bf16[4,512,512]{2,1,0:T(8,128)(2,1)}), bf16[4,512,512]{2,1,0:T(8,128)(2,1)S(1)}, u32[]{:S(2)}, u32[]{:S(2)}) async-start(bf16[4,512,512]{2,1,0:T(8,128)(2,1)} %broadcast_in_dim.13), calls=%async_computation.1 | async-start | bytes 4194304 | tf_op jit(solution)/shard_map/all_to_all | solution.py:282
  40.0 1.9 %collective-permute-start.6 = (bf16[512,512]{1,0:T(8,128)(2,1)S(1)}, bf16[512,512]{1,0:T(8,128)(2,1)S(1)}, u32[]{:S(2)}, u32[]{:S(2)}) collective-permute-start(bf16[512,512]{1,0:T(8,128)(2,1)S(1)} %multiply_convert_fusion.refs_1_.weighted), channel_id=1, source_target_pairs={{0,4},{4,8},{8,12},{12,0},{1,5},{5,9},{9,13},{13,1},{2,6},{6,10},{... | collective-permute-start | bytes 1572872 | tf_op jit(solution)/shard_map/ppermute | solution.py:226
  41.9 0.8 collective-permute-start.7
  42.7 1.2 pad_maximum_fusion.1.refs_7_
  43.9 1.6 %fusion.8 = (bf16[8,2,1,32,512]{4,3,2,1,0:T(8,128)(2,1)S(1)}, bf16[8,2,1,32,512]{4,3,2,1,0:T(8,128)(2,1)S(1)}) fusion(bf16[8,2,2,32,512]{4,3,2,1,0:T(8,128)(2,1)} %copy-done.3), kind=kLoop, calls=%fused_computation.40 | loop fusion | bytes 2097152 | tf_op jit(solution)/shard_map/slice | solution.py:283
  46.0 4.7 %collective-permute-done.9.refs_6_ = bf16[3,256,512]{2,1,0:T(8,128)(2,1)} collective-permute-done((bf16[3,256,512]{2,1,0:T(8,128)(2,1)S(1)}, bf16[3,256,512]{2,1,0:T(8,128)(2,1)}, u32[]{:S(2)}, u32[]{:S(2)}) %collective-permute-start.9) | collective-permute-done | bytes 786464 | tf_op jit(solution)/shard_map/ppermute | solution.py:226
  51.3 1.5 %fusion = f32[32,512]{1,0:T(8,128)S(1)} fusion(bf16[16,32,512]{2,1,0:T(8,128)(2,1)S(1)} %bitcast.35, bf16[512,512]{1,0:T(8,128)(2,1)} %acts.1, f32[16,512]{1,0:T(8,128)S(1)} %get-tuple-element.91), kind=kOutput, calls=%fused_computation.4 | convolution fusion | flops 268943360 | bytes 1146880 | tf_op jit(solution)/shard_map/dot_general | solution.py:306
  53.5 2.1 %collective-permute-start.17 = (f32[64,512]{1,0:T(8,128)S(1)}, f32[64,512]{1,0:T(8,128)S(1)}, u32[]{:S(2)}, u32[]{:S(2)}) collective-permute-start(f32[64,512]{1,0:T(8,128)S(1)} %pad_maximum_fusion.2), channel_id=1, source_target_pairs={{0,8},{4,12},{8,0},{12,4},{1,9},{5,13},{9,1},{13,5},{2,10},{6,14},... | collective-permute-start | bytes 393224 | tf_op jit(solution)/shard_map/ppermute | solution.py:226
  55.6 1.0 collective-permute-start.8
  56.5 2.6 %collective-permute-done.17 = f32[64,512]{1,0:T(8,128)S(1)} collective-permute-done((f32[64,512]{1,0:T(8,128)S(1)}, f32[64,512]{1,0:T(8,128)S(1)}, u32[]{:S(2)}, u32[]{:S(2)}) %collective-permute-start.17) | collective-permute-done | bytes 131104 | tf_op jit(solution)/shard_map/ppermute | solution.py:226
  59.2 1.8 %collective-permute-start.15 = (f32[64,512]{1,0:T(8,128)S(1)}, f32[64,512]{1,0:T(8,128)S(1)}, u32[]{:S(2)}, u32[]{:S(2)}) collective-permute-start(f32[64,512]{1,0:T(8,128)S(1)} %pad_maximum_fusion.2), channel_id=1, source_target_pairs={{0,4},{4,8},{8,12},{12,0},{1,5},{5,9},{9,13},{13,1},{2,6},{6,10},{... | collective-permute-start | bytes 393224 | tf_op jit(solution)/shard_map/ppermute | solution.py:226
  61.0 14.2 %collective-permute-done.15 = f32[64,512]{1,0:T(8,128)S(1)} collective-permute-done((f32[64,512]{1,0:T(8,128)S(1)}, f32[64,512]{1,0:T(8,128)S(1)}, u32[]{:S(2)}, u32[]{:S(2)}) %collective-permute-start.15) | collective-permute-done | bytes 131104 | tf_op jit(solution)/shard_map/ppermute | solution.py:226
  75.1 4.6 %collective-permute-done.16 = f32[64,512]{1,0:T(8,128)S(1)} collective-permute-done((f32[64,512]{1,0:T(8,128)S(1)}, f32[64,512]{1,0:T(8,128)S(1)}, u32[]{:S(2)}, u32[]{:S(2)}) %collective-permute-start.16) | collective-permute-done | bytes 131104 | tf_op jit(solution)/shard_map/ppermute | solution.py:226
  79.8 1.4 collective-permute-start.18
  81.2 1.5 %collective-permute-start.19 = (f32[64,512]{1,0:T(8,128)S(1)}, f32[64,512]{1,0:T(8,128)S(1)}, u32[]{:S(2)}, u32[]{:S(2)}) collective-permute-start(f32[64,512]{1,0:T(8,128)S(1)} %add_add_fusion.t0), channel_id=1, source_target_pairs={{0,3},{1,0},{2,1},{3,2},{4,7},{5,4},{6,5},{7,6},{8,11},{9,8},{10,9... | collective-permute-start | bytes 393224 | tf_op jit(solution)/shard_map/ppermute | solution.py:226
  82.7 1.6 %collective-permute-start.20 = (f32[64,512]{1,0:T(8,128)S(1)}, f32[64,512]{1,0:T(8,128)S(1)}, u32[]{:S(2)}, u32[]{:S(2)}) collective-permute-start(f32[64,512]{1,0:T(8,128)S(1)} %add_add_fusion.t0), channel_id=1, source_target_pairs={{0,2},{1,3},{2,0},{3,1},{4,6},{5,7},{6,4},{7,5},{8,10},{9,11},{10,... | collective-permute-start | bytes 393224 | tf_op jit(solution)/shard_map/ppermute | solution.py:226
  84.9 15.5 %shard_map.180 = (bf16[512,512]{1,0:T(8,128)(2,1)}, bf16[512,512]{1,0:T(8,128)(2,1)}, bf16[512,512]{1,0:T(8,128)(2,1)}, bf16[512,512]{1,0:T(8,128)(2,1)}, bf16[5...) custom-call(s32[4]{0:T(128)} %pad_add_fusion.where, ...), custom_call_target="tpu_custom_call" | custom-call | flops 1 | bytes 1 | tf_op jit(solution)/shard_map/pallas_call | solution.py:173
  100.4 1.5 %collective-permute-start.23 = (bf16[512,512]{1,0:T(8,128)(2,1)}, bf16[512,512]{1,0:T(8,128)(2,1)S(1)}, u32[]{:S(2)}, u32[]{:S(2)}) collective-permute-start(bf16[512,512]{1,0:T(8,128)(2,1)} %get-tuple-element.58), channel_id=1, source_target_pairs={{0,8},{4,12},{8,0},{12,4},{1,9},{5,13},{9,1},{13,5},{2,10},{6,14},... | collective-permute-start | bytes 1572872 | tf_op jit(solution)/shard_map/ppermute | solution.py:226
  101.9 2.6 %collective-permute-start.21 = (bf16[512,512]{1,0:T(8,128)(2,1)}, bf16[512,512]{1,0:T(8,128)(2,1)}, u32[]{:S(2)}, u32[]{:S(2)}) collective-permute-start(bf16[512,512]{1,0:T(8,128)(2,1)} %get-tuple-element.56), channel_id=1, source_target_pairs={{0,12},{4,0},{8,4},{12,8},{1,13},{5,1},{9,5},{13,9},{2,14},{6,2},{... | collective-permute-start | bytes 1572872 | tf_op jit(solution)/shard_map/ppermute | solution.py:226
  104.5 1.4 collective-permute-start.26
  105.9 1.4 collective-permute-start.25
  107.3 3.3 %shard_map.181 = (bf16[16,2,32,512]{3,2,1,0:T(8,128)(2,1)}, bf16[512,512]{1,0:T(8,128)(2,1)}, bf16[512,512]{1,0:T(8,128)(2,1)}) custom-call(f32[64,512]{1,0:T(8,128)} %copy-done.11, f32[64,512]{1,0:T(8,128)} %copy-done.13, f32[64,512]{1,0:T(8,128)} %copy-done.14, f32[64,512]{1,0:T(8,128)} %copy-done.15, bf16[16,512]{1,0:T(8,128)(2,1)} %get-tuple-element.90.hot, ...), custom_call_target="tpu_custom_call" | custom-call | flops 1 | bytes 1 | tf_op jit(solution)/shard_map/pallas_call | solution.py:215
  110.6 7.0 %all-to-all-start.2 = ((bf16[8,2,2,32,512]{4,3,2,1,0:T(8,128)(2,1)}), bf16[8,2,2,32,512]{4,3,2,1,0:T(8,128)(2,1)S(1)}, u32[]{:S(2)}, u32[]{:S(2)}) async-start(bf16[8,2,2,32,512]{4,3,2,1,0:T(8,128)(2,1)} %bitcast.38), calls=%async_computation.2 | async-start | bytes 2097152 | tf_op jit(solution)/shard_map/all_to_all | solution.py:325
  117.6 1.7 %convolution_multiply_fusion = f32[512,512]{1,0:T(8,128)S(1)} fusion(bf16[512,512]{1,0:T(8,128)(2,1)} %get-tuple-element.60, bf16[512,512]{1,0:T(8,128)(2,1)} %bitcast.36), kind=kOutput, calls=%fused_computation | convolution fusion | flops 268697600 | bytes 2097152 | tf_op jit(solution)/shard_map/dot_general | solution.py:342
  119.3 1.7 %convolution_multiply_fusion.1 = f32[512,512]{1,0:T(8,128)S(1)} fusion(bf16[512,512]{1,0:T(8,128)(2,1)} %get-tuple-element.55, bf16[512,512]{1,0:T(8,128)(2,1)} %bitcast.34), kind=kOutput, calls=%fused_computation.1 | convolution fusion | flops 268697600 | bytes 2097152 | tf_op jit(solution)/shard_map/dot_general | solution.py:339
  121.8 1.5 %convert_add_fusion = (f32[512,512]{1,0:T(8,128)S(1)}, f32[512,512]{1,0:T(8,128)S(1)}) fusion(f32[512,512]{1,0:T(8,128)S(1)} %convolution_multiply_fusion, bf16[512,512]{1,0:T(8,128)(2,1)} %get-tuple-element.59, f32[512,512]{1,0:T(8,128)S(1)} %convolution_multiply_fusion.1, bf16[512,512]{1,0:T(8,128)(2,1)} %get-tuple-element.52), kind=kLoop, calls=%fused_computation.7 | loop fusion | flops 1048576 | bytes 5242880 | tf_op jit(solution)/shard_map/add | solution.py:342
  123.3 4.0 %collective-permute-done.22 = bf16[512,512]{1,0:T(8,128)(2,1)} collective-permute-done((bf16[512,512]{1,0:T(8,128)(2,1)}, bf16[512,512]{1,0:T(8,128)(2,1)}, u32[]{:S(2)}, u32[]{:S(2)}) %collective-permute-start.22) | collective-permute-done | bytes 524320 | tf_op jit(solution)/shard_map/ppermute | solution.py:226
  127.3 2.4 %add_convert_fusion.1 = bf16[512,512]{1,0:T(8,128)(2,1)} fusion(bf16[512,512]{1,0:T(8,128)(2,1)} %copy-done.12, bf16[512,512]{1,0:T(8,128)(2,1)} %collective-permute-done.22, f32[512,512]{1,0:T(8,128)S(1)} %get-tuple-element.93, bf16[512,512]{1,0:T(8,128)(2,1)} %collective-permute-done.21), kind=kLoop, calls=%fused_computation.8 | loop fusion | flops 1835008 | bytes 3145728 | tf_op jit(solution)/shard_map/convert_element_type | solution.py:351
  129.8 3.0 %all-to-all-done.2 = bf16[8,2,2,32,512]{4,3,2,1,0:T(8,128)(2,1)S(1)} async-done(((bf16[8,2,2,32,512]{4,3,2,1,0:T(8,128)(2,1)}), bf16[8,2,2,32,512]{4,3,2,1,0:T(8,128)(2,1)S(1)}, u32[]{:S(2)}, u32[]{:S(2)}) %all-to-all-start.2) | async-done | bytes 1048608 | tf_op jit(solution)/shard_map/all_to_all | solution.py:325
  132.8 1.0 copy-done.2
  133.7 5.9 %shard_map.182 = (bf16[16,32,512]{2,1,0:T(8,128)(2,1)}, bf16[16,32,512]{2,1,0:T(8,128)(2,1)}, f32[16,32,512]{2,1,0:T(8,128)}, f32[16,32,512]{2,1,0:T(8,128)}, f3...) custom-call(s32[16]{0:T(128)} %get-tuple-element.61.pos, bf16[16,2,32,512]{3,2,1,0:T(8,128)(2,1)} %bitcast.32, ...), custom_call_target="tpu_custom_call" | custom-call | flops 1 | bytes 1 | tf_op jit(solution)/shard_map/pallas_call | solution.py:93
  139.7 2.1 %add_convert_fusion = bf16[512,512]{1,0:T(8,128)(2,1)} fusion(bf16[512,512]{1,0:T(8,128)(2,1)S(1)} %collective-permute-done.26, bf16[512,512]{1,0:T(8,128)(2,1)S(1)} %collective-permute-done.25, f32[512,512]{1,0:T(8,128)S(1)} %get-tuple-element.70, bf16[512,512]{1,0:T(8,128)(2,1)} %collective-permute-done.24), kind=kLoop, calls=%fused_computation.6 | loop fusion | flops 1835008 | bytes 3145728 | tf_op jit(solution)/shard_map/convert_element_type | solution.py:351
  (74 shorter events, 6.4 us)
Async XLA Ops:
  0.6 33.0 %copy-start.6 = (bf16[512,512]{1,0:T(8,128)(2,1)S(1)}, bf16[512,512]{1,0:T(8,128)(2,1)}, u32[]{:S(2)}) copy-start(bf16[512,512]{1,0:T(8,128)(2,1)} %acts.1) | copy-start | bytes 1572868
  2.9 22.7 %collective-permute-start.2 = (bf16[256,512]{1,0:T(8,128)(2,1)S(1)}, bf16[256,512]{1,0:T(8,128)(2,1)}, u32[]{:S(2)}, u32[]{:S(2)}) collective-permute-start(bf16[256,512]{1,0:T(8,128)(2,1)S(1)} %get-tuple-element.85), channel_id=1, source_target_pairs={{0,12},{4,0},{8,4},{12,8},{1,13},{5,1},{9,5},{13,9},{2,14},{6,2},{... | collective-permute-start | bytes 786440 | tf_op jit(solution)/shard_map/ppermute | solution.py:226
  7.5 18.2 %collective-permute-start.1 = (bf16[256,512]{1,0:T(8,128)(2,1)S(1)}, bf16[256,512]{1,0:T(8,128)(2,1)}, u32[]{:S(2)}, u32[]{:S(2)}) collective-permute-start(bf16[256,512]{1,0:T(8,128)(2,1)S(1)} %get-tuple-element.86), channel_id=1, source_target_pairs={{0,8},{4,12},{8,0},{12,4},{1,9},{5,13},{9,1},{13,5},{2,10},{6,14},... | collective-permute-start | bytes 786440 | tf_op jit(solution)/shard_map/ppermute | solution.py:226
  7.5 18.2 %collective-permute-start = (bf16[256,512]{1,0:T(8,128)(2,1)S(1)}, bf16[256,512]{1,0:T(8,128)(2,1)}, u32[]{:S(2)}, u32[]{:S(2)}) collective-permute-start(bf16[256,512]{1,0:T(8,128)(2,1)S(1)} %get-tuple-element.87), channel_id=1, source_target_pairs={{0,4},{4,8},{8,12},{12,0},{1,5},{5,9},{9,13},{13,1},{2,6},{6,10},{... | collective-permute-start | bytes 786440 | tf_op jit(solution)/shard_map/ppermute | solution.py:226
  12.6 21.0 %all-to-all-start = ((bf16[8,2,2,32,512]{4,3,2,1,0:T(8,128)(2,1)}), bf16[8,2,2,32,512]{4,3,2,1,0:T(8,128)(2,1)S(1)}, u32[]{:S(2)}, u32[]{:S(2)}) async-start(bf16[8,2,2,32,512]{4,3,2,1,0:T(8,128)(2,1)} %bitcast.37), calls=%async_computation | async-start | bytes 2097152 | tf_op jit(solution)/shard_map/all_to_all | solution.py:279
  18.4 9.7 %collective-permute-start.3 = (bf16[256,512]{1,0:T(8,128)(2,1)S(1)}, bf16[256,512]{1,0:T(8,128)(2,1)}, u32[]{:S(2)}, u32[]{:S(2)}) collective-permute-start(bf16[256,512]{1,0:T(8,128)(2,1)S(1)} %get-tuple-element.84), channel_id=1, source_target_pairs={{0,4},{4,8},{8,12},{12,0},{1,5},{5,9},{9,13},{13,1},{2,6},{6,10},{... | collective-permute-start | bytes 786440 | tf_op jit(solution)/shard_map/ppermute | solution.py:226
  20.3 7.8 %collective-permute-start.4 = (bf16[256,512]{1,0:T(8,128)(2,1)S(1)}, bf16[256,512]{1,0:T(8,128)(2,1)}, u32[]{:S(2)}, u32[]{:S(2)}) collective-permute-start(bf16[256,512]{1,0:T(8,128)(2,1)S(1)} %get-tuple-element.83), channel_id=1, source_target_pairs={{0,12},{4,0},{8,4},{12,8},{1,13},{5,1},{9,5},{13,9},{2,14},{6,2},{... | collective-permute-start | bytes 786440 | tf_op jit(solution)/shard_map/ppermute | solution.py:226
  25.6 58.7 %copy-start.1 = (bf16[512,512]{1,0:T(8,128)(2,1)}, bf16[512,512]{1,0:T(8,128)(2,1)S(1)}, u32[]{:S(2)}) copy-start(bf16[512,512]{1,0:T(8,128)(2,1)S(1)} %multiply_convert_fusion.refs_1_.weighted) | copy-start | bytes 1572868
  25.7 14.4 %collective-permute-start.5 = (bf16[256,512]{1,0:T(8,128)(2,1)}, bf16[256,512]{1,0:T(8,128)(2,1)}, u32[]{:S(2)}, u32[]{:S(2)}) collective-permute-start(bf16[256,512]{1,0:T(8,128)(2,1)} %get-tuple-element.48), channel_id=1, source_target_pairs={{0,8},{4,12},{8,0},{12,4},{1,9},{5,13},{9,1},{13,5},{2,10},{6,14},... | collective-permute-start | bytes 786440 | tf_op jit(solution)/shard_map/ppermute | solution.py:226
  28.0 56.9 %copy-start.4 = (bf16[3,256,512]{2,1,0:T(8,128)(2,1)}, bf16[3,256,512]{2,1,0:T(8,128)(2,1)S(1)}, u32[]{:S(2)}) copy-start(bf16[3,256,512]{2,1,0:T(8,128)(2,1)S(1)} %pad_maximum_fusion.refs_5_) | copy-start | bytes 2359300
  28.1 22.6 %collective-permute-start.9 = (bf16[3,256,512]{2,1,0:T(8,128)(2,1)S(1)}, bf16[3,256,512]{2,1,0:T(8,128)(2,1)}, u32[]{:S(2)}, u32[]{:S(2)}) collective-permute-start(bf16[3,256,512]{2,1,0:T(8,128)(2,1)S(1)} %pad_maximum_fusion.refs_5_), channel_id=1, source_target_pairs={{0,32},{32,64},{64,96},{96,0},{1,33},{33,65},{65,97},{97,1},{2,34}... | collective-permute-start | bytes 2359304 | tf_op jit(solution)/shard_map/ppermute | solution.py:226
  29.5 23.3 %collective-permute-start.10 = (bf16[3,256,512]{2,1,0:T(8,128)(2,1)S(1)}, bf16[3,256,512]{2,1,0:T(8,128)(2,1)}, u32[]{:S(2)}, u32[]{:S(2)}) collective-permute-start(bf16[3,256,512]{2,1,0:T(8,128)(2,1)S(1)} %pad_maximum_fusion.refs_5_), channel_id=1, source_target_pairs={{0,96},{32,0},{64,32},{96,64},{1,97},{33,1},{65,33},{97,65},{2,98}... | collective-permute-start | bytes 2359304 | tf_op jit(solution)/shard_map/ppermute | solution.py:226
  30.8 22.1 %collective-permute-start.11 = (bf16[3,256,512]{2,1,0:T(8,128)(2,1)S(1)}, bf16[3,256,512]{2,1,0:T(8,128)(2,1)}, u32[]{:S(2)}, u32[]{:S(2)}) collective-permute-start(bf16[3,256,512]{2,1,0:T(8,128)(2,1)S(1)} %pad_maximum_fusion.refs_5_), channel_id=1, source_target_pairs={{0,16},{16,0},{1,17},{17,1},{2,18},{18,2},{3,19},{19,3},{4,20},{20... | collective-permute-start | bytes 2359304 | tf_op jit(solution)/shard_map/ppermute | solution.py:273
  33.6 1.7 %copy-start.3 = (bf16[8,2,2,32,512]{4,3,2,1,0:T(8,128)(2,1)}, bf16[8,2,2,32,512]{4,3,2,1,0:T(8,128)(2,1)S(1)}, u32[]{:S(2)}) copy-start(bf16[8,2,2,32,512]{4,3,2,1,0:T(8,128)(2,1)S(1)} %all-to-all-done) | copy-start | bytes 3145732
  35.3 44.6 %all-to-all-start.1 = ((bf16[4,512,512]{2,1,0:T(8,128)(2,1)}), bf16[4,512,512]{2,1,0:T(8,128)(2,1)S(1)}, u32[]{:S(2)}, u32[]{:S(2)}) async-start(bf16[4,512,512]{2,1,0:T(8,128)(2,1)} %broadcast_in_dim.13), calls=%async_computation.1 | async-start | bytes 4194304 | tf_op jit(solution)/shard_map/all_to_all | solution.py:282
  40.0 13.4 %collective-permute-start.6 = (bf16[512,512]{1,0:T(8,128)(2,1)S(1)}, bf16[512,512]{1,0:T(8,128)(2,1)S(1)}, u32[]{:S(2)}, u32[]{:S(2)}) collective-permute-start(bf16[512,512]{1,0:T(8,128)(2,1)S(1)} %multiply_convert_fusion.refs_1_.weighted), channel_id=1, source_target_pairs={{0,4},{4,8},{8,12},{12,0},{1,5},{5,9},{9,13},{13,1},{2,6},{6,10},{... | collective-permute-start | bytes 1572872 | tf_op jit(solution)/shard_map/ppermute | solution.py:226
  41.9 13.6 %collective-permute-start.7 = (bf16[512,512]{1,0:T(8,128)(2,1)S(1)}, bf16[512,512]{1,0:T(8,128)(2,1)S(1)}, u32[]{:S(2)}, u32[]{:S(2)}) collective-permute-start(bf16[512,512]{1,0:T(8,128)(2,1)S(1)} %multiply_convert_fusion.refs_1_.weighted), channel_id=1, source_target_pairs={{0,12},{4,0},{8,4},{12,8},{1,13},{5,1},{9,5},{13,9},{2,14},{6,2},{... | collective-permute-start | bytes 1572872 | tf_op jit(solution)/shard_map/ppermute | solution.py:226
  43.9 35.8 %copy-start.5 = (bf16[3,256,512]{2,1,0:T(8,128)(2,1)}, bf16[3,256,512]{2,1,0:T(8,128)(2,1)S(1)}, u32[]{:S(2)}) copy-start(bf16[3,256,512]{2,1,0:T(8,128)(2,1)S(1)} %pad_maximum_fusion.1.refs_7_) | copy-start | bytes 2359300
  45.5 34.2 %copy-start.7 = (bf16[8,2,1,32,512]{4,3,2,1,0:T(8,128)(2,1)}, bf16[8,2,1,32,512]{4,3,2,1,0:T(8,128)(2,1)S(1)}, u32[]{:S(2)}) copy-start(bf16[8,2,1,32,512]{4,3,2,1,0:T(8,128)(2,1)S(1)} %get-tuple-element.89) | copy-start | bytes 1572868
  45.5 34.2 %copy-start.8 = (bf16[8,2,1,32,512]{4,3,2,1,0:T(8,128)(2,1)}, bf16[8,2,1,32,512]{4,3,2,1,0:T(8,128)(2,1)S(1)}, u32[]{:S(2)}) copy-start(bf16[8,2,1,32,512]{4,3,2,1,0:T(8,128)(2,1)S(1)} %get-tuple-element.88) | copy-start | bytes 1572868
  50.7 29.1 %collective-permute-start.13 = (bf16[3,256,512]{2,1,0:T(8,128)(2,1)S(1)}, bf16[3,256,512]{2,1,0:T(8,128)(2,1)}, u32[]{:S(2)}, u32[]{:S(2)}) collective-permute-start(bf16[3,256,512]{2,1,0:T(8,128)(2,1)S(1)} %pad_maximum_fusion.1.refs_7_), channel_id=1, source_target_pairs={{0,16},{16,0},{1,17},{17,1},{2,18},{18,2},{3,19},{19,3},{4,20},{20... | collective-permute-start | bytes 2359304 | tf_op jit(solution)/shard_map/ppermute | solution.py:273
  52.8 32.0 %collective-permute-start.12 = (bf16[3,256,512]{2,1,0:T(8,128)(2,1)}, bf16[3,256,512]{2,1,0:T(8,128)(2,1)}, u32[]{:S(2)}, u32[]{:S(2)}) collective-permute-start(bf16[3,256,512]{2,1,0:T(8,128)(2,1)} %collective-permute-done.9.refs_6_), channel_id=1, source_target_pairs={{0,16},{16,0},{1,17},{17,1},{2,18},{18,2},{3,19},{19,3},{4,20},{20... | collective-permute-start | bytes 2359304 | tf_op jit(solution)/shard_map/ppermute | solution.py:273
  53.0 31.9 %collective-permute-start.14 = (bf16[3,256,512]{2,1,0:T(8,128)(2,1)}, bf16[3,256,512]{2,1,0:T(8,128)(2,1)}, u32[]{:S(2)}, u32[]{:S(2)}) collective-permute-start(bf16[3,256,512]{2,1,0:T(8,128)(2,1)} %collective-permute-done.10.refs_8_), channel_id=1, source_target_pairs={{0,16},{16,0},{1,17},{17,1},{2,18},{18,2},{3,19},{19,3},{4,20},{20... | collective-permute-start | bytes 2359304 | tf_op jit(solution)/shard_map/ppermute | solution.py:273
  53.5 26.3 %copy-start.9 = (bf16[512,512]{1,0:T(8,128)(2,1)}, bf16[512,512]{1,0:T(8,128)(2,1)S(1)}, u32[]{:S(2)}) copy-start(bf16[512,512]{1,0:T(8,128)(2,1)S(1)} %collective-permute-done.6.refs_2_) | copy-start | bytes 1572868
  53.5 5.7 %collective-permute-start.17 = (f32[64,512]{1,0:T(8,128)S(1)}, f32[64,512]{1,0:T(8,128)S(1)}, u32[]{:S(2)}, u32[]{:S(2)}) collective-permute-start(f32[64,512]{1,0:T(8,128)S(1)} %pad_maximum_fusion.2), channel_id=1, source_target_pairs={{0,8},{4,12},{8,0},{12,4},{1,9},{5,13},{9,1},{13,5},{2,10},{6,14},... | collective-permute-start | bytes 393224 | tf_op jit(solution)/shard_map/ppermute | solution.py:226
  55.6 24.2 %copy-start.10 = (bf16[512,512]{1,0:T(8,128)(2,1)}, bf16[512,512]{1,0:T(8,128)(2,1)S(1)}, u32[]{:S(2)}) copy-start(bf16[512,512]{1,0:T(8,128)(2,1)S(1)} %collective-permute-done.7.refs_4_) | copy-start | bytes 1572868
  55.6 27.2 %collective-permute-start.8 = (bf16[512,512]{1,0:T(8,128)(2,1)S(1)}, bf16[512,512]{1,0:T(8,128)(2,1)}, u32[]{:S(2)}, u32[]{:S(2)}) collective-permute-start(bf16[512,512]{1,0:T(8,128)(2,1)S(1)} %multiply_convert_fusion.refs_1_.weighted), channel_id=1, source_target_pairs={{0,8},{4,12},{8,0},{12,4},{1,9},{5,13},{9,1},{13,5},{2,10},{6,14},... | collective-permute-start | bytes 1572872 | tf_op jit(solution)/shard_map/ppermute | solution.py:226
  59.2 15.9 %collective-permute-start.15 = (f32[64,512]{1,0:T(8,128)S(1)}, f32[64,512]{1,0:T(8,128)S(1)}, u32[]{:S(2)}, u32[]{:S(2)}) collective-permute-start(f32[64,512]{1,0:T(8,128)S(1)} %pad_maximum_fusion.2), channel_id=1, source_target_pairs={{0,4},{4,8},{8,12},{12,0},{1,5},{5,9},{9,13},{13,1},{2,6},{6,10},{... | collective-permute-start | bytes 393224 | tf_op jit(solution)/shard_map/ppermute | solution.py:226
  75.1 4.6 %collective-permute-start.16 = (f32[64,512]{1,0:T(8,128)S(1)}, f32[64,512]{1,0:T(8,128)S(1)}, u32[]{:S(2)}, u32[]{:S(2)}) collective-permute-start(f32[64,512]{1,0:T(8,128)S(1)} %pad_maximum_fusion.2), channel_id=1, source_target_pairs={{0,12},{4,0},{8,4},{12,8},{1,13},{5,1},{9,5},{13,9},{2,14},{6,2},{... | collective-permute-start | bytes 393224 | tf_op jit(solution)/shard_map/ppermute | solution.py:226
  79.8 27.5 %copy-start.11 = (f32[64,512]{1,0:T(8,128)}, f32[64,512]{1,0:T(8,128)S(1)}, u32[]{:S(2)}) copy-start(f32[64,512]{1,0:T(8,128)S(1)} %add_add_fusion.t0) | copy-start | bytes 393220
  79.8 5.1 %copy-start = (bf16[4,512,512]{2,1,0:T(8,128)(2,1)}, bf16[4,512,512]{2,1,0:T(8,128)(2,1)S(1)}, u32[]{:S(2)}) copy-start(bf16[4,512,512]{2,1,0:T(8,128)(2,1)S(1)} %all-to-all-done.1.refs_0_) | copy-start | bytes 6291460
  79.8 22.0 %collective-permute-start.18 = (f32[64,512]{1,0:T(8,128)S(1)}, f32[64,512]{1,0:T(8,128)S(1)}, u32[]{:S(2)}, u32[]{:S(2)}) collective-permute-start(f32[64,512]{1,0:T(8,128)S(1)} %add_add_fusion.t0), channel_id=1, source_target_pairs={{0,1},{1,2},{2,3},{3,0},{4,5},{5,6},{6,7},{7,4},{8,9},{9,10},{10,1... | collective-permute-start | bytes 393224 | tf_op jit(solution)/shard_map/ppermute | solution.py:226
  81.2 23.3 %collective-permute-start.19 = (f32[64,512]{1,0:T(8,128)S(1)}, f32[64,512]{1,0:T(8,128)S(1)}, u32[]{:S(2)}, u32[]{:S(2)}) collective-permute-start(f32[64,512]{1,0:T(8,128)S(1)} %add_add_fusion.t0), channel_id=1, source_target_pairs={{0,3},{1,0},{2,1},{3,2},{4,7},{5,4},{6,5},{7,6},{8,11},{9,8},{10,9... | collective-permute-start | bytes 393224 | tf_op jit(solution)/shard_map/ppermute | solution.py:226
  82.7 23.2 %collective-permute-start.20 = (f32[64,512]{1,0:T(8,128)S(1)}, f32[64,512]{1,0:T(8,128)S(1)}, u32[]{:S(2)}, u32[]{:S(2)}) collective-permute-start(f32[64,512]{1,0:T(8,128)S(1)} %add_add_fusion.t0), channel_id=1, source_target_pairs={{0,2},{1,3},{2,0},{3,1},{4,6},{5,7},{6,4},{7,5},{8,10},{9,11},{10,... | collective-permute-start | bytes 393224 | tf_op jit(solution)/shard_map/ppermute | solution.py:226
  100.4 20.6 %collective-permute-start.23 = (bf16[512,512]{1,0:T(8,128)(2,1)}, bf16[512,512]{1,0:T(8,128)(2,1)S(1)}, u32[]{:S(2)}, u32[]{:S(2)}) collective-permute-start(bf16[512,512]{1,0:T(8,128)(2,1)} %get-tuple-element.58), channel_id=1, source_target_pairs={{0,8},{4,12},{8,0},{12,4},{1,9},{5,13},{9,1},{13,5},{2,10},{6,14},... | collective-permute-start | bytes 1572872 | tf_op jit(solution)/shard_map/ppermute | solution.py:226
  101.8 25.5 %collective-permute-start.22 = (bf16[512,512]{1,0:T(8,128)(2,1)}, bf16[512,512]{1,0:T(8,128)(2,1)}, u32[]{:S(2)}, u32[]{:S(2)}) collective-permute-start(bf16[512,512]{1,0:T(8,128)(2,1)} %get-tuple-element.57), channel_id=1, source_target_pairs={{0,4},{4,8},{8,12},{12,0},{1,5},{5,9},{9,13},{13,1},{2,6},{6,10},{... | collective-permute-start | bytes 1572872 | tf_op jit(solution)/shard_map/ppermute | solution.py:226
  101.9 5.5 %copy-start.13 = (f32[64,512]{1,0:T(8,128)}, f32[64,512]{1,0:T(8,128)S(1)}, u32[]{:S(2)}) copy-start(f32[64,512]{1,0:T(8,128)S(1)} %collective-permute-done.18.t1) | copy-start | bytes 393220
  101.9 25.5 %collective-permute-start.21 = (bf16[512,512]{1,0:T(8,128)(2,1)}, bf16[512,512]{1,0:T(8,128)(2,1)}, u32[]{:S(2)}, u32[]{:S(2)}) collective-permute-start(bf16[512,512]{1,0:T(8,128)(2,1)} %get-tuple-element.56), channel_id=1, source_target_pairs={{0,12},{4,0},{8,4},{12,8},{1,13},{5,1},{9,5},{13,9},{2,14},{6,2},{... | collective-permute-start | bytes 1572872 | tf_op jit(solution)/shard_map/ppermute | solution.py:226
  104.5 2.8 %copy-start.14 = (f32[64,512]{1,0:T(8,128)}, f32[64,512]{1,0:T(8,128)S(1)}, u32[]{:S(2)}) copy-start(f32[64,512]{1,0:T(8,128)S(1)} %collective-permute-done.19.t2) | copy-start | bytes 393220
  104.5 35.2 %collective-permute-start.26 = (bf16[512,512]{1,0:T(8,128)(2,1)}, bf16[512,512]{1,0:T(8,128)(2,1)S(1)}, u32[]{:S(2)}, u32[]{:S(2)}) collective-permute-start(bf16[512,512]{1,0:T(8,128)(2,1)} %get-tuple-element.73), channel_id=1, source_target_pairs={{0,2},{1,3},{2,0},{3,1},{4,6},{5,7},{6,4},{7,5},{8,10},{9,11},{10,... | collective-permute-start | bytes 1572872 | tf_op jit(solution)/shard_map/ppermute | solution.py:226
  105.9 1.4 copy-start.15
  105.9 33.7 %collective-permute-start.25 = (bf16[512,512]{1,0:T(8,128)(2,1)}, bf16[512,512]{1,0:T(8,128)(2,1)S(1)}, u32[]{:S(2)}, u32[]{:S(2)}) collective-permute-start(bf16[512,512]{1,0:T(8,128)(2,1)} %get-tuple-element.72), channel_id=1, source_target_pairs={{0,3},{1,0},{2,1},{3,2},{4,7},{5,4},{6,5},{7,6},{8,11},{9,8},{10,9... | collective-permute-start | bytes 1572872 | tf_op jit(solution)/shard_map/ppermute | solution.py:226
  110.6 22.2 %all-to-all-start.2 = ((bf16[8,2,2,32,512]{4,3,2,1,0:T(8,128)(2,1)}), bf16[8,2,2,32,512]{4,3,2,1,0:T(8,128)(2,1)S(1)}, u32[]{:S(2)}, u32[]{:S(2)}) async-start(bf16[8,2,2,32,512]{4,3,2,1,0:T(8,128)(2,1)} %bitcast.38), calls=%async_computation.2 | async-start | bytes 2097152 | tf_op jit(solution)/shard_map/all_to_all | solution.py:325
  121.0 0.8 copy-start.12
  121.0 18.7 %collective-permute-start.24 = (bf16[512,512]{1,0:T(8,128)(2,1)}, bf16[512,512]{1,0:T(8,128)(2,1)}, u32[]{:S(2)}, u32[]{:S(2)}) collective-permute-start(bf16[512,512]{1,0:T(8,128)(2,1)} %get-tuple-element.71), channel_id=1, source_target_pairs={{0,1},{1,2},{2,3},{3,0},{4,5},{5,6},{6,7},{7,4},{8,9},{9,10},{10,1... | collective-permute-start | bytes 1572872 | tf_op jit(solution)/shard_map/ppermute | solution.py:226
  132.8 1.0 copy-start.2

commit v8 on v3

--- a/solution.py
+++ b/solution.py
@@ -70,8 +70,8 @@
 
 
 def adam_kernel(pos, grads, dn, up, m1d, m2d, m1u, m2u, odn, oup, o1d, o2d, o1u, o2u):
-    i0 = pl.program_id(0) * 4
-    for k in range(4):
+    i0 = pl.program_id(0) * 8
+    for k in range(8):
         q = pos[i0 + k]
         for which, (f, m1, m2, of, o1, o2) in enumerate(
             ((dn, m1d, m2d, odn, o1d, o2d), (up, m1u, m2u, oup, o1u, o2u))
@@ -87,7 +87,7 @@
 
 
 def adam(pos, grads, dn, up, m1d, m2d, m1u, m2u):
-    block = pl.BlockSpec((4, RANK, COLS), lambda i, pos: (i, 0, 0))
+    block = pl.BlockSpec((8, RANK, COLS), lambda i, pos: (i, 0, 0))
     half = jax.ShapeDtypeStruct((PROMPTS, RANK, COLS), BF16)
     full = jax.ShapeDtypeStruct((PROMPTS, RANK, COLS), F32)
     return pl.pallas_call(
@@ -95,7 +95,7 @@
         out_shape=(half, half, full, full, full, full),
         grid_spec=pltpu.PrefetchScalarGridSpec(
             num_scalar_prefetch=1,
-            grid=(4,),
+            grid=(2,),
             in_specs=[pl.BlockSpec((PROMPTS, 2, RANK, COLS), lambda i, pos: (0, 0, 0, 0))]
             + [block] * 6,
             out_specs=[block] * 6,

time: 140 us -> 139 us (level)
  transfers between devices with their start and end apart: 30 -> 30, of which waited for: 9 -> 9; matrix products, arithmetic and copies ran while one was open for 17% -> 17% of each run, Pallas kernels for 20% -> 19%
where the time goes in v8:
time: 139 us; the launch traced here: 138 us
  starting transfers between devices  51.6 us (37%)
  waiting for transfers between devices  31 us (22%)
  Pallas kernels  26.5 us (19%)
  other arithmetic  17.5 us (13%)
  matrix products  6.26 us (5%)
  local copies, waits for them, and re-layouts  4.15 us (3%)
    ppermute x23, waiting for transfers between devices, shift(): lax.ppermute(value, axis, [(i, (i + by) % size) for i in range(size)])  26 us
    ppermute x23, starting transfers between devices, shift(): lax.ppermute(value, axis, [(i, (i + by) % size) for i in range(size)])  25.4 us
    pallas_call x1, Pallas kernels, partials(): pl.pallas_call(partial_kernel, out_shape=[block] * 8, grid_spec=pltpu.Pre...  15.6 us
    ppermute x4, starting transfers between devices, local(): other = [lax.ppermute(piece, 'core', [(0, 1), (1, 0)]) for piece in own]  8.21 us
    all_to_all x1, starting transfers between devices, local(): lax.all_to_all(grads, ('x', 'core'), 0, 0).reshape(PROMPTS, 2, RANK, COLS)  7.94 us
    pallas_call x1, Pallas kernels, adam(): pl.pallas_call(adam_kernel, out_shape=(half, half, full, full, full, full...  5.92 us
    all_to_all x1, starting transfers between devices, local(): lax.all_to_all(sent.reshape(8, 2, 2, RANK, COLS), ('x', 'core'), 0, 0)  5.9 us
    pallas_call x1, Pallas kernels, pick(): pl.pallas_call(pick_kernel, out_shape=(jax.ShapeDtypeStruct((PROMPTS, 2,...  5.05 us
  transfers between devices with their start and end apart: 30, of which 9 were waited for; matrix products, arithmetic and copies ran while one was open for 17% of the time, Pallas kernels for 19%

profile of v8, /device:TPU:1, one launch (start us, length us, event | category | flops | bytes accessed | tf_op | source)
XLA Modules:
  0.0 138.1 jit_solution(10592377649103023273)
XLA Ops:
  0.7 1.5 %constant_dynamic-slice_fusion = (bf16[256,512]{1,0:T(8,128)(2,1)S(1)}, bf16[256,512]{1,0:T(8,128)(2,1)S(1)}, bf16[256,512]{1,0:T(8,128)(2,1)S(1)}, bf16[256,512...) fusion(bf16[8192,512]{1,0:T(8,128)(2,1)} %refs_13_.1, s32[]{:T(128)S(6)} %select_n.38, ...), kind=kLoop, calls=%fused_computation.41 | loop fusion | bytes 3145752 | tf_op jit(solution)/shard_map/dynamic_slice | solution.py:228
  2.2 4.7 %collective-permute-start.2 = (bf16[256,512]{1,0:T(8,128)(2,1)S(1)}, bf16[256,512]{1,0:T(8,128)(2,1)}, u32[]{:S(2)}, u32[]{:S(2)}) collective-permute-start(bf16[256,512]{1,0:T(8,128)(2,1)S(1)} %get-tuple-element.77), channel_id=1, source_target_pairs={{0,12},{4,0},{8,4},{12,8},{1,13},{5,1},{9,5},{13,9},{2,14},{6,2},{... | collective-permute-start | bytes 786440 | tf_op jit(solution)/shard_map/ppermute | solution.py:199
  7.6 5.1 %shard_map.179 = (bf16[16,2,32,512]{3,2,1,0:T(8,128)(2,1)}, s32[16]{0:T(128)}) custom-call(s32[128]{0:T(128)} %slots, s32[1]{0:T(128)} %bitcast.4.member, bf16[16,32,512]{2,1,0:T(8,128)(2,1)} %dn.1, bf16[16,32,512]{2,1,0:T(8,128)(2,1)} %up.3), custom_call_target="tpu_custom_call" | custom-call | flops 1 | bytes 1 | tf_op jit(solution)/shard_map/pallas_call | solution.py:58
  12.6 5.9 %all-to-all-start = ((bf16[8,2,2,32,512]{4,3,2,1,0:T(8,128)(2,1)}), bf16[8,2,2,32,512]{4,3,2,1,0:T(8,128)(2,1)S(1)}, u32[]{:S(2)}, u32[]{:S(2)}) async-start(bf16[8,2,2,32,512]{4,3,2,1,0:T(8,128)(2,1)} %bitcast.52), calls=%async_computation | async-start | bytes 2097152 | tf_op jit(solution)/shard_map/all_to_all | solution.py:252
  18.5 1.9 %collective-permute-start.3 = (bf16[256,512]{1,0:T(8,128)(2,1)S(1)}, bf16[256,512]{1,0:T(8,128)(2,1)S(1)}, u32[]{:S(2)}, u32[]{:S(2)}) collective-permute-start(bf16[256,512]{1,0:T(8,128)(2,1)S(1)} %get-tuple-element.76), channel_id=1, source_target_pairs={{0,4},{4,8},{8,12},{12,0},{1,5},{5,9},{9,13},{13,1},{2,6},{6,10},{... | collective-permute-start | bytes 786440 | tf_op jit(solution)/shard_map/ppermute | solution.py:199
  21.9 0.7 and_select_fusion
  22.8 0.7 multiply_add_fusion
  23.5 0.8 select_reduce_fusion.2
  24.5 2.0 %multiply_convert_fusion.refs_1_ = bf16[512,512]{1,0:T(8,128)(2,1)} fusion(bf16[512,512]{1,0:T(8,128)(2,1)} %param.13, f32[512]{0:T(512)S(1)} %sub.12), kind=kLoop, calls=%fused_computation.15 | loop fusion | flops 786432 | bytes 1050624 | tf_op jit(solution)/shard_map/convert_element_type | solution.py:270
  26.6 1.2 collective-permute-start.5
  27.7 2.1 %pad_maximum_fusion.1.refs_5_ = bf16[3,256,512]{2,1,0:T(8,128)(2,1)} fusion(bf16[1,256,512]{2,1,0:T(8,128)(2,1)} %bitcast.8, bf16[1,256,512]{2,1,0:T(8,128)(2,1)} %bitcast.7, bf16[1,256,512]{2,1,0:T(8,128)(2,1)} %bitcast.6), kind=kLoop, calls=%fused_computation.16 | loop fusion | flops 786432 | bytes 1572864 | tf_op jit(solution)/shard_map/stack | solution.py:240
  29.8 1.4 collective-permute-start.9
  31.2 1.3 collective-permute-start.10
  32.5 1.2 collective-permute-start.11
  33.7 1.8 %collective-permute-done.5 = bf16[256,512]{1,0:T(8,128)(2,1)S(1)} collective-permute-done((bf16[256,512]{1,0:T(8,128)(2,1)S(1)}, bf16[256,512]{1,0:T(8,128)(2,1)S(1)}, u32[]{:S(2)}, u32[]{:S(2)}) %collective-permute-start.5) | collective-permute-done | bytes 262176 | tf_op jit(solution)/shard_map/ppermute | solution.py:199
  35.4 0.8 collective-permute-start.6
  36.3 1.8 %collective-permute-start.7 = (bf16[512,512]{1,0:T(8,128)(2,1)}, bf16[512,512]{1,0:T(8,128)(2,1)}, u32[]{:S(2)}, u32[]{:S(2)}) collective-permute-start(bf16[512,512]{1,0:T(8,128)(2,1)} %multiply_convert_fusion.refs_1_), channel_id=1, source_target_pairs={{0,12},{4,0},{8,4},{12,8},{1,13},{5,1},{9,5},{13,9},{2,14},{6,2},{... | collective-permute-start | bytes 1572872 | tf_op jit(solution)/shard_map/ppermute | solution.py:199
  38.1 1.5 %broadcast_in_dim.13 = bf16[4,512,512]{2,1,0:T(8,128)(2,1)} broadcast(bf16[512,512]{1,0:T(8,128)(2,1)S(1)} %copy-done.8), dimensions={1,2} | broadcast | bytes 2621440 | tf_op jit(solution)/shard_map/broadcast_in_dim | solution.py:255
  39.6 4.2 %all-to-all-start.1 = ((bf16[4,512,512]{2,1,0:T(8,128)(2,1)}), bf16[4,512,512]{2,1,0:T(8,128)(2,1)S(1)}, u32[]{:S(2)}, u32[]{:S(2)}) async-start(bf16[4,512,512]{2,1,0:T(8,128)(2,1)} %broadcast_in_dim.13), calls=%async_computation.1 | async-start | bytes 4194304 | tf_op jit(solution)/shard_map/all_to_all | solution.py:255
  43.8 1.1 pad_maximum_fusion.2.refs_7_
  45.1 1.9 %fusion.3 = f32[32,512]{1,0:T(8,128)S(1)} fusion(bf16[16,32,512]{2,1,0:T(8,128)(2,1)S(1)} %bitcast.48, bf16[512,512]{1,0:T(8,128)(2,1)} %multiply_convert_fusion.refs_1_, f32[16,512]{1,0:T(8,128)S(1)} %get-tuple-element.87), kind=kOutput, calls=%fused_computation.9 | convolution fusion | flops 268943360 | bytes 1146880 | tf_op jit(solution)/shard_map/dot_general | solution.py:280
  47.0 1.5 %fusion.2 = f32[32,512]{1,0:T(8,128)S(1)} fusion(bf16[16,32,512]{2,1,0:T(8,128)(2,1)S(1)} %bitcast.50, bf16[512,512]{1,0:T(8,128)(2,1)} %param.12, f32[16,512]{1,0:T(8,128)S(1)} %get-tuple-element.87), kind=kOutput, calls=%fused_computation.8 | convolution fusion | flops 268943360 | bytes 1146880 | tf_op jit(solution)/shard_map/dot_general | solution.py:279
  49.3 2.7 %collective-permute-start.13 = (bf16[3,256,512]{2,1,0:T(8,128)(2,1)S(1)}, bf16[3,256,512]{2,1,0:T(8,128)(2,1)S(1)}, u32[]{:S(2)}, u32[]{:S(2)}) collective-permute-start(bf16[3,256,512]{2,1,0:T(8,128)(2,1)S(1)} %pad_maximum_fusion.2.refs_7_), channel_id=1, source_target_pairs={{0,16},{16,0},{1,17},{17,1},{2,18},{18,2},{3,19},{19,3},{4,20},{20... | collective-permute-start | bytes 2359304 | tf_op jit(solution)/shard_map/ppermute | solution.py:246
  52.0 0.9 collective-permute-start.15
  52.9 0.8 collective-permute-start.12
  54.3 3.6 %collective-permute-start.14 = (bf16[3,256,512]{2,1,0:T(8,128)(2,1)}, bf16[3,256,512]{2,1,0:T(8,128)(2,1)}, u32[]{:S(2)}, u32[]{:S(2)}) collective-permute-start(bf16[3,256,512]{2,1,0:T(8,128)(2,1)} %collective-permute-done.10.refs_8_), channel_id=1, source_target_pairs={{0,16},{16,0},{1,17},{17,1},{2,18},{18,2},{3,19},{19,3},{4,20},{20... | collective-permute-start | bytes 2359304 | tf_op jit(solution)/shard_map/ppermute | solution.py:246
  57.9 2.3 %collective-permute-done.15 = f32[64,512]{1,0:T(8,128)S(1)} collective-permute-done((f32[64,512]{1,0:T(8,128)S(1)}, f32[64,512]{1,0:T(8,128)S(1)}, u32[]{:S(2)}, u32[]{:S(2)}) %collective-permute-start.15) | collective-permute-done | bytes 131104 | tf_op jit(solution)/shard_map/ppermute | solution.py:199
  60.5 4.3 %collective-permute-done.16 = f32[64,512]{1,0:T(8,128)S(1)} collective-permute-done((f32[64,512]{1,0:T(8,128)S(1)}, f32[64,512]{1,0:T(8,128)S(1)}, u32[]{:S(2)}, u32[]{:S(2)}) %collective-permute-start.16) | collective-permute-done | bytes 131104 | tf_op jit(solution)/shard_map/ppermute | solution.py:199
  65.0 3.0 %all-to-all-done.1.refs_0_ = bf16[4,512,512]{2,1,0:T(8,128)(2,1)S(1)} async-done(((bf16[4,512,512]{2,1,0:T(8,128)(2,1)}), bf16[4,512,512]{2,1,0:T(8,128)(2,1)S(1)}, u32[]{:S(2)}, u32[]{:S(2)}) %all-to-all-start.1) | async-done | bytes 2097184 | tf_op jit(solution)/shard_map/all_to_all | solution.py:255
  68.3 1.1 collective-permute-start.18
  69.4 9.4 %collective-permute-done.8.refs_3_ = bf16[512,512]{1,0:T(8,128)(2,1)} collective-permute-done((bf16[512,512]{1,0:T(8,128)(2,1)}, bf16[512,512]{1,0:T(8,128)(2,1)}, u32[]{:S(2)}, u32[]{:S(2)}) %collective-permute-start.8) | collective-permute-done | bytes 524320 | tf_op jit(solution)/shard_map/ppermute | solution.py:199
  78.8 2.7 %collective-permute-start.19 = (f32[64,512]{1,0:T(8,128)S(1)}, f32[64,512]{1,0:T(8,128)}, u32[]{:S(2)}, u32[]{:S(2)}) collective-permute-start(f32[64,512]{1,0:T(8,128)S(1)} %add_add_fusion.1), channel_id=1, source_target_pairs={{0,3},{1,0},{2,1},{3,2},{4,7},{5,4},{6,5},{7,6},{8,11},{9,8},{10,9... | collective-permute-start | bytes 393224 | tf_op jit(solution)/shard_map/ppermute | solution.py:199
  82.2 15.6 %shard_map.180 = (bf16[512,512]{1,0:T(8,128)(2,1)}, bf16[512,512]{1,0:T(8,128)(2,1)}, bf16[512,512]{1,0:T(8,128)(2,1)}, bf16[512,512]{1,0:T(8,128)(2,1)}, bf16[5...) custom-call(s32[4]{0:T(128)} %pad_add_fusion.where, ...), custom_call_target="tpu_custom_call" | custom-call | flops 1 | bytes 1 | tf_op jit(solution)/shard_map/pallas_call | solution.py:173
  97.9 1.3 collective-permute-start.22
  99.2 1.5 %collective-permute-start.21 = (bf16[512,512]{1,0:T(8,128)(2,1)}, bf16[512,512]{1,0:T(8,128)(2,1)}, u32[]{:S(2)}, u32[]{:S(2)}) collective-permute-start(bf16[512,512]{1,0:T(8,128)(2,1)} %get-tuple-element.50), channel_id=1, source_target_pairs={{0,12},{4,0},{8,4},{12,8},{1,13},{5,1},{9,5},{13,9},{2,14},{6,2},{... | collective-permute-start | bytes 1572872 | tf_op jit(solution)/shard_map/ppermute | solution.py:199
  101.1 0.7 collective-permute-start.25
  101.8 0.9 add_add_fusion
  102.9 1.5 %fusion.1 = bf16[512,512]{1,0:T(8,128)(2,1)S(1)} fusion(bf16[512,512]{1,0:T(8,128)(2,1)S(1)} %bitcast.44, bf16[512,512]{1,0:T(8,128)(2,1)} %multiply_convert_fusion.refs_1_), kind=kOutput, calls=%fused_computation.7 | convolution fusion | flops 268959744 | bytes 1572864 | tf_op jit(solution)/shard_map/dot_general | solution.py:299
  104.8 1.1 pad_maximum_fusion
  105.9 7.9 %all-to-all-start.2 = ((bf16[8,2,2,32,512]{4,3,2,1,0:T(8,128)(2,1)}), bf16[8,2,2,32,512]{4,3,2,1,0:T(8,128)(2,1)S(1)}, u32[]{:S(2)}, u32[]{:S(2)}) async-start(bf16[8,2,2,32,512]{4,3,2,1,0:T(8,128)(2,1)} %pad_maximum_fusion), calls=%async_computation.2 | async-start | bytes 2097152 | tf_op jit(solution)/shard_map/all_to_all | solution.py:307
  114.8 1.1 collective-permute-start.24
  115.8 1.5 %convert_add_fusion = (f32[512,512]{1,0:T(8,128)S(1)}, f32[512,512]{1,0:T(8,128)S(1)}) fusion(f32[512,512]{1,0:T(8,128)S(1)} %convolution_multiply_fusion.2, bf16[512,512]{1,0:T(8,128)(2,1)} %get-tuple-element.53, f32[512,512]{1,0:T(8,128)S(1)} %convolution_multiply_fusion.3, bf16[512,512]{1,0:T(8,128)(2,1)} %get-tuple-element.48), kind=kLoop, calls=%fused_computation.12 | loop fusion | flops 1048576 | bytes 5242880 | tf_op jit(solution)/shard_map/add | solution.py:324
  117.3 7.0 %collective-permute-done.22 = bf16[512,512]{1,0:T(8,128)(2,1)} collective-permute-done((bf16[512,512]{1,0:T(8,128)(2,1)}, bf16[512,512]{1,0:T(8,128)(2,1)}, u32[]{:S(2)}, u32[]{:S(2)}) %collective-permute-start.22) | collective-permute-done | bytes 524320 | tf_op jit(solution)/shard_map/ppermute | solution.py:199
  124.4 2.4 %add_convert_fusion.1 = bf16[512,512]{1,0:T(8,128)(2,1)} fusion(bf16[512,512]{1,0:T(8,128)(2,1)} %collective-permute-done.23, bf16[512,512]{1,0:T(8,128)(2,1)} %collective-permute-done.22, f32[512,512]{1,0:T(8,128)S(1)} %get-tuple-element.89, bf16[512,512]{1,0:T(8,128)(2,1)} %collective-permute-done.21), kind=kLoop, calls=%fused_computation.13 | loop fusion | flops 1835008 | bytes 3145728 | tf_op jit(solution)/shard_map/convert_element_type | solution.py:333
  126.8 2.1 %all-to-all-done.2 = bf16[8,2,2,32,512]{4,3,2,1,0:T(8,128)(2,1)S(1)} async-done(((bf16[8,2,2,32,512]{4,3,2,1,0:T(8,128)(2,1)}), bf16[8,2,2,32,512]{4,3,2,1,0:T(8,128)(2,1)S(1)}, u32[]{:S(2)}, u32[]{:S(2)}) %all-to-all-start.2) | async-done | bytes 1048608 | tf_op jit(solution)/shard_map/all_to_all | solution.py:307
  128.9 1.0 copy-done.1
  129.9 5.9 %shard_map.181 = (bf16[16,32,512]{2,1,0:T(8,128)(2,1)}, bf16[16,32,512]{2,1,0:T(8,128)(2,1)}, f32[16,32,512]{2,1,0:T(8,128)}, f32[16,32,512]{2,1,0:T(8,128)}, f3...) custom-call(s32[16]{0:T(128)} %get-tuple-element.54.pos, bf16[16,2,32,512]{3,2,1,0:T(8,128)(2,1)} %bitcast.43, ...), custom_call_target="tpu_custom_call" | custom-call | flops 1 | bytes 1 | tf_op jit(solution)/shard_map/pallas_call | solution.py:93
  135.8 2.3 %add_convert_fusion = bf16[512,512]{1,0:T(8,128)(2,1)} fusion(bf16[512,512]{1,0:T(8,128)(2,1)} %collective-permute-done.26, bf16[512,512]{1,0:T(8,128)(2,1)} %collective-permute-done.25, f32[512,512]{1,0:T(8,128)S(1)} %get-tuple-element.62, bf16[512,512]{1,0:T(8,128)(2,1)S(1)} %collective-permute-done.24), kind=kLoop, calls=%fused_computation.11 | loop fusion | flops 1835008 | bytes 3145728 | tf_op jit(solution)/shard_map/convert_element_type | solution.py:333
  (69 shorter events, 7.4 us)
Async XLA Ops:
  0.6 37.5 %copy-start.8 = (bf16[512,512]{1,0:T(8,128)(2,1)S(1)}, bf16[512,512]{1,0:T(8,128)(2,1)}, u32[]{:S(2)}) copy-start(bf16[512,512]{1,0:T(8,128)(2,1)} %param.12) | copy-start | bytes 1572868
  2.2 24.3 %collective-permute-start.2 = (bf16[256,512]{1,0:T(8,128)(2,1)S(1)}, bf16[256,512]{1,0:T(8,128)(2,1)}, u32[]{:S(2)}, u32[]{:S(2)}) collective-permute-start(bf16[256,512]{1,0:T(8,128)(2,1)S(1)} %get-tuple-element.77), channel_id=1, source_target_pairs={{0,12},{4,0},{8,4},{12,8},{1,13},{5,1},{9,5},{13,9},{2,14},{6,2},{... | collective-permute-start | bytes 786440 | tf_op jit(solution)/shard_map/ppermute | solution.py:199
  6.9 19.7 %collective-permute-start.1 = (bf16[256,512]{1,0:T(8,128)(2,1)S(1)}, bf16[256,512]{1,0:T(8,128)(2,1)}, u32[]{:S(2)}, u32[]{:S(2)}) collective-permute-start(bf16[256,512]{1,0:T(8,128)(2,1)S(1)} %get-tuple-element.78), channel_id=1, source_target_pairs={{0,8},{4,12},{8,0},{12,4},{1,9},{5,13},{9,1},{13,5},{2,10},{6,14},... | collective-permute-start | bytes 786440 | tf_op jit(solution)/shard_map/ppermute | solution.py:199
  6.9 19.7 %collective-permute-start = (bf16[256,512]{1,0:T(8,128)(2,1)S(1)}, bf16[256,512]{1,0:T(8,128)(2,1)}, u32[]{:S(2)}, u32[]{:S(2)}) collective-permute-start(bf16[256,512]{1,0:T(8,128)(2,1)S(1)} %get-tuple-element.79), channel_id=1, source_target_pairs={{0,4},{4,8},{8,12},{12,0},{1,5},{5,9},{9,13},{13,1},{2,6},{6,10},{... | collective-permute-start | bytes 786440 | tf_op jit(solution)/shard_map/ppermute | solution.py:199
  12.6 25.5 %all-to-all-start = ((bf16[8,2,2,32,512]{4,3,2,1,0:T(8,128)(2,1)}), bf16[8,2,2,32,512]{4,3,2,1,0:T(8,128)(2,1)S(1)}, u32[]{:S(2)}, u32[]{:S(2)}) async-start(bf16[8,2,2,32,512]{4,3,2,1,0:T(8,128)(2,1)} %bitcast.52), calls=%async_computation | async-start | bytes 2097152 | tf_op jit(solution)/shard_map/all_to_all | solution.py:252
  18.5 11.3 %collective-permute-start.3 = (bf16[256,512]{1,0:T(8,128)(2,1)S(1)}, bf16[256,512]{1,0:T(8,128)(2,1)S(1)}, u32[]{:S(2)}, u32[]{:S(2)}) collective-permute-start(bf16[256,512]{1,0:T(8,128)(2,1)S(1)} %get-tuple-element.76), channel_id=1, source_target_pairs={{0,4},{4,8},{8,12},{12,0},{1,5},{5,9},{9,13},{13,1},{2,6},{6,10},{... | collective-permute-start | bytes 786440 | tf_op jit(solution)/shard_map/ppermute | solution.py:199
  20.5 9.3 %collective-permute-start.4 = (bf16[256,512]{1,0:T(8,128)(2,1)S(1)}, bf16[256,512]{1,0:T(8,128)(2,1)}, u32[]{:S(2)}, u32[]{:S(2)}) collective-permute-start(bf16[256,512]{1,0:T(8,128)(2,1)S(1)} %get-tuple-element.75), channel_id=1, source_target_pairs={{0,12},{4,0},{8,4},{12,8},{1,13},{5,1},{9,5},{13,9},{2,14},{6,2},{... | collective-permute-start | bytes 786440 | tf_op jit(solution)/shard_map/ppermute | solution.py:199
  26.6 8.9 %collective-permute-start.5 = (bf16[256,512]{1,0:T(8,128)(2,1)S(1)}, bf16[256,512]{1,0:T(8,128)(2,1)S(1)}, u32[]{:S(2)}, u32[]{:S(2)}) collective-permute-start(bf16[256,512]{1,0:T(8,128)(2,1)S(1)} %get-tuple-element.44), channel_id=1, source_target_pairs={{0,8},{4,12},{8,0},{12,4},{1,9},{5,13},{9,1},{13,5},{2,10},{6,14},... | collective-permute-start | bytes 786440 | tf_op jit(solution)/shard_map/ppermute | solution.py:199
  29.8 22.2 %collective-permute-start.9 = (bf16[3,256,512]{2,1,0:T(8,128)(2,1)}, bf16[3,256,512]{2,1,0:T(8,128)(2,1)}, u32[]{:S(2)}, u32[]{:S(2)}) collective-permute-start(bf16[3,256,512]{2,1,0:T(8,128)(2,1)} %pad_maximum_fusion.1.refs_5_), channel_id=1, source_target_pairs={{0,32},{32,64},{64,96},{96,0},{1,33},{33,65},{65,97},{97,1},{2,34}... | collective-permute-start | bytes 2359304 | tf_op jit(solution)/shard_map/ppermute | solution.py:199
  31.2 21.7 %collective-permute-start.10 = (bf16[3,256,512]{2,1,0:T(8,128)(2,1)}, bf16[3,256,512]{2,1,0:T(8,128)(2,1)}, u32[]{:S(2)}, u32[]{:S(2)}) collective-permute-start(bf16[3,256,512]{2,1,0:T(8,128)(2,1)} %pad_maximum_fusion.1.refs_5_), channel_id=1, source_target_pairs={{0,96},{32,0},{64,32},{96,64},{1,97},{33,1},{65,33},{97,65},{2,98}... | collective-permute-start | bytes 2359304 | tf_op jit(solution)/shard_map/ppermute | solution.py:199
  32.5 32.4 %collective-permute-start.11 = (bf16[3,256,512]{2,1,0:T(8,128)(2,1)}, bf16[3,256,512]{2,1,0:T(8,128)(2,1)}, u32[]{:S(2)}, u32[]{:S(2)}) collective-permute-start(bf16[3,256,512]{2,1,0:T(8,128)(2,1)} %pad_maximum_fusion.1.refs_5_), channel_id=1, source_target_pairs={{0,16},{16,0},{1,17},{17,1},{2,18},{18,2},{3,19},{19,3},{4,20},{20... | collective-permute-start | bytes 2359304 | tf_op jit(solution)/shard_map/ppermute | solution.py:246
  35.4 4.2 %copy-start.10 = (bf16[256,512]{1,0:T(8,128)(2,1)}, bf16[256,512]{1,0:T(8,128)(2,1)S(1)}, u32[]{:S(2)}) copy-start(bf16[256,512]{1,0:T(8,128)(2,1)S(1)} %collective-permute-done.5) | copy-start | bytes 786436
  35.4 13.5 %collective-permute-start.6 = (bf16[512,512]{1,0:T(8,128)(2,1)}, bf16[512,512]{1,0:T(8,128)(2,1)}, u32[]{:S(2)}, u32[]{:S(2)}) collective-permute-start(bf16[512,512]{1,0:T(8,128)(2,1)} %multiply_convert_fusion.refs_1_), channel_id=1, source_target_pairs={{0,4},{4,8},{8,12},{12,0},{1,5},{5,9},{9,13},{13,1},{2,6},{6,10},{... | collective-permute-start | bytes 1572872 | tf_op jit(solution)/shard_map/ppermute | solution.py:199
  36.3 13.0 %collective-permute-start.7 = (bf16[512,512]{1,0:T(8,128)(2,1)}, bf16[512,512]{1,0:T(8,128)(2,1)}, u32[]{:S(2)}, u32[]{:S(2)}) collective-permute-start(bf16[512,512]{1,0:T(8,128)(2,1)} %multiply_convert_fusion.refs_1_), channel_id=1, source_target_pairs={{0,12},{4,0},{8,4},{12,8},{1,13},{5,1},{9,5},{13,9},{2,14},{6,2},{... | collective-permute-start | bytes 1572872 | tf_op jit(solution)/shard_map/ppermute | solution.py:199
  39.6 28.3 %all-to-all-start.1 = ((bf16[4,512,512]{2,1,0:T(8,128)(2,1)}), bf16[4,512,512]{2,1,0:T(8,128)(2,1)S(1)}, u32[]{:S(2)}, u32[]{:S(2)}) async-start(bf16[4,512,512]{2,1,0:T(8,128)(2,1)} %broadcast_in_dim.13), calls=%async_computation.1 | async-start | bytes 4194304 | tf_op jit(solution)/shard_map/all_to_all | solution.py:255
  45.0 20.0 %copy-start.2 = (bf16[3,256,512]{2,1,0:T(8,128)(2,1)}, bf16[3,256,512]{2,1,0:T(8,128)(2,1)S(1)}, u32[]{:S(2)}) copy-start(bf16[3,256,512]{2,1,0:T(8,128)(2,1)S(1)} %pad_maximum_fusion.2.refs_7_) | copy-start | bytes 2359300
  45.1 19.8 %copy-start.3 = (bf16[8,2,1,32,512]{4,3,2,1,0:T(8,128)(2,1)}, bf16[8,2,1,32,512]{4,3,2,1,0:T(8,128)(2,1)S(1)}, u32[]{:S(2)}) copy-start(bf16[8,2,1,32,512]{4,3,2,1,0:T(8,128)(2,1)S(1)} %get-tuple-element.81) | copy-start | bytes 1572868
  45.1 19.8 %copy-start.5 = (bf16[8,2,1,32,512]{4,3,2,1,0:T(8,128)(2,1)}, bf16[8,2,1,32,512]{4,3,2,1,0:T(8,128)(2,1)S(1)}, u32[]{:S(2)}) copy-start(bf16[8,2,1,32,512]{4,3,2,1,0:T(8,128)(2,1)S(1)} %get-tuple-element.80) | copy-start | bytes 1572868
  49.0 5.3 %collective-permute-start.17 = (f32[64,512]{1,0:T(8,128)S(1)}, f32[64,512]{1,0:T(8,128)S(1)}, u32[]{:S(2)}, u32[]{:S(2)}) collective-permute-start(f32[64,512]{1,0:T(8,128)S(1)} %pad_maximum_fusion.3), channel_id=1, source_target_pairs={{0,8},{4,12},{8,0},{12,4},{1,9},{5,13},{9,1},{13,5},{2,10},{6,14},... | collective-permute-start | bytes 393224 | tf_op jit(solution)/shard_map/ppermute | solution.py:199
  49.3 15.6 %collective-permute-start.13 = (bf16[3,256,512]{2,1,0:T(8,128)(2,1)S(1)}, bf16[3,256,512]{2,1,0:T(8,128)(2,1)S(1)}, u32[]{:S(2)}, u32[]{:S(2)}) collective-permute-start(bf16[3,256,512]{2,1,0:T(8,128)(2,1)S(1)} %pad_maximum_fusion.2.refs_7_), channel_id=1, source_target_pairs={{0,16},{16,0},{1,17},{17,1},{2,18},{18,2},{3,19},{19,3},{4,20},{20... | collective-permute-start | bytes 2359304 | tf_op jit(solution)/shard_map/ppermute | solution.py:246
  52.0 8.2 %collective-permute-start.15 = (f32[64,512]{1,0:T(8,128)S(1)}, f32[64,512]{1,0:T(8,128)S(1)}, u32[]{:S(2)}, u32[]{:S(2)}) collective-permute-start(f32[64,512]{1,0:T(8,128)S(1)} %pad_maximum_fusion.3), channel_id=1, source_target_pairs={{0,4},{4,8},{8,12},{12,0},{1,5},{5,9},{9,13},{13,1},{2,6},{6,10},{... | collective-permute-start | bytes 393224 | tf_op jit(solution)/shard_map/ppermute | solution.py:199
  52.9 29.3 %collective-permute-start.12 = (bf16[3,256,512]{2,1,0:T(8,128)(2,1)}, bf16[3,256,512]{2,1,0:T(8,128)(2,1)}, u32[]{:S(2)}, u32[]{:S(2)}) collective-permute-start(bf16[3,256,512]{2,1,0:T(8,128)(2,1)} %collective-permute-done.9.refs_6_), channel_id=1, source_target_pairs={{0,16},{16,0},{1,17},{17,1},{2,18},{18,2},{3,19},{19,3},{4,20},{20... | collective-permute-start | bytes 2359304 | tf_op jit(solution)/shard_map/ppermute | solution.py:246
  54.3 27.9 %collective-permute-start.14 = (bf16[3,256,512]{2,1,0:T(8,128)(2,1)}, bf16[3,256,512]{2,1,0:T(8,128)(2,1)}, u32[]{:S(2)}, u32[]{:S(2)}) collective-permute-start(bf16[3,256,512]{2,1,0:T(8,128)(2,1)} %collective-permute-done.10.refs_8_), channel_id=1, source_target_pairs={{0,16},{16,0},{1,17},{17,1},{2,18},{18,2},{3,19},{19,3},{4,20},{20... | collective-permute-start | bytes 2359304 | tf_op jit(solution)/shard_map/ppermute | solution.py:246
  60.2 4.7 %collective-permute-start.16 = (f32[64,512]{1,0:T(8,128)S(1)}, f32[64,512]{1,0:T(8,128)S(1)}, u32[]{:S(2)}, u32[]{:S(2)}) collective-permute-start(f32[64,512]{1,0:T(8,128)S(1)} %pad_maximum_fusion.3), channel_id=1, source_target_pairs={{0,12},{4,0},{8,4},{12,8},{1,13},{5,1},{9,5},{13,9},{2,14},{6,2},{... | collective-permute-start | bytes 393224 | tf_op jit(solution)/shard_map/ppermute | solution.py:199
  64.8 14.0 %collective-permute-start.8 = (bf16[512,512]{1,0:T(8,128)(2,1)}, bf16[512,512]{1,0:T(8,128)(2,1)}, u32[]{:S(2)}, u32[]{:S(2)}) collective-permute-start(bf16[512,512]{1,0:T(8,128)(2,1)} %multiply_convert_fusion.refs_1_), channel_id=1, source_target_pairs={{0,8},{4,12},{8,0},{12,4},{1,9},{5,13},{9,1},{13,5},{2,10},{6,14},... | collective-permute-start | bytes 1572872 | tf_op jit(solution)/shard_map/ppermute | solution.py:199
  64.9 17.3 %copy-start.7 = (bf16[3,256,512]{2,1,0:T(8,128)(2,1)}, bf16[3,256,512]{2,1,0:T(8,128)(2,1)S(1)}, u32[]{:S(2)}) copy-start(bf16[3,256,512]{2,1,0:T(8,128)(2,1)S(1)} %collective-permute-done.13.refs_11_) | copy-start | bytes 2359300
  67.9 14.3 %copy-start = (bf16[4,512,512]{2,1,0:T(8,128)(2,1)}, bf16[4,512,512]{2,1,0:T(8,128)(2,1)S(1)}, u32[]{:S(2)}) copy-start(bf16[4,512,512]{2,1,0:T(8,128)(2,1)S(1)} %all-to-all-done.1.refs_0_) | copy-start | bytes 6291460
  67.9 31.2 %collective-permute-start.20 = (f32[64,512]{1,0:T(8,128)S(1)}, f32[64,512]{1,0:T(8,128)S(1)}, u32[]{:S(2)}, u32[]{:S(2)}) collective-permute-start(f32[64,512]{1,0:T(8,128)S(1)} %add_add_fusion.1), channel_id=1, source_target_pairs={{0,2},{1,3},{2,0},{3,1},{4,6},{5,7},{6,4},{7,5},{8,10},{9,11},{10,... | collective-permute-start | bytes 393224 | tf_op jit(solution)/shard_map/ppermute | solution.py:199
  68.3 32.4 %collective-permute-start.18 = (f32[64,512]{1,0:T(8,128)S(1)}, f32[64,512]{1,0:T(8,128)S(1)}, u32[]{:S(2)}, u32[]{:S(2)}) collective-permute-start(f32[64,512]{1,0:T(8,128)S(1)} %add_add_fusion.1), channel_id=1, source_target_pairs={{0,1},{1,2},{2,3},{3,0},{4,5},{5,6},{6,7},{7,4},{8,9},{9,10},{10,1... | collective-permute-start | bytes 393224 | tf_op jit(solution)/shard_map/ppermute | solution.py:199
  78.8 22.2 %collective-permute-start.19 = (f32[64,512]{1,0:T(8,128)S(1)}, f32[64,512]{1,0:T(8,128)}, u32[]{:S(2)}, u32[]{:S(2)}) collective-permute-start(f32[64,512]{1,0:T(8,128)S(1)} %add_add_fusion.1), channel_id=1, source_target_pairs={{0,3},{1,0},{2,1},{3,2},{4,7},{5,4},{6,5},{7,6},{8,11},{9,8},{10,9... | collective-permute-start | bytes 393224 | tf_op jit(solution)/shard_map/ppermute | solution.py:199
  82.2 22.1 %copy-start.9 = (bf16[512,512]{1,0:T(8,128)(2,1)S(1)}, bf16[512,512]{1,0:T(8,128)(2,1)}, u32[]{:S(2)}) copy-start(bf16[512,512]{1,0:T(8,128)(2,1)} %param.12) | copy-start | bytes 1572868
  97.8 16.0 %copy-start.6 = (bf16[8,2,1,32,512]{4,3,2,1,0:T(8,128)(2,1)S(1)}, bf16[8,2,1,32,512]{4,3,2,1,0:T(8,128)(2,1)}, u32[]{:S(2)}) copy-start(bf16[8,2,1,32,512]{4,3,2,1,0:T(8,128)(2,1)} %copy-done.5) | copy-start | bytes 1572868
  97.8 16.5 %copy-start.4 = (bf16[8,2,1,32,512]{4,3,2,1,0:T(8,128)(2,1)S(1)}, bf16[8,2,1,32,512]{4,3,2,1,0:T(8,128)(2,1)}, u32[]{:S(2)}) copy-start(bf16[8,2,1,32,512]{4,3,2,1,0:T(8,128)(2,1)} %copy-done.3) | copy-start | bytes 1572868
  97.8 16.9 %collective-permute-start.23 = (bf16[512,512]{1,0:T(8,128)(2,1)}, bf16[512,512]{1,0:T(8,128)(2,1)}, u32[]{:S(2)}, u32[]{:S(2)}) collective-permute-start(bf16[512,512]{1,0:T(8,128)(2,1)} %get-tuple-element.52), channel_id=1, source_target_pairs={{0,8},{4,12},{8,0},{12,4},{1,9},{5,13},{9,1},{13,5},{2,10},{6,14},... | collective-permute-start | bytes 1572872 | tf_op jit(solution)/shard_map/ppermute | solution.py:199
  97.9 26.5 %collective-permute-start.22 = (bf16[512,512]{1,0:T(8,128)(2,1)}, bf16[512,512]{1,0:T(8,128)(2,1)}, u32[]{:S(2)}, u32[]{:S(2)}) collective-permute-start(bf16[512,512]{1,0:T(8,128)(2,1)} %get-tuple-element.51), channel_id=1, source_target_pairs={{0,4},{4,8},{8,12},{12,0},{1,5},{5,9},{9,13},{13,1},{2,6},{6,10},{... | collective-permute-start | bytes 1572872 | tf_op jit(solution)/shard_map/ppermute | solution.py:199
  99.2 25.2 %collective-permute-start.21 = (bf16[512,512]{1,0:T(8,128)(2,1)}, bf16[512,512]{1,0:T(8,128)(2,1)}, u32[]{:S(2)}, u32[]{:S(2)}) collective-permute-start(bf16[512,512]{1,0:T(8,128)(2,1)} %get-tuple-element.50), channel_id=1, source_target_pairs={{0,12},{4,0},{8,4},{12,8},{1,13},{5,1},{9,5},{13,9},{2,14},{6,2},{... | collective-permute-start | bytes 1572872 | tf_op jit(solution)/shard_map/ppermute | solution.py:199
  100.7 35.1 %collective-permute-start.26 = (bf16[512,512]{1,0:T(8,128)(2,1)}, bf16[512,512]{1,0:T(8,128)(2,1)}, u32[]{:S(2)}, u32[]{:S(2)}) collective-permute-start(bf16[512,512]{1,0:T(8,128)(2,1)} %get-tuple-element.65), channel_id=1, source_target_pairs={{0,2},{1,3},{2,0},{3,1},{4,6},{5,7},{6,4},{7,5},{8,10},{9,11},{10,... | collective-permute-start | bytes 1572872 | tf_op jit(solution)/shard_map/ppermute | solution.py:199
  101.1 34.7 %collective-permute-start.25 = (bf16[512,512]{1,0:T(8,128)(2,1)}, bf16[512,512]{1,0:T(8,128)(2,1)}, u32[]{:S(2)}, u32[]{:S(2)}) collective-permute-start(bf16[512,512]{1,0:T(8,128)(2,1)} %get-tuple-element.64), channel_id=1, source_target_pairs={{0,3},{1,0},{2,1},{3,2},{4,7},{5,4},{6,5},{7,6},{8,11},{9,8},{10,9... | collective-permute-start | bytes 1572872 | tf_op jit(solution)/shard_map/ppermute | solution.py:199
  105.9 23.0 %all-to-all-start.2 = ((bf16[8,2,2,32,512]{4,3,2,1,0:T(8,128)(2,1)}), bf16[8,2,2,32,512]{4,3,2,1,0:T(8,128)(2,1)S(1)}, u32[]{:S(2)}, u32[]{:S(2)}) async-start(bf16[8,2,2,32,512]{4,3,2,1,0:T(8,128)(2,1)} %pad_maximum_fusion), calls=%async_computation.2 | async-start | bytes 2097152 | tf_op jit(solution)/shard_map/all_to_all | solution.py:307
  114.8 21.1 %collective-permute-start.24 = (bf16[512,512]{1,0:T(8,128)(2,1)}, bf16[512,512]{1,0:T(8,128)(2,1)S(1)}, u32[]{:S(2)}, u32[]{:S(2)}) collective-permute-start(bf16[512,512]{1,0:T(8,128)(2,1)} %get-tuple-element.63), channel_id=1, source_target_pairs={{0,1},{1,2},{2,3},{3,0},{4,5},{5,6},{6,7},{7,4},{8,9},{9,10},{10,1... | collective-permute-start | bytes 1572872 | tf_op jit(solution)/shard_map/ppermute | solution.py:199
  128.9 1.0 copy-start.1
